TPU v7x, 32 devices: a whole 2x2x4 slice. The times are simulated.
32 devices in a mesh: pipe: 2 (over x), dp: 4 (over z), et: 4 (over y, core).
Axes of the slice: x: 2, y: 2, z: 4, core: 2. Of those that a mesh axis runs over, the one named last changes fastest.
Arguments:
- tokens: bfloat16 [2, 4, 64, 3072], P('pipe', 'dp', 'et'), may hold values from -6 to 6
- out_grad: bfloat16 [2, 4, 64, 3072], P('pipe', 'dp', 'et'), may hold values from -6 to 6
- top_ids: int32 [2, 4, 64, 4], P('pipe', 'dp', 'et'), may hold values from 0 to 15, as said below
- route_probs: float32 [2, 4, 64, 4], P('pipe', 'dp', 'et'), may hold values from 0.05 to 0.6
- w_gate: bfloat16 [2, 5376, 3072], P('pipe', ('dp', 'et')), may hold values from -0.109375 to 0.109375
- w_up: bfloat16 [2, 5376, 3072], P('pipe', ('dp', 'et')), may hold values from -0.109375 to 0.109375
- w_down: bfloat16 [2, 5376, 3072], P('pipe', ('dp', 'et')), may hold values from -0.078125 to 0.078125
Outputs:
- handed: bfloat16 [2, 4, 64, 3072], P('pipe', 'dp', 'et')
- grad_gate: bfloat16 [2, 5376, 3072], P('pipe', ('dp', 'et'))
- grad_up: bfloat16 [2, 5376, 3072], P('pipe', ('dp', 'et'))
- grad_down: bfloat16 [2, 5376, 3072], P('pipe', ('dp', 'et'))
Inputs may be any that keep to these rules, and one draw needn't show every extreme that they name: `top_ids`: each token names 4 distinct experts. In every group (one section's 64 tokens of one index of dp) at most 32 tokens name expert 0, and in every section some group has exactly 32; every group has at least one.
All inputs are finite; a program needn't handle non-finite values.
Results may differ from a plain program's by a relative error of at most 0.02.
Values may be sent and summed in bfloat16 or wider, within the bound.
No kernel may reach another device: no remote copies, remote signals or barrier semaphores. Data moves between devices by JAX's collectives and lax.ppermute only.
A program may use at most 64 MiB of HBM per device.

v0:
```python
import jax
import jax.numpy as jnp
from jax import lax
from jax.sharding import PartitionSpec as P


def from_behind(value, axis, steps):
    count = lax.axis_size(axis)
    pairs = [(source, (source + steps) % count) for source in range(count)]
    return lax.ppermute(value, axis, pairs)


def slot_layout(routed, capacity):
    flags = routed.astype(jnp.int32)
    position = jnp.cumsum(flags, axis=-1, dtype=jnp.int32) - 1
    slot_ids = jnp.arange(capacity, dtype=jnp.int32)
    matches = (position[:, None, :] == slot_ids[None, :, None]) & routed[:, None, :]
    token_ids = jnp.arange(routed.shape[-1], dtype=jnp.int32)
    source = jnp.sum(jnp.where(matches, token_ids[None, None, :], 0), axis=-1)
    filled = jnp.any(matches, axis=-1)
    return (source, filled, position)


def gather_slots(rows, source, filled):
    picked = jnp.take_along_axis(rows, source[:, :, None], axis=1)
    return jnp.where(filled[:, :, None], picked, jnp.zeros_like(picked))


def contract(left, right, left_dim, right_dim):
    return lax.dot_general(
        left, right, (((left_dim,), (right_dim,)), ((), ())), preferred_element_type=jnp.float32
    )


def on_device(tokens, out_grad, top_ids, route_probs, w_gate, w_up, w_down):
    tok_dev = tokens.shape[2]
    model_width = tokens.shape[3]
    et_size = lax.axis_size("et")
    dp_size = lax.axis_size("dp")
    group_tokens = tok_dev * et_size
    capacity = group_tokens // 2
    token_rows = tokens[0, 0]
    chosen = top_ids[0, 0] == 0
    routed_flag = jnp.any(chosen, axis=-1).astype(jnp.bfloat16)
    route_weight = jnp.sum(jnp.where(chosen, route_probs[0, 0], jnp.float32(0.0)), axis=-1)
    scaled_rows = (route_weight[:, None] * out_grad[0, 0].astype(jnp.float32)).astype(jnp.bfloat16)
    group_x, group_dz, group_flag = (
        lax.all_gather(token_rows, "et", axis=0, tiled=True),
        lax.all_gather(scaled_rows, "et", axis=0, tiled=True),
        lax.all_gather(routed_flag, "et", axis=0, tiled=True),
    )
    routed = group_flag[None, :] > 0
    source, filled, position = slot_layout(routed, capacity)
    own_x = gather_slots(group_x[None], source, filled)
    own_dz = gather_slots(group_dz[None], source, filled)
    all_x, all_dz = (
        lax.all_gather(own_x, "dp", axis=0, tiled=True),
        lax.all_gather(own_dz, "dp", axis=0, tiled=True),
    )
    own_position = position[0]
    own_routed = routed[0]
    slot_x = all_x.reshape(dp_size * capacity, model_width)
    slot_dz = all_dz.reshape(dp_size * capacity, model_width)
    gate_rows = w_gate[0]
    up_rows = w_up[0]
    down_rows = w_down[0]
    gate = contract(slot_x, gate_rows, 1, 1)
    upper = contract(slot_x, up_rows, 1, 1)
    sigmoid_gate = jax.nn.sigmoid(gate)
    silu_gate = gate * sigmoid_gate
    act = (silu_gate * upper).astype(jnp.bfloat16)
    act_grad = contract(slot_dz, down_rows, 1, 1)
    gate_grad = (act_grad * upper * sigmoid_gate * (1.0 + gate * (1.0 - sigmoid_gate))).astype(
        jnp.bfloat16
    )
    up_grad = (act_grad * silu_gate).astype(jnp.bfloat16)
    grad_down = contract(act, slot_dz, 0, 0).astype(jnp.bfloat16)
    grad_gate = contract(gate_grad, slot_x, 0, 0).astype(jnp.bfloat16)
    grad_up = contract(up_grad, slot_x, 0, 0).astype(jnp.bfloat16)
    hidden_terms = jnp.dot(gate_grad, gate_rows, preferred_element_type=jnp.float32) + jnp.dot(
        up_grad, up_rows, preferred_element_type=jnp.float32
    )
    rounded = lax.optimization_barrier(hidden_terms.astype(jnp.bfloat16)).astype(jnp.float32)
    rounded = rounded.reshape(dp_size, capacity, model_width)
    hidden_sum = lax.psum_scatter(
        rounded.astype(jnp.bfloat16), "et", scatter_dimension=1, tiled=True
    )
    group_sum = lax.psum_scatter(hidden_sum, "dp", scatter_dimension=0, tiled=True).astype(
        jnp.float32
    )
    slot_share = group_sum.astype(jnp.bfloat16)
    slot_grad = lax.all_gather(slot_share, "et", axis=1, tiled=True)[0]
    start = lax.axis_index("et") * tok_dev
    my_position = lax.dynamic_slice_in_dim(own_position, start, tok_dev)
    my_routed = lax.dynamic_slice_in_dim(own_routed, start, tok_dev)
    picked = jnp.take(slot_grad, jnp.maximum(my_position, 0), axis=0)
    input_grad = jnp.where(my_routed[:, None], picked, jnp.zeros_like(picked))
    handed = from_behind(input_grad[None, None], "pipe", -1)
    return (handed, grad_gate[None], grad_up[None], grad_down[None])


def solution(mesh):
    placed = (
        P("pipe", "dp", "et", None),
        P("pipe", "dp", "et", None),
        P("pipe", "dp", "et", None),
        P("pipe", "dp", "et", None),
        P("pipe", ("dp", "et"), None),
        P("pipe", ("dp", "et"), None),
        P("pipe", ("dp", "et"), None),
    )
    return jax.shard_map(
        on_device,
        mesh=mesh,
        in_specs=placed,
        out_specs=(
            P("pipe", "dp", "et", None),
            P("pipe", ("dp", "et"), None),
            P("pipe", ("dp", "et"), None),
            P("pipe", ("dp", "et"), None),
        ),
        check_vma=False,
    )
```

profile of v0, /device:TPU:0, one launch (start us, length us, event | category | flops | bytes accessed | tf_op | source)
XLA Modules:
  0.0 141.6 jit_solution(2367594462634154058)
XLA Ops:
  7.2 0.0 copy-start
  7.2 0.0 reduce-scatter.7.cloned.1.call-start
  7.2 0.9 select_reduce_fusion.1
  8.1 1.2 dynamic-slice.6
  10.0 0.2 dynamic-update-slice
  10.3 8.3 %all-reduce = bf16[64]{0:T(256)(128)(2,1)S(1)} all-reduce(bf16[64]{0:T(256)(128)(2,1)S(1)} %dynamic-update-slice), channel_id=1, replica_groups=mesh['pipe'=2,'dp'=4,'et'=4] {'et'}, use_global_device_ids=true, to_apply=%add | all-reduce | flops 64 | bytes 256
  18.6 0.2 reduce_window_sum.11
  18.9 0.1 select_reduce_fusion
  19.0 0.1 fusion.20
  19.1 1.0 fusion.13
  20.1 6.1 %all_gather.19 = bf16[64,3072]{1,0:T(8,128)(2,1)S(1)} all-gather(bf16[16,3072]{1,0:T(8,128)(2,1)S(1)} %fusion.13), channel_id=1, replica_groups=mesh['pipe'=2,'dp'=4,'et'=4] {'et'}, dimensions={0}, use_global_device_ids=true | all-gather | bytes 491520 | tf_op jit(solution)/shard_map/all_gather | solution.py:49
  26.3 6.8 %all-gather = bf16[1,1,64,3072]{3,2,1,0:T(8,128)(2,1)S(1)} all-gather(bf16[1,1,16,3072]{3,2,1,0:T(8,128)(2,1)} %param.9), channel_id=2, replica_groups=mesh['pipe'=2,'dp'=4,'et'=4] {'et'}, dimensions={2}, use_global_device_ids=true | all-gather | bytes 491520 | tf_op jit(solution)/shard_map/all_gather | solution.py:48
  33.1 0.7 gather_fusion.1
  33.7 0.7 gather_fusion.2
  34.4 0.1 fusion.15
  34.5 19.8 %all_gather.20 = bf16[4,32,3072]{2,1,0:T(8,128)(2,1)S(1)} all-gather(bf16[1,32,3072]{2,1,0:T(8,128)(2,1)S(1)} %get-tuple-element.9), channel_id=1, replica_groups=mesh['pipe'=2,'dp'=4,'et'=4] {'dp'}, dimensions={0}, use_global_device_ids=true | all-gather | bytes 983040 | tf_op jit(solution)/shard_map/all_gather | solution.py:58
  54.3 18.3 %all_gather.22 = bf16[4,32,3072]{2,1,0:T(8,128)(2,1)S(1)} all-gather(bf16[1,32,3072]{2,1,0:T(8,128)(2,1)S(1)} %get-tuple-element.10), channel_id=1, replica_groups=mesh['pipe'=2,'dp'=4,'et'=4] {'dp'}, dimensions={0}, use_global_device_ids=true | all-gather | bytes 983040 | tf_op jit(solution)/shard_map/all_gather | solution.py:57
  72.6 0.7 fusion.6
  73.3 0.0 copy-start.6
  73.3 0.7 fusion.9
  74.1 0.8 copy-done.6
  74.9 0.7 multiply_convert_fusion.1
  75.6 0.0 copy-start.4
  75.6 0.6 fusion.4
  76.3 0.6 fusion.3
  76.9 0.6 copy.11
  77.5 1.1 copy.13
  78.6 0.0 reduce-scatter.7.cloned.1.call-update
  78.7 0.0 reduce-scatter.5.cloned.1.call-start
  78.7 0.1 dynamic-slice.5
  78.8 0.1 fusion.23
  78.9 21.9 %reduce-scatter.7.cloned.1.call-done = bf16[8,12288]{1,0:T(8,128)(2,1)} async-done(((bf16[32,12288]{1,0:T(8,128)(2,1)}), bf16[8,12288]{1,0:T(8,128)(2,1)}) %reduce-scatter.7.cloned.1.call-update) | async-done | bytes 196624
  100.8 1.1 reshape.334
  101.9 0.7 copy.12
  102.6 0.0 reduce-scatter.5.cloned.1.call-update
  102.6 0.0 copy-start.3
  102.6 0.1 compare_bitcast_fusion
  102.7 2.0 %fusion.1 = bf16[1,336,3072]{2,1,0:T(8,128)(2,1)} fusion(bf16[128,336]{0,1:T(8,128)(2,1)S(1)} %get-tuple-element.7, bf16[128,3072]{1,0:T(8,128)(2,1)S(1)} %bitcast.81), kind=kOutput, calls=%fused_computation.7 | convolution fusion | flops 265273344 | bytes 2936832 | tf_op jit(solution)/shard_map/dot_general | solution.py:30
  104.7 2.0 %fusion.2 = bf16[1,336,3072]{2,1,0:T(8,128)(2,1)} fusion(bf16[128,3072]{1,0:T(8,128)(2,1)S(1)} %bitcast.89, f32[128,336]{0,1:T(8,128)S(1)} %fusion.9, f32[128,336]{0,1:T(8,128)S(1)} %fusion.6), kind=kOutput, calls=%fused_computation.8 | convolution fusion | flops 265531392 | bytes 3194880 | tf_op jit(solution)/shard_map/dot_general | solution.py:30
  106.7 15.8 %reduce-scatter.5.cloned.1.call-done = bf16[1,8,3072]{2,1,0:T(8,128)(2,1)} async-done(((bf16[4,8,3072]{2,1,0:T(8,128)(2,1)}), bf16[1,8,3072]{2,1,0:T(8,128)(2,1)}) %reduce-scatter.5.cloned.1.call-update) | async-done | bytes 49168 | tf_op jit(solution)/shard_map/reduce_scatter | solution.py:88
  122.5 5.8 %all_gather.23 = bf16[1,32,3072]{2,1,0:T(8,128)(2,1)S(1)} all-gather(bf16[1,8,3072]{2,1,0:T(8,128)(2,1)} %reduce-scatter.5.cloned.1.call-done), channel_id=1, replica_groups=mesh['pipe'=2,'dp'=4,'et'=4] {'et'}, dimensions={1}, use_global_device_ids=true | all-gather | bytes 245760 | tf_op jit(solution)/shard_map/all_gather | solution.py:92
  128.3 0.6 gather_fusion
  129.0 0.1 fusion.17
  129.0 1.5 %collective-permute-start = (bf16[1,1,16,3072]{3,2,1,0:T(8,128)(2,1)S(1)}, bf16[1,1,16,3072]{3,2,1,0:T(8,128)(2,1)S(1)}, u32[]{:S(2)}, u32[]{:S(2)}) collective-permute-start(bf16[1,1,16,3072]{3,2,1,0:T(8,128)(2,1)S(1)} %fusion.17), channel_id=1, source_target_pairs={{0,16},{16,0},{1,17},{17,1},{2,18},{18,2},{3,19},{19,3},{4,20},{20... | collective-permute-start | bytes 294920 | tf_op jit(solution)/shard_map/ppermute | solution.py:10
  130.6 0.0 copy-done.5
  130.6 2.0 %fusion = bf16[1,336,3072]{2,1,0:T(8,128)(2,1)} fusion(bf16[128,336]{0,1:T(8,128)(2,1)S(1)} %copy-done.5, bf16[128,3072]{1,0:T(8,128)(2,1)S(1)} %bitcast.82), kind=kOutput, calls=%fused_computation.6 | convolution fusion | flops 265273344 | bytes 2936832 | tf_op jit(solution)/shard_map/dot_general | solution.py:30
  132.6 1.6 %collective-permute-done = bf16[1,1,16,3072]{3,2,1,0:T(8,128)(2,1)S(1)} collective-permute-done((bf16[1,1,16,3072]{3,2,1,0:T(8,128)(2,1)S(1)}, bf16[1,1,16,3072]{3,2,1,0:T(8,128)(2,1)S(1)}, u32[]{:S(2)}, u32[]{:S(2)}) %collective-permute-start) | collective-permute-done | bytes 98336 | tf_op jit(solution)/shard_map/ppermute | solution.py:10
  134.1 0.6 copy.16
  (17 shorter events, 0.1 us)
Async XLA Ops:
  7.2 65.5 %copy-start = (bf16[1,336,3072]{2,1,0:T(8,128)(2,1)S(1)}, bf16[1,336,3072]{2,1,0:T(8,128)(2,1)}, u32[]{:S(2)}) copy-start(bf16[1,336,3072]{2,1,0:T(8,128)(2,1)} %param.13) | copy-start | bytes 6193156
  7.2 93.6 %reduce-scatter.7.cloned.1.call-start = ((), (), s32[]{:S(2)}) async-start(), calls=%async_computation.3 | async-start | bytes 983040
  54.3 19.8 %copy-start.2 = (bf16[4,32,3072]{2,1,0:T(8,128)(2,1)}, bf16[4,32,3072]{2,1,0:T(8,128)(2,1)S(1)}, u32[]{:S(2)}) copy-start(bf16[4,32,3072]{2,1,0:T(8,128)(2,1)S(1)} %all_gather.20) | copy-start | bytes 2359300
  54.3 19.0 %copy-start.1 = (bf16[1,336,3072]{2,1,0:T(8,128)(2,1)S(1)}, bf16[1,336,3072]{2,1,0:T(8,128)(2,1)}, u32[]{:S(2)}) copy-start(bf16[1,336,3072]{2,1,0:T(8,128)(2,1)} %param.14) | copy-start | bytes 6193156
  73.3 1.6 %copy-start.6 = (bf16[1,336,3072]{2,1,0:T(8,128)(2,1)S(1)}, bf16[1,336,3072]{2,1,0:T(8,128)(2,1)}, u32[]{:S(2)}) copy-start(bf16[1,336,3072]{2,1,0:T(8,128)(2,1)} %param.15) | copy-start | bytes 6193156
  75.6 1.3 copy-start.4
  78.7 43.9 %reduce-scatter.5.cloned.1.call-start = ((), (), s32[]{:S(2)}) async-start(), calls=%async_computation.2 | async-start | bytes 245760 | tf_op jit(solution)/shard_map/reduce_scatter | solution.py:88
  102.6 2.1 %copy-start.3 = (bf16[4,32,3072]{2,1,0:T(8,128)(2,1)S(1)}, bf16[4,32,3072]{2,1,0:T(8,128)(2,1)}, u32[]{:S(2)}) copy-start(bf16[4,32,3072]{2,1,0:T(8,128)(2,1)} %copy-done.2) | copy-start | bytes 2359300
  104.7 25.9 %copy-start.5 = (bf16[128,336]{0,1:T(8,128)(2,1)S(1)}, bf16[128,336]{0,1:T(8,128)(2,1)}, u32[]{:S(2)}) copy-start(bf16[128,336]{0,1:T(8,128)(2,1)} %copy-done.4) | copy-start | bytes 258052
  129.0 5.1 %collective-permute-start = (bf16[1,1,16,3072]{3,2,1,0:T(8,128)(2,1)S(1)}, bf16[1,1,16,3072]{3,2,1,0:T(8,128)(2,1)S(1)}, u32[]{:S(2)}, u32[]{:S(2)}) collective-permute-start(bf16[1,1,16,3072]{3,2,1,0:T(8,128)(2,1)S(1)} %fusion.17), channel_id=1, source_target_pairs={{0,16},{16,0},{1,17},{17,1},{2,18},{18,2},{3,19},{19,3},{4,20},{20... | collective-permute-start | bytes 294920 | tf_op jit(solution)/shard_map/ppermute | solution.py:10
Sparse Core Ops, SparseCore 0:
  78.8 21.9 reduce-scatter.6
  103.1 19.3 reduce-scatter.4
where the time goes:
time: 142 us
  blocking collectives  65.2 us (46%)
  waiting for transfers between devices  39.3 us (28%)
  between operations  14.9 us (10%)
  matrix products  9.35 us (7%)
  local copies, waits for them, and re-layouts  8.55 us (6%)
  other arithmetic  2.73 us (2%)
  starting transfers between devices  1.63 us (1%)
    unnamed x3, waiting for transfers between devices  22 us
    all_gather x1, blocking collectives, on_device(): lax.all_gather(own_dz, 'dp', axis=0, tiled=True)  19.8 us
    all_gather x1, blocking collectives, on_device(): lax.all_gather(own_x, 'dp', axis=0, tiled=True)  18.3 us
    reduce_scatter x1, waiting for transfers between devices, on_device(): lax.psum_scatter(hidden_sum, 'dp', scatter_dimension=0, tiled=True)  15.8 us
    unnamed x1, blocking collectives  8.34 us
    dot_general x6, matrix products, contract(): lax.dot_general(left, right, (((left_dim,), (right_dim,)), ((), ())), pre...  8.11 us
    all_gather x1, blocking collectives, on_device(): lax.all_gather(token_rows, 'et', axis=0, tiled=True)  6.77 us
    unnamed x22, local copies, waits for them, and re-layouts  6.53 us
  transfers between devices with their start and end apart: 3, of which 3 were waited for; matrix products, arithmetic and copies ran while one was open for 4% of the time, Pallas kernels for 0%

commit v1 on v0

--- a/solution.py
+++ b/solution.py
@@ -1,7 +1,17 @@
+import functools
+
 import jax
 import jax.numpy as jnp
 from jax import lax
+from jax.experimental import pallas as pl
+from jax.experimental.pallas import tpu as pltpu
 from jax.sharding import PartitionSpec as P
+
+FLAG = 128
+BF16 = jnp.bfloat16
+F32 = jnp.float32
+VMEM = pl.BlockSpec(memory_space=pltpu.VMEM)
+HBM = pl.BlockSpec(memory_space=pltpu.HBM)
 
 
 def from_behind(value, axis, steps):
@@ -28,11 +38,11 @@
 
 def contract(left, right, left_dim, right_dim):
     return lax.dot_general(
-        left, right, (((left_dim,), (right_dim,)), ((), ())), preferred_element_type=jnp.float32
-    )
-
-
-def on_device(tokens, out_grad, top_ids, route_probs, w_gate, w_up, w_down):
+        left, right, (((left_dim,), (right_dim,)), ((), ())), preferred_element_type=F32
+    )
+
+
+def on_device_any(tokens, out_grad, top_ids, route_probs, w_gate, w_up, w_down):
     tok_dev = tokens.shape[2]
     model_width = tokens.shape[3]
     et_size = lax.axis_size("et")
@@ -41,9 +51,9 @@
     capacity = group_tokens // 2
     token_rows = tokens[0, 0]
     chosen = top_ids[0, 0] == 0
-    routed_flag = jnp.any(chosen, axis=-1).astype(jnp.bfloat16)
-    route_weight = jnp.sum(jnp.where(chosen, route_probs[0, 0], jnp.float32(0.0)), axis=-1)
-    scaled_rows = (route_weight[:, None] * out_grad[0, 0].astype(jnp.float32)).astype(jnp.bfloat16)
+    routed_flag = jnp.any(chosen, axis=-1).astype(BF16)
+    route_weight = jnp.sum(jnp.where(chosen, route_probs[0, 0], F32(0.0)), axis=-1)
+    scaled_rows = (route_weight[:, None] * out_grad[0, 0].astype(F32)).astype(BF16)
     group_x, group_dz, group_flag = (
         lax.all_gather(token_rows, "et", axis=0, tiled=True),
         lax.all_gather(scaled_rows, "et", axis=0, tiled=True),
@@ -68,27 +78,17 @@
     upper = contract(slot_x, up_rows, 1, 1)
     sigmoid_gate = jax.nn.sigmoid(gate)
     silu_gate = gate * sigmoid_gate
-    act = (silu_gate * upper).astype(jnp.bfloat16)
+    act = (silu_gate * upper).astype(BF16)
     act_grad = contract(slot_dz, down_rows, 1, 1)
-    gate_grad = (act_grad * upper * sigmoid_gate * (1.0 + gate * (1.0 - sigmoid_gate))).astype(
-        jnp.bfloat16
-    )
-    up_grad = (act_grad * silu_gate).astype(jnp.bfloat16)
-    grad_down = contract(act, slot_dz, 0, 0).astype(jnp.bfloat16)
-    grad_gate = contract(gate_grad, slot_x, 0, 0).astype(jnp.bfloat16)
-    grad_up = contract(up_grad, slot_x, 0, 0).astype(jnp.bfloat16)
-    hidden_terms = jnp.dot(gate_grad, gate_rows, preferred_element_type=jnp.float32) + jnp.dot(
-        up_grad, up_rows, preferred_element_type=jnp.float32
-    )
-    rounded = lax.optimization_barrier(hidden_terms.astype(jnp.bfloat16)).astype(jnp.float32)
-    rounded = rounded.reshape(dp_size, capacity, model_width)
-    hidden_sum = lax.psum_scatter(
-        rounded.astype(jnp.bfloat16), "et", scatter_dimension=1, tiled=True
-    )
-    group_sum = lax.psum_scatter(hidden_sum, "dp", scatter_dimension=0, tiled=True).astype(
-        jnp.float32
-    )
-    slot_share = group_sum.astype(jnp.bfloat16)
+    gate_grad = (act_grad * upper * sigmoid_gate * (1.0 + gate * (1.0 - sigmoid_gate))).astype(BF16)
+    up_grad = (act_grad * silu_gate).astype(BF16)
+    grad_down = contract(act, slot_dz, 0, 0).astype(BF16)
+    grad_gate = contract(gate_grad, slot_x, 0, 0).astype(BF16)
+    grad_up = contract(up_grad, slot_x, 0, 0).astype(BF16)
+    hidden_terms = contract(gate_grad, gate_rows, 1, 0) + contract(up_grad, up_rows, 1, 0)
+    rounded = hidden_terms.astype(BF16).reshape(dp_size, capacity, model_width)
+    hidden_sum = lax.psum_scatter(rounded, "et", scatter_dimension=1, tiled=True)
+    slot_share = lax.psum_scatter(hidden_sum, "dp", scatter_dimension=0, tiled=True)
     slot_grad = lax.all_gather(slot_share, "et", axis=1, tiled=True)[0]
     start = lax.axis_index("et") * tok_dev
     my_position = lax.dynamic_slice_in_dim(own_position, start, tok_dev)
@@ -97,6 +97,244 @@
     input_grad = jnp.where(my_routed[:, None], picked, jnp.zeros_like(picked))
     handed = from_behind(input_grad[None, None], "pipe", -1)
     return (handed, grad_gate[None], grad_up[None], grad_down[None])
+
+
+def call(kernel, outs, *args, scratch=(), flops=0, vmem=16, space=VMEM):
+    moved = sum(a.size * a.dtype.itemsize for a in args)
+    moved += sum(o.size * o.dtype.itemsize for o in outs)
+    if space is HBM:
+        args = [pltpu.with_memory_space_constraint(a, pltpu.HBM) for a in args]
+    return pl.pallas_call(
+        kernel,
+        out_shape=outs,
+        in_specs=[space] * len(args),
+        out_specs=[VMEM] * len(outs),
+        scratch_shapes=list(scratch),
+        compiler_params=pltpu.CompilerParams(vmem_limit_bytes=vmem * 2**20),
+        cost_estimate=pl.CostEstimate(flops=flops, bytes_accessed=moved, transcendentals=0),
+    )(*args)
+
+
+def like(shape, dtype=BF16):
+    return jax.ShapeDtypeStruct(shape, dtype)
+
+
+def spread(steps):
+    return [(e, e ^ steps) for e in range(4)]
+
+
+def bring(sources, targets, sems):
+    copies = [
+        pltpu.make_async_copy(source, target, sems.at[i])
+        for i, (source, target) in enumerate(zip(sources, targets))
+    ]
+    for copy in copies:
+        copy.start()
+    return copies
+
+
+def stage_kernel(*refs):
+    count = len(refs) // 2
+    for copy in bring(refs[:count], refs[count : 2 * count], refs[-1]):
+        copy.wait()
+
+
+def pack_kernel(*refs):
+    outs, (x_ref, dz_ref, ids_ref, probs_ref, sems) = refs[4:8], refs[8:]
+    for copy in bring(refs[:4], refs[8:12], sems):
+        copy.wait()
+    rows, width = x_ref.shape
+    piece = width // 4
+    e = lax.axis_index("et")
+    chosen = ids_ref[...] == 0
+    weight_row = jnp.sum(jnp.where(chosen, probs_ref[...], 0.0), axis=0, keepdims=True)
+    flag_row = jnp.max(jnp.where(chosen, 1.0, 0.0), axis=0, keepdims=True)
+    on_diagonal = lax.broadcasted_iota(jnp.int32, (rows, rows), 0) == lax.broadcasted_iota(
+        jnp.int32, (rows, rows), 1
+    )
+    weight = jnp.sum(jnp.where(on_diagonal, weight_row, 0.0), axis=1, keepdims=True)
+    flag = jnp.sum(jnp.where(on_diagonal, flag_row, 0.0), axis=1, keepdims=True)
+    for steps, out in enumerate(outs):
+        start = pl.multiple_of((e ^ steps) * piece, 128)
+        out[:, :piece] = x_ref[:, pl.ds(start, piece)]
+        out[:, piece : 2 * piece] = (weight * dz_ref[:, pl.ds(start, piece)].astype(F32)).astype(BF16)
+        out[:, 2 * piece :] = jnp.broadcast_to(flag, (rows, FLAG)).astype(BF16)
+
+
+def compact_kernel(*refs):
+    parts, (slots_ref, pick_ref, all_rows) = refs[:4], refs[4:]
+    rows, wide = parts[0].shape
+    tokens = 4 * rows
+    data = wide - FLAG
+    cap = slots_ref.shape[0]
+    e = lax.axis_index("et")
+    for steps, part in enumerate(parts):
+        all_rows[pl.ds(pl.multiple_of((e ^ steps) * rows, 16), rows), :] = part[...]
+    flags = all_rows[:, data:]
+    before = lax.broadcasted_iota(jnp.int32, (tokens, tokens), 0)
+    after = lax.broadcasted_iota(jnp.int32, (tokens, tokens), 1)
+    count = contract(flags, (before <= after).astype(F32).astype(BF16), 0, 0)[:cap]
+    here = contract(flags, (before == after).astype(F32).astype(BF16), 0, 0)[:cap]
+    slot = lax.broadcasted_iota(jnp.int32, (cap, tokens), 0).astype(F32)
+    pick = jnp.where((count - 1.0 == slot) & (here > 0.5), 1.0, 0.0).astype(BF16)
+    slots_ref[...] = jnp.dot(pick, all_rows[:, :data], preferred_element_type=F32).astype(BF16)
+    pick_ref[...] = pick
+
+
+def expert_kernel(*refs):
+    blocks, (wg_ref, wu_ref, wd_ref), outs = refs[:16], refs[16:19], refs[19:]
+    x_ref, dz_ref, act_ref, gg_ref, ug_ref, own_ref, other_ref = outs
+    cap, wide = blocks[0].shape
+    piece = wide // 2
+    half = wide
+    e = lax.axis_index("et")
+    for steps in range(4):
+        start = pl.multiple_of((e ^ steps) * piece, 128)
+        for k in range(4):
+            block = blocks[4 * steps + k]
+            rows = pl.ds(k * cap, cap)
+            x_ref[rows, pl.ds(start, piece)] = block[:, :piece]
+            dz_ref[rows, pl.ds(start, piece)] = block[:, piece:]
+    gate = contract(x_ref[...], wg_ref[...], 1, 1)
+    upper = contract(x_ref[...], wu_ref[...], 1, 1)
+    act_grad = contract(dz_ref[...], wd_ref[...], 1, 1)
+    sigmoid_gate = jax.nn.sigmoid(gate)
+    silu_gate = gate * sigmoid_gate
+    act_ref[...] = (silu_gate * upper).astype(BF16)
+    gg_ref[...] = (act_grad * upper * sigmoid_gate * (1.0 + gate * (1.0 - sigmoid_gate))).astype(BF16)
+    ug_ref[...] = (act_grad * silu_gate).astype(BF16)
+    core = e % 2
+    for out, side in ((other_ref, 1 - core), (own_ref, core)):
+        start = pl.multiple_of(side * half, 128)
+        terms = contract(gg_ref[...], wg_ref[:, pl.ds(start, half)], 1, 0)
+        terms += contract(ug_ref[...], wu_ref[:, pl.ds(start, half)], 1, 0)
+        out[...] = terms.astype(BF16)
+
+
+def pair_kernel(own_ref, other_ref, *outs):
+    cap = outs[0].shape[0]
+    for k, out in enumerate(outs):
+        rows = pl.ds(k * cap, cap)
+        out[...] = (own_ref[rows, :].astype(F32) + other_ref[rows, :].astype(F32)).astype(BF16)
+
+
+def add_kernel(left_ref, right_ref, out_ref):
+    out_ref[...] = (left_ref[...].astype(F32) + right_ref[...].astype(F32)).astype(BF16)
+
+
+def expand_kernel(own_ref, near_ref, far_ref, pick_ref, *refs):
+    outs, tokens_ref = refs[:4], refs[4]
+    rows = outs[0].shape[0]
+    e = lax.axis_index("et")
+    total = own_ref[...].astype(F32) + near_ref[...].astype(F32) + far_ref[...].astype(F32)
+    tokens_ref[...] = contract(pick_ref[...], total.astype(BF16), 0, 0).astype(BF16)
+    for steps, out in enumerate(outs):
+        out[...] = tokens_ref[pl.ds(pl.multiple_of((e ^ steps) * rows, 16), rows), :]
+
+
+def finish_kernel(own_ref, core_ref, chip_ref, both_ref, out_ref):
+    half = own_ref.shape[1]
+    core = lax.axis_index("et") % 2
+    mine = own_ref[...].astype(F32) + chip_ref[...].astype(F32)
+    out_ref[:, pl.ds(pl.multiple_of(core * half, 128), half)] = mine.astype(BF16)
+    theirs = core_ref[...].astype(F32) + both_ref[...].astype(F32)
+    out_ref[:, pl.ds(pl.multiple_of((1 - core) * half, 128), half)] = theirs.astype(BF16)
+
+
+def swap(value, axis, steps):
+    return lax.ppermute(value, axis, spread(steps))
+
+
+def on_device_four(tokens, out_grad, top_ids, route_probs, w_gate, w_up, w_down):
+    rows, width = tokens.shape[2:]
+    hidden = w_gate.shape[1]
+    top = top_ids.shape[3]
+    pipe_size = lax.axis_size("pipe")
+    cap = 2 * rows
+    slots = 4 * cap
+    piece, half = width // 4, width // 2
+
+    packed = call(
+        pack_kernel,
+        [like((rows, 2 * piece + FLAG))] * 4,
+        tokens[0, 0],
+        out_grad[0, 0],
+        top_ids[0, 0].T,
+        route_probs[0, 0].T,
+        scratch=[
+            pltpu.VMEM((rows, width), BF16),
+            pltpu.VMEM((rows, width), BF16),
+            pltpu.VMEM((top, rows), jnp.int32),
+            pltpu.VMEM((top, rows), F32),
+            pltpu.SemaphoreType.DMA((4,)),
+        ],
+        space=HBM,
+    )
+    arrived = [packed[0]] + [swap(packed[s], "et", s) for s in (1, 2, 3)]
+    wg, wu, wd = call(
+        stage_kernel,
+        [like((hidden, width))] * 3,
+        w_gate[0],
+        w_up[0],
+        w_down[0],
+        scratch=[pltpu.SemaphoreType.DMA((3,))],
+        space=HBM,
+    )
+    slot_block, pick = call(
+        compact_kernel,
+        [like((cap, 2 * piece)), like((cap, 4 * rows))],
+        *arrived,
+        scratch=[pltpu.VMEM((4 * rows, 2 * piece + FLAG), BF16)],
+    )
+    near = swap(slot_block, "dp", 1)
+    far = swap(slot_block, "dp", 2)
+    chip_own = swap(slot_block, "et", 2)
+    near, far, chip_own, wg, wu, wd = lax.optimization_barrier((near, far, chip_own, wg, wu, wd))
+    last = swap(far, "dp", 1)
+    own = [slot_block, near, far, last]
+    chip = [chip_own] + [swap(block, "et", 2) for block in own[1:]]
+    core = [swap(block, "et", 1) for block in own]
+    both = [swap(block, "et", 1) for block in chip]
+    x, dz, act, gate_grad, up_grad, terms, away = call(
+        expert_kernel,
+        [like((slots, width))] * 2 + [like((slots, hidden))] * 3 + [like((slots, half))] * 2,
+        *own,
+        *core,
+        *chip,
+        *both,
+        wg,
+        wu,
+        wd,
+        flops=10 * slots * hidden * width,
+        vmem=32,
+    )
+    theirs = swap(away, "et", 1)
+    home, to_near, to_far, to_last = call(
+        pair_kernel, [like((cap, half))] * 4, terms, theirs
+    )
+    (to_far,) = call(add_kernel, [like((cap, half))], to_far, swap(to_last, "dp", 1))
+    by_token = call(
+        expand_kernel,
+        [like((rows, half))] * 4,
+        home,
+        swap(to_near, "dp", 1),
+        swap(to_far, "dp", 2),
+        pick,
+        scratch=[pltpu.VMEM((4 * rows, half), BF16)],
+    )
+    back = []
+    for s in range(4):
+        pairs = [
+            (4 * p + e, 4 * ((p - 1) % pipe_size) + (e ^ s))
+            for p in range(pipe_size)
+            for e in range(4)
+        ]
+        back.append(lax.ppermute(by_token[s], ("pipe", "et"), pairs))
+    (handed,) = call(finish_kernel, [like((rows, width))], *back)
+    grad_down = contract(act, dz, 0, 0).astype(BF16)
+    grad_gate = contract(gate_grad, x, 0, 0).astype(BF16)
+    grad_up = contract(up_grad, x, 0, 0).astype(BF16)
+    return (handed[None, None], grad_gate[None], grad_up[None], grad_down[None])
 
 
 def solution(mesh):
@@ -109,8 +347,9 @@
         P("pipe", ("dp", "et"), None),
         P("pipe", ("dp", "et"), None),
     )
+    four = mesh.shape["et"] == 4 and mesh.shape["dp"] == 4
     return jax.shard_map(
-        on_device,
+        on_device_four if four else on_device_any,
         mesh=mesh,
         in_specs=placed,
         out_specs=(

time: 142 us -> 56.1 us (0.40)
  blocking collectives: 65.2 us -> 0 us
  waiting for transfers between devices: 39.3 us -> 17.5 us
  starting transfers between devices: 1.63 us -> 22.8 us
  between operations: 14.9 us -> 0.74 us
  local copies, waits for them, and re-layouts: 8.55 us -> 0 us
  Pallas kernels: 0 us -> 8.45 us
  matrix products: 9.35 us -> 6.07 us
  other arithmetic: 2.73 us -> 0 us
    all_gather x5 -> x0, blocking collectives: 56.8 us -> none  [the longest x1 19.8 us: on_device(): lax.all_gather(own_dz, 'dp', axis=0, tiled=True)]
    unnamed x3 -> x0, waiting for transfers between devices: 22 us -> none
    ppermute x1 -> x26, starting transfers between devices: 1.55 us -> 22.8 us  [the longest x22 18.3 us: swap(): return lax.ppermute(value, axis, spread(steps))]
    ppermute x1 -> x26, waiting for transfers between devices: 1.57 us -> 17.5 us  [the longest x22 16.7 us: swap(): return lax.ppermute(value, axis, spread(steps))]
    reduce_scatter x1 -> x0, waiting for transfers between devices: 15.8 us -> none  [on_device(): lax.psum_scatter(hidden_sum, 'dp', scatter_dimension=0, tiled=True)]
    pallas_call x0 -> x8, Pallas kernels: none -> 8.45 us  [call(): pl.pallas_call(kernel, out_shape=outs, in_specs=[space] * len(args), out_...]
    unnamed x1 -> x0, blocking collectives: 8.34 us -> none
    unnamed x22 -> x0, local copies, waits for them, and re-layouts: 6.53 us -> none
  transfers between devices with their start and end apart: 3 -> 26, of which waited for: 3 -> 14; matrix products, arithmetic and copies ran while one was open for 4% -> 11% of each run, Pallas kernels for 0% -> 5%
where the time goes in v1:
time: 56.1 us; the launch traced here: 55.5 us
  starting transfers between devices  22.8 us (41%)
  waiting for transfers between devices  17.5 us (31%)
  Pallas kernels  8.45 us (15%)
  matrix products  6.07 us (11%)
  between operations  0.74 us (1%)
    ppermute x22, starting transfers between devices, swap(): return lax.ppermute(value, axis, spread(steps))  18.3 us
    ppermute x22, waiting for transfers between devices, swap(): return lax.ppermute(value, axis, spread(steps))  16.7 us
    pallas_call x8, Pallas kernels, call(): pl.pallas_call(kernel, out_shape=outs, in_specs=[space] * len(args), out_...  8.45 us
    dot_general x3, matrix products, contract(): lax.dot_general(left, right, (((left_dim,), (right_dim,)), ((), ())), pre...  6.07 us
    ppermute x4, starting transfers between devices, on_device_four(): back.append(lax.ppermute(by_token[s], ('pipe', 'et'), pairs))  4.46 us
  transfers between devices with their start and end apart: 26, of which 14 were waited for; matrix products, arithmetic and copies ran while one was open for 11% of the time, Pallas kernels for 5%

profile of v1, /device:TPU:0, one launch (start us, length us, event | category | flops | bytes accessed | tf_op | source)
XLA Modules:
  0.0 55.5 jit_solution(1592467779083207352)
XLA Ops:
  0.6 1.1 %shard_map.102 = (bf16[16,1664]{1,0:T(8,128)(2,1)S(1)}, bf16[16,1664]{1,0:T(8,128)(2,1)S(1)}, bf16[16,1664]{1,0:T(8,128)(2,1)S(1)}, bf16[16,1664]{1,0:T(8,128)(2,1)S(1)}) custom-call(bf16[16,3072]{1,0:T(8,128)(2,1)} %bitcast.27, bf16[16,3072]{1,0:T(8,128)(2,1)} %bitcast.28, s32[4,16]{1,0:T(4,128)} %bitcast.30, f32[4,16]{1,0:T(4,128)} %bitcast.31), custom_call_target="tpu_custom_call" | custom-call | bytes 410112 | tf_op jit(solution)/shard_map/pallas_call | solution.py:107
  1.7 0.5 collective-permute-start
  2.2 2.6 %collective-permute-start.1 = (bf16[16,1664]{1,0:T(8,128)(2,1)S(1)}, bf16[16,1664]{1,0:T(8,128)(2,1)S(1)}, u32[]{:S(2)}, u32[]{:S(2)}) collective-permute-start(bf16[16,1664]{1,0:T(8,128)(2,1)S(1)} %get-tuple-element.36), channel_id=1, source_target_pairs={{0,2},{1,3},{2,0},{3,1},{4,6},{5,7},{6,4},{7,5},{8,10},{9,11},{10,... | collective-permute-start | bytes 159752 | tf_op jit(solution)/shard_map/ppermute | solution.py:245
  4.8 0.1 collective-permute-start.2
  4.9 2.3 %collective-permute-done.1.refs_2_ = bf16[16,1664]{1,0:T(8,128)(2,1)S(1)} collective-permute-done((bf16[16,1664]{1,0:T(8,128)(2,1)S(1)}, bf16[16,1664]{1,0:T(8,128)(2,1)S(1)}, u32[]{:S(2)}, u32[]{:S(2)}) %collective-permute-start.1) | collective-permute-done | bytes 53280 | tf_op jit(solution)/shard_map/ppermute | solution.py:245
  7.2 1.4 %collective-permute-done.2.refs_3_ = bf16[16,1664]{1,0:T(8,128)(2,1)S(1)} collective-permute-done((bf16[16,1664]{1,0:T(8,128)(2,1)S(1)}, bf16[16,1664]{1,0:T(8,128)(2,1)S(1)}, u32[]{:S(2)}, u32[]{:S(2)}) %collective-permute-start.2) | collective-permute-done | bytes 53280 | tf_op jit(solution)/shard_map/ppermute | solution.py:245
  8.6 0.3 shard_map.103
  9.0 1.1 %collective-permute-start.5 = (bf16[32,1536]{1,0:T(8,128)(2,1)S(1)}, bf16[32,1536]{1,0:T(8,128)(2,1)S(1)}, u32[]{:S(2)}, u32[]{:S(2)}) collective-permute-start(bf16[32,1536]{1,0:T(8,128)(2,1)S(1)} %get-tuple-element.38.refs_0_), channel_id=1, source_target_pairs={{0,2},{1,3},{2,0},{3,1},{4,6},{5,7},{6,4},{7,5},{8,10},{9,11},{10,... | collective-permute-start | bytes 294920 | tf_op jit(solution)/shard_map/ppermute | solution.py:245
  10.1 2.6 %collective-permute-start.4 = (bf16[32,1536]{1,0:T(8,128)(2,1)S(1)}, bf16[32,1536]{1,0:T(8,128)(2,1)S(1)}, u32[]{:S(2)}, u32[]{:S(2)}) collective-permute-start(bf16[32,1536]{1,0:T(8,128)(2,1)S(1)} %get-tuple-element.38.refs_0_), channel_id=1, source_target_pairs={{0,8},{4,12},{8,0},{12,4},{1,9},{5,13},{9,1},{13,5},{2,10},{6,14},... | collective-permute-start | bytes 294920 | tf_op jit(solution)/shard_map/ppermute | solution.py:245
  12.7 1.6 %collective-permute-start.3 = (bf16[32,1536]{1,0:T(8,128)(2,1)S(1)}, bf16[32,1536]{1,0:T(8,128)(2,1)S(1)}, u32[]{:S(2)}, u32[]{:S(2)}) collective-permute-start(bf16[32,1536]{1,0:T(8,128)(2,1)S(1)} %get-tuple-element.38.refs_0_), channel_id=1, source_target_pairs={{0,4},{4,0},{8,12},{12,8},{1,5},{5,1},{9,13},{13,9},{2,6},{6,2},{1... | collective-permute-start | bytes 294920 | tf_op jit(solution)/shard_map/ppermute | solution.py:245
  14.3 2.9 %shard_map.104 = (bf16[336,3072]{1,0:T(8,128)(2,1)S(1)}, bf16[336,3072]{1,0:T(8,128)(2,1)S(1)}, bf16[336,3072]{1,0:T(8,128)(2,1)S(1)}) custom-call(bf16[336,3072]{1,0:T(8,128)(2,1)} %bitcast.24, bf16[336,3072]{1,0:T(8,128)(2,1)} %bitcast.25, bf16[336,3072]{1,0:T(8,128)(2,1)} %bitcast.26), custom_call_target="tpu_custom_call" | custom-call | bytes 12386304 | tf_op jit(solution)/shard_map/pallas_call | solution.py:107
  17.1 0.1 collective-permute-start.7
  17.2 0.0 collective-permute-done.5.refs_8_
  17.2 0.7 %collective-permute-done.4.refs_2_ = bf16[32,1536]{1,0:T(8,128)(2,1)S(1)} collective-permute-done((bf16[32,1536]{1,0:T(8,128)(2,1)S(1)}, bf16[32,1536]{1,0:T(8,128)(2,1)S(1)}, u32[]{:S(2)}, u32[]{:S(2)}) %collective-permute-start.4) | collective-permute-done | bytes 98336 | tf_op jit(solution)/shard_map/ppermute | solution.py:245
  17.9 0.2 collective-permute-done.3.refs_1_
  18.1 1.4 %collective-permute-start.6 = (bf16[32,1536]{1,0:T(8,128)(2,1)S(1)}, bf16[32,1536]{1,0:T(8,128)(2,1)S(1)}, u32[]{:S(2)}, u32[]{:S(2)}) collective-permute-start(bf16[32,1536]{1,0:T(8,128)(2,1)S(1)} %collective-permute-done.4.refs_2_), channel_id=1, source_target_pairs={{0,4},{4,0},{8,12},{12,8},{1,5},{5,1},{9,13},{13,9},{2,6},{6,2},{1... | collective-permute-start | bytes 294920 | tf_op jit(solution)/shard_map/ppermute | solution.py:245
  19.5 0.0 collective-permute-start.14
  19.5 0.9 %collective-permute-start.11 = (bf16[32,1536]{1,0:T(8,128)(2,1)S(1)}, bf16[32,1536]{1,0:T(8,128)(2,1)S(1)}, u32[]{:S(2)}, u32[]{:S(2)}) collective-permute-start(bf16[32,1536]{1,0:T(8,128)(2,1)S(1)} %collective-permute-done.3.refs_1_), channel_id=1, source_target_pairs={{0,2},{1,3},{2,0},{3,1},{4,6},{5,7},{6,4},{7,5},{8,10},{9,11},{10,... | collective-permute-start | bytes 294920 | tf_op jit(solution)/shard_map/ppermute | solution.py:245
  20.4 0.2 collective-permute-start.8
  20.6 1.2 %collective-permute-start.12 = (bf16[32,1536]{1,0:T(8,128)(2,1)S(1)}, bf16[32,1536]{1,0:T(8,128)(2,1)S(1)}, u32[]{:S(2)}, u32[]{:S(2)}) collective-permute-start(bf16[32,1536]{1,0:T(8,128)(2,1)S(1)} %collective-permute-done.4.refs_2_), channel_id=1, source_target_pairs={{0,2},{1,3},{2,0},{3,1},{4,6},{5,7},{6,4},{7,5},{8,10},{9,11},{10,... | collective-permute-start | bytes 294920 | tf_op jit(solution)/shard_map/ppermute | solution.py:245
  21.8 1.0 %collective-permute-done.6.refs_3_ = bf16[32,1536]{1,0:T(8,128)(2,1)S(1)} collective-permute-done((bf16[32,1536]{1,0:T(8,128)(2,1)S(1)}, bf16[32,1536]{1,0:T(8,128)(2,1)S(1)}, u32[]{:S(2)}, u32[]{:S(2)}) %collective-permute-start.6) | collective-permute-done | bytes 98336 | tf_op jit(solution)/shard_map/ppermute | solution.py:245
  22.8 0.8 %collective-permute-start.13 = (bf16[32,1536]{1,0:T(8,128)(2,1)S(1)}, bf16[32,1536]{1,0:T(8,128)(2,1)S(1)}, u32[]{:S(2)}, u32[]{:S(2)}) collective-permute-start(bf16[32,1536]{1,0:T(8,128)(2,1)S(1)} %collective-permute-done.6.refs_3_), channel_id=1, source_target_pairs={{0,2},{1,3},{2,0},{3,1},{4,6},{5,7},{6,4},{7,5},{8,10},{9,11},{10,... | collective-permute-start | bytes 294920 | tf_op jit(solution)/shard_map/ppermute | solution.py:245
  23.6 1.5 %collective-permute-done.11.refs_9_ = bf16[32,1536]{1,0:T(8,128)(2,1)S(1)} collective-permute-done((bf16[32,1536]{1,0:T(8,128)(2,1)S(1)}, bf16[32,1536]{1,0:T(8,128)(2,1)S(1)}, u32[]{:S(2)}, u32[]{:S(2)}) %collective-permute-start.11) | collective-permute-done | bytes 98336 | tf_op jit(solution)/shard_map/ppermute | solution.py:245
  25.1 0.0 collective-permute-start.10
  25.1 0.0 collective-permute-done.8.refs_5_
  25.1 0.5 collective-permute-start.15
  25.6 1.6 %collective-permute-done.12.refs_10_ = bf16[32,1536]{1,0:T(8,128)(2,1)S(1)} collective-permute-done((bf16[32,1536]{1,0:T(8,128)(2,1)S(1)}, bf16[32,1536]{1,0:T(8,128)(2,1)S(1)}, u32[]{:S(2)}, u32[]{:S(2)}) %collective-permute-start.12) | collective-permute-done | bytes 98336 | tf_op jit(solution)/shard_map/ppermute | solution.py:245
  27.2 1.7 %collective-permute-done.13.refs_11_ = bf16[32,1536]{1,0:T(8,128)(2,1)S(1)} collective-permute-done((bf16[32,1536]{1,0:T(8,128)(2,1)S(1)}, bf16[32,1536]{1,0:T(8,128)(2,1)S(1)}, u32[]{:S(2)}, u32[]{:S(2)}) %collective-permute-start.13) | collective-permute-done | bytes 98336 | tf_op jit(solution)/shard_map/ppermute | solution.py:245
  29.0 1.3 %collective-permute-done.17.refs_15_ = bf16[32,1536]{1,0:T(8,128)(2,1)S(1)} collective-permute-done((bf16[32,1536]{1,0:T(8,128)(2,1)S(1)}, bf16[32,1536]{1,0:T(8,128)(2,1)S(1)}, u32[]{:S(2)}, u32[]{:S(2)}) %collective-permute-start.17) | collective-permute-done | bytes 98336 | tf_op jit(solution)/shard_map/ppermute | solution.py:245
  30.2 3.2 %shard_map.105 = (bf16[128,3072]{1,0:T(8,128)(2,1)S(1)}, bf16[128,3072]{1,0:T(8,128)(2,1)S(1)}, bf16[128,336]{1,0:T(8,128)(2,1)S(1)}, bf16[128,336]{1,0:T(8,128)...) custom-call(bf16[32,1536]{1,0:T(8,128)(2,1)S(1)} %get-tuple-element.38.refs_0_, ...), custom_call_target="tpu_custom_call" | custom-call | flops 1321205760 | bytes 10383360 | tf_op jit(solution)/shard_map/pallas_call | solution.py:107
  33.4 0.2 collective-permute-start.18
  33.6 1.6 %collective-permute-done.18.other_ref = bf16[128,1536]{1,0:T(8,128)(2,1)S(1)} collective-permute-done((bf16[128,1536]{1,0:T(8,128)(2,1)S(1)}, bf16[128,1536]{1,0:T(8,128)(2,1)S(1)}, u32[]{:S(2)}, u32[]{:S(2)}) %collective-permute-start.18) | collective-permute-done | bytes 393248 | tf_op jit(solution)/shard_map/ppermute | solution.py:245
  35.2 0.1 shard_map.106
  35.3 0.7 %collective-permute-start.20 = (bf16[32,1536]{1,0:T(8,128)(2,1)S(1)}, bf16[32,1536]{1,0:T(8,128)(2,1)S(1)}, u32[]{:S(2)}, u32[]{:S(2)}) collective-permute-start(bf16[32,1536]{1,0:T(8,128)(2,1)S(1)} %get-tuple-element.53), channel_id=1, source_target_pairs={{0,4},{4,0},{8,12},{12,8},{1,5},{5,1},{9,13},{13,9},{2,6},{6,2},{1... | collective-permute-start | bytes 294920 | tf_op jit(solution)/shard_map/ppermute | solution.py:245
  36.0 2.0 %fusion = bf16[1,336,3072]{2,1,0:T(8,128)(2,1)} fusion(bf16[128,336]{1,0:T(8,128)(2,1)S(1)} %get-tuple-element.59, bf16[128,3072]{1,0:T(8,128)(2,1)S(1)} %get-tuple-element.60), kind=kOutput, calls=%fused_computation.3 | convolution fusion | flops 265273344 | bytes 2936832 | tf_op jit(solution)/shard_map/dot_general | solution.py:40
  38.0 1.4 %collective-permute-start.19 = (bf16[32,1536]{1,0:T(8,128)(2,1)S(1)}, bf16[32,1536]{1,0:T(8,128)(2,1)S(1)}, u32[]{:S(2)}, u32[]{:S(2)}) collective-permute-start(bf16[32,1536]{1,0:T(8,128)(2,1)S(1)} %get-tuple-element.51), channel_id=1, source_target_pairs={{0,4},{4,0},{8,12},{12,8},{1,5},{5,1},{9,13},{13,9},{2,6},{6,2},{1... | collective-permute-start | bytes 294920 | tf_op jit(solution)/shard_map/ppermute | solution.py:245
  39.4 0.8 %collective-permute-done.20.right_ref = bf16[32,1536]{1,0:T(8,128)(2,1)S(1)} collective-permute-done((bf16[32,1536]{1,0:T(8,128)(2,1)S(1)}, bf16[32,1536]{1,0:T(8,128)(2,1)S(1)}, u32[]{:S(2)}, u32[]{:S(2)}) %collective-permute-start.20) | collective-permute-done | bytes 98336 | tf_op jit(solution)/shard_map/ppermute | solution.py:245
  40.2 2.5 %collective-permute-start.21 = (bf16[32,1536]{1,0:T(8,128)(2,1)S(1)}, bf16[32,1536]{1,0:T(8,128)(2,1)S(1)}, u32[]{:S(2)}, u32[]{:S(2)}) collective-permute-start(bf16[32,1536]{1,0:T(8,128)(2,1)S(1)} %shard_map.107), channel_id=1, source_target_pairs={{0,8},{4,12},{8,0},{12,4},{1,9},{5,13},{9,1},{13,5},{2,10},{6,14},... | collective-permute-start | bytes 294920 | tf_op jit(solution)/shard_map/ppermute | solution.py:245
  42.7 2.0 %fusion.1 = bf16[1,336,3072]{2,1,0:T(8,128)(2,1)} fusion(bf16[128,336]{1,0:T(8,128)(2,1)S(1)} %get-tuple-element.61, bf16[128,3072]{1,0:T(8,128)(2,1)S(1)} %get-tuple-element.60), kind=kOutput, calls=%fused_computation.4 | convolution fusion | flops 265273344 | bytes 2936832 | tf_op jit(solution)/shard_map/dot_general | solution.py:40
  44.7 2.6 %collective-permute-done.21.far_ref = bf16[32,1536]{1,0:T(8,128)(2,1)S(1)} collective-permute-done((bf16[32,1536]{1,0:T(8,128)(2,1)S(1)}, bf16[32,1536]{1,0:T(8,128)(2,1)S(1)}, u32[]{:S(2)}, u32[]{:S(2)}) %collective-permute-start.21) | collective-permute-done | bytes 98336 | tf_op jit(solution)/shard_map/ppermute | solution.py:245
  47.3 0.2 shard_map.108
  47.6 1.6 %collective-permute-start.22 = (bf16[16,1536]{1,0:T(8,128)(2,1)S(1)}, bf16[16,1536]{1,0:T(8,128)(2,1)S(1)}, u32[]{:S(2)}, u32[]{:S(2)}) collective-permute-start(bf16[16,1536]{1,0:T(8,128)(2,1)S(1)} %get-tuple-element.55), channel_id=1, source_target_pairs={{0,16},{1,17},{2,18},{3,19},{16,0},{17,1},{18,2},{19,3},{4,20},{5,... | collective-permute-start | bytes 147464 | tf_op jit(solution)/shard_map/ppermute | solution.py:332
  49.1 0.8 %collective-permute-start.24 = (bf16[16,1536]{1,0:T(8,128)(2,1)S(1)}, bf16[16,1536]{1,0:T(8,128)(2,1)S(1)}, u32[]{:S(2)}, u32[]{:S(2)}) collective-permute-start(bf16[16,1536]{1,0:T(8,128)(2,1)S(1)} %get-tuple-element.57), channel_id=1, source_target_pairs={{0,18},{1,19},{2,16},{3,17},{16,2},{17,3},{18,0},{19,1},{4,22},{5,... | collective-permute-start | bytes 147464 | tf_op jit(solution)/shard_map/ppermute | solution.py:332
  50.0 2.0 %collective-permute-start.25 = (bf16[16,1536]{1,0:T(8,128)(2,1)S(1)}, bf16[16,1536]{1,0:T(8,128)(2,1)S(1)}, u32[]{:S(2)}, u32[]{:S(2)}) collective-permute-start(bf16[16,1536]{1,0:T(8,128)(2,1)S(1)} %get-tuple-element.58), channel_id=1, source_target_pairs={{0,19},{1,18},{2,17},{3,16},{16,3},{17,2},{18,1},{19,0},{4,23},{5,... | collective-permute-start | bytes 147464 | tf_op jit(solution)/shard_map/ppermute | solution.py:332
  52.0 2.0 %fusion.2 = bf16[1,336,3072]{2,1,0:T(8,128)(2,1)} fusion(bf16[128,336]{1,0:T(8,128)(2,1)S(1)} %get-tuple-element.62, bf16[128,3072]{1,0:T(8,128)(2,1)S(1)} %get-tuple-element.63), kind=kOutput, calls=%fused_computation.5 | convolution fusion | flops 265273344 | bytes 2936832 | tf_op jit(solution)/shard_map/dot_general | solution.py:40
  54.1 0.6 %collective-permute-done.24.chip_ref = bf16[16,1536]{1,0:T(8,128)(2,1)S(1)} collective-permute-done((bf16[16,1536]{1,0:T(8,128)(2,1)S(1)}, bf16[16,1536]{1,0:T(8,128)(2,1)S(1)}, u32[]{:S(2)}, u32[]{:S(2)}) %collective-permute-start.24) | collective-permute-done | bytes 49184 | tf_op jit(solution)/shard_map/ppermute | solution.py:332
  54.7 0.2 collective-permute-done.25.both_ref
  54.8 0.7 %shard_map.109 = bf16[16,3072]{1,0:T(8,128)(2,1)} custom-call(bf16[16,1536]{1,0:T(8,128)(2,1)S(1)} %collective-permute-done.22.own_ref, bf16[16,1536]{1,0:T(8,128)(2,1)S(1)} %collective-permute-done.23.core_ref, bf16[16,1536]{1,0:T(8,128)(2,1)S(1)} %collective-permute-done.24.chip_ref, bf16[16,1536]{1,0:T(8,128)(2,1)S(1)} %collective-permute-done.25.both_ref), custom_call_target="tpu_custom_call" | custom-call | bytes 294912 | tf_op jit(solution)/shard_map/pallas_call | solution.py:107
  (15 shorter events, 0.1 us)
Async XLA Ops:
  1.7 3.2 %collective-permute-start = (bf16[16,1664]{1,0:T(8,128)(2,1)S(1)}, bf16[16,1664]{1,0:T(8,128)(2,1)S(1)}, u32[]{:S(2)}, u32[]{:S(2)}) collective-permute-start(bf16[16,1664]{1,0:T(8,128)(2,1)S(1)} %get-tuple-element.35), channel_id=1, source_target_pairs={{0,1},{1,0},{2,3},{3,2},{4,5},{5,4},{6,7},{7,6},{8,9},{9,8},{10,11... | collective-permute-start | bytes 159752 | tf_op jit(solution)/shard_map/ppermute | solution.py:245
  2.2 5.0 %collective-permute-start.1 = (bf16[16,1664]{1,0:T(8,128)(2,1)S(1)}, bf16[16,1664]{1,0:T(8,128)(2,1)S(1)}, u32[]{:S(2)}, u32[]{:S(2)}) collective-permute-start(bf16[16,1664]{1,0:T(8,128)(2,1)S(1)} %get-tuple-element.36), channel_id=1, source_target_pairs={{0,2},{1,3},{2,0},{3,1},{4,6},{5,7},{6,4},{7,5},{8,10},{9,11},{10,... | collective-permute-start | bytes 159752 | tf_op jit(solution)/shard_map/ppermute | solution.py:245
  4.8 3.8 %collective-permute-start.2 = (bf16[16,1664]{1,0:T(8,128)(2,1)S(1)}, bf16[16,1664]{1,0:T(8,128)(2,1)S(1)}, u32[]{:S(2)}, u32[]{:S(2)}) collective-permute-start(bf16[16,1664]{1,0:T(8,128)(2,1)S(1)} %get-tuple-element.37), channel_id=1, source_target_pairs={{0,3},{1,2},{2,1},{3,0},{4,7},{5,6},{6,5},{7,4},{8,11},{9,10},{10,... | collective-permute-start | bytes 159752 | tf_op jit(solution)/shard_map/ppermute | solution.py:245
  9.0 8.3 %collective-permute-start.5 = (bf16[32,1536]{1,0:T(8,128)(2,1)S(1)}, bf16[32,1536]{1,0:T(8,128)(2,1)S(1)}, u32[]{:S(2)}, u32[]{:S(2)}) collective-permute-start(bf16[32,1536]{1,0:T(8,128)(2,1)S(1)} %get-tuple-element.38.refs_0_), channel_id=1, source_target_pairs={{0,2},{1,3},{2,0},{3,1},{4,6},{5,7},{6,4},{7,5},{8,10},{9,11},{10,... | collective-permute-start | bytes 294920 | tf_op jit(solution)/shard_map/ppermute | solution.py:245
  10.1 7.8 %collective-permute-start.4 = (bf16[32,1536]{1,0:T(8,128)(2,1)S(1)}, bf16[32,1536]{1,0:T(8,128)(2,1)S(1)}, u32[]{:S(2)}, u32[]{:S(2)}) collective-permute-start(bf16[32,1536]{1,0:T(8,128)(2,1)S(1)} %get-tuple-element.38.refs_0_), channel_id=1, source_target_pairs={{0,8},{4,12},{8,0},{12,4},{1,9},{5,13},{9,1},{13,5},{2,10},{6,14},... | collective-permute-start | bytes 294920 | tf_op jit(solution)/shard_map/ppermute | solution.py:245
  12.7 5.4 %collective-permute-start.3 = (bf16[32,1536]{1,0:T(8,128)(2,1)S(1)}, bf16[32,1536]{1,0:T(8,128)(2,1)S(1)}, u32[]{:S(2)}, u32[]{:S(2)}) collective-permute-start(bf16[32,1536]{1,0:T(8,128)(2,1)S(1)} %get-tuple-element.38.refs_0_), channel_id=1, source_target_pairs={{0,4},{4,0},{8,12},{12,8},{1,5},{5,1},{9,13},{13,9},{2,6},{6,2},{1... | collective-permute-start | bytes 294920 | tf_op jit(solution)/shard_map/ppermute | solution.py:245
  17.1 3.5 %collective-permute-start.7 = (bf16[32,1536]{1,0:T(8,128)(2,1)S(1)}, bf16[32,1536]{1,0:T(8,128)(2,1)S(1)}, u32[]{:S(2)}, u32[]{:S(2)}) collective-permute-start(bf16[32,1536]{1,0:T(8,128)(2,1)S(1)} %get-tuple-element.38.refs_0_), channel_id=1, source_target_pairs={{0,1},{1,0},{2,3},{3,2},{4,5},{5,4},{6,7},{7,6},{8,9},{9,8},{10,11... | collective-permute-start | bytes 294920 | tf_op jit(solution)/shard_map/ppermute | solution.py:245
  18.1 4.6 %collective-permute-start.6 = (bf16[32,1536]{1,0:T(8,128)(2,1)S(1)}, bf16[32,1536]{1,0:T(8,128)(2,1)S(1)}, u32[]{:S(2)}, u32[]{:S(2)}) collective-permute-start(bf16[32,1536]{1,0:T(8,128)(2,1)S(1)} %collective-permute-done.4.refs_2_), channel_id=1, source_target_pairs={{0,4},{4,0},{8,12},{12,8},{1,5},{5,1},{9,13},{13,9},{2,6},{6,2},{1... | collective-permute-start | bytes 294920 | tf_op jit(solution)/shard_map/ppermute | solution.py:245
  19.5 4.1 %collective-permute-start.14 = (bf16[32,1536]{1,0:T(8,128)(2,1)S(1)}, bf16[32,1536]{1,0:T(8,128)(2,1)S(1)}, u32[]{:S(2)}, u32[]{:S(2)}) collective-permute-start(bf16[32,1536]{1,0:T(8,128)(2,1)S(1)} %collective-permute-done.5.refs_8_), channel_id=1, source_target_pairs={{0,1},{1,0},{2,3},{3,2},{4,5},{5,4},{6,7},{7,6},{8,9},{9,8},{10,11... | collective-permute-start | bytes 294920 | tf_op jit(solution)/shard_map/ppermute | solution.py:245
  19.5 5.6 %collective-permute-start.11 = (bf16[32,1536]{1,0:T(8,128)(2,1)S(1)}, bf16[32,1536]{1,0:T(8,128)(2,1)S(1)}, u32[]{:S(2)}, u32[]{:S(2)}) collective-permute-start(bf16[32,1536]{1,0:T(8,128)(2,1)S(1)} %collective-permute-done.3.refs_1_), channel_id=1, source_target_pairs={{0,2},{1,3},{2,0},{3,1},{4,6},{5,7},{6,4},{7,5},{8,10},{9,11},{10,... | collective-permute-start | bytes 294920 | tf_op jit(solution)/shard_map/ppermute | solution.py:245
  20.4 4.7 %collective-permute-start.8 = (bf16[32,1536]{1,0:T(8,128)(2,1)S(1)}, bf16[32,1536]{1,0:T(8,128)(2,1)S(1)}, u32[]{:S(2)}, u32[]{:S(2)}) collective-permute-start(bf16[32,1536]{1,0:T(8,128)(2,1)S(1)} %collective-permute-done.3.refs_1_), channel_id=1, source_target_pairs={{0,1},{1,0},{2,3},{3,2},{4,5},{5,4},{6,7},{7,6},{8,9},{9,8},{10,11... | collective-permute-start | bytes 294920 | tf_op jit(solution)/shard_map/ppermute | solution.py:245
  20.6 6.6 %collective-permute-start.12 = (bf16[32,1536]{1,0:T(8,128)(2,1)S(1)}, bf16[32,1536]{1,0:T(8,128)(2,1)S(1)}, u32[]{:S(2)}, u32[]{:S(2)}) collective-permute-start(bf16[32,1536]{1,0:T(8,128)(2,1)S(1)} %collective-permute-done.4.refs_2_), channel_id=1, source_target_pairs={{0,2},{1,3},{2,0},{3,1},{4,6},{5,7},{6,4},{7,5},{8,10},{9,11},{10,... | collective-permute-start | bytes 294920 | tf_op jit(solution)/shard_map/ppermute | solution.py:245
  22.8 6.2 %collective-permute-start.13 = (bf16[32,1536]{1,0:T(8,128)(2,1)S(1)}, bf16[32,1536]{1,0:T(8,128)(2,1)S(1)}, u32[]{:S(2)}, u32[]{:S(2)}) collective-permute-start(bf16[32,1536]{1,0:T(8,128)(2,1)S(1)} %collective-permute-done.6.refs_3_), channel_id=1, source_target_pairs={{0,2},{1,3},{2,0},{3,1},{4,6},{5,7},{6,4},{7,5},{8,10},{9,11},{10,... | collective-permute-start | bytes 294920 | tf_op jit(solution)/shard_map/ppermute | solution.py:245
  23.6 5.3 %collective-permute-start.9 = (bf16[32,1536]{1,0:T(8,128)(2,1)S(1)}, bf16[32,1536]{1,0:T(8,128)(2,1)S(1)}, u32[]{:S(2)}, u32[]{:S(2)}) collective-permute-start(bf16[32,1536]{1,0:T(8,128)(2,1)S(1)} %collective-permute-done.4.refs_2_), channel_id=1, source_target_pairs={{0,1},{1,0},{2,3},{3,2},{4,5},{5,4},{6,7},{7,6},{8,9},{9,8},{10,11... | collective-permute-start | bytes 294920 | tf_op jit(solution)/shard_map/ppermute | solution.py:245
  25.1 3.9 %collective-permute-start.10 = (bf16[32,1536]{1,0:T(8,128)(2,1)S(1)}, bf16[32,1536]{1,0:T(8,128)(2,1)S(1)}, u32[]{:S(2)}, u32[]{:S(2)}) collective-permute-start(bf16[32,1536]{1,0:T(8,128)(2,1)S(1)} %collective-permute-done.6.refs_3_), channel_id=1, source_target_pairs={{0,1},{1,0},{2,3},{3,2},{4,5},{5,4},{6,7},{7,6},{8,9},{9,8},{10,11... | collective-permute-start | bytes 294920 | tf_op jit(solution)/shard_map/ppermute | solution.py:245
  25.1 3.8 %collective-permute-start.15 = (bf16[32,1536]{1,0:T(8,128)(2,1)S(1)}, bf16[32,1536]{1,0:T(8,128)(2,1)S(1)}, u32[]{:S(2)}, u32[]{:S(2)}) collective-permute-start(bf16[32,1536]{1,0:T(8,128)(2,1)S(1)} %collective-permute-done.11.refs_9_), channel_id=1, source_target_pairs={{0,1},{1,0},{2,3},{3,2},{4,5},{5,4},{6,7},{7,6},{8,9},{9,8},{10,11... | collective-permute-start | bytes 294920 | tf_op jit(solution)/shard_map/ppermute | solution.py:245
  27.2 1.7 %collective-permute-start.16 = (bf16[32,1536]{1,0:T(8,128)(2,1)S(1)}, bf16[32,1536]{1,0:T(8,128)(2,1)S(1)}, u32[]{:S(2)}, u32[]{:S(2)}) collective-permute-start(bf16[32,1536]{1,0:T(8,128)(2,1)S(1)} %collective-permute-done.12.refs_10_), channel_id=1, source_target_pairs={{0,1},{1,0},{2,3},{3,2},{4,5},{5,4},{6,7},{7,6},{8,9},{9,8},{10,11... | collective-permute-start | bytes 294920 | tf_op jit(solution)/shard_map/ppermute | solution.py:245
  28.9 1.3 %collective-permute-start.17 = (bf16[32,1536]{1,0:T(8,128)(2,1)S(1)}, bf16[32,1536]{1,0:T(8,128)(2,1)S(1)}, u32[]{:S(2)}, u32[]{:S(2)}) collective-permute-start(bf16[32,1536]{1,0:T(8,128)(2,1)S(1)} %collective-permute-done.13.refs_11_), channel_id=1, source_target_pairs={{0,1},{1,0},{2,3},{3,2},{4,5},{5,4},{6,7},{7,6},{8,9},{9,8},{10,11... | collective-permute-start | bytes 294920 | tf_op jit(solution)/shard_map/ppermute | solution.py:245
  33.4 1.8 %collective-permute-start.18 = (bf16[128,1536]{1,0:T(8,128)(2,1)S(1)}, bf16[128,1536]{1,0:T(8,128)(2,1)S(1)}, u32[]{:S(2)}, u32[]{:S(2)}) collective-permute-start(bf16[128,1536]{1,0:T(8,128)(2,1)S(1)} %get-tuple-element.49), channel_id=1, source_target_pairs={{0,1},{1,0},{2,3},{3,2},{4,5},{5,4},{6,7},{7,6},{8,9},{9,8},{10,11... | collective-permute-start | bytes 1179656 | tf_op jit(solution)/shard_map/ppermute | solution.py:245
  35.3 4.9 %collective-permute-start.20 = (bf16[32,1536]{1,0:T(8,128)(2,1)S(1)}, bf16[32,1536]{1,0:T(8,128)(2,1)S(1)}, u32[]{:S(2)}, u32[]{:S(2)}) collective-permute-start(bf16[32,1536]{1,0:T(8,128)(2,1)S(1)} %get-tuple-element.53), channel_id=1, source_target_pairs={{0,4},{4,0},{8,12},{12,8},{1,5},{5,1},{9,13},{13,9},{2,6},{6,2},{1... | collective-permute-start | bytes 294920 | tf_op jit(solution)/shard_map/ppermute | solution.py:245
  38.0 6.7 %collective-permute-start.19 = (bf16[32,1536]{1,0:T(8,128)(2,1)S(1)}, bf16[32,1536]{1,0:T(8,128)(2,1)S(1)}, u32[]{:S(2)}, u32[]{:S(2)}) collective-permute-start(bf16[32,1536]{1,0:T(8,128)(2,1)S(1)} %get-tuple-element.51), channel_id=1, source_target_pairs={{0,4},{4,0},{8,12},{12,8},{1,5},{5,1},{9,13},{13,9},{2,6},{6,2},{1... | collective-permute-start | bytes 294920 | tf_op jit(solution)/shard_map/ppermute | solution.py:245
  40.2 7.1 %collective-permute-start.21 = (bf16[32,1536]{1,0:T(8,128)(2,1)S(1)}, bf16[32,1536]{1,0:T(8,128)(2,1)S(1)}, u32[]{:S(2)}, u32[]{:S(2)}) collective-permute-start(bf16[32,1536]{1,0:T(8,128)(2,1)S(1)} %shard_map.107), channel_id=1, source_target_pairs={{0,8},{4,12},{8,0},{12,4},{1,9},{5,13},{9,1},{13,5},{2,10},{6,14},... | collective-permute-start | bytes 294920 | tf_op jit(solution)/shard_map/ppermute | solution.py:245
  47.6 6.5 %collective-permute-start.22 = (bf16[16,1536]{1,0:T(8,128)(2,1)S(1)}, bf16[16,1536]{1,0:T(8,128)(2,1)S(1)}, u32[]{:S(2)}, u32[]{:S(2)}) collective-permute-start(bf16[16,1536]{1,0:T(8,128)(2,1)S(1)} %get-tuple-element.55), channel_id=1, source_target_pairs={{0,16},{1,17},{2,18},{3,19},{16,0},{17,1},{18,2},{19,3},{4,20},{5,... | collective-permute-start | bytes 147464 | tf_op jit(solution)/shard_map/ppermute | solution.py:332
  49.1 4.9 %collective-permute-start.23 = (bf16[16,1536]{1,0:T(8,128)(2,1)S(1)}, bf16[16,1536]{1,0:T(8,128)(2,1)S(1)}, u32[]{:S(2)}, u32[]{:S(2)}) collective-permute-start(bf16[16,1536]{1,0:T(8,128)(2,1)S(1)} %get-tuple-element.56), channel_id=1, source_target_pairs={{0,17},{1,16},{2,19},{3,18},{16,1},{17,0},{18,3},{19,2},{4,21},{5,... | collective-permute-start | bytes 147464 | tf_op jit(solution)/shard_map/ppermute | solution.py:332
  49.1 5.5 %collective-permute-start.24 = (bf16[16,1536]{1,0:T(8,128)(2,1)S(1)}, bf16[16,1536]{1,0:T(8,128)(2,1)S(1)}, u32[]{:S(2)}, u32[]{:S(2)}) collective-permute-start(bf16[16,1536]{1,0:T(8,128)(2,1)S(1)} %get-tuple-element.57), channel_id=1, source_target_pairs={{0,18},{1,19},{2,16},{3,17},{16,2},{17,3},{18,0},{19,1},{4,22},{5,... | collective-permute-start | bytes 147464 | tf_op jit(solution)/shard_map/ppermute | solution.py:332
  50.0 4.9 %collective-permute-start.25 = (bf16[16,1536]{1,0:T(8,128)(2,1)S(1)}, bf16[16,1536]{1,0:T(8,128)(2,1)S(1)}, u32[]{:S(2)}, u32[]{:S(2)}) collective-permute-start(bf16[16,1536]{1,0:T(8,128)(2,1)S(1)} %get-tuple-element.58), channel_id=1, source_target_pairs={{0,19},{1,18},{2,17},{3,16},{16,3},{17,2},{18,1},{19,0},{4,23},{5,... | collective-permute-start | bytes 147464 | tf_op jit(solution)/shard_map/ppermute | solution.py:332

commit v2 on v1

--- a/solution.py
+++ b/solution.py
@@ -178,7 +178,8 @@
     slot = lax.broadcasted_iota(jnp.int32, (cap, tokens), 0).astype(F32)
     pick = jnp.where((count - 1.0 == slot) & (here > 0.5), 1.0, 0.0).astype(BF16)
     slots_ref[...] = jnp.dot(pick, all_rows[:, :data], preferred_element_type=F32).astype(BF16)
-    pick_ref[...] = pick
+    pick_ref[...] = jnp.zeros_like(pick_ref)
+    pick_ref[:, :tokens] = pick
 
 
 def expert_kernel(*refs):
@@ -211,23 +212,24 @@
         out[...] = terms.astype(BF16)
 
 
-def pair_kernel(own_ref, other_ref, *outs):
-    cap = outs[0].shape[0]
+def pair_kernel(own_ref, other_ref, pick_ref, *outs):
+    cap, half = outs[1].shape
     for k, out in enumerate(outs):
         rows = pl.ds(k * cap, cap)
-        out[...] = (own_ref[rows, :].astype(F32) + other_ref[rows, :].astype(F32)).astype(BF16)
+        out[:, :half] = (own_ref[rows, :].astype(F32) + other_ref[rows, :].astype(F32)).astype(BF16)
+    outs[0][:, half:] = pick_ref[...]
 
 
 def add_kernel(left_ref, right_ref, out_ref):
     out_ref[...] = (left_ref[...].astype(F32) + right_ref[...].astype(F32)).astype(BF16)
 
 
-def expand_kernel(own_ref, near_ref, far_ref, pick_ref, *refs):
+def expand_kernel(own_ref, near_ref, far_ref, *refs):
     outs, tokens_ref = refs[:4], refs[4]
-    rows = outs[0].shape[0]
+    rows, half = outs[0].shape
     e = lax.axis_index("et")
-    total = own_ref[...].astype(F32) + near_ref[...].astype(F32) + far_ref[...].astype(F32)
-    tokens_ref[...] = contract(pick_ref[...], total.astype(BF16), 0, 0).astype(BF16)
+    total = own_ref[:, :half].astype(F32) + near_ref[...].astype(F32) + far_ref[...].astype(F32)
+    tokens_ref[...] = contract(own_ref[:, half:], total.astype(BF16), 0, 0).astype(BF16)
     for steps, out in enumerate(outs):
         out[...] = tokens_ref[pl.ds(pl.multiple_of((e ^ steps) * rows, 16), rows), :]
 
@@ -243,6 +245,13 @@
 
 def swap(value, axis, steps):
     return lax.ppermute(value, axis, spread(steps))
+
+
+def hand(value, pipe_size, steps):
+    pairs = [
+        (4 * p + z, 4 * ((p - 1) % pipe_size) + (z ^ steps)) for p in range(pipe_size) for z in range(4)
+    ]
+    return lax.ppermute(value, ("pipe", "dp"), pairs)
 
 
 def on_device_four(tokens, out_grad, top_ids, route_probs, w_gate, w_up, w_down):
@@ -271,7 +280,7 @@
         space=HBM,
     )
     arrived = [packed[0]] + [swap(packed[s], "et", s) for s in (1, 2, 3)]
-    wg, wu, wd = call(
+    weights = call(
         stage_kernel,
         [like((hidden, width))] * 3,
         w_gate[0],
@@ -280,19 +289,20 @@
         scratch=[pltpu.SemaphoreType.DMA((3,))],
         space=HBM,
     )
+    arrived, (wg, wu, wd) = lax.optimization_barrier((arrived, weights))
     slot_block, pick = call(
         compact_kernel,
-        [like((cap, 2 * piece)), like((cap, 4 * rows))],
+        [like((cap, 2 * piece)), like((cap, FLAG))],
         *arrived,
         scratch=[pltpu.VMEM((4 * rows, 2 * piece + FLAG), BF16)],
     )
     near = swap(slot_block, "dp", 1)
     far = swap(slot_block, "dp", 2)
-    chip_own = swap(slot_block, "et", 2)
-    near, far, chip_own, wg, wu, wd = lax.optimization_barrier((near, far, chip_own, wg, wu, wd))
+    near, far = lax.optimization_barrier((near, far))
+    chip_near = swap(near, "et", 2)
     last = swap(far, "dp", 1)
     own = [slot_block, near, far, last]
-    chip = [chip_own] + [swap(block, "et", 2) for block in own[1:]]
+    chip = [swap(slot_block, "et", 2), chip_near, swap(far, "et", 2), swap(last, "et", 2)]
     core = [swap(block, "et", 1) for block in own]
     both = [swap(block, "et", 1) for block in chip]
     x, dz, act, gate_grad, up_grad, terms, away = call(
@@ -310,30 +320,32 @@
     )
     theirs = swap(away, "et", 1)
     home, to_near, to_far, to_last = call(
-        pair_kernel, [like((cap, half))] * 4, terms, theirs
-    )
-    (to_far,) = call(add_kernel, [like((cap, half))], to_far, swap(to_last, "dp", 1))
+        pair_kernel,
+        [like((cap, half + FLAG))] + [like((cap, half))] * 3,
+        terms,
+        theirs,
+        pick,
+    )
+    from_last = swap(to_last, "dp", 1)
+    home = hand(home, pipe_size, 0)
+    (to_far,) = call(add_kernel, [like((cap, half))], to_far, from_last)
+    to_far, to_near = lax.optimization_barrier((to_far, to_near))
+    from_far = hand(to_far, pipe_size, 2)
+    from_near = hand(to_near, pipe_size, 1)
+    grad_gate = contract(gate_grad, x, 0, 0).astype(BF16)
+    grad_up = contract(up_grad, x, 0, 0).astype(BF16)
+    from_far, grad_gate, grad_up = lax.optimization_barrier((from_far, grad_gate, grad_up))
     by_token = call(
         expand_kernel,
         [like((rows, half))] * 4,
         home,
-        swap(to_near, "dp", 1),
-        swap(to_far, "dp", 2),
-        pick,
-        scratch=[pltpu.VMEM((4 * rows, half), BF16)],
-    )
-    back = []
-    for s in range(4):
-        pairs = [
-            (4 * p + e, 4 * ((p - 1) % pipe_size) + (e ^ s))
-            for p in range(pipe_size)
-            for e in range(4)
-        ]
-        back.append(lax.ppermute(by_token[s], ("pipe", "et"), pairs))
+        from_near,
+        from_far,
+        scratch=[pltpu.VMEM((FLAG, half), BF16)],
+    )
+    back = [by_token[0]] + [swap(by_token[s], "et", s) for s in (1, 2, 3)]
     (handed,) = call(finish_kernel, [like((rows, width))], *back)
     grad_down = contract(act, dz, 0, 0).astype(BF16)
-    grad_gate = contract(gate_grad, x, 0, 0).astype(BF16)
-    grad_up = contract(up_grad, x, 0, 0).astype(BF16)
     return (handed[None, None], grad_gate[None], grad_up[None], grad_down[None])
 
 

time: 56.1 us -> 54.9 us (0.979)
  starting transfers between devices: 22.8 us -> 22.2 us
    ppermute x22 -> x23, waiting for transfers between devices: 16.7 us -> 13.8 us  [swap(): return lax.ppermute(value, axis, spread(steps))]
    ppermute x4 -> x3, waiting for transfers between devices: 0.8 us -> 3.41 us  [hand(): return lax.ppermute(value, ('pipe', 'dp'), pairs)]
    ppermute x22 -> x23, starting transfers between devices: 18.3 us -> 16.7 us  [swap(): return lax.ppermute(value, axis, spread(steps))]
    ppermute x4 -> x3, starting transfers between devices: 4.46 us -> 5.51 us  [hand(): return lax.ppermute(value, ('pipe', 'dp'), pairs)]
  transfers between devices with their start and end apart: 26 -> 26, of which waited for: 14 -> 13; matrix products, arithmetic and copies ran while one was open for 11% -> 11% of each run, Pallas kernels for 5% -> 5%
where the time goes in v2:
time: 54.9 us; the launch traced here: 54.8 us
  starting transfers between devices  22.2 us (40%)
  waiting for transfers between devices  17.3 us (32%)
  Pallas kernels  8.52 us (16%)
  matrix products  6.07 us (11%)
  between operations  0.74 us (1%)
    ppermute x23, starting transfers between devices, swap(): return lax.ppermute(value, axis, spread(steps))  16.7 us
    ppermute x23, waiting for transfers between devices, swap(): return lax.ppermute(value, axis, spread(steps))  13.8 us
    pallas_call x8, Pallas kernels, call(): pl.pallas_call(kernel, out_shape=outs, in_specs=[space] * len(args), out_...  8.52 us
    dot_general x3, matrix products, contract(): lax.dot_general(left, right, (((left_dim,), (right_dim,)), ((), ())), pre...  6.07 us
    ppermute x3, starting transfers between devices, hand(): return lax.ppermute(value, ('pipe', 'dp'), pairs)  5.51 us
    ppermute x3, waiting for transfers between devices, hand(): return lax.ppermute(value, ('pipe', 'dp'), pairs)  3.41 us
  transfers between devices with their start and end apart: 26, of which 13 were waited for; matrix products, arithmetic and copies ran while one was open for 11% of the time, Pallas kernels for 5%

profile of v2, /device:TPU:0, one launch (start us, length us, event | category | flops | bytes accessed | tf_op | source)
XLA Modules:
  0.0 54.8 jit_solution(15403039465725735570)
XLA Ops:
  0.6 1.1 %shard_map.102 = (bf16[16,1664]{1,0:T(8,128)(2,1)S(1)}, bf16[16,1664]{1,0:T(8,128)(2,1)S(1)}, bf16[16,1664]{1,0:T(8,128)(2,1)S(1)}, bf16[16,1664]{1,0:T(8,128)(2,1)S(1)}) custom-call(bf16[16,3072]{1,0:T(8,128)(2,1)} %bitcast.27, bf16[16,3072]{1,0:T(8,128)(2,1)} %bitcast.28, s32[4,16]{1,0:T(4,128)} %bitcast.30, f32[4,16]{1,0:T(4,128)} %bitcast.31), custom_call_target="tpu_custom_call" | custom-call | bytes 410112 | tf_op jit(solution)/shard_map/pallas_call | solution.py:107
  1.7 0.5 collective-permute-start
  2.2 2.6 %collective-permute-start.1 = (bf16[16,1664]{1,0:T(8,128)(2,1)S(1)}, bf16[16,1664]{1,0:T(8,128)(2,1)S(1)}, u32[]{:S(2)}, u32[]{:S(2)}) collective-permute-start(bf16[16,1664]{1,0:T(8,128)(2,1)S(1)} %get-tuple-element.44), channel_id=1, source_target_pairs={{0,2},{1,3},{2,0},{3,1},{4,6},{5,7},{6,4},{7,5},{8,10},{9,11},{10,... | collective-permute-start | bytes 159752 | tf_op jit(solution)/shard_map/ppermute | solution.py:247
  4.8 0.1 collective-permute-start.2
  4.9 2.9 %shard_map.103 = (bf16[336,3072]{1,0:T(8,128)(2,1)S(1)}, bf16[336,3072]{1,0:T(8,128)(2,1)S(1)}, bf16[336,3072]{1,0:T(8,128)(2,1)S(1)}) custom-call(bf16[336,3072]{1,0:T(8,128)(2,1)} %bitcast.22, bf16[336,3072]{1,0:T(8,128)(2,1)} %bitcast.23, bf16[336,3072]{1,0:T(8,128)(2,1)} %bitcast.24), custom_call_target="tpu_custom_call" | custom-call | bytes 12386304 | tf_op jit(solution)/shard_map/pallas_call | solution.py:107
  7.8 0.0 collective-permute-done.refs_1_
  7.8 0.0 collective-permute-done.1.refs_2_
  7.8 0.8 %collective-permute-done.2.refs_3_ = bf16[16,1664]{1,0:T(8,128)(2,1)S(1)} collective-permute-done((bf16[16,1664]{1,0:T(8,128)(2,1)S(1)}, bf16[16,1664]{1,0:T(8,128)(2,1)S(1)}, u32[]{:S(2)}, u32[]{:S(2)}) %collective-permute-start.2) | collective-permute-done | bytes 53280 | tf_op jit(solution)/shard_map/ppermute | solution.py:247
  8.6 0.3 shard_map.104
  9.0 2.7 %collective-permute-start.4 = (bf16[32,1536]{1,0:T(8,128)(2,1)S(1)}, bf16[32,1536]{1,0:T(8,128)(2,1)S(1)}, u32[]{:S(2)}, u32[]{:S(2)}) collective-permute-start(bf16[32,1536]{1,0:T(8,128)(2,1)S(1)} %get-tuple-element.53.refs_0_), channel_id=1, source_target_pairs={{0,8},{4,12},{8,0},{12,4},{1,9},{5,13},{9,1},{13,5},{2,10},{6,14},... | collective-permute-start | bytes 294920 | tf_op jit(solution)/shard_map/ppermute | solution.py:247
  11.6 1.6 %collective-permute-start.3 = (bf16[32,1536]{1,0:T(8,128)(2,1)S(1)}, bf16[32,1536]{1,0:T(8,128)(2,1)S(1)}, u32[]{:S(2)}, u32[]{:S(2)}) collective-permute-start(bf16[32,1536]{1,0:T(8,128)(2,1)S(1)} %get-tuple-element.53.refs_0_), channel_id=1, source_target_pairs={{0,4},{4,0},{8,12},{12,8},{1,5},{5,1},{9,13},{13,9},{2,6},{6,2},{1... | collective-permute-start | bytes 294920 | tf_op jit(solution)/shard_map/ppermute | solution.py:247
  13.2 1.1 %collective-permute-start.10 = (bf16[32,1536]{1,0:T(8,128)(2,1)S(1)}, bf16[32,1536]{1,0:T(8,128)(2,1)S(1)}, u32[]{:S(2)}, u32[]{:S(2)}) collective-permute-start(bf16[32,1536]{1,0:T(8,128)(2,1)S(1)} %get-tuple-element.53.refs_0_), channel_id=1, source_target_pairs={{0,2},{1,3},{2,0},{3,1},{4,6},{5,7},{6,4},{7,5},{8,10},{9,11},{10,... | collective-permute-start | bytes 294920 | tf_op jit(solution)/shard_map/ppermute | solution.py:247
  14.3 0.0 collective-permute-start.6
  14.3 2.7 %collective-permute-done.4.refs_2_ = bf16[32,1536]{1,0:T(8,128)(2,1)S(1)} collective-permute-done((bf16[32,1536]{1,0:T(8,128)(2,1)S(1)}, bf16[32,1536]{1,0:T(8,128)(2,1)S(1)}, u32[]{:S(2)}, u32[]{:S(2)}) %collective-permute-start.4) | collective-permute-done | bytes 98336 | tf_op jit(solution)/shard_map/ppermute | solution.py:247
  17.0 0.2 collective-permute-done.3.refs_1_
  17.2 1.4 %collective-permute-start.5 = (bf16[32,1536]{1,0:T(8,128)(2,1)S(1)}, bf16[32,1536]{1,0:T(8,128)(2,1)S(1)}, u32[]{:S(2)}, u32[]{:S(2)}) collective-permute-start(bf16[32,1536]{1,0:T(8,128)(2,1)S(1)} %collective-permute-done.4.refs_2_), channel_id=1, source_target_pairs={{0,4},{4,0},{8,12},{12,8},{1,5},{5,1},{9,13},{13,9},{2,6},{6,2},{1... | collective-permute-start | bytes 294920 | tf_op jit(solution)/shard_map/ppermute | solution.py:247
  18.6 1.2 %collective-permute-start.11 = (bf16[32,1536]{1,0:T(8,128)(2,1)S(1)}, bf16[32,1536]{1,0:T(8,128)(2,1)S(1)}, u32[]{:S(2)}, u32[]{:S(2)}) collective-permute-start(bf16[32,1536]{1,0:T(8,128)(2,1)S(1)} %collective-permute-done.3.refs_1_), channel_id=1, source_target_pairs={{0,2},{1,3},{2,0},{3,1},{4,6},{5,7},{6,4},{7,5},{8,10},{9,11},{10,... | collective-permute-start | bytes 294920 | tf_op jit(solution)/shard_map/ppermute | solution.py:247
  19.8 0.2 collective-permute-start.7
  20.0 0.8 %collective-permute-start.12 = (bf16[32,1536]{1,0:T(8,128)(2,1)S(1)}, bf16[32,1536]{1,0:T(8,128)(2,1)S(1)}, u32[]{:S(2)}, u32[]{:S(2)}) collective-permute-start(bf16[32,1536]{1,0:T(8,128)(2,1)S(1)} %collective-permute-done.4.refs_2_), channel_id=1, source_target_pairs={{0,2},{1,3},{2,0},{3,1},{4,6},{5,7},{6,4},{7,5},{8,10},{9,11},{10,... | collective-permute-start | bytes 294920 | tf_op jit(solution)/shard_map/ppermute | solution.py:247
  20.9 1.0 %collective-permute-done.5.refs_3_ = bf16[32,1536]{1,0:T(8,128)(2,1)S(1)} collective-permute-done((bf16[32,1536]{1,0:T(8,128)(2,1)S(1)}, bf16[32,1536]{1,0:T(8,128)(2,1)S(1)}, u32[]{:S(2)}, u32[]{:S(2)}) %collective-permute-start.5) | collective-permute-done | bytes 98336 | tf_op jit(solution)/shard_map/ppermute | solution.py:247
  21.9 1.2 %collective-permute-start.13 = (bf16[32,1536]{1,0:T(8,128)(2,1)S(1)}, bf16[32,1536]{1,0:T(8,128)(2,1)S(1)}, u32[]{:S(2)}, u32[]{:S(2)}) collective-permute-start(bf16[32,1536]{1,0:T(8,128)(2,1)S(1)} %collective-permute-done.5.refs_3_), channel_id=1, source_target_pairs={{0,2},{1,3},{2,0},{3,1},{4,6},{5,7},{6,4},{7,5},{8,10},{9,11},{10,... | collective-permute-start | bytes 294920 | tf_op jit(solution)/shard_map/ppermute | solution.py:247
  23.0 0.0 collective-permute-done.14.refs_12_
  23.0 0.0 collective-permute-start.8
  23.0 1.2 %collective-permute-done.11.refs_9_ = bf16[32,1536]{1,0:T(8,128)(2,1)S(1)} collective-permute-done((bf16[32,1536]{1,0:T(8,128)(2,1)S(1)}, bf16[32,1536]{1,0:T(8,128)(2,1)S(1)}, u32[]{:S(2)}, u32[]{:S(2)}) %collective-permute-start.11) | collective-permute-done | bytes 98336 | tf_op jit(solution)/shard_map/ppermute | solution.py:247
  24.2 0.5 collective-permute-start.15
  24.7 1.6 %collective-permute-done.12.refs_10_ = bf16[32,1536]{1,0:T(8,128)(2,1)S(1)} collective-permute-done((bf16[32,1536]{1,0:T(8,128)(2,1)S(1)}, bf16[32,1536]{1,0:T(8,128)(2,1)S(1)}, u32[]{:S(2)}, u32[]{:S(2)}) %collective-permute-start.12) | collective-permute-done | bytes 98336 | tf_op jit(solution)/shard_map/ppermute | solution.py:247
  26.3 1.7 %collective-permute-done.13.refs_11_ = bf16[32,1536]{1,0:T(8,128)(2,1)S(1)} collective-permute-done((bf16[32,1536]{1,0:T(8,128)(2,1)S(1)}, bf16[32,1536]{1,0:T(8,128)(2,1)S(1)}, u32[]{:S(2)}, u32[]{:S(2)}) %collective-permute-start.13) | collective-permute-done | bytes 98336 | tf_op jit(solution)/shard_map/ppermute | solution.py:247
  28.1 1.3 %collective-permute-done.17.refs_15_ = bf16[32,1536]{1,0:T(8,128)(2,1)S(1)} collective-permute-done((bf16[32,1536]{1,0:T(8,128)(2,1)S(1)}, bf16[32,1536]{1,0:T(8,128)(2,1)S(1)}, u32[]{:S(2)}, u32[]{:S(2)}) %collective-permute-start.17) | collective-permute-done | bytes 98336 | tf_op jit(solution)/shard_map/ppermute | solution.py:247
  29.3 3.2 %shard_map.105 = (bf16[128,3072]{1,0:T(8,128)(2,1)S(1)}, bf16[128,3072]{1,0:T(8,128)(2,1)S(1)}, bf16[128,336]{1,0:T(8,128)(2,1)S(1)}, bf16[128,336]{1,0:T(8,128)...) custom-call(bf16[32,1536]{1,0:T(8,128)(2,1)S(1)} %get-tuple-element.53.refs_0_, ...), custom_call_target="tpu_custom_call" | custom-call | flops 1321205760 | bytes 10383360 | tf_op jit(solution)/shard_map/pallas_call | solution.py:107
  32.5 0.2 collective-permute-start.18
  32.7 1.6 %collective-permute-done.18.other_ref = bf16[128,1536]{1,0:T(8,128)(2,1)S(1)} collective-permute-done((bf16[128,1536]{1,0:T(8,128)(2,1)S(1)}, bf16[128,1536]{1,0:T(8,128)(2,1)S(1)}, u32[]{:S(2)}, u32[]{:S(2)}) %collective-permute-start.18) | collective-permute-done | bytes 393248 | tf_op jit(solution)/shard_map/ppermute | solution.py:247
  34.3 0.1 shard_map.106
  34.4 0.7 %collective-permute-start.20 = (bf16[32,1536]{1,0:T(8,128)(2,1)S(1)}, bf16[32,1536]{1,0:T(8,128)(2,1)S(1)}, u32[]{:S(2)}, u32[]{:S(2)}) collective-permute-start(bf16[32,1536]{1,0:T(8,128)(2,1)S(1)} %get-tuple-element.64), channel_id=1, source_target_pairs={{0,4},{4,0},{8,12},{12,8},{1,5},{5,1},{9,13},{13,9},{2,6},{6,2},{1... | collective-permute-start | bytes 294920 | tf_op jit(solution)/shard_map/ppermute | solution.py:247
  35.1 2.0 %convolution_convert_fusion.2 = bf16[336,3072]{1,0:T(8,128)(2,1)} fusion(bf16[128,336]{1,0:T(8,128)(2,1)S(1)} %get-tuple-element.68, bf16[128,3072]{1,0:T(8,128)(2,1)S(1)} %get-tuple-element.69), kind=kOutput, calls=%fused_computation.2 | convolution fusion | flops 265273344 | bytes 2936832 | tf_op jit(solution)/shard_map/dot_general | solution.py:40
  37.1 1.5 %collective-permute-start.19 = (bf16[32,1664]{1,0:T(8,128)(2,1)S(1)}, bf16[32,1664]{1,0:T(8,128)(2,1)S(1)}, u32[]{:S(2)}, u32[]{:S(2)}) collective-permute-start(bf16[32,1664]{1,0:T(8,128)(2,1)S(1)} %get-tuple-element.62), channel_id=1, source_target_pairs={{0,16},{4,20},{8,24},{12,28},{16,0},{20,4},{24,8},{28,12},{1,17},{... | collective-permute-start | bytes 319496 | tf_op jit(solution)/shard_map/ppermute | solution.py:254
  38.6 0.7 %collective-permute-done.20.right_ref = bf16[32,1536]{1,0:T(8,128)(2,1)S(1)} collective-permute-done((bf16[32,1536]{1,0:T(8,128)(2,1)S(1)}, bf16[32,1536]{1,0:T(8,128)(2,1)S(1)}, u32[]{:S(2)}, u32[]{:S(2)}) %collective-permute-start.20) | collective-permute-done | bytes 98336 | tf_op jit(solution)/shard_map/ppermute | solution.py:247
  39.3 1.6 %collective-permute-start.21 = (bf16[32,1536]{1,0:T(8,128)(2,1)S(1)}, bf16[32,1536]{1,0:T(8,128)(2,1)S(1)}, u32[]{:S(2)}, u32[]{:S(2)}) collective-permute-start(bf16[32,1536]{1,0:T(8,128)(2,1)S(1)} %get-tuple-element.66), channel_id=1, source_target_pairs={{0,20},{4,16},{8,28},{12,24},{16,4},{20,0},{24,12},{28,8},{1,21},{... | collective-permute-start | bytes 294920 | tf_op jit(solution)/shard_map/ppermute | solution.py:254
  41.0 2.4 %collective-permute-start.22 = (bf16[32,1536]{1,0:T(8,128)(2,1)S(1)}, bf16[32,1536]{1,0:T(8,128)(2,1)S(1)}, u32[]{:S(2)}, u32[]{:S(2)}) collective-permute-start(bf16[32,1536]{1,0:T(8,128)(2,1)S(1)} %shard_map.107), channel_id=1, source_target_pairs={{0,24},{4,28},{8,16},{12,20},{16,8},{20,12},{24,0},{28,4},{1,25},{... | collective-permute-start | bytes 294920 | tf_op jit(solution)/shard_map/ppermute | solution.py:254
  43.3 2.0 %convolution_convert_fusion.1 = bf16[336,3072]{1,0:T(8,128)(2,1)} fusion(bf16[128,336]{1,0:T(8,128)(2,1)S(1)} %get-tuple-element.70, bf16[128,3072]{1,0:T(8,128)(2,1)S(1)} %get-tuple-element.69), kind=kOutput, calls=%fused_computation.1 | convolution fusion | flops 265273344 | bytes 2936832 | tf_op jit(solution)/shard_map/dot_general | solution.py:40
  45.4 3.4 %collective-permute-done.22.far_ref = bf16[32,1536]{1,0:T(8,128)(2,1)S(1)} collective-permute-done((bf16[32,1536]{1,0:T(8,128)(2,1)S(1)}, bf16[32,1536]{1,0:T(8,128)(2,1)S(1)}, u32[]{:S(2)}, u32[]{:S(2)}) %collective-permute-start.22) | collective-permute-done | bytes 98336 | tf_op jit(solution)/shard_map/ppermute | solution.py:254
  48.8 0.3 shard_map.108
  49.1 0.1 collective-permute-start.23
  49.2 1.2 %collective-permute-start.24 = (bf16[16,1536]{1,0:T(8,128)(2,1)S(1)}, bf16[16,1536]{1,0:T(8,128)(2,1)S(1)}, u32[]{:S(2)}, u32[]{:S(2)}) collective-permute-start(bf16[16,1536]{1,0:T(8,128)(2,1)S(1)} %get-tuple-element.74), channel_id=1, source_target_pairs={{0,2},{1,3},{2,0},{3,1},{4,6},{5,7},{6,4},{7,5},{8,10},{9,11},{10,... | collective-permute-start | bytes 147464 | tf_op jit(solution)/shard_map/ppermute | solution.py:247
  50.4 0.6 %collective-permute-start.25 = (bf16[16,1536]{1,0:T(8,128)(2,1)S(1)}, bf16[16,1536]{1,0:T(8,128)(2,1)S(1)}, u32[]{:S(2)}, u32[]{:S(2)}) collective-permute-start(bf16[16,1536]{1,0:T(8,128)(2,1)S(1)} %get-tuple-element.75), channel_id=1, source_target_pairs={{0,3},{1,2},{2,1},{3,0},{4,7},{5,6},{6,5},{7,4},{8,11},{9,10},{10,... | collective-permute-start | bytes 147464 | tf_op jit(solution)/shard_map/ppermute | solution.py:247
  51.0 2.0 %fusion = bf16[1,336,3072]{2,1,0:T(8,128)(2,1)} fusion(bf16[128,336]{1,0:T(8,128)(2,1)S(1)} %get-tuple-element.78, bf16[128,3072]{1,0:T(8,128)(2,1)S(1)} %get-tuple-element.79), kind=kOutput, calls=%fused_computation.3 | convolution fusion | flops 265273344 | bytes 2936832 | tf_op jit(solution)/shard_map/dot_general | solution.py:40
  53.0 0.3 collective-permute-done.24.chip_ref
  53.3 0.8 %collective-permute-done.25.both_ref = bf16[16,1536]{1,0:T(8,128)(2,1)S(1)} collective-permute-done((bf16[16,1536]{1,0:T(8,128)(2,1)S(1)}, bf16[16,1536]{1,0:T(8,128)(2,1)S(1)}, u32[]{:S(2)}, u32[]{:S(2)}) %collective-permute-start.25) | collective-permute-done | bytes 49184 | tf_op jit(solution)/shard_map/ppermute | solution.py:247
  54.1 0.7 %shard_map.109 = bf16[16,3072]{1,0:T(8,128)(2,1)} custom-call(bf16[16,1536]{1,0:T(8,128)(2,1)S(1)} %get-tuple-element.72.own_ref, bf16[16,1536]{1,0:T(8,128)(2,1)S(1)} %collective-permute-done.23.core_ref, bf16[16,1536]{1,0:T(8,128)(2,1)S(1)} %collective-permute-done.24.chip_ref, bf16[16,1536]{1,0:T(8,128)(2,1)S(1)} %collective-permute-done.25.both_ref), custom_call_target="tpu_custom_call" | custom-call | bytes 294912 | tf_op jit(solution)/shard_map/pallas_call | solution.py:107
  (15 shorter events, 0.1 us)
Async XLA Ops:
  1.7 6.0 %collective-permute-start = (bf16[16,1664]{1,0:T(8,128)(2,1)S(1)}, bf16[16,1664]{1,0:T(8,128)(2,1)S(1)}, u32[]{:S(2)}, u32[]{:S(2)}) collective-permute-start(bf16[16,1664]{1,0:T(8,128)(2,1)S(1)} %get-tuple-element.43), channel_id=1, source_target_pairs={{0,1},{1,0},{2,3},{3,2},{4,5},{5,4},{6,7},{7,6},{8,9},{9,8},{10,11... | collective-permute-start | bytes 159752 | tf_op jit(solution)/shard_map/ppermute | solution.py:247
  2.2 5.5 %collective-permute-start.1 = (bf16[16,1664]{1,0:T(8,128)(2,1)S(1)}, bf16[16,1664]{1,0:T(8,128)(2,1)S(1)}, u32[]{:S(2)}, u32[]{:S(2)}) collective-permute-start(bf16[16,1664]{1,0:T(8,128)(2,1)S(1)} %get-tuple-element.44), channel_id=1, source_target_pairs={{0,2},{1,3},{2,0},{3,1},{4,6},{5,7},{6,4},{7,5},{8,10},{9,11},{10,... | collective-permute-start | bytes 159752 | tf_op jit(solution)/shard_map/ppermute | solution.py:247
  4.8 3.8 %collective-permute-start.2 = (bf16[16,1664]{1,0:T(8,128)(2,1)S(1)}, bf16[16,1664]{1,0:T(8,128)(2,1)S(1)}, u32[]{:S(2)}, u32[]{:S(2)}) collective-permute-start(bf16[16,1664]{1,0:T(8,128)(2,1)S(1)} %get-tuple-element.45), channel_id=1, source_target_pairs={{0,3},{1,2},{2,1},{3,0},{4,7},{5,6},{6,5},{7,4},{8,11},{9,10},{10,... | collective-permute-start | bytes 159752 | tf_op jit(solution)/shard_map/ppermute | solution.py:247
  9.0 8.0 %collective-permute-start.4 = (bf16[32,1536]{1,0:T(8,128)(2,1)S(1)}, bf16[32,1536]{1,0:T(8,128)(2,1)S(1)}, u32[]{:S(2)}, u32[]{:S(2)}) collective-permute-start(bf16[32,1536]{1,0:T(8,128)(2,1)S(1)} %get-tuple-element.53.refs_0_), channel_id=1, source_target_pairs={{0,8},{4,12},{8,0},{12,4},{1,9},{5,13},{9,1},{13,5},{2,10},{6,14},... | collective-permute-start | bytes 294920 | tf_op jit(solution)/shard_map/ppermute | solution.py:247
  11.6 5.6 %collective-permute-start.3 = (bf16[32,1536]{1,0:T(8,128)(2,1)S(1)}, bf16[32,1536]{1,0:T(8,128)(2,1)S(1)}, u32[]{:S(2)}, u32[]{:S(2)}) collective-permute-start(bf16[32,1536]{1,0:T(8,128)(2,1)S(1)} %get-tuple-element.53.refs_0_), channel_id=1, source_target_pairs={{0,4},{4,0},{8,12},{12,8},{1,5},{5,1},{9,13},{13,9},{2,6},{6,2},{1... | collective-permute-start | bytes 294920 | tf_op jit(solution)/shard_map/ppermute | solution.py:247
  13.2 5.4 %collective-permute-start.10 = (bf16[32,1536]{1,0:T(8,128)(2,1)S(1)}, bf16[32,1536]{1,0:T(8,128)(2,1)S(1)}, u32[]{:S(2)}, u32[]{:S(2)}) collective-permute-start(bf16[32,1536]{1,0:T(8,128)(2,1)S(1)} %get-tuple-element.53.refs_0_), channel_id=1, source_target_pairs={{0,2},{1,3},{2,0},{3,1},{4,6},{5,7},{6,4},{7,5},{8,10},{9,11},{10,... | collective-permute-start | bytes 294920 | tf_op jit(solution)/shard_map/ppermute | solution.py:247
  14.3 5.7 %collective-permute-start.6 = (bf16[32,1536]{1,0:T(8,128)(2,1)S(1)}, bf16[32,1536]{1,0:T(8,128)(2,1)S(1)}, u32[]{:S(2)}, u32[]{:S(2)}) collective-permute-start(bf16[32,1536]{1,0:T(8,128)(2,1)S(1)} %get-tuple-element.53.refs_0_), channel_id=1, source_target_pairs={{0,1},{1,0},{2,3},{3,2},{4,5},{5,4},{6,7},{7,6},{8,9},{9,8},{10,11... | collective-permute-start | bytes 294920 | tf_op jit(solution)/shard_map/ppermute | solution.py:247
  17.2 4.6 %collective-permute-start.5 = (bf16[32,1536]{1,0:T(8,128)(2,1)S(1)}, bf16[32,1536]{1,0:T(8,128)(2,1)S(1)}, u32[]{:S(2)}, u32[]{:S(2)}) collective-permute-start(bf16[32,1536]{1,0:T(8,128)(2,1)S(1)} %collective-permute-done.4.refs_2_), channel_id=1, source_target_pairs={{0,4},{4,0},{8,12},{12,8},{1,5},{5,1},{9,13},{13,9},{2,6},{6,2},{1... | collective-permute-start | bytes 294920 | tf_op jit(solution)/shard_map/ppermute | solution.py:247
  18.6 4.4 %collective-permute-start.14 = (bf16[32,1536]{1,0:T(8,128)(2,1)S(1)}, bf16[32,1536]{1,0:T(8,128)(2,1)S(1)}, u32[]{:S(2)}, u32[]{:S(2)}) collective-permute-start(bf16[32,1536]{1,0:T(8,128)(2,1)S(1)} %collective-permute-done.10.refs_8_), channel_id=1, source_target_pairs={{0,1},{1,0},{2,3},{3,2},{4,5},{5,4},{6,7},{7,6},{8,9},{9,8},{10,11... | collective-permute-start | bytes 294920 | tf_op jit(solution)/shard_map/ppermute | solution.py:247
  18.6 5.6 %collective-permute-start.11 = (bf16[32,1536]{1,0:T(8,128)(2,1)S(1)}, bf16[32,1536]{1,0:T(8,128)(2,1)S(1)}, u32[]{:S(2)}, u32[]{:S(2)}) collective-permute-start(bf16[32,1536]{1,0:T(8,128)(2,1)S(1)} %collective-permute-done.3.refs_1_), channel_id=1, source_target_pairs={{0,2},{1,3},{2,0},{3,1},{4,6},{5,7},{6,4},{7,5},{8,10},{9,11},{10,... | collective-permute-start | bytes 294920 | tf_op jit(solution)/shard_map/ppermute | solution.py:247
  19.8 4.4 %collective-permute-start.7 = (bf16[32,1536]{1,0:T(8,128)(2,1)S(1)}, bf16[32,1536]{1,0:T(8,128)(2,1)S(1)}, u32[]{:S(2)}, u32[]{:S(2)}) collective-permute-start(bf16[32,1536]{1,0:T(8,128)(2,1)S(1)} %collective-permute-done.3.refs_1_), channel_id=1, source_target_pairs={{0,1},{1,0},{2,3},{3,2},{4,5},{5,4},{6,7},{7,6},{8,9},{9,8},{10,11... | collective-permute-start | bytes 294920 | tf_op jit(solution)/shard_map/ppermute | solution.py:247
  20.0 6.3 %collective-permute-start.12 = (bf16[32,1536]{1,0:T(8,128)(2,1)S(1)}, bf16[32,1536]{1,0:T(8,128)(2,1)S(1)}, u32[]{:S(2)}, u32[]{:S(2)}) collective-permute-start(bf16[32,1536]{1,0:T(8,128)(2,1)S(1)} %collective-permute-done.4.refs_2_), channel_id=1, source_target_pairs={{0,2},{1,3},{2,0},{3,1},{4,6},{5,7},{6,4},{7,5},{8,10},{9,11},{10,... | collective-permute-start | bytes 294920 | tf_op jit(solution)/shard_map/ppermute | solution.py:247
  21.9 6.2 %collective-permute-start.13 = (bf16[32,1536]{1,0:T(8,128)(2,1)S(1)}, bf16[32,1536]{1,0:T(8,128)(2,1)S(1)}, u32[]{:S(2)}, u32[]{:S(2)}) collective-permute-start(bf16[32,1536]{1,0:T(8,128)(2,1)S(1)} %collective-permute-done.5.refs_3_), channel_id=1, source_target_pairs={{0,2},{1,3},{2,0},{3,1},{4,6},{5,7},{6,4},{7,5},{8,10},{9,11},{10,... | collective-permute-start | bytes 294920 | tf_op jit(solution)/shard_map/ppermute | solution.py:247
  23.0 5.0 %collective-permute-start.8 = (bf16[32,1536]{1,0:T(8,128)(2,1)S(1)}, bf16[32,1536]{1,0:T(8,128)(2,1)S(1)}, u32[]{:S(2)}, u32[]{:S(2)}) collective-permute-start(bf16[32,1536]{1,0:T(8,128)(2,1)S(1)} %collective-permute-done.4.refs_2_), channel_id=1, source_target_pairs={{0,1},{1,0},{2,3},{3,2},{4,5},{5,4},{6,7},{7,6},{8,9},{9,8},{10,11... | collective-permute-start | bytes 294920 | tf_op jit(solution)/shard_map/ppermute | solution.py:247
  24.2 3.9 %collective-permute-start.9 = (bf16[32,1536]{1,0:T(8,128)(2,1)S(1)}, bf16[32,1536]{1,0:T(8,128)(2,1)S(1)}, u32[]{:S(2)}, u32[]{:S(2)}) collective-permute-start(bf16[32,1536]{1,0:T(8,128)(2,1)S(1)} %collective-permute-done.5.refs_3_), channel_id=1, source_target_pairs={{0,1},{1,0},{2,3},{3,2},{4,5},{5,4},{6,7},{7,6},{8,9},{9,8},{10,11... | collective-permute-start | bytes 294920 | tf_op jit(solution)/shard_map/ppermute | solution.py:247
  24.2 3.8 %collective-permute-start.15 = (bf16[32,1536]{1,0:T(8,128)(2,1)S(1)}, bf16[32,1536]{1,0:T(8,128)(2,1)S(1)}, u32[]{:S(2)}, u32[]{:S(2)}) collective-permute-start(bf16[32,1536]{1,0:T(8,128)(2,1)S(1)} %collective-permute-done.11.refs_9_), channel_id=1, source_target_pairs={{0,1},{1,0},{2,3},{3,2},{4,5},{5,4},{6,7},{7,6},{8,9},{9,8},{10,11... | collective-permute-start | bytes 294920 | tf_op jit(solution)/shard_map/ppermute | solution.py:247
  26.3 1.7 %collective-permute-start.16 = (bf16[32,1536]{1,0:T(8,128)(2,1)S(1)}, bf16[32,1536]{1,0:T(8,128)(2,1)S(1)}, u32[]{:S(2)}, u32[]{:S(2)}) collective-permute-start(bf16[32,1536]{1,0:T(8,128)(2,1)S(1)} %collective-permute-done.12.refs_10_), channel_id=1, source_target_pairs={{0,1},{1,0},{2,3},{3,2},{4,5},{5,4},{6,7},{7,6},{8,9},{9,8},{10,11... | collective-permute-start | bytes 294920 | tf_op jit(solution)/shard_map/ppermute | solution.py:247
  28.0 1.3 %collective-permute-start.17 = (bf16[32,1536]{1,0:T(8,128)(2,1)S(1)}, bf16[32,1536]{1,0:T(8,128)(2,1)S(1)}, u32[]{:S(2)}, u32[]{:S(2)}) collective-permute-start(bf16[32,1536]{1,0:T(8,128)(2,1)S(1)} %collective-permute-done.13.refs_11_), channel_id=1, source_target_pairs={{0,1},{1,0},{2,3},{3,2},{4,5},{5,4},{6,7},{7,6},{8,9},{9,8},{10,11... | collective-permute-start | bytes 294920 | tf_op jit(solution)/shard_map/ppermute | solution.py:247
  32.5 1.8 %collective-permute-start.18 = (bf16[128,1536]{1,0:T(8,128)(2,1)S(1)}, bf16[128,1536]{1,0:T(8,128)(2,1)S(1)}, u32[]{:S(2)}, u32[]{:S(2)}) collective-permute-start(bf16[128,1536]{1,0:T(8,128)(2,1)S(1)} %get-tuple-element.60), channel_id=1, source_target_pairs={{0,1},{1,0},{2,3},{3,2},{4,5},{5,4},{6,7},{7,6},{8,9},{9,8},{10,11... | collective-permute-start | bytes 1179656 | tf_op jit(solution)/shard_map/ppermute | solution.py:247
  34.4 4.9 %collective-permute-start.20 = (bf16[32,1536]{1,0:T(8,128)(2,1)S(1)}, bf16[32,1536]{1,0:T(8,128)(2,1)S(1)}, u32[]{:S(2)}, u32[]{:S(2)}) collective-permute-start(bf16[32,1536]{1,0:T(8,128)(2,1)S(1)} %get-tuple-element.64), channel_id=1, source_target_pairs={{0,4},{4,0},{8,12},{12,8},{1,5},{5,1},{9,13},{13,9},{2,6},{6,2},{1... | collective-permute-start | bytes 294920 | tf_op jit(solution)/shard_map/ppermute | solution.py:247
  37.1 11.7 %collective-permute-start.19 = (bf16[32,1664]{1,0:T(8,128)(2,1)S(1)}, bf16[32,1664]{1,0:T(8,128)(2,1)S(1)}, u32[]{:S(2)}, u32[]{:S(2)}) collective-permute-start(bf16[32,1664]{1,0:T(8,128)(2,1)S(1)} %get-tuple-element.62), channel_id=1, source_target_pairs={{0,16},{4,20},{8,24},{12,28},{16,0},{20,4},{24,8},{28,12},{1,17},{... | collective-permute-start | bytes 319496 | tf_op jit(solution)/shard_map/ppermute | solution.py:254
  39.3 9.4 %collective-permute-start.21 = (bf16[32,1536]{1,0:T(8,128)(2,1)S(1)}, bf16[32,1536]{1,0:T(8,128)(2,1)S(1)}, u32[]{:S(2)}, u32[]{:S(2)}) collective-permute-start(bf16[32,1536]{1,0:T(8,128)(2,1)S(1)} %get-tuple-element.66), channel_id=1, source_target_pairs={{0,20},{4,16},{8,28},{12,24},{16,4},{20,0},{24,12},{28,8},{1,21},{... | collective-permute-start | bytes 294920 | tf_op jit(solution)/shard_map/ppermute | solution.py:254
  41.0 7.8 %collective-permute-start.22 = (bf16[32,1536]{1,0:T(8,128)(2,1)S(1)}, bf16[32,1536]{1,0:T(8,128)(2,1)S(1)}, u32[]{:S(2)}, u32[]{:S(2)}) collective-permute-start(bf16[32,1536]{1,0:T(8,128)(2,1)S(1)} %shard_map.107), channel_id=1, source_target_pairs={{0,24},{4,28},{8,16},{12,20},{16,8},{20,12},{24,0},{28,4},{1,25},{... | collective-permute-start | bytes 294920 | tf_op jit(solution)/shard_map/ppermute | solution.py:254
  49.1 4.0 %collective-permute-start.23 = (bf16[16,1536]{1,0:T(8,128)(2,1)S(1)}, bf16[16,1536]{1,0:T(8,128)(2,1)S(1)}, u32[]{:S(2)}, u32[]{:S(2)}) collective-permute-start(bf16[16,1536]{1,0:T(8,128)(2,1)S(1)} %get-tuple-element.73), channel_id=1, source_target_pairs={{0,1},{1,0},{2,3},{3,2},{4,5},{5,4},{6,7},{7,6},{8,9},{9,8},{10,11... | collective-permute-start | bytes 147464 | tf_op jit(solution)/shard_map/ppermute | solution.py:247
  49.2 4.2 %collective-permute-start.24 = (bf16[16,1536]{1,0:T(8,128)(2,1)S(1)}, bf16[16,1536]{1,0:T(8,128)(2,1)S(1)}, u32[]{:S(2)}, u32[]{:S(2)}) collective-permute-start(bf16[16,1536]{1,0:T(8,128)(2,1)S(1)} %get-tuple-element.74), channel_id=1, source_target_pairs={{0,2},{1,3},{2,0},{3,1},{4,6},{5,7},{6,4},{7,5},{8,10},{9,11},{10,... | collective-permute-start | bytes 147464 | tf_op jit(solution)/shard_map/ppermute | solution.py:247
  50.4 3.7 %collective-permute-start.25 = (bf16[16,1536]{1,0:T(8,128)(2,1)S(1)}, bf16[16,1536]{1,0:T(8,128)(2,1)S(1)}, u32[]{:S(2)}, u32[]{:S(2)}) collective-permute-start(bf16[16,1536]{1,0:T(8,128)(2,1)S(1)} %get-tuple-element.75), channel_id=1, source_target_pairs={{0,3},{1,2},{2,1},{3,0},{4,7},{5,6},{6,5},{7,4},{8,11},{9,10},{10,... | collective-permute-start | bytes 147464 | tf_op jit(solution)/shard_map/ppermute | solution.py:247

commit v3 on v2

--- a/solution.py
+++ b/solution.py
@@ -99,7 +99,7 @@
     return (handed, grad_gate[None], grad_up[None], grad_down[None])
 
 
-def call(kernel, outs, *args, scratch=(), flops=0, vmem=16, space=VMEM):
+def call(kernel, outs, *args, scratch=(), flops=0, vmem=16, space=VMEM, aliases=None):
     moved = sum(a.size * a.dtype.itemsize for a in args)
     moved += sum(o.size * o.dtype.itemsize for o in outs)
     if space is HBM:
@@ -110,6 +110,7 @@
         in_specs=[space] * len(args),
         out_specs=[VMEM] * len(outs),
         scratch_shapes=list(scratch),
+        input_output_aliases=aliases or {},
         compiler_params=pltpu.CompilerParams(vmem_limit_bytes=vmem * 2**20),
         cost_estimate=pl.CostEstimate(flops=flops, bytes_accessed=moved, transcendentals=0),
     )(*args)
@@ -202,13 +203,15 @@
     sigmoid_gate = jax.nn.sigmoid(gate)
     silu_gate = gate * sigmoid_gate
     act_ref[...] = (silu_gate * upper).astype(BF16)
-    gg_ref[...] = (act_grad * upper * sigmoid_gate * (1.0 + gate * (1.0 - sigmoid_gate))).astype(BF16)
-    ug_ref[...] = (act_grad * silu_gate).astype(BF16)
+    gate_grad = (act_grad * upper * sigmoid_gate * (1.0 + gate * (1.0 - sigmoid_gate))).astype(BF16)
+    up_grad = (act_grad * silu_gate).astype(BF16)
+    gg_ref[...] = gate_grad
+    ug_ref[...] = up_grad
     core = e % 2
     for out, side in ((other_ref, 1 - core), (own_ref, core)):
         start = pl.multiple_of(side * half, 128)
-        terms = contract(gg_ref[...], wg_ref[:, pl.ds(start, half)], 1, 0)
-        terms += contract(ug_ref[...], wu_ref[:, pl.ds(start, half)], 1, 0)
+        terms = contract(gate_grad, wg_ref[:, pl.ds(start, half)], 1, 0)
+        terms += contract(up_grad, wu_ref[:, pl.ds(start, half)], 1, 0)
         out[...] = terms.astype(BF16)
 
 
@@ -220,15 +223,13 @@
     outs[0][:, half:] = pick_ref[...]
 
 
-def add_kernel(left_ref, right_ref, out_ref):
-    out_ref[...] = (left_ref[...].astype(F32) + right_ref[...].astype(F32)).astype(BF16)
-
-
-def expand_kernel(own_ref, near_ref, far_ref, *refs):
-    outs, tokens_ref = refs[:4], refs[4]
+def expand_kernel(own_ref, *refs):
+    others, outs, tokens_ref = refs[:3], refs[3:7], refs[7]
     rows, half = outs[0].shape
     e = lax.axis_index("et")
-    total = own_ref[:, :half].astype(F32) + near_ref[...].astype(F32) + far_ref[...].astype(F32)
+    total = own_ref[:, :half].astype(F32)
+    for other in others:
+        total += other[...].astype(F32)
     tokens_ref[...] = contract(own_ref[:, half:], total.astype(BF16), 0, 0).astype(BF16)
     for steps, out in enumerate(outs):
         out[...] = tokens_ref[pl.ds(pl.multiple_of((e ^ steps) * rows, 16), rows), :]
@@ -296,13 +297,11 @@
         *arrived,
         scratch=[pltpu.VMEM((4 * rows, 2 * piece + FLAG), BF16)],
     )
+    diag = swap(slot_block, "dp", 3)
     near = swap(slot_block, "dp", 1)
     far = swap(slot_block, "dp", 2)
-    near, far = lax.optimization_barrier((near, far))
-    chip_near = swap(near, "et", 2)
-    last = swap(far, "dp", 1)
-    own = [slot_block, near, far, last]
-    chip = [swap(slot_block, "et", 2), chip_near, swap(far, "et", 2), swap(last, "et", 2)]
+    own = [slot_block, diag, near, far]
+    chip = [swap(block, "et", 2) for block in own]
     core = [swap(block, "et", 1) for block in own]
     both = [swap(block, "et", 1) for block in chip]
     x, dz, act, gate_grad, up_grad, terms, away = call(
@@ -319,28 +318,21 @@
         vmem=32,
     )
     theirs = swap(away, "et", 1)
-    home, to_near, to_far, to_last = call(
+    sums = call(
         pair_kernel,
         [like((cap, half + FLAG))] + [like((cap, half))] * 3,
         terms,
         theirs,
         pick,
     )
-    from_last = swap(to_last, "dp", 1)
-    home = hand(home, pipe_size, 0)
-    (to_far,) = call(add_kernel, [like((cap, half))], to_far, from_last)
-    to_far, to_near = lax.optimization_barrier((to_far, to_near))
-    from_far = hand(to_far, pipe_size, 2)
-    from_near = hand(to_near, pipe_size, 1)
+    home = [hand(sums[k], pipe_size, s) for k, s in ((0, 0), (3, 2), (1, 3), (2, 1))]
     grad_gate = contract(gate_grad, x, 0, 0).astype(BF16)
     grad_up = contract(up_grad, x, 0, 0).astype(BF16)
-    from_far, grad_gate, grad_up = lax.optimization_barrier((from_far, grad_gate, grad_up))
+    home, grad_gate, grad_up = lax.optimization_barrier((home, grad_gate, grad_up))
     by_token = call(
         expand_kernel,
         [like((rows, half))] * 4,
-        home,
-        from_near,
-        from_far,
+        *home,
         scratch=[pltpu.VMEM((FLAG, half), BF16)],
     )
     back = [by_token[0]] + [swap(by_token[s], "et", s) for s in (1, 2, 3)]

time: 54.9 us -> 54.9 us (level)
  starting transfers between devices: 22.2 us -> 21 us
  waiting for transfers between devices: 17.3 us -> 18.5 us
    ppermute x3 -> x4, waiting for transfers between devices: 3.41 us -> 6.5 us  [hand(): return lax.ppermute(value, ('pipe', 'dp'), pairs)]
    ppermute x23 -> x22, starting transfers between devices: 16.7 us -> 14.4 us  [swap(): return lax.ppermute(value, axis, spread(steps))]
    ppermute x23 -> x22, waiting for transfers between devices: 13.8 us -> 12 us  [swap(): return lax.ppermute(value, axis, spread(steps))]
    ppermute x3 -> x4, starting transfers between devices: 5.51 us -> 6.55 us  [hand(): return lax.ppermute(value, ('pipe', 'dp'), pairs)]
    pallas_call x8 -> x7, Pallas kernels: 8.52 us -> 8.49 us  [call(): pl.pallas_call(kernel, out_shape=outs, in_specs=[space] * len(args), out_...]
  transfers between devices with their start and end apart: 26 -> 26, of which waited for: 13 -> 12; matrix products, arithmetic and copies ran while one was open for 11% -> 11% of each run, Pallas kernels for 5% -> 5%
where the time goes in v3:
time: 54.9 us; the launch traced here: 54.8 us
  starting transfers between devices  21 us (38%)
  waiting for transfers between devices  18.5 us (34%)
  Pallas kernels  8.49 us (15%)
  matrix products  6.07 us (11%)
  between operations  0.75 us (1%)
    ppermute x22, starting transfers between devices, swap(): return lax.ppermute(value, axis, spread(steps))  14.4 us
    ppermute x22, waiting for transfers between devices, swap(): return lax.ppermute(value, axis, spread(steps))  12 us
    pallas_call x7, Pallas kernels, call(): pl.pallas_call(kernel, out_shape=outs, in_specs=[space] * len(args), out_...  8.49 us
    ppermute x4, starting transfers between devices, hand(): return lax.ppermute(value, ('pipe', 'dp'), pairs)  6.55 us
    ppermute x4, waiting for transfers between devices, hand(): return lax.ppermute(value, ('pipe', 'dp'), pairs)  6.5 us
    dot_general x3, matrix products, contract(): lax.dot_general(left, right, (((left_dim,), (right_dim,)), ((), ())), pre...  6.07 us
  transfers between devices with their start and end apart: 26, of which 12 were waited for; matrix products, arithmetic and copies ran while one was open for 11% of the time, Pallas kernels for 5%

profile of v3, /device:TPU:0, one launch (start us, length us, event | category | flops | bytes accessed | tf_op | source)
XLA Modules:
  0.0 54.8 jit_solution(1068118913310398728)
XLA Ops:
  0.6 1.1 %shard_map.102 = (bf16[16,1664]{1,0:T(8,128)(2,1)S(1)}, bf16[16,1664]{1,0:T(8,128)(2,1)S(1)}, bf16[16,1664]{1,0:T(8,128)(2,1)S(1)}, bf16[16,1664]{1,0:T(8,128)(2,1)S(1)}) custom-call(bf16[16,3072]{1,0:T(8,128)(2,1)} %bitcast.27, bf16[16,3072]{1,0:T(8,128)(2,1)} %bitcast.28, s32[4,16]{1,0:T(4,128)} %bitcast.30, f32[4,16]{1,0:T(4,128)} %bitcast.31), custom_call_target="tpu_custom_call" | custom-call | bytes 410112 | tf_op jit(solution)/shard_map/pallas_call | solution.py:107
  1.7 0.5 collective-permute-start
  2.2 2.6 %collective-permute-start.1 = (bf16[16,1664]{1,0:T(8,128)(2,1)S(1)}, bf16[16,1664]{1,0:T(8,128)(2,1)S(1)}, u32[]{:S(2)}, u32[]{:S(2)}) collective-permute-start(bf16[16,1664]{1,0:T(8,128)(2,1)S(1)} %get-tuple-element.43), channel_id=1, source_target_pairs={{0,2},{1,3},{2,0},{3,1},{4,6},{5,7},{6,4},{7,5},{8,10},{9,11},{10,... | collective-permute-start | bytes 159752 | tf_op jit(solution)/shard_map/ppermute | solution.py:248
  4.8 0.1 collective-permute-start.2
  4.9 2.9 %shard_map.103 = (bf16[336,3072]{1,0:T(8,128)(2,1)S(1)}, bf16[336,3072]{1,0:T(8,128)(2,1)S(1)}, bf16[336,3072]{1,0:T(8,128)(2,1)S(1)}) custom-call(bf16[336,3072]{1,0:T(8,128)(2,1)} %bitcast.22, bf16[336,3072]{1,0:T(8,128)(2,1)} %bitcast.23, bf16[336,3072]{1,0:T(8,128)(2,1)} %bitcast.24), custom_call_target="tpu_custom_call" | custom-call | bytes 12386304 | tf_op jit(solution)/shard_map/pallas_call | solution.py:107
  7.8 0.0 collective-permute-done.refs_1_
  7.8 0.8 %collective-permute-done.2.refs_3_ = bf16[16,1664]{1,0:T(8,128)(2,1)S(1)} collective-permute-done((bf16[16,1664]{1,0:T(8,128)(2,1)S(1)}, bf16[16,1664]{1,0:T(8,128)(2,1)S(1)}, u32[]{:S(2)}, u32[]{:S(2)}) %collective-permute-start.2) | collective-permute-done | bytes 53280 | tf_op jit(solution)/shard_map/ppermute | solution.py:248
  8.6 0.3 shard_map.104
  9.0 1.1 %collective-permute-start.10 = (bf16[32,1536]{1,0:T(8,128)(2,1)S(1)}, bf16[32,1536]{1,0:T(8,128)(2,1)S(1)}, u32[]{:S(2)}, u32[]{:S(2)}) collective-permute-start(bf16[32,1536]{1,0:T(8,128)(2,1)S(1)} %get-tuple-element.52.refs_0_), channel_id=1, source_target_pairs={{0,2},{1,3},{2,0},{3,1},{4,6},{5,7},{6,4},{7,5},{8,10},{9,11},{10,... | collective-permute-start | bytes 294920 | tf_op jit(solution)/shard_map/ppermute | solution.py:248
  10.1 2.6 %collective-permute-start.5 = (bf16[32,1536]{1,0:T(8,128)(2,1)S(1)}, bf16[32,1536]{1,0:T(8,128)(2,1)S(1)}, u32[]{:S(2)}, u32[]{:S(2)}) collective-permute-start(bf16[32,1536]{1,0:T(8,128)(2,1)S(1)} %get-tuple-element.52.refs_0_), channel_id=1, source_target_pairs={{0,8},{4,12},{8,0},{12,4},{1,9},{5,13},{9,1},{13,5},{2,10},{6,14},... | collective-permute-start | bytes 294920 | tf_op jit(solution)/shard_map/ppermute | solution.py:248
  12.7 0.0 collective-permute-start.6
  12.7 1.6 %collective-permute-start.4 = (bf16[32,1536]{1,0:T(8,128)(2,1)S(1)}, bf16[32,1536]{1,0:T(8,128)(2,1)S(1)}, u32[]{:S(2)}, u32[]{:S(2)}) collective-permute-start(bf16[32,1536]{1,0:T(8,128)(2,1)S(1)} %get-tuple-element.52.refs_0_), channel_id=1, source_target_pairs={{0,4},{4,0},{8,12},{12,8},{1,5},{5,1},{9,13},{13,9},{2,6},{6,2},{1... | collective-permute-start | bytes 294920 | tf_op jit(solution)/shard_map/ppermute | solution.py:248
  14.3 0.2 collective-permute-start.3
  14.5 0.0 collective-permute-start.14
  14.5 3.7 %collective-permute-done.5.refs_3_ = bf16[32,1536]{1,0:T(8,128)(2,1)S(1)} collective-permute-done((bf16[32,1536]{1,0:T(8,128)(2,1)S(1)}, bf16[32,1536]{1,0:T(8,128)(2,1)S(1)}, u32[]{:S(2)}, u32[]{:S(2)}) %collective-permute-start.5) | collective-permute-done | bytes 98336 | tf_op jit(solution)/shard_map/ppermute | solution.py:248
  18.2 0.7 %collective-permute-start.13 = (bf16[32,1536]{1,0:T(8,128)(2,1)S(1)}, bf16[32,1536]{1,0:T(8,128)(2,1)S(1)}, u32[]{:S(2)}, u32[]{:S(2)}) collective-permute-start(bf16[32,1536]{1,0:T(8,128)(2,1)S(1)} %collective-permute-done.5.refs_3_), channel_id=1, source_target_pairs={{0,2},{1,3},{2,0},{3,1},{4,6},{5,7},{6,4},{7,5},{8,10},{9,11},{10,... | collective-permute-start | bytes 294920 | tf_op jit(solution)/shard_map/ppermute | solution.py:248
  19.0 0.0 collective-permute-done.6.refs_4_
  19.0 0.0 collective-permute-start.9
  19.0 0.0 collective-permute-done.4.refs_2_
  19.0 1.4 %collective-permute-start.12 = (bf16[32,1536]{1,0:T(8,128)(2,1)S(1)}, bf16[32,1536]{1,0:T(8,128)(2,1)S(1)}, u32[]{:S(2)}, u32[]{:S(2)}) collective-permute-start(bf16[32,1536]{1,0:T(8,128)(2,1)S(1)} %collective-permute-done.4.refs_2_), channel_id=1, source_target_pairs={{0,2},{1,3},{2,0},{3,1},{4,6},{5,7},{6,4},{7,5},{8,10},{9,11},{10,... | collective-permute-start | bytes 294920 | tf_op jit(solution)/shard_map/ppermute | solution.py:248
  20.3 0.8 %collective-permute-done.3.refs_1_ = bf16[32,1536]{1,0:T(8,128)(2,1)S(1)} collective-permute-done((bf16[32,1536]{1,0:T(8,128)(2,1)S(1)}, bf16[32,1536]{1,0:T(8,128)(2,1)S(1)}, u32[]{:S(2)}, u32[]{:S(2)}) %collective-permute-start.3) | collective-permute-done | bytes 98336 | tf_op jit(solution)/shard_map/ppermute | solution.py:248
  21.1 0.9 %collective-permute-start.11 = (bf16[32,1536]{1,0:T(8,128)(2,1)S(1)}, bf16[32,1536]{1,0:T(8,128)(2,1)S(1)}, u32[]{:S(2)}, u32[]{:S(2)}) collective-permute-start(bf16[32,1536]{1,0:T(8,128)(2,1)S(1)} %collective-permute-done.3.refs_1_), channel_id=1, source_target_pairs={{0,2},{1,3},{2,0},{3,1},{4,6},{5,7},{6,4},{7,5},{8,10},{9,11},{10,... | collective-permute-start | bytes 294920 | tf_op jit(solution)/shard_map/ppermute | solution.py:248
  22.1 1.5 %collective-permute-done.13.refs_11_ = bf16[32,1536]{1,0:T(8,128)(2,1)S(1)} collective-permute-done((bf16[32,1536]{1,0:T(8,128)(2,1)S(1)}, bf16[32,1536]{1,0:T(8,128)(2,1)S(1)}, u32[]{:S(2)}, u32[]{:S(2)}) %collective-permute-start.13) | collective-permute-done | bytes 98336 | tf_op jit(solution)/shard_map/ppermute | solution.py:248
  23.6 0.5 collective-permute-start.17
  24.1 1.6 %collective-permute-done.12.refs_10_ = bf16[32,1536]{1,0:T(8,128)(2,1)S(1)} collective-permute-done((bf16[32,1536]{1,0:T(8,128)(2,1)S(1)}, bf16[32,1536]{1,0:T(8,128)(2,1)S(1)}, u32[]{:S(2)}, u32[]{:S(2)}) %collective-permute-start.12) | collective-permute-done | bytes 98336 | tf_op jit(solution)/shard_map/ppermute | solution.py:248
  25.7 1.3 %collective-permute-done.11.refs_9_ = bf16[32,1536]{1,0:T(8,128)(2,1)S(1)} collective-permute-done((bf16[32,1536]{1,0:T(8,128)(2,1)S(1)}, bf16[32,1536]{1,0:T(8,128)(2,1)S(1)}, u32[]{:S(2)}, u32[]{:S(2)}) %collective-permute-start.11) | collective-permute-done | bytes 98336 | tf_op jit(solution)/shard_map/ppermute | solution.py:248
  27.1 1.3 %collective-permute-done.15.refs_13_ = bf16[32,1536]{1,0:T(8,128)(2,1)S(1)} collective-permute-done((bf16[32,1536]{1,0:T(8,128)(2,1)S(1)}, bf16[32,1536]{1,0:T(8,128)(2,1)S(1)}, u32[]{:S(2)}, u32[]{:S(2)}) %collective-permute-start.15) | collective-permute-done | bytes 98336 | tf_op jit(solution)/shard_map/ppermute | solution.py:248
  28.3 3.2 %shard_map.105 = (bf16[128,3072]{1,0:T(8,128)(2,1)S(1)}, bf16[128,3072]{1,0:T(8,128)(2,1)S(1)}, bf16[128,336]{1,0:T(8,128)(2,1)S(1)}, bf16[128,336]{1,0:T(8,128)...) custom-call(bf16[32,1536]{1,0:T(8,128)(2,1)S(1)} %get-tuple-element.52.refs_0_, ...), custom_call_target="tpu_custom_call" | custom-call | flops 1321205760 | bytes 10383360 | tf_op jit(solution)/shard_map/pallas_call | solution.py:107
  31.5 0.2 collective-permute-start.18
  31.7 2.0 %convolution_convert_fusion.2 = bf16[336,3072]{1,0:T(8,128)(2,1)} fusion(bf16[128,336]{1,0:T(8,128)(2,1)S(1)} %get-tuple-element.63, bf16[128,3072]{1,0:T(8,128)(2,1)S(1)} %get-tuple-element.64), kind=kOutput, calls=%fused_computation.2 | convolution fusion | flops 265273344 | bytes 2936832 | tf_op jit(solution)/shard_map/dot_general | solution.py:40
  33.8 0.1 shard_map.106
  33.9 3.3 %collective-permute-start.20 = (bf16[32,1536]{1,0:T(8,128)(2,1)S(1)}, bf16[32,1536]{1,0:T(8,128)(2,1)S(1)}, u32[]{:S(2)}, u32[]{:S(2)}) collective-permute-start(bf16[32,1536]{1,0:T(8,128)(2,1)S(1)} %get-tuple-element.60), channel_id=1, source_target_pairs={{0,24},{4,28},{8,16},{12,20},{16,8},{20,12},{24,0},{28,4},{1,25},{... | collective-permute-start | bytes 294920 | tf_op jit(solution)/shard_map/ppermute | solution.py:255
  37.2 1.3 %collective-permute-start.21 = (bf16[32,1536]{1,0:T(8,128)(2,1)S(1)}, bf16[32,1536]{1,0:T(8,128)(2,1)S(1)}, u32[]{:S(2)}, u32[]{:S(2)}) collective-permute-start(bf16[32,1536]{1,0:T(8,128)(2,1)S(1)} %get-tuple-element.61), channel_id=1, source_target_pairs={{0,28},{4,24},{8,20},{12,16},{16,12},{20,8},{24,4},{28,0},{1,29},{... | collective-permute-start | bytes 294920 | tf_op jit(solution)/shard_map/ppermute | solution.py:255
  38.5 0.8 %collective-permute-start.22 = (bf16[32,1536]{1,0:T(8,128)(2,1)S(1)}, bf16[32,1536]{1,0:T(8,128)(2,1)S(1)}, u32[]{:S(2)}, u32[]{:S(2)}) collective-permute-start(bf16[32,1536]{1,0:T(8,128)(2,1)S(1)} %get-tuple-element.62), channel_id=1, source_target_pairs={{0,20},{4,16},{8,28},{12,24},{16,4},{20,0},{24,12},{28,8},{1,21},{... | collective-permute-start | bytes 294920 | tf_op jit(solution)/shard_map/ppermute | solution.py:255
  39.3 1.2 %collective-permute-start.19 = (bf16[32,1664]{1,0:T(8,128)(2,1)S(1)}, bf16[32,1664]{1,0:T(8,128)(2,1)S(1)}, u32[]{:S(2)}, u32[]{:S(2)}) collective-permute-start(bf16[32,1664]{1,0:T(8,128)(2,1)S(1)} %get-tuple-element.59), channel_id=1, source_target_pairs={{0,16},{4,20},{8,24},{12,28},{16,0},{20,4},{24,8},{28,12},{1,17},{... | collective-permute-start | bytes 319496 | tf_op jit(solution)/shard_map/ppermute | solution.py:255
  40.4 2.0 %convolution_convert_fusion.1 = bf16[336,3072]{1,0:T(8,128)(2,1)} fusion(bf16[128,336]{1,0:T(8,128)(2,1)S(1)} %get-tuple-element.65, bf16[128,3072]{1,0:T(8,128)(2,1)S(1)} %get-tuple-element.64), kind=kOutput, calls=%fused_computation.1 | convolution fusion | flops 265273344 | bytes 2936832 | tf_op jit(solution)/shard_map/dot_general | solution.py:40
  42.4 3.2 %collective-permute-done.20.refs_0_ = bf16[32,1536]{1,0:T(8,128)(2,1)S(1)} collective-permute-done((bf16[32,1536]{1,0:T(8,128)(2,1)S(1)}, bf16[32,1536]{1,0:T(8,128)(2,1)S(1)}, u32[]{:S(2)}, u32[]{:S(2)}) %collective-permute-start.20) | collective-permute-done | bytes 98336 | tf_op jit(solution)/shard_map/ppermute | solution.py:255
  45.6 0.0 collective-permute-done.21.refs_1_
  45.6 1.6 %collective-permute-done.22.refs_2_ = bf16[32,1536]{1,0:T(8,128)(2,1)S(1)} collective-permute-done((bf16[32,1536]{1,0:T(8,128)(2,1)S(1)}, bf16[32,1536]{1,0:T(8,128)(2,1)S(1)}, u32[]{:S(2)}, u32[]{:S(2)}) %collective-permute-start.22) | collective-permute-done | bytes 98336 | tf_op jit(solution)/shard_map/ppermute | solution.py:255
  47.2 1.7 %collective-permute-done.19.own_ref = bf16[32,1664]{1,0:T(8,128)(2,1)S(1)} collective-permute-done((bf16[32,1664]{1,0:T(8,128)(2,1)S(1)}, bf16[32,1664]{1,0:T(8,128)(2,1)S(1)}, u32[]{:S(2)}, u32[]{:S(2)}) %collective-permute-start.19) | collective-permute-done | bytes 106528 | tf_op jit(solution)/shard_map/ppermute | solution.py:255
  48.9 0.3 shard_map.107
  49.2 0.1 collective-permute-start.23
  49.3 0.8 %collective-permute-start.24 = (bf16[16,1536]{1,0:T(8,128)(2,1)S(1)}, bf16[16,1536]{1,0:T(8,128)(2,1)S(1)}, u32[]{:S(2)}, u32[]{:S(2)}) collective-permute-start(bf16[16,1536]{1,0:T(8,128)(2,1)S(1)} %get-tuple-element.72), channel_id=1, source_target_pairs={{0,2},{1,3},{2,0},{3,1},{4,6},{5,7},{6,4},{7,5},{8,10},{9,11},{10,... | collective-permute-start | bytes 147464 | tf_op jit(solution)/shard_map/ppermute | solution.py:248
  50.1 1.1 %collective-permute-start.25 = (bf16[16,1536]{1,0:T(8,128)(2,1)S(1)}, bf16[16,1536]{1,0:T(8,128)(2,1)S(1)}, u32[]{:S(2)}, u32[]{:S(2)}) collective-permute-start(bf16[16,1536]{1,0:T(8,128)(2,1)S(1)} %get-tuple-element.73), channel_id=1, source_target_pairs={{0,3},{1,2},{2,1},{3,0},{4,7},{5,6},{6,5},{7,4},{8,11},{9,10},{10,... | collective-permute-start | bytes 147464 | tf_op jit(solution)/shard_map/ppermute | solution.py:248
  51.2 2.0 %fusion = bf16[1,336,3072]{2,1,0:T(8,128)(2,1)} fusion(bf16[128,336]{1,0:T(8,128)(2,1)S(1)} %get-tuple-element.76, bf16[128,3072]{1,0:T(8,128)(2,1)S(1)} %get-tuple-element.77), kind=kOutput, calls=%fused_computation.3 | convolution fusion | flops 265273344 | bytes 2936832 | tf_op jit(solution)/shard_map/dot_general | solution.py:40
  53.2 0.7 %collective-permute-done.24.chip_ref = bf16[16,1536]{1,0:T(8,128)(2,1)S(1)} collective-permute-done((bf16[16,1536]{1,0:T(8,128)(2,1)S(1)}, bf16[16,1536]{1,0:T(8,128)(2,1)S(1)}, u32[]{:S(2)}, u32[]{:S(2)}) %collective-permute-start.24) | collective-permute-done | bytes 49184 | tf_op jit(solution)/shard_map/ppermute | solution.py:248
  53.9 0.2 collective-permute-done.25.both_ref
  54.1 0.7 %shard_map.108 = bf16[16,3072]{1,0:T(8,128)(2,1)} custom-call(bf16[16,1536]{1,0:T(8,128)(2,1)S(1)} %get-tuple-element.70.own_ref, bf16[16,1536]{1,0:T(8,128)(2,1)S(1)} %collective-permute-done.23.core_ref, bf16[16,1536]{1,0:T(8,128)(2,1)S(1)} %collective-permute-done.24.chip_ref, bf16[16,1536]{1,0:T(8,128)(2,1)S(1)} %collective-permute-done.25.both_ref), custom_call_target="tpu_custom_call" | custom-call | bytes 294912 | tf_op jit(solution)/shard_map/pallas_call | solution.py:107
  (14 shorter events, 0.0 us)
Async XLA Ops:
  1.7 6.0 %collective-permute-start = (bf16[16,1664]{1,0:T(8,128)(2,1)S(1)}, bf16[16,1664]{1,0:T(8,128)(2,1)S(1)}, u32[]{:S(2)}, u32[]{:S(2)}) collective-permute-start(bf16[16,1664]{1,0:T(8,128)(2,1)S(1)} %get-tuple-element.42), channel_id=1, source_target_pairs={{0,1},{1,0},{2,3},{3,2},{4,5},{5,4},{6,7},{7,6},{8,9},{9,8},{10,11... | collective-permute-start | bytes 159752 | tf_op jit(solution)/shard_map/ppermute | solution.py:248
  2.2 5.5 %collective-permute-start.1 = (bf16[16,1664]{1,0:T(8,128)(2,1)S(1)}, bf16[16,1664]{1,0:T(8,128)(2,1)S(1)}, u32[]{:S(2)}, u32[]{:S(2)}) collective-permute-start(bf16[16,1664]{1,0:T(8,128)(2,1)S(1)} %get-tuple-element.43), channel_id=1, source_target_pairs={{0,2},{1,3},{2,0},{3,1},{4,6},{5,7},{6,4},{7,5},{8,10},{9,11},{10,... | collective-permute-start | bytes 159752 | tf_op jit(solution)/shard_map/ppermute | solution.py:248
  4.8 3.8 %collective-permute-start.2 = (bf16[16,1664]{1,0:T(8,128)(2,1)S(1)}, bf16[16,1664]{1,0:T(8,128)(2,1)S(1)}, u32[]{:S(2)}, u32[]{:S(2)}) collective-permute-start(bf16[16,1664]{1,0:T(8,128)(2,1)S(1)} %get-tuple-element.44), channel_id=1, source_target_pairs={{0,3},{1,2},{2,1},{3,0},{4,7},{5,6},{6,5},{7,4},{8,11},{9,10},{10,... | collective-permute-start | bytes 159752 | tf_op jit(solution)/shard_map/ppermute | solution.py:248
  9.0 5.5 %collective-permute-start.10 = (bf16[32,1536]{1,0:T(8,128)(2,1)S(1)}, bf16[32,1536]{1,0:T(8,128)(2,1)S(1)}, u32[]{:S(2)}, u32[]{:S(2)}) collective-permute-start(bf16[32,1536]{1,0:T(8,128)(2,1)S(1)} %get-tuple-element.52.refs_0_), channel_id=1, source_target_pairs={{0,2},{1,3},{2,0},{3,1},{4,6},{5,7},{6,4},{7,5},{8,10},{9,11},{10,... | collective-permute-start | bytes 294920 | tf_op jit(solution)/shard_map/ppermute | solution.py:248
  10.1 8.1 %collective-permute-start.5 = (bf16[32,1536]{1,0:T(8,128)(2,1)S(1)}, bf16[32,1536]{1,0:T(8,128)(2,1)S(1)}, u32[]{:S(2)}, u32[]{:S(2)}) collective-permute-start(bf16[32,1536]{1,0:T(8,128)(2,1)S(1)} %get-tuple-element.52.refs_0_), channel_id=1, source_target_pairs={{0,8},{4,12},{8,0},{12,4},{1,9},{5,13},{9,1},{13,5},{2,10},{6,14},... | collective-permute-start | bytes 294920 | tf_op jit(solution)/shard_map/ppermute | solution.py:248
  12.7 6.3 %collective-permute-start.6 = (bf16[32,1536]{1,0:T(8,128)(2,1)S(1)}, bf16[32,1536]{1,0:T(8,128)(2,1)S(1)}, u32[]{:S(2)}, u32[]{:S(2)}) collective-permute-start(bf16[32,1536]{1,0:T(8,128)(2,1)S(1)} %get-tuple-element.52.refs_0_), channel_id=1, source_target_pairs={{0,1},{1,0},{2,3},{3,2},{4,5},{5,4},{6,7},{7,6},{8,9},{9,8},{10,11... | collective-permute-start | bytes 294920 | tf_op jit(solution)/shard_map/ppermute | solution.py:248
  12.7 6.3 %collective-permute-start.4 = (bf16[32,1536]{1,0:T(8,128)(2,1)S(1)}, bf16[32,1536]{1,0:T(8,128)(2,1)S(1)}, u32[]{:S(2)}, u32[]{:S(2)}) collective-permute-start(bf16[32,1536]{1,0:T(8,128)(2,1)S(1)} %get-tuple-element.52.refs_0_), channel_id=1, source_target_pairs={{0,4},{4,0},{8,12},{12,8},{1,5},{5,1},{9,13},{13,9},{2,6},{6,2},{1... | collective-permute-start | bytes 294920 | tf_op jit(solution)/shard_map/ppermute | solution.py:248
  14.3 6.8 %collective-permute-start.3 = (bf16[32,1536]{1,0:T(8,128)(2,1)S(1)}, bf16[32,1536]{1,0:T(8,128)(2,1)S(1)}, u32[]{:S(2)}, u32[]{:S(2)}) collective-permute-start(bf16[32,1536]{1,0:T(8,128)(2,1)S(1)} %get-tuple-element.52.refs_0_), channel_id=1, source_target_pairs={{0,12},{4,8},{8,4},{12,0},{1,13},{5,9},{9,5},{13,1},{2,14},{6,10},... | collective-permute-start | bytes 294920 | tf_op jit(solution)/shard_map/ppermute | solution.py:248
  14.5 7.6 %collective-permute-start.14 = (bf16[32,1536]{1,0:T(8,128)(2,1)S(1)}, bf16[32,1536]{1,0:T(8,128)(2,1)S(1)}, u32[]{:S(2)}, u32[]{:S(2)}) collective-permute-start(bf16[32,1536]{1,0:T(8,128)(2,1)S(1)} %collective-permute-done.10.refs_8_), channel_id=1, source_target_pairs={{0,1},{1,0},{2,3},{3,2},{4,5},{5,4},{6,7},{7,6},{8,9},{9,8},{10,11... | collective-permute-start | bytes 294920 | tf_op jit(solution)/shard_map/ppermute | solution.py:248
  18.2 5.4 %collective-permute-start.13 = (bf16[32,1536]{1,0:T(8,128)(2,1)S(1)}, bf16[32,1536]{1,0:T(8,128)(2,1)S(1)}, u32[]{:S(2)}, u32[]{:S(2)}) collective-permute-start(bf16[32,1536]{1,0:T(8,128)(2,1)S(1)} %collective-permute-done.5.refs_3_), channel_id=1, source_target_pairs={{0,2},{1,3},{2,0},{3,1},{4,6},{5,7},{6,4},{7,5},{8,10},{9,11},{10,... | collective-permute-start | bytes 294920 | tf_op jit(solution)/shard_map/ppermute | solution.py:248
  19.0 4.6 %collective-permute-start.9 = (bf16[32,1536]{1,0:T(8,128)(2,1)S(1)}, bf16[32,1536]{1,0:T(8,128)(2,1)S(1)}, u32[]{:S(2)}, u32[]{:S(2)}) collective-permute-start(bf16[32,1536]{1,0:T(8,128)(2,1)S(1)} %collective-permute-done.5.refs_3_), channel_id=1, source_target_pairs={{0,1},{1,0},{2,3},{3,2},{4,5},{5,4},{6,7},{7,6},{8,9},{9,8},{10,11... | collective-permute-start | bytes 294920 | tf_op jit(solution)/shard_map/ppermute | solution.py:248
  19.0 6.7 %collective-permute-start.12 = (bf16[32,1536]{1,0:T(8,128)(2,1)S(1)}, bf16[32,1536]{1,0:T(8,128)(2,1)S(1)}, u32[]{:S(2)}, u32[]{:S(2)}) collective-permute-start(bf16[32,1536]{1,0:T(8,128)(2,1)S(1)} %collective-permute-done.4.refs_2_), channel_id=1, source_target_pairs={{0,2},{1,3},{2,0},{3,1},{4,6},{5,7},{6,4},{7,5},{8,10},{9,11},{10,... | collective-permute-start | bytes 294920 | tf_op jit(solution)/shard_map/ppermute | solution.py:248
  21.1 5.9 %collective-permute-start.11 = (bf16[32,1536]{1,0:T(8,128)(2,1)S(1)}, bf16[32,1536]{1,0:T(8,128)(2,1)S(1)}, u32[]{:S(2)}, u32[]{:S(2)}) collective-permute-start(bf16[32,1536]{1,0:T(8,128)(2,1)S(1)} %collective-permute-done.3.refs_1_), channel_id=1, source_target_pairs={{0,2},{1,3},{2,0},{3,1},{4,6},{5,7},{6,4},{7,5},{8,10},{9,11},{10,... | collective-permute-start | bytes 294920 | tf_op jit(solution)/shard_map/ppermute | solution.py:248
  22.1 5.0 %collective-permute-start.8 = (bf16[32,1536]{1,0:T(8,128)(2,1)S(1)}, bf16[32,1536]{1,0:T(8,128)(2,1)S(1)}, u32[]{:S(2)}, u32[]{:S(2)}) collective-permute-start(bf16[32,1536]{1,0:T(8,128)(2,1)S(1)} %collective-permute-done.4.refs_2_), channel_id=1, source_target_pairs={{0,1},{1,0},{2,3},{3,2},{4,5},{5,4},{6,7},{7,6},{8,9},{9,8},{10,11... | collective-permute-start | bytes 294920 | tf_op jit(solution)/shard_map/ppermute | solution.py:248
  23.6 3.5 %collective-permute-start.7 = (bf16[32,1536]{1,0:T(8,128)(2,1)S(1)}, bf16[32,1536]{1,0:T(8,128)(2,1)S(1)}, u32[]{:S(2)}, u32[]{:S(2)}) collective-permute-start(bf16[32,1536]{1,0:T(8,128)(2,1)S(1)} %collective-permute-done.3.refs_1_), channel_id=1, source_target_pairs={{0,1},{1,0},{2,3},{3,2},{4,5},{5,4},{6,7},{7,6},{8,9},{9,8},{10,11... | collective-permute-start | bytes 294920 | tf_op jit(solution)/shard_map/ppermute | solution.py:248
  23.6 3.5 %collective-permute-start.17 = (bf16[32,1536]{1,0:T(8,128)(2,1)S(1)}, bf16[32,1536]{1,0:T(8,128)(2,1)S(1)}, u32[]{:S(2)}, u32[]{:S(2)}) collective-permute-start(bf16[32,1536]{1,0:T(8,128)(2,1)S(1)} %collective-permute-done.13.refs_11_), channel_id=1, source_target_pairs={{0,1},{1,0},{2,3},{3,2},{4,5},{5,4},{6,7},{7,6},{8,9},{9,8},{10,11... | collective-permute-start | bytes 294920 | tf_op jit(solution)/shard_map/ppermute | solution.py:248
  25.7 1.4 %collective-permute-start.16 = (bf16[32,1536]{1,0:T(8,128)(2,1)S(1)}, bf16[32,1536]{1,0:T(8,128)(2,1)S(1)}, u32[]{:S(2)}, u32[]{:S(2)}) collective-permute-start(bf16[32,1536]{1,0:T(8,128)(2,1)S(1)} %collective-permute-done.12.refs_10_), channel_id=1, source_target_pairs={{0,1},{1,0},{2,3},{3,2},{4,5},{5,4},{6,7},{7,6},{8,9},{9,8},{10,11... | collective-permute-start | bytes 294920 | tf_op jit(solution)/shard_map/ppermute | solution.py:248
  27.0 1.3 %collective-permute-start.15 = (bf16[32,1536]{1,0:T(8,128)(2,1)S(1)}, bf16[32,1536]{1,0:T(8,128)(2,1)S(1)}, u32[]{:S(2)}, u32[]{:S(2)}) collective-permute-start(bf16[32,1536]{1,0:T(8,128)(2,1)S(1)} %collective-permute-done.11.refs_9_), channel_id=1, source_target_pairs={{0,1},{1,0},{2,3},{3,2},{4,5},{5,4},{6,7},{7,6},{8,9},{9,8},{10,11... | collective-permute-start | bytes 294920 | tf_op jit(solution)/shard_map/ppermute | solution.py:248
  31.5 2.2 %collective-permute-start.18 = (bf16[128,1536]{1,0:T(8,128)(2,1)S(1)}, bf16[128,1536]{1,0:T(8,128)(2,1)S(1)}, u32[]{:S(2)}, u32[]{:S(2)}) collective-permute-start(bf16[128,1536]{1,0:T(8,128)(2,1)S(1)} %get-tuple-element.57), channel_id=1, source_target_pairs={{0,1},{1,0},{2,3},{3,2},{4,5},{5,4},{6,7},{7,6},{8,9},{9,8},{10,11... | collective-permute-start | bytes 1179656 | tf_op jit(solution)/shard_map/ppermute | solution.py:248
  33.9 11.7 %collective-permute-start.20 = (bf16[32,1536]{1,0:T(8,128)(2,1)S(1)}, bf16[32,1536]{1,0:T(8,128)(2,1)S(1)}, u32[]{:S(2)}, u32[]{:S(2)}) collective-permute-start(bf16[32,1536]{1,0:T(8,128)(2,1)S(1)} %get-tuple-element.60), channel_id=1, source_target_pairs={{0,24},{4,28},{8,16},{12,20},{16,8},{20,12},{24,0},{28,4},{1,25},{... | collective-permute-start | bytes 294920 | tf_op jit(solution)/shard_map/ppermute | solution.py:255
  37.2 8.5 %collective-permute-start.21 = (bf16[32,1536]{1,0:T(8,128)(2,1)S(1)}, bf16[32,1536]{1,0:T(8,128)(2,1)S(1)}, u32[]{:S(2)}, u32[]{:S(2)}) collective-permute-start(bf16[32,1536]{1,0:T(8,128)(2,1)S(1)} %get-tuple-element.61), channel_id=1, source_target_pairs={{0,28},{4,24},{8,20},{12,16},{16,12},{20,8},{24,4},{28,0},{1,29},{... | collective-permute-start | bytes 294920 | tf_op jit(solution)/shard_map/ppermute | solution.py:255
  38.5 8.7 %collective-permute-start.22 = (bf16[32,1536]{1,0:T(8,128)(2,1)S(1)}, bf16[32,1536]{1,0:T(8,128)(2,1)S(1)}, u32[]{:S(2)}, u32[]{:S(2)}) collective-permute-start(bf16[32,1536]{1,0:T(8,128)(2,1)S(1)} %get-tuple-element.62), channel_id=1, source_target_pairs={{0,20},{4,16},{8,28},{12,24},{16,4},{20,0},{24,12},{28,8},{1,21},{... | collective-permute-start | bytes 294920 | tf_op jit(solution)/shard_map/ppermute | solution.py:255
  39.3 9.7 %collective-permute-start.19 = (bf16[32,1664]{1,0:T(8,128)(2,1)S(1)}, bf16[32,1664]{1,0:T(8,128)(2,1)S(1)}, u32[]{:S(2)}, u32[]{:S(2)}) collective-permute-start(bf16[32,1664]{1,0:T(8,128)(2,1)S(1)} %get-tuple-element.59), channel_id=1, source_target_pairs={{0,16},{4,20},{8,24},{12,28},{16,0},{20,4},{24,8},{28,12},{1,17},{... | collective-permute-start | bytes 319496 | tf_op jit(solution)/shard_map/ppermute | solution.py:255
  49.2 4.0 %collective-permute-start.23 = (bf16[16,1536]{1,0:T(8,128)(2,1)S(1)}, bf16[16,1536]{1,0:T(8,128)(2,1)S(1)}, u32[]{:S(2)}, u32[]{:S(2)}) collective-permute-start(bf16[16,1536]{1,0:T(8,128)(2,1)S(1)} %get-tuple-element.71), channel_id=1, source_target_pairs={{0,1},{1,0},{2,3},{3,2},{4,5},{5,4},{6,7},{7,6},{8,9},{9,8},{10,11... | collective-permute-start | bytes 147464 | tf_op jit(solution)/shard_map/ppermute | solution.py:248
  49.3 4.6 %collective-permute-start.24 = (bf16[16,1536]{1,0:T(8,128)(2,1)S(1)}, bf16[16,1536]{1,0:T(8,128)(2,1)S(1)}, u32[]{:S(2)}, u32[]{:S(2)}) collective-permute-start(bf16[16,1536]{1,0:T(8,128)(2,1)S(1)} %get-tuple-element.72), channel_id=1, source_target_pairs={{0,2},{1,3},{2,0},{3,1},{4,6},{5,7},{6,4},{7,5},{8,10},{9,11},{10,... | collective-permute-start | bytes 147464 | tf_op jit(solution)/shard_map/ppermute | solution.py:248
  50.1 4.0 %collective-permute-start.25 = (bf16[16,1536]{1,0:T(8,128)(2,1)S(1)}, bf16[16,1536]{1,0:T(8,128)(2,1)S(1)}, u32[]{:S(2)}, u32[]{:S(2)}) collective-permute-start(bf16[16,1536]{1,0:T(8,128)(2,1)S(1)} %get-tuple-element.73), channel_id=1, source_target_pairs={{0,3},{1,2},{2,1},{3,0},{4,7},{5,6},{6,5},{7,4},{8,11},{9,10},{10,... | collective-permute-start | bytes 147464 | tf_op jit(solution)/shard_map/ppermute | solution.py:248

commit v4 on v3

--- a/solution.py
+++ b/solution.py
@@ -100,8 +100,10 @@
 
 
 def call(kernel, outs, *args, scratch=(), flops=0, vmem=16, space=VMEM, aliases=None):
-    moved = sum(a.size * a.dtype.itemsize for a in args)
-    moved += sum(o.size * o.dtype.itemsize for o in outs)
+    moved = 0
+    if space is HBM or flops:
+        moved = sum(a.size * a.dtype.itemsize for a in args)
+        moved += sum(o.size * o.dtype.itemsize for o in outs)
     if space is HBM:
         args = [pltpu.with_memory_space_constraint(a, pltpu.HBM) for a in args]
     return pl.pallas_call(
@@ -135,8 +137,15 @@
 
 
 def stage_kernel(*refs):
-    count = len(refs) // 2
-    for copy in bring(refs[:count], refs[count : 2 * count], refs[-1]):
+    weights, outs, sems = refs[:3], refs[3:6], refs[6]
+    third = weights[0].shape[0] // 3
+    sources, targets = [], []
+    for weight, out in zip(weights, outs):
+        for part in range(3):
+            rows = pl.ds(part * third, third)
+            sources.append(weight.at[rows, :])
+            targets.append(out.at[rows, :])
+    for copy in bring(sources, targets, sems):
         copy.wait()
 
 
@@ -183,48 +192,79 @@
     pick_ref[:, :tokens] = pick
 
 
-def expert_kernel(*refs):
-    blocks, (wg_ref, wu_ref, wd_ref), outs = refs[:16], refs[16:19], refs[19:]
-    x_ref, dz_ref, act_ref, gg_ref, ug_ref, own_ref, other_ref = outs
-    cap, wide = blocks[0].shape
-    piece = wide // 2
-    half = wide
-    e = lax.axis_index("et")
-    for steps in range(4):
-        start = pl.multiple_of((e ^ steps) * piece, 128)
-        for k in range(4):
-            block = blocks[4 * steps + k]
-            rows = pl.ds(k * cap, cap)
-            x_ref[rows, pl.ds(start, piece)] = block[:, :piece]
-            dz_ref[rows, pl.ds(start, piece)] = block[:, piece:]
-    gate = contract(x_ref[...], wg_ref[...], 1, 1)
-    upper = contract(x_ref[...], wu_ref[...], 1, 1)
-    act_grad = contract(dz_ref[...], wd_ref[...], 1, 1)
+def add_quarter(steps, blocks, x_ref, dz_ref, weights):
+    piece = blocks[0].shape[1] // 2
+    columns = pl.ds(pl.multiple_of((lax.axis_index("et") ^ steps) * piece, 128), piece)
+    start = 0
+    for block in blocks:
+        rows = pl.ds(start, block.shape[0])
+        x_ref[rows, columns] = block[:, :piece]
+        dz_ref[rows, columns] = block[:, piece:]
+        start += block.shape[0]
+    wg_ref, wu_ref, wd_ref = weights
+    x, dz = x_ref[:, columns], dz_ref[:, columns]
+    return (
+        contract(x, wg_ref[:, columns], 1, 1),
+        contract(x, wu_ref[:, columns], 1, 1),
+        contract(dz, wd_ref[:, columns], 1, 1),
+    )
+
+
+def first_kernel(*refs):
+    weights, (x_ref, dz_ref, *sums) = refs[12:15], refs[15:]
+    for steps in range(3):
+        parts = add_quarter(steps, refs[4 * steps : 4 * steps + 4], x_ref, dz_ref, weights)
+        for out, part in zip(sums, parts):
+            out[...] = out[...] + part if steps else part
+
+
+def half_terms(other, gate_grad, up_grad, weights, half):
+    side = lax.axis_index("et") % 2 ^ other
+    columns = pl.ds(pl.multiple_of(side * half, 128), half)
+    terms = contract(gate_grad, weights[0][:, columns], 1, 0)
+    return terms + contract(up_grad, weights[1][:, columns], 1, 0)
+
+
+def third_kernel(*refs):
+    both, weights, olds, outs = refs[:4], refs[4:7], refs[9:12], refs[12:]
+    x_ref, dz_ref, act_ref, gg_ref, ug_ref, grads_ref, away_ref = outs
+    slots = x_ref.shape[0]
+    parts = add_quarter(3, both, x_ref, dz_ref, weights)
+    gate, upper, act_grad = (old[...] + part for old, part in zip(olds, parts))
     sigmoid_gate = jax.nn.sigmoid(gate)
     silu_gate = gate * sigmoid_gate
-    act_ref[...] = (silu_gate * upper).astype(BF16)
     gate_grad = (act_grad * upper * sigmoid_gate * (1.0 + gate * (1.0 - sigmoid_gate))).astype(BF16)
     up_grad = (act_grad * silu_gate).astype(BF16)
     gg_ref[...] = gate_grad
     ug_ref[...] = up_grad
-    core = e % 2
-    for out, side in ((other_ref, 1 - core), (own_ref, core)):
-        start = pl.multiple_of(side * half, 128)
-        terms = contract(gate_grad, wg_ref[:, pl.ds(start, half)], 1, 0)
-        terms += contract(up_grad, wu_ref[:, pl.ds(start, half)], 1, 0)
-        out[...] = terms.astype(BF16)
+    act_ref[...] = (silu_gate * upper).astype(BF16)
+    grads_ref[:slots, :] = gate_grad
+    grads_ref[slots:, :] = up_grad
+    away_ref[...] = half_terms(1, gate_grad, up_grad, weights, away_ref.shape[1]).astype(BF16)
+
+
+def own_terms_kernel(grads_ref, wg_ref, wu_ref, out_ref):
+    slots, half = out_ref.shape
+    grads = grads_ref[:slots, :], grads_ref[slots:, :]
+    out_ref[...] = half_terms(0, *grads, (wg_ref, wu_ref), half)
 
 
 def pair_kernel(own_ref, other_ref, pick_ref, *outs):
-    cap, half = outs[1].shape
+    cap, half = outs[0].shape
     for k, out in enumerate(outs):
         rows = pl.ds(k * cap, cap)
-        out[:, :half] = (own_ref[rows, :].astype(F32) + other_ref[rows, :].astype(F32)).astype(BF16)
-    outs[0][:, half:] = pick_ref[...]
-
-
-def expand_kernel(own_ref, *refs):
-    others, outs, tokens_ref = refs[:3], refs[3:7], refs[7]
+        out[:, :half] = (own_ref[rows, :] + other_ref[rows, :].astype(F32)).astype(BF16)
+    outs[3][:, half:] = pick_ref[...]
+
+
+def add_kernel(left_ref, right_ref, near_ref, out_ref, pass_ref, ready_ref):
+    out_ref[...] = (left_ref[...].astype(F32) + right_ref[...].astype(F32)).astype(BF16)
+    pass_ref[...] = near_ref[...]
+    ready_ref[...] = jnp.zeros_like(ready_ref)
+
+
+def expand_kernel(own_ref, ready_ref, *refs):
+    others, outs, tokens_ref = refs[:2], refs[2:6], refs[6]
     rows, half = outs[0].shape
     e = lax.axis_index("et")
     total = own_ref[:, :half].astype(F32)
@@ -287,10 +327,10 @@
         w_gate[0],
         w_up[0],
         w_down[0],
-        scratch=[pltpu.SemaphoreType.DMA((3,))],
+        scratch=[pltpu.SemaphoreType.DMA((9,))],
         space=HBM,
     )
-    arrived, (wg, wu, wd) = lax.optimization_barrier((arrived, weights))
+    arrived, weights = lax.optimization_barrier((arrived, weights))
     slot_block, pick = call(
         compact_kernel,
         [like((cap, 2 * piece)), like((cap, FLAG))],
@@ -300,39 +340,61 @@
     diag = swap(slot_block, "dp", 3)
     near = swap(slot_block, "dp", 1)
     far = swap(slot_block, "dp", 2)
-    own = [slot_block, diag, near, far]
+    own = [diag, near, far, slot_block]
     chip = [swap(block, "et", 2) for block in own]
     core = [swap(block, "et", 1) for block in own]
     both = [swap(block, "et", 1) for block in chip]
-    x, dz, act, gate_grad, up_grad, terms, away = call(
-        expert_kernel,
-        [like((slots, width))] * 2 + [like((slots, hidden))] * 3 + [like((slots, half))] * 2,
-        *own,
-        *core,
-        *chip,
+    wide, sums = [like((slots, width))] * 2, [like((slots, hidden), F32)] * 3
+    state = call(first_kernel, wide + sums, *own, *core, *chip, *weights, vmem=32)
+    x, dz, act, gate_grad, up_grad, grads, away = call(
+        third_kernel,
+        wide + [like((slots, hidden))] * 3 + [like((2 * slots, hidden)), like((slots, half))],
         *both,
-        wg,
-        wu,
-        wd,
-        flops=10 * slots * hidden * width,
+        *weights,
+        *state,
         vmem=32,
+        aliases={7: 0, 8: 1},
     )
     theirs = swap(away, "et", 1)
-    sums = call(
+    (own_terms,) = call(
+        own_terms_kernel,
+        [like((slots, half), F32)],
+        grads,
+        *weights[:2],
+        flops=4 * slots * hidden * half,
+        vmem=32,
+    )
+    to_last, to_near, to_far, home = call(
         pair_kernel,
-        [like((cap, half + FLAG))] + [like((cap, half))] * 3,
-        terms,
+        [like((cap, half))] * 3 + [like((cap, half + FLAG))],
+        own_terms,
         theirs,
         pick,
     )
-    home = [hand(sums[k], pipe_size, s) for k, s in ((0, 0), (3, 2), (1, 3), (2, 1))]
+    from_last = swap(to_last, "dp", 1)
+    home = hand(home, pipe_size, 0)
+    to_far, to_near, ready = call(
+        add_kernel,
+        [like((cap, half))] * 2 + [like((8, 128), F32)],
+        to_far,
+        from_last,
+        to_near,
+    )
+    x, dz, act, gate_grad, up_grad, ready = lax.optimization_barrier(
+        (x, dz, act, gate_grad, up_grad, ready)
+    )
     grad_gate = contract(gate_grad, x, 0, 0).astype(BF16)
     grad_up = contract(up_grad, x, 0, 0).astype(BF16)
-    home, grad_gate, grad_up = lax.optimization_barrier((home, grad_gate, grad_up))
+    from_far = hand(to_far, pipe_size, 2)
+    from_near = hand(to_near, pipe_size, 1)
+    from_far, grad_gate, grad_up = lax.optimization_barrier((from_far, grad_gate, grad_up))
     by_token = call(
         expand_kernel,
         [like((rows, half))] * 4,
-        *home,
+        home,
+        ready,
+        from_far,
+        from_near,
         scratch=[pltpu.VMEM((FLAG, half), BF16)],
     )
     back = [by_token[0]] + [swap(by_token[s], "et", s) for s in (1, 2, 3)]

time: 54.9 us -> 52.6 us (0.958)
  waiting for transfers between devices: 18.5 us -> 14.3 us
  starting transfers between devices: 21 us -> 22.3 us
    ppermute x4 -> x3, waiting for transfers between devices: 6.5 us -> 0.29 us  [hand(): return lax.ppermute(value, ('pipe', 'dp'), pairs)]
    ppermute x22 -> x23, waiting for transfers between devices: 12 us -> 14 us  [swap(): return lax.ppermute(value, axis, spread(steps))]
    ppermute x22 -> x23, starting transfers between devices: 14.4 us -> 15.6 us  [swap(): return lax.ppermute(value, axis, spread(steps))]
    pallas_call x7 -> x10, Pallas kernels: 8.49 us -> 8.93 us  [call(): pl.pallas_call(kernel, out_shape=outs, in_specs=[space] * len(args), out_...]
    ppermute x4 -> x3, starting transfers between devices: 6.55 us -> 6.7 us  [hand(): return lax.ppermute(value, ('pipe', 'dp'), pairs)]
  transfers between devices with their start and end apart: 26 -> 26, of which waited for: 12 -> 11; matrix products, arithmetic and copies ran while one was open for 11% -> 12% of each run, Pallas kernels for 5% -> 10%
where the time goes in v4:
time: 52.6 us; the launch traced here: 52.4 us
  starting transfers between devices  22.3 us (42%)
  waiting for transfers between devices  14.3 us (27%)
  Pallas kernels  8.93 us (17%)
  matrix products  6.07 us (12%)
  between operations  0.77 us (1%)
    ppermute x23, starting transfers between devices, swap(): return lax.ppermute(value, axis, spread(steps))  15.6 us
    ppermute x23, waiting for transfers between devices, swap(): return lax.ppermute(value, axis, spread(steps))  14 us
    pallas_call x10, Pallas kernels, call(): pl.pallas_call(kernel, out_shape=outs, in_specs=[space] * len(args), out_...  8.93 us
    ppermute x3, starting transfers between devices, hand(): return lax.ppermute(value, ('pipe', 'dp'), pairs)  6.7 us
    dot_general x3, matrix products, contract(): lax.dot_general(left, right, (((left_dim,), (right_dim,)), ((), ())), pre...  6.07 us
  transfers between devices with their start and end apart: 26, of which 11 were waited for; matrix products, arithmetic and copies ran while one was open for 12% of the time, Pallas kernels for 10%

profile of v4, /device:TPU:0, one launch (start us, length us, event | category | flops | bytes accessed | tf_op | source)
XLA Modules:
  0.0 52.4 jit_solution(4467439583814503296)
XLA Ops:
  0.6 1.1 %shard_map.102 = (bf16[16,1664]{1,0:T(8,128)(2,1)S(1)}, bf16[16,1664]{1,0:T(8,128)(2,1)S(1)}, bf16[16,1664]{1,0:T(8,128)(2,1)S(1)}, bf16[16,1664]{1,0:T(8,128)(2,1)S(1)}) custom-call(bf16[16,3072]{1,0:T(8,128)(2,1)} %bitcast.27, bf16[16,3072]{1,0:T(8,128)(2,1)} %bitcast.28, s32[4,16]{1,0:T(4,128)} %bitcast.30, f32[4,16]{1,0:T(4,128)} %bitcast.31), custom_call_target="tpu_custom_call" | custom-call | bytes 410112 | tf_op jit(solution)/shard_map/pallas_call | solution.py:109
  1.7 0.5 collective-permute-start
  2.2 2.6 %collective-permute-start.1 = (bf16[16,1664]{1,0:T(8,128)(2,1)S(1)}, bf16[16,1664]{1,0:T(8,128)(2,1)S(1)}, u32[]{:S(2)}, u32[]{:S(2)}) collective-permute-start(bf16[16,1664]{1,0:T(8,128)(2,1)S(1)} %get-tuple-element.54), channel_id=1, source_target_pairs={{0,2},{1,3},{2,0},{3,1},{4,6},{5,7},{6,4},{7,5},{8,10},{9,11},{10,... | collective-permute-start | bytes 159752 | tf_op jit(solution)/shard_map/ppermute | solution.py:288
  4.8 0.1 collective-permute-start.2
  4.9 2.8 %shard_map.103 = (bf16[336,3072]{1,0:T(8,128)(2,1)S(1)}, bf16[336,3072]{1,0:T(8,128)(2,1)S(1)}, bf16[336,3072]{1,0:T(8,128)(2,1)S(1)}) custom-call(bf16[336,3072]{1,0:T(8,128)(2,1)} %bitcast.22, bf16[336,3072]{1,0:T(8,128)(2,1)} %bitcast.23, bf16[336,3072]{1,0:T(8,128)(2,1)} %bitcast.24), custom_call_target="tpu_custom_call" | custom-call | bytes 12386304 | tf_op jit(solution)/shard_map/pallas_call | solution.py:109
  7.7 0.0 collective-permute-done.refs_1_
  7.7 0.0 collective-permute-done.1.refs_2_
  7.8 0.9 %collective-permute-done.2.refs_3_ = bf16[16,1664]{1,0:T(8,128)(2,1)S(1)} collective-permute-done((bf16[16,1664]{1,0:T(8,128)(2,1)S(1)}, bf16[16,1664]{1,0:T(8,128)(2,1)S(1)}, u32[]{:S(2)}, u32[]{:S(2)}) %collective-permute-start.2) | collective-permute-done | bytes 53280 | tf_op jit(solution)/shard_map/ppermute | solution.py:288
  8.6 0.3 shard_map.104
  9.0 2.7 %collective-permute-start.9 = (bf16[32,1536]{1,0:T(8,128)(2,1)S(1)}, bf16[32,1536]{1,0:T(8,128)(2,1)S(1)}, u32[]{:S(2)}, u32[]{:S(2)}) collective-permute-start(bf16[32,1536]{1,0:T(8,128)(2,1)S(1)} %get-tuple-element.63.refs_3_), channel_id=1, source_target_pairs={{0,8},{4,12},{8,0},{12,4},{1,9},{5,13},{9,1},{13,5},{2,10},{6,14},... | collective-permute-start | bytes 294920 | tf_op jit(solution)/shard_map/ppermute | solution.py:288
  11.6 0.0 collective-permute-start.17
  11.6 1.6 %collective-permute-start.6 = (bf16[32,1536]{1,0:T(8,128)(2,1)S(1)}, bf16[32,1536]{1,0:T(8,128)(2,1)S(1)}, u32[]{:S(2)}, u32[]{:S(2)}) collective-permute-start(bf16[32,1536]{1,0:T(8,128)(2,1)S(1)} %get-tuple-element.63.refs_3_), channel_id=1, source_target_pairs={{0,4},{4,0},{8,12},{12,8},{1,5},{5,1},{9,13},{13,9},{2,6},{6,2},{1... | collective-permute-start | bytes 294920 | tf_op jit(solution)/shard_map/ppermute | solution.py:288
  13.2 1.1 %collective-permute-start.12 = (bf16[32,1536]{1,0:T(8,128)(2,1)S(1)}, bf16[32,1536]{1,0:T(8,128)(2,1)S(1)}, u32[]{:S(2)}, u32[]{:S(2)}) collective-permute-start(bf16[32,1536]{1,0:T(8,128)(2,1)S(1)} %get-tuple-element.63.refs_3_), channel_id=1, source_target_pairs={{0,2},{1,3},{2,0},{3,1},{4,6},{5,7},{6,4},{7,5},{8,10},{9,11},{10,... | collective-permute-start | bytes 294920 | tf_op jit(solution)/shard_map/ppermute | solution.py:288
  14.3 0.2 collective-permute-start.3
  14.5 2.5 %collective-permute-done.9.refs_2_ = bf16[32,1536]{1,0:T(8,128)(2,1)S(1)} collective-permute-done((bf16[32,1536]{1,0:T(8,128)(2,1)S(1)}, bf16[32,1536]{1,0:T(8,128)(2,1)S(1)}, u32[]{:S(2)}, u32[]{:S(2)}) %collective-permute-start.9) | collective-permute-done | bytes 98336 | tf_op jit(solution)/shard_map/ppermute | solution.py:288
  17.0 0.0 collective-permute-done.17.refs_7_
  17.0 1.4 %collective-permute-start.10 = (bf16[32,1536]{1,0:T(8,128)(2,1)S(1)}, bf16[32,1536]{1,0:T(8,128)(2,1)S(1)}, u32[]{:S(2)}, u32[]{:S(2)}) collective-permute-start(bf16[32,1536]{1,0:T(8,128)(2,1)S(1)} %collective-permute-done.9.refs_2_), channel_id=1, source_target_pairs={{0,2},{1,3},{2,0},{3,1},{4,6},{5,7},{6,4},{7,5},{8,10},{9,11},{10,... | collective-permute-start | bytes 294920 | tf_op jit(solution)/shard_map/ppermute | solution.py:288
  18.5 0.2 collective-permute-start.15
  18.7 0.0 collective-permute-done.12.refs_11_
  18.7 0.6 %collective-permute-start.7 = (bf16[32,1536]{1,0:T(8,128)(2,1)S(1)}, bf16[32,1536]{1,0:T(8,128)(2,1)S(1)}, u32[]{:S(2)}, u32[]{:S(2)}) collective-permute-start(bf16[32,1536]{1,0:T(8,128)(2,1)S(1)} %collective-permute-done.6.refs_1_), channel_id=1, source_target_pairs={{0,2},{1,3},{2,0},{3,1},{4,6},{5,7},{6,4},{7,5},{8,10},{9,11},{10,... | collective-permute-start | bytes 294920 | tf_op jit(solution)/shard_map/ppermute | solution.py:288
  19.3 1.5 %collective-permute-done.3.refs_0_ = bf16[32,1536]{1,0:T(8,128)(2,1)S(1)} collective-permute-done((bf16[32,1536]{1,0:T(8,128)(2,1)S(1)}, bf16[32,1536]{1,0:T(8,128)(2,1)S(1)}, u32[]{:S(2)}, u32[]{:S(2)}) %collective-permute-start.3) | collective-permute-done | bytes 98336 | tf_op jit(solution)/shard_map/ppermute | solution.py:288
  20.8 0.9 %collective-permute-start.4 = (bf16[32,1536]{1,0:T(8,128)(2,1)S(1)}, bf16[32,1536]{1,0:T(8,128)(2,1)S(1)}, u32[]{:S(2)}, u32[]{:S(2)}) collective-permute-start(bf16[32,1536]{1,0:T(8,128)(2,1)S(1)} %collective-permute-done.3.refs_0_), channel_id=1, source_target_pairs={{0,2},{1,3},{2,0},{3,1},{4,6},{5,7},{6,4},{7,5},{8,10},{9,11},{10,... | collective-permute-start | bytes 294920 | tf_op jit(solution)/shard_map/ppermute | solution.py:288
  21.8 0.8 %collective-permute-done.10.refs_10_ = bf16[32,1536]{1,0:T(8,128)(2,1)S(1)} collective-permute-done((bf16[32,1536]{1,0:T(8,128)(2,1)S(1)}, bf16[32,1536]{1,0:T(8,128)(2,1)S(1)}, u32[]{:S(2)}, u32[]{:S(2)}) %collective-permute-start.10) | collective-permute-done | bytes 98336 | tf_op jit(solution)/shard_map/ppermute | solution.py:288
  22.6 0.5 collective-permute-start.11
  23.2 1.6 %collective-permute-done.7.refs_9_ = bf16[32,1536]{1,0:T(8,128)(2,1)S(1)} collective-permute-done((bf16[32,1536]{1,0:T(8,128)(2,1)S(1)}, bf16[32,1536]{1,0:T(8,128)(2,1)S(1)}, u32[]{:S(2)}, u32[]{:S(2)}) %collective-permute-start.7) | collective-permute-done | bytes 98336 | tf_op jit(solution)/shard_map/ppermute | solution.py:288
  24.7 1.7 %collective-permute-done.4.refs_8_ = bf16[32,1536]{1,0:T(8,128)(2,1)S(1)} collective-permute-done((bf16[32,1536]{1,0:T(8,128)(2,1)S(1)}, bf16[32,1536]{1,0:T(8,128)(2,1)S(1)}, u32[]{:S(2)}, u32[]{:S(2)}) %collective-permute-start.4) | collective-permute-done | bytes 98336 | tf_op jit(solution)/shard_map/ppermute | solution.py:288
  26.5 1.6 %shard_map.105 = (bf16[128,3072]{1,0:T(8,128)(2,1)S(1)}, bf16[128,3072]{1,0:T(8,128)(2,1)S(1)}, f32[128,336]{1,0:T(8,128)S(1)}, f32[128,336]{1,0:T(8,128)S(1)}, f32[128,336]{1,0:T(8,128)S(1)}) custom-call(bf16[32,1536]{1,0:T(8,128)(2,1)S(1)} %collective-permute-done.3.refs_0_, bf16[32,1536]{1,0:T(8,128)(2,1)S(1)} %collective-permute-done.6.refs_1_, ...), custom_call_target="tpu_custom_call" | custom-call | tf_op jit(solution)/shard_map/pallas_call | solution.py:109
  28.1 1.4 %shard_map.106 = (bf16[128,3072]{1,0:T(8,128)(2,1)S(1)}, bf16[128,3072]{1,0:T(8,128)(2,1)S(1)}, bf16[128,336]{1,0:T(8,128)(2,1)S(1)}, bf16[128,336]{1,0:T(8,128)...) custom-call(bf16[32,1536]{1,0:T(8,128)(2,1)S(1)} %collective-permute, ...), custom_call_target="tpu_custom_call", output_to_operand_aliasing={{0}: (7, {}), {1}: (8, {})} | custom-call | tf_op jit(solution)/shard_map/pallas_call | solution.py:109
  29.6 0.6 %collective-permute-start.18 = (bf16[128,1536]{1,0:T(8,128)(2,1)S(1)}, bf16[128,1536]{1,0:T(8,128)(2,1)S(1)}, u32[]{:S(2)}, u32[]{:S(2)}) collective-permute-start(bf16[128,1536]{1,0:T(8,128)(2,1)S(1)} %get-tuple-element.73), channel_id=1, source_target_pairs={{0,1},{1,0},{2,3},{3,2},{4,5},{5,4},{6,7},{7,6},{8,9},{9,8},{10,11... | collective-permute-start | bytes 1179656 | tf_op jit(solution)/shard_map/ppermute | solution.py:288
  30.1 0.6 %shard_map.107.own_ref = f32[128,1536]{1,0:T(8,128)S(1)} custom-call(bf16[256,336]{1,0:T(8,128)(2,1)S(1)} %get-tuple-element.72.grads_ref, bf16[336,3072]{1,0:T(8,128)(2,1)S(1)} %get-tuple-element.64.refs_12_.refs_4_.wg_ref, bf16[336,3072]{1,0:T(8,128)(2,1)S(1)} %get-tuple-element.65.refs_13_.refs_5_.wu_ref), custom_call_target="tpu_custom_call" | custom-call | flops 264241152 | bytes 5087232 | tf_op jit(solution)/shard_map/pallas_call | solution.py:109
  30.7 0.8 %collective-permute-done.18.other_ref = bf16[128,1536]{1,0:T(8,128)(2,1)S(1)} collective-permute-done((bf16[128,1536]{1,0:T(8,128)(2,1)S(1)}, bf16[128,1536]{1,0:T(8,128)(2,1)S(1)}, u32[]{:S(2)}, u32[]{:S(2)}) %collective-permute-start.18) | collective-permute-done | bytes 393248 | tf_op jit(solution)/shard_map/ppermute | solution.py:288
  31.5 0.1 shard_map.108
  31.6 0.7 %collective-permute-start.20 = (bf16[32,1536]{1,0:T(8,128)(2,1)S(1)}, bf16[32,1536]{1,0:T(8,128)(2,1)S(1)}, u32[]{:S(2)}, u32[]{:S(2)}) collective-permute-start(bf16[32,1536]{1,0:T(8,128)(2,1)S(1)} %get-tuple-element.82), channel_id=1, source_target_pairs={{0,4},{4,0},{8,12},{12,8},{1,5},{5,1},{9,13},{13,9},{2,6},{6,2},{1... | collective-permute-start | bytes 294920 | tf_op jit(solution)/shard_map/ppermute | solution.py:288
  32.3 1.5 %collective-permute-start.19 = (bf16[32,1664]{1,0:T(8,128)(2,1)S(1)}, bf16[32,1664]{1,0:T(8,128)(2,1)S(1)}, u32[]{:S(2)}, u32[]{:S(2)}) collective-permute-start(bf16[32,1664]{1,0:T(8,128)(2,1)S(1)} %get-tuple-element.75), channel_id=1, source_target_pairs={{0,16},{4,20},{8,24},{12,28},{16,0},{20,4},{24,8},{28,12},{1,17},{... | collective-permute-start | bytes 319496 | tf_op jit(solution)/shard_map/ppermute | solution.py:295
  33.7 3.0 %collective-permute-done.20.right_ref = bf16[32,1536]{1,0:T(8,128)(2,1)S(1)} collective-permute-done((bf16[32,1536]{1,0:T(8,128)(2,1)S(1)}, bf16[32,1536]{1,0:T(8,128)(2,1)S(1)}, u32[]{:S(2)}, u32[]{:S(2)}) %collective-permute-start.20) | collective-permute-done | bytes 98336 | tf_op jit(solution)/shard_map/ppermute | solution.py:288
  36.7 3.5 %collective-permute-start.21 = (bf16[32,1536]{1,0:T(8,128)(2,1)S(1)}, bf16[32,1536]{1,0:T(8,128)(2,1)S(1)}, u32[]{:S(2)}, u32[]{:S(2)}) collective-permute-start(bf16[32,1536]{1,0:T(8,128)(2,1)S(1)} %get-tuple-element.86), channel_id=1, source_target_pairs={{0,24},{4,28},{8,16},{12,20},{16,8},{20,12},{24,0},{28,4},{1,25},{... | collective-permute-start | bytes 294920 | tf_op jit(solution)/shard_map/ppermute | solution.py:295
  40.2 1.7 %collective-permute-start.22 = (bf16[32,1536]{1,0:T(8,128)(2,1)S(1)}, bf16[32,1536]{1,0:T(8,128)(2,1)S(1)}, u32[]{:S(2)}, u32[]{:S(2)}) collective-permute-start(bf16[32,1536]{1,0:T(8,128)(2,1)S(1)} %get-tuple-element.91), channel_id=1, source_target_pairs={{0,20},{4,16},{8,28},{12,24},{16,4},{20,0},{24,12},{28,8},{1,21},{... | collective-permute-start | bytes 294920 | tf_op jit(solution)/shard_map/ppermute | solution.py:295
  41.9 2.0 %convolution_convert_fusion.2 = bf16[336,3072]{1,0:T(8,128)(2,1)} fusion(bf16[128,336]{1,0:T(8,128)(2,1)S(1)} %get-tuple-element.87, bf16[128,3072]{1,0:T(8,128)(2,1)S(1)} %get-tuple-element.88), kind=kOutput, calls=%fused_computation.2 | convolution fusion | flops 265273344 | bytes 2936832 | tf_op jit(solution)/shard_map/dot_general | solution.py:40
  44.0 2.0 %convolution_convert_fusion.1 = bf16[336,3072]{1,0:T(8,128)(2,1)} fusion(bf16[128,336]{1,0:T(8,128)(2,1)S(1)} %get-tuple-element.89, bf16[128,3072]{1,0:T(8,128)(2,1)S(1)} %get-tuple-element.88), kind=kOutput, calls=%fused_computation.1 | convolution fusion | flops 265273344 | bytes 2936832 | tf_op jit(solution)/shard_map/dot_general | solution.py:40
  46.0 0.3 collective-permute-done.22.refs_1_
  46.3 0.3 shard_map.110
  46.6 0.1 collective-permute-start.23
  46.7 1.4 %collective-permute-start.24 = (bf16[16,1536]{1,0:T(8,128)(2,1)S(1)}, bf16[16,1536]{1,0:T(8,128)(2,1)S(1)}, u32[]{:S(2)}, u32[]{:S(2)}) collective-permute-start(bf16[16,1536]{1,0:T(8,128)(2,1)S(1)} %get-tuple-element.94), channel_id=1, source_target_pairs={{0,2},{1,3},{2,0},{3,1},{4,6},{5,7},{6,4},{7,5},{8,10},{9,11},{10,... | collective-permute-start | bytes 147464 | tf_op jit(solution)/shard_map/ppermute | solution.py:288
  48.1 0.5 collective-permute-start.25
  48.5 2.0 %fusion = bf16[1,336,3072]{2,1,0:T(8,128)(2,1)} fusion(bf16[128,336]{1,0:T(8,128)(2,1)S(1)} %get-tuple-element.98, bf16[128,3072]{1,0:T(8,128)(2,1)S(1)} %get-tuple-element.99), kind=kOutput, calls=%fused_computation.3 | convolution fusion | flops 265273344 | bytes 2936832 | tf_op jit(solution)/shard_map/dot_general | solution.py:40
  50.6 0.3 collective-permute-done.24.chip_ref
  50.8 0.9 %collective-permute-done.25.both_ref = bf16[16,1536]{1,0:T(8,128)(2,1)S(1)} collective-permute-done((bf16[16,1536]{1,0:T(8,128)(2,1)S(1)}, bf16[16,1536]{1,0:T(8,128)(2,1)S(1)}, u32[]{:S(2)}, u32[]{:S(2)}) %collective-permute-start.25) | collective-permute-done | bytes 49184 | tf_op jit(solution)/shard_map/ppermute | solution.py:288
  51.8 0.7 %shard_map.111 = bf16[16,3072]{1,0:T(8,128)(2,1)} custom-call(bf16[16,1536]{1,0:T(8,128)(2,1)S(1)} %get-tuple-element.92.own_ref, bf16[16,1536]{1,0:T(8,128)(2,1)S(1)} %collective-permute-done.23.core_ref, bf16[16,1536]{1,0:T(8,128)(2,1)S(1)} %collective-permute-done.24.chip_ref, bf16[16,1536]{1,0:T(8,128)(2,1)S(1)} %collective-permute-done.25.both_ref), custom_call_target="tpu_custom_call" | custom-call | tf_op jit(solution)/shard_map/pallas_call | solution.py:109
  (17 shorter events, 0.1 us)
Async XLA Ops:
  1.7 6.0 %collective-permute-start = (bf16[16,1664]{1,0:T(8,128)(2,1)S(1)}, bf16[16,1664]{1,0:T(8,128)(2,1)S(1)}, u32[]{:S(2)}, u32[]{:S(2)}) collective-permute-start(bf16[16,1664]{1,0:T(8,128)(2,1)S(1)} %get-tuple-element.53), channel_id=1, source_target_pairs={{0,1},{1,0},{2,3},{3,2},{4,5},{5,4},{6,7},{7,6},{8,9},{9,8},{10,11... | collective-permute-start | bytes 159752 | tf_op jit(solution)/shard_map/ppermute | solution.py:288
  2.2 5.5 %collective-permute-start.1 = (bf16[16,1664]{1,0:T(8,128)(2,1)S(1)}, bf16[16,1664]{1,0:T(8,128)(2,1)S(1)}, u32[]{:S(2)}, u32[]{:S(2)}) collective-permute-start(bf16[16,1664]{1,0:T(8,128)(2,1)S(1)} %get-tuple-element.54), channel_id=1, source_target_pairs={{0,2},{1,3},{2,0},{3,1},{4,6},{5,7},{6,4},{7,5},{8,10},{9,11},{10,... | collective-permute-start | bytes 159752 | tf_op jit(solution)/shard_map/ppermute | solution.py:288
  4.8 3.8 %collective-permute-start.2 = (bf16[16,1664]{1,0:T(8,128)(2,1)S(1)}, bf16[16,1664]{1,0:T(8,128)(2,1)S(1)}, u32[]{:S(2)}, u32[]{:S(2)}) collective-permute-start(bf16[16,1664]{1,0:T(8,128)(2,1)S(1)} %get-tuple-element.55), channel_id=1, source_target_pairs={{0,3},{1,2},{2,1},{3,0},{4,7},{5,6},{6,5},{7,4},{8,11},{9,10},{10,... | collective-permute-start | bytes 159752 | tf_op jit(solution)/shard_map/ppermute | solution.py:288
  9.0 8.1 %collective-permute-start.9 = (bf16[32,1536]{1,0:T(8,128)(2,1)S(1)}, bf16[32,1536]{1,0:T(8,128)(2,1)S(1)}, u32[]{:S(2)}, u32[]{:S(2)}) collective-permute-start(bf16[32,1536]{1,0:T(8,128)(2,1)S(1)} %get-tuple-element.63.refs_3_), channel_id=1, source_target_pairs={{0,8},{4,12},{8,0},{12,4},{1,9},{5,13},{9,1},{13,5},{2,10},{6,14},... | collective-permute-start | bytes 294920 | tf_op jit(solution)/shard_map/ppermute | solution.py:288
  11.6 5.4 %collective-permute-start.17 = (bf16[32,1536]{1,0:T(8,128)(2,1)S(1)}, bf16[32,1536]{1,0:T(8,128)(2,1)S(1)}, u32[]{:S(2)}, u32[]{:S(2)}) collective-permute-start(bf16[32,1536]{1,0:T(8,128)(2,1)S(1)} %get-tuple-element.63.refs_3_), channel_id=1, source_target_pairs={{0,1},{1,0},{2,3},{3,2},{4,5},{5,4},{6,7},{7,6},{8,9},{9,8},{10,11... | collective-permute-start | bytes 294920 | tf_op jit(solution)/shard_map/ppermute | solution.py:288
  11.6 6.8 %collective-permute-start.6 = (bf16[32,1536]{1,0:T(8,128)(2,1)S(1)}, bf16[32,1536]{1,0:T(8,128)(2,1)S(1)}, u32[]{:S(2)}, u32[]{:S(2)}) collective-permute-start(bf16[32,1536]{1,0:T(8,128)(2,1)S(1)} %get-tuple-element.63.refs_3_), channel_id=1, source_target_pairs={{0,4},{4,0},{8,12},{12,8},{1,5},{5,1},{9,13},{13,9},{2,6},{6,2},{1... | collective-permute-start | bytes 294920 | tf_op jit(solution)/shard_map/ppermute | solution.py:288
  13.2 5.5 %collective-permute-start.12 = (bf16[32,1536]{1,0:T(8,128)(2,1)S(1)}, bf16[32,1536]{1,0:T(8,128)(2,1)S(1)}, u32[]{:S(2)}, u32[]{:S(2)}) collective-permute-start(bf16[32,1536]{1,0:T(8,128)(2,1)S(1)} %get-tuple-element.63.refs_3_), channel_id=1, source_target_pairs={{0,2},{1,3},{2,0},{3,1},{4,6},{5,7},{6,4},{7,5},{8,10},{9,11},{10,... | collective-permute-start | bytes 294920 | tf_op jit(solution)/shard_map/ppermute | solution.py:288
  14.3 6.6 %collective-permute-start.3 = (bf16[32,1536]{1,0:T(8,128)(2,1)S(1)}, bf16[32,1536]{1,0:T(8,128)(2,1)S(1)}, u32[]{:S(2)}, u32[]{:S(2)}) collective-permute-start(bf16[32,1536]{1,0:T(8,128)(2,1)S(1)} %get-tuple-element.63.refs_3_), channel_id=1, source_target_pairs={{0,12},{4,8},{8,4},{12,0},{1,13},{5,9},{9,5},{13,1},{2,14},{6,10},... | collective-permute-start | bytes 294920 | tf_op jit(solution)/shard_map/ppermute | solution.py:288
  17.0 4.8 %collective-permute-start.16 = (bf16[32,1536]{1,0:T(8,128)(2,1)S(1)}, bf16[32,1536]{1,0:T(8,128)(2,1)S(1)}, u32[]{:S(2)}, u32[]{:S(2)}) collective-permute-start(bf16[32,1536]{1,0:T(8,128)(2,1)S(1)} %collective-permute-done.9.refs_2_), channel_id=1, source_target_pairs={{0,1},{1,0},{2,3},{3,2},{4,5},{5,4},{6,7},{7,6},{8,9},{9,8},{10,11... | collective-permute-start | bytes 294920 | tf_op jit(solution)/shard_map/ppermute | solution.py:288
  17.0 5.6 %collective-permute-start.10 = (bf16[32,1536]{1,0:T(8,128)(2,1)S(1)}, bf16[32,1536]{1,0:T(8,128)(2,1)S(1)}, u32[]{:S(2)}, u32[]{:S(2)}) collective-permute-start(bf16[32,1536]{1,0:T(8,128)(2,1)S(1)} %collective-permute-done.9.refs_2_), channel_id=1, source_target_pairs={{0,2},{1,3},{2,0},{3,1},{4,6},{5,7},{6,4},{7,5},{8,10},{9,11},{10,... | collective-permute-start | bytes 294920 | tf_op jit(solution)/shard_map/ppermute | solution.py:288
  18.5 4.2 %collective-permute-start.15 = (bf16[32,1536]{1,0:T(8,128)(2,1)S(1)}, bf16[32,1536]{1,0:T(8,128)(2,1)S(1)}, u32[]{:S(2)}, u32[]{:S(2)}) collective-permute-start(bf16[32,1536]{1,0:T(8,128)(2,1)S(1)} %collective-permute-done.6.refs_1_), channel_id=1, source_target_pairs={{0,1},{1,0},{2,3},{3,2},{4,5},{5,4},{6,7},{7,6},{8,9},{9,8},{10,11... | collective-permute-start | bytes 294920 | tf_op jit(solution)/shard_map/ppermute | solution.py:288
  18.7 6.0 %collective-permute-start.7 = (bf16[32,1536]{1,0:T(8,128)(2,1)S(1)}, bf16[32,1536]{1,0:T(8,128)(2,1)S(1)}, u32[]{:S(2)}, u32[]{:S(2)}) collective-permute-start(bf16[32,1536]{1,0:T(8,128)(2,1)S(1)} %collective-permute-done.6.refs_1_), channel_id=1, source_target_pairs={{0,2},{1,3},{2,0},{3,1},{4,6},{5,7},{6,4},{7,5},{8,10},{9,11},{10,... | collective-permute-start | bytes 294920 | tf_op jit(solution)/shard_map/ppermute | solution.py:288
  20.8 5.6 %collective-permute-start.4 = (bf16[32,1536]{1,0:T(8,128)(2,1)S(1)}, bf16[32,1536]{1,0:T(8,128)(2,1)S(1)}, u32[]{:S(2)}, u32[]{:S(2)}) collective-permute-start(bf16[32,1536]{1,0:T(8,128)(2,1)S(1)} %collective-permute-done.3.refs_0_), channel_id=1, source_target_pairs={{0,2},{1,3},{2,0},{3,1},{4,6},{5,7},{6,4},{7,5},{8,10},{9,11},{10,... | collective-permute-start | bytes 294920 | tf_op jit(solution)/shard_map/ppermute | solution.py:288
  21.8 4.7 %collective-permute-start.14 = (bf16[32,1536]{1,0:T(8,128)(2,1)S(1)}, bf16[32,1536]{1,0:T(8,128)(2,1)S(1)}, u32[]{:S(2)}, u32[]{:S(2)}) collective-permute-start(bf16[32,1536]{1,0:T(8,128)(2,1)S(1)} %collective-permute-done.3.refs_0_), channel_id=1, source_target_pairs={{0,1},{1,0},{2,3},{3,2},{4,5},{5,4},{6,7},{7,6},{8,9},{9,8},{10,11... | collective-permute-start | bytes 294920 | tf_op jit(solution)/shard_map/ppermute | solution.py:288
  22.6 5.5 %collective-permute-start.13 = (bf16[32,1536]{1,0:T(8,128)(2,1)S(1)}, bf16[32,1536]{1,0:T(8,128)(2,1)S(1)}, u32[]{:S(2)}, u32[]{:S(2)}) collective-permute-start(bf16[32,1536]{1,0:T(8,128)(2,1)S(1)} %collective-permute-done.12.refs_11_), channel_id=1, source_target_pairs={{0,1},{1,0},{2,3},{3,2},{4,5},{5,4},{6,7},{7,6},{8,9},{9,8},{10,11... | collective-permute-start | bytes 294920 | tf_op jit(solution)/shard_map/ppermute | solution.py:288
  22.6 5.5 %collective-permute-start.11 = (bf16[32,1536]{1,0:T(8,128)(2,1)S(1)}, bf16[32,1536]{1,0:T(8,128)(2,1)S(1)}, u32[]{:S(2)}, u32[]{:S(2)}) collective-permute-start(bf16[32,1536]{1,0:T(8,128)(2,1)S(1)} %collective-permute-done.10.refs_10_), channel_id=1, source_target_pairs={{0,1},{1,0},{2,3},{3,2},{4,5},{5,4},{6,7},{7,6},{8,9},{9,8},{10,11... | collective-permute-start | bytes 294920 | tf_op jit(solution)/shard_map/ppermute | solution.py:288
  24.7 3.4 %collective-permute-start.8 = (bf16[32,1536]{1,0:T(8,128)(2,1)S(1)}, bf16[32,1536]{1,0:T(8,128)(2,1)S(1)}, u32[]{:S(2)}, u32[]{:S(2)}) collective-permute-start(bf16[32,1536]{1,0:T(8,128)(2,1)S(1)} %collective-permute-done.7.refs_9_), channel_id=1, source_target_pairs={{0,1},{1,0},{2,3},{3,2},{4,5},{5,4},{6,7},{7,6},{8,9},{9,8},{10,11... | collective-permute-start | bytes 294920 | tf_op jit(solution)/shard_map/ppermute | solution.py:288
  26.5 1.7 %collective-permute-start.5 = (bf16[32,1536]{1,0:T(8,128)(2,1)S(1)}, bf16[32,1536]{1,0:T(8,128)(2,1)S(1)}, u32[]{:S(2)}, u32[]{:S(2)}) collective-permute-start(bf16[32,1536]{1,0:T(8,128)(2,1)S(1)} %collective-permute-done.4.refs_8_), channel_id=1, source_target_pairs={{0,1},{1,0},{2,3},{3,2},{4,5},{5,4},{6,7},{7,6},{8,9},{9,8},{10,11... | collective-permute-start | bytes 294920 | tf_op jit(solution)/shard_map/ppermute | solution.py:288
  29.6 1.9 %collective-permute-start.18 = (bf16[128,1536]{1,0:T(8,128)(2,1)S(1)}, bf16[128,1536]{1,0:T(8,128)(2,1)S(1)}, u32[]{:S(2)}, u32[]{:S(2)}) collective-permute-start(bf16[128,1536]{1,0:T(8,128)(2,1)S(1)} %get-tuple-element.73), channel_id=1, source_target_pairs={{0,1},{1,0},{2,3},{3,2},{4,5},{5,4},{6,7},{7,6},{8,9},{9,8},{10,11... | collective-permute-start | bytes 1179656 | tf_op jit(solution)/shard_map/ppermute | solution.py:288
  31.6 5.1 %collective-permute-start.20 = (bf16[32,1536]{1,0:T(8,128)(2,1)S(1)}, bf16[32,1536]{1,0:T(8,128)(2,1)S(1)}, u32[]{:S(2)}, u32[]{:S(2)}) collective-permute-start(bf16[32,1536]{1,0:T(8,128)(2,1)S(1)} %get-tuple-element.82), channel_id=1, source_target_pairs={{0,4},{4,0},{8,12},{12,8},{1,5},{5,1},{9,13},{13,9},{2,6},{6,2},{1... | collective-permute-start | bytes 294920 | tf_op jit(solution)/shard_map/ppermute | solution.py:288
  32.3 13.7 %collective-permute-start.19 = (bf16[32,1664]{1,0:T(8,128)(2,1)S(1)}, bf16[32,1664]{1,0:T(8,128)(2,1)S(1)}, u32[]{:S(2)}, u32[]{:S(2)}) collective-permute-start(bf16[32,1664]{1,0:T(8,128)(2,1)S(1)} %get-tuple-element.75), channel_id=1, source_target_pairs={{0,16},{4,20},{8,24},{12,28},{16,0},{20,4},{24,8},{28,12},{1,17},{... | collective-permute-start | bytes 319496 | tf_op jit(solution)/shard_map/ppermute | solution.py:295
  36.7 9.3 %collective-permute-start.21 = (bf16[32,1536]{1,0:T(8,128)(2,1)S(1)}, bf16[32,1536]{1,0:T(8,128)(2,1)S(1)}, u32[]{:S(2)}, u32[]{:S(2)}) collective-permute-start(bf16[32,1536]{1,0:T(8,128)(2,1)S(1)} %get-tuple-element.86), channel_id=1, source_target_pairs={{0,24},{4,28},{8,16},{12,20},{16,8},{20,12},{24,0},{28,4},{1,25},{... | collective-permute-start | bytes 294920 | tf_op jit(solution)/shard_map/ppermute | solution.py:295
  40.2 6.1 %collective-permute-start.22 = (bf16[32,1536]{1,0:T(8,128)(2,1)S(1)}, bf16[32,1536]{1,0:T(8,128)(2,1)S(1)}, u32[]{:S(2)}, u32[]{:S(2)}) collective-permute-start(bf16[32,1536]{1,0:T(8,128)(2,1)S(1)} %get-tuple-element.91), channel_id=1, source_target_pairs={{0,20},{4,16},{8,28},{12,24},{16,4},{20,0},{24,12},{28,8},{1,21},{... | collective-permute-start | bytes 294920 | tf_op jit(solution)/shard_map/ppermute | solution.py:295
  46.6 4.0 %collective-permute-start.23 = (bf16[16,1536]{1,0:T(8,128)(2,1)S(1)}, bf16[16,1536]{1,0:T(8,128)(2,1)S(1)}, u32[]{:S(2)}, u32[]{:S(2)}) collective-permute-start(bf16[16,1536]{1,0:T(8,128)(2,1)S(1)} %get-tuple-element.93), channel_id=1, source_target_pairs={{0,1},{1,0},{2,3},{3,2},{4,5},{5,4},{6,7},{7,6},{8,9},{9,8},{10,11... | collective-permute-start | bytes 147464 | tf_op jit(solution)/shard_map/ppermute | solution.py:288
  46.7 4.2 %collective-permute-start.24 = (bf16[16,1536]{1,0:T(8,128)(2,1)S(1)}, bf16[16,1536]{1,0:T(8,128)(2,1)S(1)}, u32[]{:S(2)}, u32[]{:S(2)}) collective-permute-start(bf16[16,1536]{1,0:T(8,128)(2,1)S(1)} %get-tuple-element.94), channel_id=1, source_target_pairs={{0,2},{1,3},{2,0},{3,1},{4,6},{5,7},{6,4},{7,5},{8,10},{9,11},{10,... | collective-permute-start | bytes 147464 | tf_op jit(solution)/shard_map/ppermute | solution.py:288
  48.1 3.7 %collective-permute-start.25 = (bf16[16,1536]{1,0:T(8,128)(2,1)S(1)}, bf16[16,1536]{1,0:T(8,128)(2,1)S(1)}, u32[]{:S(2)}, u32[]{:S(2)}) collective-permute-start(bf16[16,1536]{1,0:T(8,128)(2,1)S(1)} %get-tuple-element.95), channel_id=1, source_target_pairs={{0,3},{1,2},{2,1},{3,0},{4,7},{5,6},{6,5},{7,4},{8,11},{9,10},{10,... | collective-permute-start | bytes 147464 | tf_op jit(solution)/shard_map/ppermute | solution.py:288

commit v5 on v4

--- a/solution.py
+++ b/solution.py
@@ -340,8 +340,9 @@
     diag = swap(slot_block, "dp", 3)
     near = swap(slot_block, "dp", 1)
     far = swap(slot_block, "dp", 2)
+    beside = swap(slot_block, "et", 2)
     own = [diag, near, far, slot_block]
-    chip = [swap(block, "et", 2) for block in own]
+    chip = [swap(diag, "et", 2), swap(beside, "dp", 1), swap(far, "et", 2), beside]
     core = [swap(block, "et", 1) for block in own]
     both = [swap(block, "et", 1) for block in chip]
     wide, sums = [like((slots, width))] * 2, [like((slots, hidden), F32)] * 3

time: 52.6 us -> 53.4 us (1.015)
  starting transfers between devices: 22.3 us -> 25.6 us
  waiting for transfers between devices: 14.3 us -> 11.9 us
    ppermute x23, starting transfers between devices: 15.6 us -> 18.3 us  [swap(): return lax.ppermute(value, axis, spread(steps))]
    ppermute x23, waiting for transfers between devices: 14 us -> 11.7 us  [swap(): return lax.ppermute(value, axis, spread(steps))]
    ppermute x3, starting transfers between devices: 6.7 us -> 7.38 us  [hand(): return lax.ppermute(value, ('pipe', 'dp'), pairs)]
  transfers between devices with their start and end apart: 26 -> 26, of which waited for: 11 -> 9; matrix products, arithmetic and copies ran while one was open for 12% -> 11% of each run, Pallas kernels for 10% -> 9%
where the time goes in v5:
time: 53.4 us; the launch traced here: 53.3 us
  starting transfers between devices  25.6 us (48%)
  waiting for transfers between devices  11.9 us (22%)
  Pallas kernels  8.92 us (17%)
  matrix products  6.07 us (11%)
  between operations  0.77 us (1%)
    ppermute x23, starting transfers between devices, swap(): return lax.ppermute(value, axis, spread(steps))  18.3 us
    ppermute x23, waiting for transfers between devices, swap(): return lax.ppermute(value, axis, spread(steps))  11.7 us
    pallas_call x10, Pallas kernels, call(): pl.pallas_call(kernel, out_shape=outs, in_specs=[space] * len(args), out_...  8.92 us
    ppermute x3, starting transfers between devices, hand(): return lax.ppermute(value, ('pipe', 'dp'), pairs)  7.38 us
    dot_general x3, matrix products, contract(): lax.dot_general(left, right, (((left_dim,), (right_dim,)), ((), ())), pre...  6.07 us
  transfers between devices with their start and end apart: 26, of which 9 were waited for; matrix products, arithmetic and copies ran while one was open for 11% of the time, Pallas kernels for 9%

profile of v5, /device:TPU:0, one launch (start us, length us, event | category | flops | bytes accessed | tf_op | source)
XLA Modules:
  0.0 53.3 jit_solution(12980534240807767046)
XLA Ops:
  0.6 1.1 %shard_map.102 = (bf16[16,1664]{1,0:T(8,128)(2,1)S(1)}, bf16[16,1664]{1,0:T(8,128)(2,1)S(1)}, bf16[16,1664]{1,0:T(8,128)(2,1)S(1)}, bf16[16,1664]{1,0:T(8,128)(2,1)S(1)}) custom-call(bf16[16,3072]{1,0:T(8,128)(2,1)} %bitcast.27, bf16[16,3072]{1,0:T(8,128)(2,1)} %bitcast.28, s32[4,16]{1,0:T(4,128)} %bitcast.30, f32[4,16]{1,0:T(4,128)} %bitcast.31), custom_call_target="tpu_custom_call" | custom-call | bytes 410112 | tf_op jit(solution)/shard_map/pallas_call | solution.py:109
  1.7 0.5 collective-permute-start
  2.2 2.6 %collective-permute-start.1 = (bf16[16,1664]{1,0:T(8,128)(2,1)S(1)}, bf16[16,1664]{1,0:T(8,128)(2,1)S(1)}, u32[]{:S(2)}, u32[]{:S(2)}) collective-permute-start(bf16[16,1664]{1,0:T(8,128)(2,1)S(1)} %get-tuple-element.54), channel_id=1, source_target_pairs={{0,2},{1,3},{2,0},{3,1},{4,6},{5,7},{6,4},{7,5},{8,10},{9,11},{10,... | collective-permute-start | bytes 159752 | tf_op jit(solution)/shard_map/ppermute | solution.py:288
  4.8 0.1 collective-permute-start.2
  4.9 2.8 %shard_map.103 = (bf16[336,3072]{1,0:T(8,128)(2,1)S(1)}, bf16[336,3072]{1,0:T(8,128)(2,1)S(1)}, bf16[336,3072]{1,0:T(8,128)(2,1)S(1)}) custom-call(bf16[336,3072]{1,0:T(8,128)(2,1)} %bitcast.22, bf16[336,3072]{1,0:T(8,128)(2,1)} %bitcast.23, bf16[336,3072]{1,0:T(8,128)(2,1)} %bitcast.24), custom_call_target="tpu_custom_call" | custom-call | bytes 12386304 | tf_op jit(solution)/shard_map/pallas_call | solution.py:109
  7.7 0.0 collective-permute-done.refs_1_
  7.7 0.0 collective-permute-done.1.refs_2_
  7.8 0.9 %collective-permute-done.2.refs_3_ = bf16[16,1664]{1,0:T(8,128)(2,1)S(1)} collective-permute-done((bf16[16,1664]{1,0:T(8,128)(2,1)S(1)}, bf16[16,1664]{1,0:T(8,128)(2,1)S(1)}, u32[]{:S(2)}, u32[]{:S(2)}) %collective-permute-start.2) | collective-permute-done | bytes 53280 | tf_op jit(solution)/shard_map/ppermute | solution.py:288
  8.6 0.3 shard_map.104
  9.0 1.6 %collective-permute-start.13 = (bf16[32,1536]{1,0:T(8,128)(2,1)S(1)}, bf16[32,1536]{1,0:T(8,128)(2,1)S(1)}, u32[]{:S(2)}, u32[]{:S(2)}) collective-permute-start(bf16[32,1536]{1,0:T(8,128)(2,1)S(1)} %get-tuple-element.63.refs_3_), channel_id=1, source_target_pairs={{0,4},{4,0},{8,12},{12,8},{1,5},{5,1},{9,13},{13,9},{2,6},{6,2},{1... | collective-permute-start | bytes 294920 | tf_op jit(solution)/shard_map/ppermute | solution.py:288
  10.6 2.6 %collective-permute-start.9 = (bf16[32,1536]{1,0:T(8,128)(2,1)S(1)}, bf16[32,1536]{1,0:T(8,128)(2,1)S(1)}, u32[]{:S(2)}, u32[]{:S(2)}) collective-permute-start(bf16[32,1536]{1,0:T(8,128)(2,1)S(1)} %get-tuple-element.63.refs_3_), channel_id=1, source_target_pairs={{0,8},{4,12},{8,0},{12,4},{1,9},{5,13},{9,1},{13,5},{2,10},{6,14},... | collective-permute-start | bytes 294920 | tf_op jit(solution)/shard_map/ppermute | solution.py:288
  13.2 1.1 %collective-permute-start.6 = (bf16[32,1536]{1,0:T(8,128)(2,1)S(1)}, bf16[32,1536]{1,0:T(8,128)(2,1)S(1)}, u32[]{:S(2)}, u32[]{:S(2)}) collective-permute-start(bf16[32,1536]{1,0:T(8,128)(2,1)S(1)} %get-tuple-element.63.refs_3_), channel_id=1, source_target_pairs={{0,2},{1,3},{2,0},{3,1},{4,6},{5,7},{6,4},{7,5},{8,10},{9,11},{10,... | collective-permute-start | bytes 294920 | tf_op jit(solution)/shard_map/ppermute | solution.py:288
  14.3 0.2 collective-permute-start.3
  14.5 0.0 collective-permute-done.13.refs_1_
  14.5 0.0 collective-permute-start.15
  14.5 3.7 %collective-permute-done.9.refs_2_ = bf16[32,1536]{1,0:T(8,128)(2,1)S(1)} collective-permute-done((bf16[32,1536]{1,0:T(8,128)(2,1)S(1)}, bf16[32,1536]{1,0:T(8,128)(2,1)S(1)}, u32[]{:S(2)}, u32[]{:S(2)}) %collective-permute-start.9) | collective-permute-done | bytes 98336 | tf_op jit(solution)/shard_map/ppermute | solution.py:288
  18.3 0.0 collective-permute-start.16
  18.3 0.0 collective-permute-done.17.refs_7_
  18.3 1.1 %collective-permute-start.10 = (bf16[32,1536]{1,0:T(8,128)(2,1)S(1)}, bf16[32,1536]{1,0:T(8,128)(2,1)S(1)}, u32[]{:S(2)}, u32[]{:S(2)}) collective-permute-start(bf16[32,1536]{1,0:T(8,128)(2,1)S(1)} %collective-permute-done.9.refs_2_), channel_id=1, source_target_pairs={{0,2},{1,3},{2,0},{3,1},{4,6},{5,7},{6,4},{7,5},{8,10},{9,11},{10,... | collective-permute-start | bytes 294920 | tf_op jit(solution)/shard_map/ppermute | solution.py:288
  19.4 0.0 collective-permute-done.6.refs_11_
  19.4 2.8 %collective-permute-start.7 = (bf16[32,1536]{1,0:T(8,128)(2,1)S(1)}, bf16[32,1536]{1,0:T(8,128)(2,1)S(1)}, u32[]{:S(2)}, u32[]{:S(2)}) collective-permute-start(bf16[32,1536]{1,0:T(8,128)(2,1)S(1)} %collective-permute-done.6.refs_11_), channel_id=1, source_target_pairs={{0,4},{4,0},{8,12},{12,8},{1,5},{5,1},{9,13},{13,9},{2,6},{6,2},{1... | collective-permute-start | bytes 294920 | tf_op jit(solution)/shard_map/ppermute | solution.py:288
  22.2 0.9 %collective-permute-start.4 = (bf16[32,1536]{1,0:T(8,128)(2,1)S(1)}, bf16[32,1536]{1,0:T(8,128)(2,1)S(1)}, u32[]{:S(2)}, u32[]{:S(2)}) collective-permute-start(bf16[32,1536]{1,0:T(8,128)(2,1)S(1)} %collective-permute-done.3.refs_0_), channel_id=1, source_target_pairs={{0,2},{1,3},{2,0},{3,1},{4,6},{5,7},{6,4},{7,5},{8,10},{9,11},{10,... | collective-permute-start | bytes 294920 | tf_op jit(solution)/shard_map/ppermute | solution.py:288
  23.1 0.5 collective-permute-start.12
  23.6 0.1 collective-permute-start.11
  23.7 1.7 %collective-permute-done.7.refs_9_ = bf16[32,1536]{1,0:T(8,128)(2,1)S(1)} collective-permute-done((bf16[32,1536]{1,0:T(8,128)(2,1)S(1)}, bf16[32,1536]{1,0:T(8,128)(2,1)S(1)}, u32[]{:S(2)}, u32[]{:S(2)}) %collective-permute-start.7) | collective-permute-done | bytes 98336 | tf_op jit(solution)/shard_map/ppermute | solution.py:288
  25.4 1.5 %collective-permute-done.4.refs_8_ = bf16[32,1536]{1,0:T(8,128)(2,1)S(1)} collective-permute-done((bf16[32,1536]{1,0:T(8,128)(2,1)S(1)}, bf16[32,1536]{1,0:T(8,128)(2,1)S(1)}, u32[]{:S(2)}, u32[]{:S(2)}) %collective-permute-start.4) | collective-permute-done | bytes 98336 | tf_op jit(solution)/shard_map/ppermute | solution.py:288
  26.8 1.6 %shard_map.105 = (bf16[128,3072]{1,0:T(8,128)(2,1)S(1)}, bf16[128,3072]{1,0:T(8,128)(2,1)S(1)}, f32[128,336]{1,0:T(8,128)S(1)}, f32[128,336]{1,0:T(8,128)S(1)}, f32[128,336]{1,0:T(8,128)S(1)}) custom-call(bf16[32,1536]{1,0:T(8,128)(2,1)S(1)} %collective-permute-done.3.refs_0_, bf16[32,1536]{1,0:T(8,128)(2,1)S(1)} %collective-permute-done.13.refs_1_, ...), custom_call_target="tpu_custom_call" | custom-call | tf_op jit(solution)/shard_map/pallas_call | solution.py:109
  28.5 1.4 %shard_map.106 = (bf16[128,3072]{1,0:T(8,128)(2,1)S(1)}, bf16[128,3072]{1,0:T(8,128)(2,1)S(1)}, bf16[128,336]{1,0:T(8,128)(2,1)S(1)}, bf16[128,336]{1,0:T(8,128)...) custom-call(bf16[32,1536]{1,0:T(8,128)(2,1)S(1)} %collective-permute, ...), custom_call_target="tpu_custom_call", output_to_operand_aliasing={{0}: (7, {}), {1}: (8, {})} | custom-call | tf_op jit(solution)/shard_map/pallas_call | solution.py:109
  29.9 0.6 %collective-permute-start.18 = (bf16[128,1536]{1,0:T(8,128)(2,1)S(1)}, bf16[128,1536]{1,0:T(8,128)(2,1)S(1)}, u32[]{:S(2)}, u32[]{:S(2)}) collective-permute-start(bf16[128,1536]{1,0:T(8,128)(2,1)S(1)} %get-tuple-element.73), channel_id=1, source_target_pairs={{0,1},{1,0},{2,3},{3,2},{4,5},{5,4},{6,7},{7,6},{8,9},{9,8},{10,11... | collective-permute-start | bytes 1179656 | tf_op jit(solution)/shard_map/ppermute | solution.py:288
  30.5 0.6 %shard_map.107.own_ref = f32[128,1536]{1,0:T(8,128)S(1)} custom-call(bf16[256,336]{1,0:T(8,128)(2,1)S(1)} %get-tuple-element.72.grads_ref, bf16[336,3072]{1,0:T(8,128)(2,1)S(1)} %get-tuple-element.64.refs_12_.refs_4_.wg_ref, bf16[336,3072]{1,0:T(8,128)(2,1)S(1)} %get-tuple-element.65.refs_13_.refs_5_.wu_ref), custom_call_target="tpu_custom_call" | custom-call | flops 264241152 | bytes 5087232 | tf_op jit(solution)/shard_map/pallas_call | solution.py:109
  31.1 0.8 %collective-permute-done.18.other_ref = bf16[128,1536]{1,0:T(8,128)(2,1)S(1)} collective-permute-done((bf16[128,1536]{1,0:T(8,128)(2,1)S(1)}, bf16[128,1536]{1,0:T(8,128)(2,1)S(1)}, u32[]{:S(2)}, u32[]{:S(2)}) %collective-permute-start.18) | collective-permute-done | bytes 393248 | tf_op jit(solution)/shard_map/ppermute | solution.py:288
  31.9 0.1 shard_map.108
  31.9 1.6 %collective-permute-start.20 = (bf16[32,1536]{1,0:T(8,128)(2,1)S(1)}, bf16[32,1536]{1,0:T(8,128)(2,1)S(1)}, u32[]{:S(2)}, u32[]{:S(2)}) collective-permute-start(bf16[32,1536]{1,0:T(8,128)(2,1)S(1)} %get-tuple-element.82), channel_id=1, source_target_pairs={{0,4},{4,0},{8,12},{12,8},{1,5},{5,1},{9,13},{13,9},{2,6},{6,2},{1... | collective-permute-start | bytes 294920 | tf_op jit(solution)/shard_map/ppermute | solution.py:288
  33.6 1.5 %collective-permute-start.19 = (bf16[32,1664]{1,0:T(8,128)(2,1)S(1)}, bf16[32,1664]{1,0:T(8,128)(2,1)S(1)}, u32[]{:S(2)}, u32[]{:S(2)}) collective-permute-start(bf16[32,1664]{1,0:T(8,128)(2,1)S(1)} %get-tuple-element.75), channel_id=1, source_target_pairs={{0,16},{4,20},{8,24},{12,28},{16,0},{20,4},{24,8},{28,12},{1,17},{... | collective-permute-start | bytes 319496 | tf_op jit(solution)/shard_map/ppermute | solution.py:295
  35.0 2.0 %collective-permute-done.20.right_ref = bf16[32,1536]{1,0:T(8,128)(2,1)S(1)} collective-permute-done((bf16[32,1536]{1,0:T(8,128)(2,1)S(1)}, bf16[32,1536]{1,0:T(8,128)(2,1)S(1)}, u32[]{:S(2)}, u32[]{:S(2)}) %collective-permute-start.20) | collective-permute-done | bytes 98336 | tf_op jit(solution)/shard_map/ppermute | solution.py:288
  37.1 4.4 %collective-permute-start.21 = (bf16[32,1536]{1,0:T(8,128)(2,1)S(1)}, bf16[32,1536]{1,0:T(8,128)(2,1)S(1)}, u32[]{:S(2)}, u32[]{:S(2)}) collective-permute-start(bf16[32,1536]{1,0:T(8,128)(2,1)S(1)} %get-tuple-element.86), channel_id=1, source_target_pairs={{0,24},{4,28},{8,16},{12,20},{16,8},{20,12},{24,0},{28,4},{1,25},{... | collective-permute-start | bytes 294920 | tf_op jit(solution)/shard_map/ppermute | solution.py:295
  41.5 1.5 %collective-permute-start.22 = (bf16[32,1536]{1,0:T(8,128)(2,1)S(1)}, bf16[32,1536]{1,0:T(8,128)(2,1)S(1)}, u32[]{:S(2)}, u32[]{:S(2)}) collective-permute-start(bf16[32,1536]{1,0:T(8,128)(2,1)S(1)} %get-tuple-element.91), channel_id=1, source_target_pairs={{0,20},{4,16},{8,28},{12,24},{16,4},{20,0},{24,12},{28,8},{1,21},{... | collective-permute-start | bytes 294920 | tf_op jit(solution)/shard_map/ppermute | solution.py:295
  43.0 2.0 %convolution_convert_fusion.2 = bf16[336,3072]{1,0:T(8,128)(2,1)} fusion(bf16[128,336]{1,0:T(8,128)(2,1)S(1)} %get-tuple-element.87, bf16[128,3072]{1,0:T(8,128)(2,1)S(1)} %get-tuple-element.88), kind=kOutput, calls=%fused_computation.2 | convolution fusion | flops 265273344 | bytes 2936832 | tf_op jit(solution)/shard_map/dot_general | solution.py:40
  45.0 2.0 %convolution_convert_fusion.1 = bf16[336,3072]{1,0:T(8,128)(2,1)} fusion(bf16[128,336]{1,0:T(8,128)(2,1)S(1)} %get-tuple-element.89, bf16[128,3072]{1,0:T(8,128)(2,1)S(1)} %get-tuple-element.88), kind=kOutput, calls=%fused_computation.1 | convolution fusion | flops 265273344 | bytes 2936832 | tf_op jit(solution)/shard_map/dot_general | solution.py:40
  47.0 0.2 collective-permute-done.22.refs_1_
  47.3 0.3 shard_map.110
  47.5 0.1 collective-permute-start.23
  47.6 1.0 %collective-permute-start.24 = (bf16[16,1536]{1,0:T(8,128)(2,1)S(1)}, bf16[16,1536]{1,0:T(8,128)(2,1)S(1)}, u32[]{:S(2)}, u32[]{:S(2)}) collective-permute-start(bf16[16,1536]{1,0:T(8,128)(2,1)S(1)} %get-tuple-element.94), channel_id=1, source_target_pairs={{0,2},{1,3},{2,0},{3,1},{4,6},{5,7},{6,4},{7,5},{8,10},{9,11},{10,... | collective-permute-start | bytes 147464 | tf_op jit(solution)/shard_map/ppermute | solution.py:288
  48.6 0.9 %collective-permute-start.25 = (bf16[16,1536]{1,0:T(8,128)(2,1)S(1)}, bf16[16,1536]{1,0:T(8,128)(2,1)S(1)}, u32[]{:S(2)}, u32[]{:S(2)}) collective-permute-start(bf16[16,1536]{1,0:T(8,128)(2,1)S(1)} %get-tuple-element.95), channel_id=1, source_target_pairs={{0,3},{1,2},{2,1},{3,0},{4,7},{5,6},{6,5},{7,4},{8,11},{9,10},{10,... | collective-permute-start | bytes 147464 | tf_op jit(solution)/shard_map/ppermute | solution.py:288
  49.5 2.0 %fusion = bf16[1,336,3072]{2,1,0:T(8,128)(2,1)} fusion(bf16[128,336]{1,0:T(8,128)(2,1)S(1)} %get-tuple-element.98, bf16[128,3072]{1,0:T(8,128)(2,1)S(1)} %get-tuple-element.99), kind=kOutput, calls=%fused_computation.3 | convolution fusion | flops 265273344 | bytes 2936832 | tf_op jit(solution)/shard_map/dot_general | solution.py:40
  51.5 0.5 collective-permute-done.24.chip_ref
  52.0 0.7 %collective-permute-done.25.both_ref = bf16[16,1536]{1,0:T(8,128)(2,1)S(1)} collective-permute-done((bf16[16,1536]{1,0:T(8,128)(2,1)S(1)}, bf16[16,1536]{1,0:T(8,128)(2,1)S(1)}, u32[]{:S(2)}, u32[]{:S(2)}) %collective-permute-start.25) | collective-permute-done | bytes 49184 | tf_op jit(solution)/shard_map/ppermute | solution.py:288
  52.6 0.7 %shard_map.111 = bf16[16,3072]{1,0:T(8,128)(2,1)} custom-call(bf16[16,1536]{1,0:T(8,128)(2,1)S(1)} %get-tuple-element.92.own_ref, bf16[16,1536]{1,0:T(8,128)(2,1)S(1)} %collective-permute-done.23.core_ref, bf16[16,1536]{1,0:T(8,128)(2,1)S(1)} %collective-permute-done.24.chip_ref, bf16[16,1536]{1,0:T(8,128)(2,1)S(1)} %collective-permute-done.25.both_ref), custom_call_target="tpu_custom_call" | custom-call | tf_op jit(solution)/shard_map/pallas_call | solution.py:109
  (17 shorter events, 0.1 us)
Async XLA Ops:
  1.7 6.0 %collective-permute-start = (bf16[16,1664]{1,0:T(8,128)(2,1)S(1)}, bf16[16,1664]{1,0:T(8,128)(2,1)S(1)}, u32[]{:S(2)}, u32[]{:S(2)}) collective-permute-start(bf16[16,1664]{1,0:T(8,128)(2,1)S(1)} %get-tuple-element.53), channel_id=1, source_target_pairs={{0,1},{1,0},{2,3},{3,2},{4,5},{5,4},{6,7},{7,6},{8,9},{9,8},{10,11... | collective-permute-start | bytes 159752 | tf_op jit(solution)/shard_map/ppermute | solution.py:288
  2.2 5.5 %collective-permute-start.1 = (bf16[16,1664]{1,0:T(8,128)(2,1)S(1)}, bf16[16,1664]{1,0:T(8,128)(2,1)S(1)}, u32[]{:S(2)}, u32[]{:S(2)}) collective-permute-start(bf16[16,1664]{1,0:T(8,128)(2,1)S(1)} %get-tuple-element.54), channel_id=1, source_target_pairs={{0,2},{1,3},{2,0},{3,1},{4,6},{5,7},{6,4},{7,5},{8,10},{9,11},{10,... | collective-permute-start | bytes 159752 | tf_op jit(solution)/shard_map/ppermute | solution.py:288
  4.8 3.8 %collective-permute-start.2 = (bf16[16,1664]{1,0:T(8,128)(2,1)S(1)}, bf16[16,1664]{1,0:T(8,128)(2,1)S(1)}, u32[]{:S(2)}, u32[]{:S(2)}) collective-permute-start(bf16[16,1664]{1,0:T(8,128)(2,1)S(1)} %get-tuple-element.55), channel_id=1, source_target_pairs={{0,3},{1,2},{2,1},{3,0},{4,7},{5,6},{6,5},{7,4},{8,11},{9,10},{10,... | collective-permute-start | bytes 159752 | tf_op jit(solution)/shard_map/ppermute | solution.py:288
  9.0 5.5 %collective-permute-start.13 = (bf16[32,1536]{1,0:T(8,128)(2,1)S(1)}, bf16[32,1536]{1,0:T(8,128)(2,1)S(1)}, u32[]{:S(2)}, u32[]{:S(2)}) collective-permute-start(bf16[32,1536]{1,0:T(8,128)(2,1)S(1)} %get-tuple-element.63.refs_3_), channel_id=1, source_target_pairs={{0,4},{4,0},{8,12},{12,8},{1,5},{5,1},{9,13},{13,9},{2,6},{6,2},{1... | collective-permute-start | bytes 294920 | tf_op jit(solution)/shard_map/ppermute | solution.py:288
  10.6 7.7 %collective-permute-start.9 = (bf16[32,1536]{1,0:T(8,128)(2,1)S(1)}, bf16[32,1536]{1,0:T(8,128)(2,1)S(1)}, u32[]{:S(2)}, u32[]{:S(2)}) collective-permute-start(bf16[32,1536]{1,0:T(8,128)(2,1)S(1)} %get-tuple-element.63.refs_3_), channel_id=1, source_target_pairs={{0,8},{4,12},{8,0},{12,4},{1,9},{5,13},{9,1},{13,5},{2,10},{6,14},... | collective-permute-start | bytes 294920 | tf_op jit(solution)/shard_map/ppermute | solution.py:288
  13.2 5.1 %collective-permute-start.17 = (bf16[32,1536]{1,0:T(8,128)(2,1)S(1)}, bf16[32,1536]{1,0:T(8,128)(2,1)S(1)}, u32[]{:S(2)}, u32[]{:S(2)}) collective-permute-start(bf16[32,1536]{1,0:T(8,128)(2,1)S(1)} %get-tuple-element.63.refs_3_), channel_id=1, source_target_pairs={{0,1},{1,0},{2,3},{3,2},{4,5},{5,4},{6,7},{7,6},{8,9},{9,8},{10,11... | collective-permute-start | bytes 294920 | tf_op jit(solution)/shard_map/ppermute | solution.py:288
  13.2 6.2 %collective-permute-start.6 = (bf16[32,1536]{1,0:T(8,128)(2,1)S(1)}, bf16[32,1536]{1,0:T(8,128)(2,1)S(1)}, u32[]{:S(2)}, u32[]{:S(2)}) collective-permute-start(bf16[32,1536]{1,0:T(8,128)(2,1)S(1)} %get-tuple-element.63.refs_3_), channel_id=1, source_target_pairs={{0,2},{1,3},{2,0},{3,1},{4,6},{5,7},{6,4},{7,5},{8,10},{9,11},{10,... | collective-permute-start | bytes 294920 | tf_op jit(solution)/shard_map/ppermute | solution.py:288
  14.3 7.9 %collective-permute-start.3 = (bf16[32,1536]{1,0:T(8,128)(2,1)S(1)}, bf16[32,1536]{1,0:T(8,128)(2,1)S(1)}, u32[]{:S(2)}, u32[]{:S(2)}) collective-permute-start(bf16[32,1536]{1,0:T(8,128)(2,1)S(1)} %get-tuple-element.63.refs_3_), channel_id=1, source_target_pairs={{0,12},{4,8},{8,4},{12,0},{1,13},{5,9},{9,5},{13,1},{2,14},{6,10},... | collective-permute-start | bytes 294920 | tf_op jit(solution)/shard_map/ppermute | solution.py:288
  14.5 8.6 %collective-permute-start.15 = (bf16[32,1536]{1,0:T(8,128)(2,1)S(1)}, bf16[32,1536]{1,0:T(8,128)(2,1)S(1)}, u32[]{:S(2)}, u32[]{:S(2)}) collective-permute-start(bf16[32,1536]{1,0:T(8,128)(2,1)S(1)} %collective-permute-done.13.refs_1_), channel_id=1, source_target_pairs={{0,1},{1,0},{2,3},{3,2},{4,5},{5,4},{6,7},{7,6},{8,9},{9,8},{10,11... | collective-permute-start | bytes 294920 | tf_op jit(solution)/shard_map/ppermute | solution.py:288
  18.3 4.8 %collective-permute-start.16 = (bf16[32,1536]{1,0:T(8,128)(2,1)S(1)}, bf16[32,1536]{1,0:T(8,128)(2,1)S(1)}, u32[]{:S(2)}, u32[]{:S(2)}) collective-permute-start(bf16[32,1536]{1,0:T(8,128)(2,1)S(1)} %collective-permute-done.9.refs_2_), channel_id=1, source_target_pairs={{0,1},{1,0},{2,3},{3,2},{4,5},{5,4},{6,7},{7,6},{8,9},{9,8},{10,11... | collective-permute-start | bytes 294920 | tf_op jit(solution)/shard_map/ppermute | solution.py:288
  18.3 5.3 %collective-permute-start.10 = (bf16[32,1536]{1,0:T(8,128)(2,1)S(1)}, bf16[32,1536]{1,0:T(8,128)(2,1)S(1)}, u32[]{:S(2)}, u32[]{:S(2)}) collective-permute-start(bf16[32,1536]{1,0:T(8,128)(2,1)S(1)} %collective-permute-done.9.refs_2_), channel_id=1, source_target_pairs={{0,2},{1,3},{2,0},{3,1},{4,6},{5,7},{6,4},{7,5},{8,10},{9,11},{10,... | collective-permute-start | bytes 294920 | tf_op jit(solution)/shard_map/ppermute | solution.py:288
  19.4 5.9 %collective-permute-start.7 = (bf16[32,1536]{1,0:T(8,128)(2,1)S(1)}, bf16[32,1536]{1,0:T(8,128)(2,1)S(1)}, u32[]{:S(2)}, u32[]{:S(2)}) collective-permute-start(bf16[32,1536]{1,0:T(8,128)(2,1)S(1)} %collective-permute-done.6.refs_11_), channel_id=1, source_target_pairs={{0,4},{4,0},{8,12},{12,8},{1,5},{5,1},{9,13},{13,9},{2,6},{6,2},{1... | collective-permute-start | bytes 294920 | tf_op jit(solution)/shard_map/ppermute | solution.py:288
  22.2 4.6 %collective-permute-start.4 = (bf16[32,1536]{1,0:T(8,128)(2,1)S(1)}, bf16[32,1536]{1,0:T(8,128)(2,1)S(1)}, u32[]{:S(2)}, u32[]{:S(2)}) collective-permute-start(bf16[32,1536]{1,0:T(8,128)(2,1)S(1)} %collective-permute-done.3.refs_0_), channel_id=1, source_target_pairs={{0,2},{1,3},{2,0},{3,1},{4,6},{5,7},{6,4},{7,5},{8,10},{9,11},{10,... | collective-permute-start | bytes 294920 | tf_op jit(solution)/shard_map/ppermute | solution.py:288
  23.1 3.7 %collective-permute-start.14 = (bf16[32,1536]{1,0:T(8,128)(2,1)S(1)}, bf16[32,1536]{1,0:T(8,128)(2,1)S(1)}, u32[]{:S(2)}, u32[]{:S(2)}) collective-permute-start(bf16[32,1536]{1,0:T(8,128)(2,1)S(1)} %collective-permute-done.3.refs_0_), channel_id=1, source_target_pairs={{0,1},{1,0},{2,3},{3,2},{4,5},{5,4},{6,7},{7,6},{8,9},{9,8},{10,11... | collective-permute-start | bytes 294920 | tf_op jit(solution)/shard_map/ppermute | solution.py:288
  23.1 5.4 %collective-permute-start.12 = (bf16[32,1536]{1,0:T(8,128)(2,1)S(1)}, bf16[32,1536]{1,0:T(8,128)(2,1)S(1)}, u32[]{:S(2)}, u32[]{:S(2)}) collective-permute-start(bf16[32,1536]{1,0:T(8,128)(2,1)S(1)} %collective-permute-done.6.refs_11_), channel_id=1, source_target_pairs={{0,1},{1,0},{2,3},{3,2},{4,5},{5,4},{6,7},{7,6},{8,9},{9,8},{10,11... | collective-permute-start | bytes 294920 | tf_op jit(solution)/shard_map/ppermute | solution.py:288
  23.6 4.9 %collective-permute-start.11 = (bf16[32,1536]{1,0:T(8,128)(2,1)S(1)}, bf16[32,1536]{1,0:T(8,128)(2,1)S(1)}, u32[]{:S(2)}, u32[]{:S(2)}) collective-permute-start(bf16[32,1536]{1,0:T(8,128)(2,1)S(1)} %collective-permute-done.10.refs_10_), channel_id=1, source_target_pairs={{0,1},{1,0},{2,3},{3,2},{4,5},{5,4},{6,7},{7,6},{8,9},{9,8},{10,11... | collective-permute-start | bytes 294920 | tf_op jit(solution)/shard_map/ppermute | solution.py:288
  25.4 3.1 %collective-permute-start.8 = (bf16[32,1536]{1,0:T(8,128)(2,1)S(1)}, bf16[32,1536]{1,0:T(8,128)(2,1)S(1)}, u32[]{:S(2)}, u32[]{:S(2)}) collective-permute-start(bf16[32,1536]{1,0:T(8,128)(2,1)S(1)} %collective-permute-done.7.refs_9_), channel_id=1, source_target_pairs={{0,1},{1,0},{2,3},{3,2},{4,5},{5,4},{6,7},{7,6},{8,9},{9,8},{10,11... | collective-permute-start | bytes 294920 | tf_op jit(solution)/shard_map/ppermute | solution.py:288
  26.8 1.7 %collective-permute-start.5 = (bf16[32,1536]{1,0:T(8,128)(2,1)S(1)}, bf16[32,1536]{1,0:T(8,128)(2,1)S(1)}, u32[]{:S(2)}, u32[]{:S(2)}) collective-permute-start(bf16[32,1536]{1,0:T(8,128)(2,1)S(1)} %collective-permute-done.4.refs_8_), channel_id=1, source_target_pairs={{0,1},{1,0},{2,3},{3,2},{4,5},{5,4},{6,7},{7,6},{8,9},{9,8},{10,11... | collective-permute-start | bytes 294920 | tf_op jit(solution)/shard_map/ppermute | solution.py:288
  29.9 1.9 %collective-permute-start.18 = (bf16[128,1536]{1,0:T(8,128)(2,1)S(1)}, bf16[128,1536]{1,0:T(8,128)(2,1)S(1)}, u32[]{:S(2)}, u32[]{:S(2)}) collective-permute-start(bf16[128,1536]{1,0:T(8,128)(2,1)S(1)} %get-tuple-element.73), channel_id=1, source_target_pairs={{0,1},{1,0},{2,3},{3,2},{4,5},{5,4},{6,7},{7,6},{8,9},{9,8},{10,11... | collective-permute-start | bytes 1179656 | tf_op jit(solution)/shard_map/ppermute | solution.py:288
  31.9 5.1 %collective-permute-start.20 = (bf16[32,1536]{1,0:T(8,128)(2,1)S(1)}, bf16[32,1536]{1,0:T(8,128)(2,1)S(1)}, u32[]{:S(2)}, u32[]{:S(2)}) collective-permute-start(bf16[32,1536]{1,0:T(8,128)(2,1)S(1)} %get-tuple-element.82), channel_id=1, source_target_pairs={{0,4},{4,0},{8,12},{12,8},{1,5},{5,1},{9,13},{13,9},{2,6},{6,2},{1... | collective-permute-start | bytes 294920 | tf_op jit(solution)/shard_map/ppermute | solution.py:288
  33.6 13.5 %collective-permute-start.19 = (bf16[32,1664]{1,0:T(8,128)(2,1)S(1)}, bf16[32,1664]{1,0:T(8,128)(2,1)S(1)}, u32[]{:S(2)}, u32[]{:S(2)}) collective-permute-start(bf16[32,1664]{1,0:T(8,128)(2,1)S(1)} %get-tuple-element.75), channel_id=1, source_target_pairs={{0,16},{4,20},{8,24},{12,28},{16,0},{20,4},{24,8},{28,12},{1,17},{... | collective-permute-start | bytes 319496 | tf_op jit(solution)/shard_map/ppermute | solution.py:295
  37.1 9.9 %collective-permute-start.21 = (bf16[32,1536]{1,0:T(8,128)(2,1)S(1)}, bf16[32,1536]{1,0:T(8,128)(2,1)S(1)}, u32[]{:S(2)}, u32[]{:S(2)}) collective-permute-start(bf16[32,1536]{1,0:T(8,128)(2,1)S(1)} %get-tuple-element.86), channel_id=1, source_target_pairs={{0,24},{4,28},{8,16},{12,20},{16,8},{20,12},{24,0},{28,4},{1,25},{... | collective-permute-start | bytes 294920 | tf_op jit(solution)/shard_map/ppermute | solution.py:295
  41.5 5.8 %collective-permute-start.22 = (bf16[32,1536]{1,0:T(8,128)(2,1)S(1)}, bf16[32,1536]{1,0:T(8,128)(2,1)S(1)}, u32[]{:S(2)}, u32[]{:S(2)}) collective-permute-start(bf16[32,1536]{1,0:T(8,128)(2,1)S(1)} %get-tuple-element.91), channel_id=1, source_target_pairs={{0,20},{4,16},{8,28},{12,24},{16,4},{20,0},{24,12},{28,8},{1,21},{... | collective-permute-start | bytes 294920 | tf_op jit(solution)/shard_map/ppermute | solution.py:295
  47.5 4.0 %collective-permute-start.23 = (bf16[16,1536]{1,0:T(8,128)(2,1)S(1)}, bf16[16,1536]{1,0:T(8,128)(2,1)S(1)}, u32[]{:S(2)}, u32[]{:S(2)}) collective-permute-start(bf16[16,1536]{1,0:T(8,128)(2,1)S(1)} %get-tuple-element.93), channel_id=1, source_target_pairs={{0,1},{1,0},{2,3},{3,2},{4,5},{5,4},{6,7},{7,6},{8,9},{9,8},{10,11... | collective-permute-start | bytes 147464 | tf_op jit(solution)/shard_map/ppermute | solution.py:288
  47.6 4.4 %collective-permute-start.24 = (bf16[16,1536]{1,0:T(8,128)(2,1)S(1)}, bf16[16,1536]{1,0:T(8,128)(2,1)S(1)}, u32[]{:S(2)}, u32[]{:S(2)}) collective-permute-start(bf16[16,1536]{1,0:T(8,128)(2,1)S(1)} %get-tuple-element.94), channel_id=1, source_target_pairs={{0,2},{1,3},{2,0},{3,1},{4,6},{5,7},{6,4},{7,5},{8,10},{9,11},{10,... | collective-permute-start | bytes 147464 | tf_op jit(solution)/shard_map/ppermute | solution.py:288
  48.6 4.0 %collective-permute-start.25 = (bf16[16,1536]{1,0:T(8,128)(2,1)S(1)}, bf16[16,1536]{1,0:T(8,128)(2,1)S(1)}, u32[]{:S(2)}, u32[]{:S(2)}) collective-permute-start(bf16[16,1536]{1,0:T(8,128)(2,1)S(1)} %get-tuple-element.95), channel_id=1, source_target_pairs={{0,3},{1,2},{2,1},{3,0},{4,7},{5,6},{6,5},{7,4},{8,11},{9,10},{10,... | collective-permute-start | bytes 147464 | tf_op jit(solution)/shard_map/ppermute | solution.py:288

commit v6 on v4

--- a/solution.py
+++ b/solution.py
@@ -249,18 +249,20 @@
     out_ref[...] = half_terms(0, *grads, (wg_ref, wu_ref), half)
 
 
-def pair_kernel(own_ref, other_ref, pick_ref, *outs):
+def pair_kernel(own_ref, other_ref, pick_ref, *refs):
+    outs, ready_ref = refs[:4], refs[4]
     cap, half = outs[0].shape
     for k, out in enumerate(outs):
         rows = pl.ds(k * cap, cap)
         out[:, :half] = (own_ref[rows, :] + other_ref[rows, :].astype(F32)).astype(BF16)
     outs[3][:, half:] = pick_ref[...]
-
-
-def add_kernel(left_ref, right_ref, near_ref, out_ref, pass_ref, ready_ref):
+    ready_ref[...] = jnp.zeros_like(ready_ref)
+
+
+def add_kernel(left_ref, right_ref, near_ref, first_ref, out_ref, pass_ref, ready_ref):
     out_ref[...] = (left_ref[...].astype(F32) + right_ref[...].astype(F32)).astype(BF16)
     pass_ref[...] = near_ref[...]
-    ready_ref[...] = jnp.zeros_like(ready_ref)
+    ready_ref[...] = first_ref[...]
 
 
 def expand_kernel(own_ref, ready_ref, *refs):
@@ -364,30 +366,35 @@
         flops=4 * slots * hidden * half,
         vmem=32,
     )
-    to_last, to_near, to_far, home = call(
+    to_last, to_near, to_far, home, first = call(
         pair_kernel,
-        [like((cap, half))] * 3 + [like((cap, half + FLAG))],
+        [like((cap, half))] * 3 + [like((cap, half + FLAG)), like((8, 128), F32)],
         own_terms,
         theirs,
         pick,
     )
     from_last = swap(to_last, "dp", 1)
     home = hand(home, pipe_size, 0)
+    x, dz, act, gate_grad, up_grad, first = lax.optimization_barrier(
+        (x, dz, act, gate_grad, up_grad, first)
+    )
+    grad_down = contract(act, dz, 0, 0).astype(BF16)
+    from_last, grad_down = lax.optimization_barrier((from_last, grad_down))
     to_far, to_near, ready = call(
         add_kernel,
         [like((cap, half))] * 2 + [like((8, 128), F32)],
         to_far,
         from_last,
         to_near,
+        first,
     )
     x, dz, act, gate_grad, up_grad, ready = lax.optimization_barrier(
         (x, dz, act, gate_grad, up_grad, ready)
     )
     grad_gate = contract(gate_grad, x, 0, 0).astype(BF16)
-    grad_up = contract(up_grad, x, 0, 0).astype(BF16)
     from_far = hand(to_far, pipe_size, 2)
     from_near = hand(to_near, pipe_size, 1)
-    from_far, grad_gate, grad_up = lax.optimization_barrier((from_far, grad_gate, grad_up))
+    from_far, grad_gate = lax.optimization_barrier((from_far, grad_gate))
     by_token = call(
         expand_kernel,
         [like((rows, half))] * 4,
@@ -399,7 +406,7 @@
     )
     back = [by_token[0]] + [swap(by_token[s], "et", s) for s in (1, 2, 3)]
     (handed,) = call(finish_kernel, [like((rows, width))], *back)
-    grad_down = contract(act, dz, 0, 0).astype(BF16)
+    grad_up = contract(up_grad, x, 0, 0).astype(BF16)
     return (handed[None, None], grad_gate[None], grad_up[None], grad_down[None])
 
 

time: 52.6 us -> 52.6 us (level)
    ppermute x23, waiting for transfers between devices: 14 us -> 12 us  [swap(): return lax.ppermute(value, axis, spread(steps))]
    ppermute x3, waiting for transfers between devices: 0.29 us -> 2.31 us  [hand(): return lax.ppermute(value, ('pipe', 'dp'), pairs)]
  transfers between devices with their start and end apart: 26 -> 26, of which waited for: 11 -> 12; matrix products, arithmetic and copies ran while one was open for 12% -> 12% of each run, Pallas kernels for 10% -> 10%
where the time goes in v6:
time: 52.6 us; the launch traced here: 52.4 us
  starting transfers between devices  22.3 us (42%)
  waiting for transfers between devices  14.3 us (27%)
  Pallas kernels  8.93 us (17%)
  matrix products  6.07 us (12%)
  between operations  0.77 us (1%)
    ppermute x23, starting transfers between devices, swap(): return lax.ppermute(value, axis, spread(steps))  15.6 us
    ppermute x23, waiting for transfers between devices, swap(): return lax.ppermute(value, axis, spread(steps))  12 us
    pallas_call x10, Pallas kernels, call(): pl.pallas_call(kernel, out_shape=outs, in_specs=[space] * len(args), out_...  8.93 us
    ppermute x3, starting transfers between devices, hand(): return lax.ppermute(value, ('pipe', 'dp'), pairs)  6.7 us
    dot_general x3, matrix products, contract(): lax.dot_general(left, right, (((left_dim,), (right_dim,)), ((), ())), pre...  6.07 us
    ppermute x3, waiting for transfers between devices, hand(): return lax.ppermute(value, ('pipe', 'dp'), pairs)  2.31 us
  transfers between devices with their start and end apart: 26, of which 12 were waited for; matrix products, arithmetic and copies ran while one was open for 12% of the time, Pallas kernels for 10%

profile of v6, /device:TPU:0, one launch (start us, length us, event | category | flops | bytes accessed | tf_op | source)
XLA Modules:
  0.0 52.4 jit_solution(15989261814717499187)
XLA Ops:
  0.6 1.1 %shard_map.102 = (bf16[16,1664]{1,0:T(8,128)(2,1)S(1)}, bf16[16,1664]{1,0:T(8,128)(2,1)S(1)}, bf16[16,1664]{1,0:T(8,128)(2,1)S(1)}, bf16[16,1664]{1,0:T(8,128)(2,1)S(1)}) custom-call(bf16[16,3072]{1,0:T(8,128)(2,1)} %bitcast.27, bf16[16,3072]{1,0:T(8,128)(2,1)} %bitcast.28, s32[4,16]{1,0:T(4,128)} %bitcast.30, f32[4,16]{1,0:T(4,128)} %bitcast.31), custom_call_target="tpu_custom_call" | custom-call | bytes 410112 | tf_op jit(solution)/shard_map/pallas_call | solution.py:109
  1.7 0.5 collective-permute-start
  2.2 2.6 %collective-permute-start.1 = (bf16[16,1664]{1,0:T(8,128)(2,1)S(1)}, bf16[16,1664]{1,0:T(8,128)(2,1)S(1)}, u32[]{:S(2)}, u32[]{:S(2)}) collective-permute-start(bf16[16,1664]{1,0:T(8,128)(2,1)S(1)} %get-tuple-element.60), channel_id=1, source_target_pairs={{0,2},{1,3},{2,0},{3,1},{4,6},{5,7},{6,4},{7,5},{8,10},{9,11},{10,... | collective-permute-start | bytes 159752 | tf_op jit(solution)/shard_map/ppermute | solution.py:290
  4.8 0.1 collective-permute-start.2
  4.9 2.8 %shard_map.103 = (bf16[336,3072]{1,0:T(8,128)(2,1)S(1)}, bf16[336,3072]{1,0:T(8,128)(2,1)S(1)}, bf16[336,3072]{1,0:T(8,128)(2,1)S(1)}) custom-call(bf16[336,3072]{1,0:T(8,128)(2,1)} %bitcast.22, bf16[336,3072]{1,0:T(8,128)(2,1)} %bitcast.23, bf16[336,3072]{1,0:T(8,128)(2,1)} %bitcast.24), custom_call_target="tpu_custom_call" | custom-call | bytes 12386304 | tf_op jit(solution)/shard_map/pallas_call | solution.py:109
  7.7 0.0 collective-permute-done.refs_1_
  7.8 0.9 %collective-permute-done.2.refs_3_ = bf16[16,1664]{1,0:T(8,128)(2,1)S(1)} collective-permute-done((bf16[16,1664]{1,0:T(8,128)(2,1)S(1)}, bf16[16,1664]{1,0:T(8,128)(2,1)S(1)}, u32[]{:S(2)}, u32[]{:S(2)}) %collective-permute-start.2) | collective-permute-done | bytes 53280 | tf_op jit(solution)/shard_map/ppermute | solution.py:290
  8.6 0.3 shard_map.104
  9.0 2.7 %collective-permute-start.9 = (bf16[32,1536]{1,0:T(8,128)(2,1)S(1)}, bf16[32,1536]{1,0:T(8,128)(2,1)S(1)}, u32[]{:S(2)}, u32[]{:S(2)}) collective-permute-start(bf16[32,1536]{1,0:T(8,128)(2,1)S(1)} %get-tuple-element.69.refs_3_), channel_id=1, source_target_pairs={{0,8},{4,12},{8,0},{12,4},{1,9},{5,13},{9,1},{13,5},{2,10},{6,14},... | collective-permute-start | bytes 294920 | tf_op jit(solution)/shard_map/ppermute | solution.py:290
  11.6 0.0 collective-permute-start.17
  11.6 1.6 %collective-permute-start.6 = (bf16[32,1536]{1,0:T(8,128)(2,1)S(1)}, bf16[32,1536]{1,0:T(8,128)(2,1)S(1)}, u32[]{:S(2)}, u32[]{:S(2)}) collective-permute-start(bf16[32,1536]{1,0:T(8,128)(2,1)S(1)} %get-tuple-element.69.refs_3_), channel_id=1, source_target_pairs={{0,4},{4,0},{8,12},{12,8},{1,5},{5,1},{9,13},{13,9},{2,6},{6,2},{1... | collective-permute-start | bytes 294920 | tf_op jit(solution)/shard_map/ppermute | solution.py:290
  13.2 1.1 %collective-permute-start.12 = (bf16[32,1536]{1,0:T(8,128)(2,1)S(1)}, bf16[32,1536]{1,0:T(8,128)(2,1)S(1)}, u32[]{:S(2)}, u32[]{:S(2)}) collective-permute-start(bf16[32,1536]{1,0:T(8,128)(2,1)S(1)} %get-tuple-element.69.refs_3_), channel_id=1, source_target_pairs={{0,2},{1,3},{2,0},{3,1},{4,6},{5,7},{6,4},{7,5},{8,10},{9,11},{10,... | collective-permute-start | bytes 294920 | tf_op jit(solution)/shard_map/ppermute | solution.py:290
  14.3 0.2 collective-permute-start.3
  14.5 2.5 %collective-permute-done.9.refs_2_ = bf16[32,1536]{1,0:T(8,128)(2,1)S(1)} collective-permute-done((bf16[32,1536]{1,0:T(8,128)(2,1)S(1)}, bf16[32,1536]{1,0:T(8,128)(2,1)S(1)}, u32[]{:S(2)}, u32[]{:S(2)}) %collective-permute-start.9) | collective-permute-done | bytes 98336 | tf_op jit(solution)/shard_map/ppermute | solution.py:290
  17.0 0.0 collective-permute-start.16
  17.0 1.4 %collective-permute-start.10 = (bf16[32,1536]{1,0:T(8,128)(2,1)S(1)}, bf16[32,1536]{1,0:T(8,128)(2,1)S(1)}, u32[]{:S(2)}, u32[]{:S(2)}) collective-permute-start(bf16[32,1536]{1,0:T(8,128)(2,1)S(1)} %collective-permute-done.9.refs_2_), channel_id=1, source_target_pairs={{0,2},{1,3},{2,0},{3,1},{4,6},{5,7},{6,4},{7,5},{8,10},{9,11},{10,... | collective-permute-start | bytes 294920 | tf_op jit(solution)/shard_map/ppermute | solution.py:290
  18.5 0.0 collective-permute-done.6.refs_1_
  18.5 0.2 collective-permute-start.15
  18.7 0.6 %collective-permute-start.7 = (bf16[32,1536]{1,0:T(8,128)(2,1)S(1)}, bf16[32,1536]{1,0:T(8,128)(2,1)S(1)}, u32[]{:S(2)}, u32[]{:S(2)}) collective-permute-start(bf16[32,1536]{1,0:T(8,128)(2,1)S(1)} %collective-permute-done.6.refs_1_), channel_id=1, source_target_pairs={{0,2},{1,3},{2,0},{3,1},{4,6},{5,7},{6,4},{7,5},{8,10},{9,11},{10,... | collective-permute-start | bytes 294920 | tf_op jit(solution)/shard_map/ppermute | solution.py:290
  19.3 1.5 %collective-permute-done.3.refs_0_ = bf16[32,1536]{1,0:T(8,128)(2,1)S(1)} collective-permute-done((bf16[32,1536]{1,0:T(8,128)(2,1)S(1)}, bf16[32,1536]{1,0:T(8,128)(2,1)S(1)}, u32[]{:S(2)}, u32[]{:S(2)}) %collective-permute-start.3) | collective-permute-done | bytes 98336 | tf_op jit(solution)/shard_map/ppermute | solution.py:290
  20.8 0.9 %collective-permute-start.4 = (bf16[32,1536]{1,0:T(8,128)(2,1)S(1)}, bf16[32,1536]{1,0:T(8,128)(2,1)S(1)}, u32[]{:S(2)}, u32[]{:S(2)}) collective-permute-start(bf16[32,1536]{1,0:T(8,128)(2,1)S(1)} %collective-permute-done.3.refs_0_), channel_id=1, source_target_pairs={{0,2},{1,3},{2,0},{3,1},{4,6},{5,7},{6,4},{7,5},{8,10},{9,11},{10,... | collective-permute-start | bytes 294920 | tf_op jit(solution)/shard_map/ppermute | solution.py:290
  21.8 0.8 %collective-permute-done.10.refs_10_ = bf16[32,1536]{1,0:T(8,128)(2,1)S(1)} collective-permute-done((bf16[32,1536]{1,0:T(8,128)(2,1)S(1)}, bf16[32,1536]{1,0:T(8,128)(2,1)S(1)}, u32[]{:S(2)}, u32[]{:S(2)}) %collective-permute-start.10) | collective-permute-done | bytes 98336 | tf_op jit(solution)/shard_map/ppermute | solution.py:290
  22.6 0.5 collective-permute-start.11
  23.2 1.6 %collective-permute-done.7.refs_9_ = bf16[32,1536]{1,0:T(8,128)(2,1)S(1)} collective-permute-done((bf16[32,1536]{1,0:T(8,128)(2,1)S(1)}, bf16[32,1536]{1,0:T(8,128)(2,1)S(1)}, u32[]{:S(2)}, u32[]{:S(2)}) %collective-permute-start.7) | collective-permute-done | bytes 98336 | tf_op jit(solution)/shard_map/ppermute | solution.py:290
  24.7 1.7 %collective-permute-done.4.refs_8_ = bf16[32,1536]{1,0:T(8,128)(2,1)S(1)} collective-permute-done((bf16[32,1536]{1,0:T(8,128)(2,1)S(1)}, bf16[32,1536]{1,0:T(8,128)(2,1)S(1)}, u32[]{:S(2)}, u32[]{:S(2)}) %collective-permute-start.4) | collective-permute-done | bytes 98336 | tf_op jit(solution)/shard_map/ppermute | solution.py:290
  26.5 1.6 %shard_map.105 = (bf16[128,3072]{1,0:T(8,128)(2,1)S(1)}, bf16[128,3072]{1,0:T(8,128)(2,1)S(1)}, f32[128,336]{1,0:T(8,128)S(1)}, f32[128,336]{1,0:T(8,128)S(1)}, f32[128,336]{1,0:T(8,128)S(1)}) custom-call(bf16[32,1536]{1,0:T(8,128)(2,1)S(1)} %collective-permute-done.3.refs_0_, bf16[32,1536]{1,0:T(8,128)(2,1)S(1)} %collective-permute-done.6.refs_1_, ...), custom_call_target="tpu_custom_call" | custom-call | tf_op jit(solution)/shard_map/pallas_call | solution.py:109
  28.1 1.4 %shard_map.106 = (bf16[128,3072]{1,0:T(8,128)(2,1)S(1)}, bf16[128,3072]{1,0:T(8,128)(2,1)S(1)}, bf16[128,336]{1,0:T(8,128)(2,1)S(1)}, bf16[128,336]{1,0:T(8,128)...) custom-call(bf16[32,1536]{1,0:T(8,128)(2,1)S(1)} %collective-permute, ...), custom_call_target="tpu_custom_call", output_to_operand_aliasing={{0}: (7, {}), {1}: (8, {})} | custom-call | tf_op jit(solution)/shard_map/pallas_call | solution.py:109
  29.6 0.6 %collective-permute-start.18 = (bf16[128,1536]{1,0:T(8,128)(2,1)S(1)}, bf16[128,1536]{1,0:T(8,128)(2,1)S(1)}, u32[]{:S(2)}, u32[]{:S(2)}) collective-permute-start(bf16[128,1536]{1,0:T(8,128)(2,1)S(1)} %get-tuple-element.79), channel_id=1, source_target_pairs={{0,1},{1,0},{2,3},{3,2},{4,5},{5,4},{6,7},{7,6},{8,9},{9,8},{10,11... | collective-permute-start | bytes 1179656 | tf_op jit(solution)/shard_map/ppermute | solution.py:290
  30.1 0.6 %shard_map.107.own_ref = f32[128,1536]{1,0:T(8,128)S(1)} custom-call(bf16[256,336]{1,0:T(8,128)(2,1)S(1)} %get-tuple-element.78.grads_ref, bf16[336,3072]{1,0:T(8,128)(2,1)S(1)} %get-tuple-element.70.refs_12_.refs_4_.wg_ref, bf16[336,3072]{1,0:T(8,128)(2,1)S(1)} %get-tuple-element.71.refs_13_.refs_5_.wu_ref), custom_call_target="tpu_custom_call" | custom-call | flops 264241152 | bytes 5087232 | tf_op jit(solution)/shard_map/pallas_call | solution.py:109
  30.7 0.8 %collective-permute-done.18.other_ref = bf16[128,1536]{1,0:T(8,128)(2,1)S(1)} collective-permute-done((bf16[128,1536]{1,0:T(8,128)(2,1)S(1)}, bf16[128,1536]{1,0:T(8,128)(2,1)S(1)}, u32[]{:S(2)}, u32[]{:S(2)}) %collective-permute-start.18) | collective-permute-done | bytes 393248 | tf_op jit(solution)/shard_map/ppermute | solution.py:290
  31.5 0.1 shard_map.108
  31.6 0.7 %collective-permute-start.20 = (bf16[32,1536]{1,0:T(8,128)(2,1)S(1)}, bf16[32,1536]{1,0:T(8,128)(2,1)S(1)}, u32[]{:S(2)}, u32[]{:S(2)}) collective-permute-start(bf16[32,1536]{1,0:T(8,128)(2,1)S(1)} %get-tuple-element.94), channel_id=1, source_target_pairs={{0,4},{4,0},{8,12},{12,8},{1,5},{5,1},{9,13},{13,9},{2,6},{6,2},{1... | collective-permute-start | bytes 294920 | tf_op jit(solution)/shard_map/ppermute | solution.py:290
  32.3 1.5 %collective-permute-start.19 = (bf16[32,1664]{1,0:T(8,128)(2,1)S(1)}, bf16[32,1664]{1,0:T(8,128)(2,1)S(1)}, u32[]{:S(2)}, u32[]{:S(2)}) collective-permute-start(bf16[32,1664]{1,0:T(8,128)(2,1)S(1)} %get-tuple-element.81), channel_id=1, source_target_pairs={{0,16},{4,20},{8,24},{12,28},{16,0},{20,4},{24,8},{28,12},{1,17},{... | collective-permute-start | bytes 319496 | tf_op jit(solution)/shard_map/ppermute | solution.py:297
  33.7 2.0 %convolution_convert_fusion.2 = bf16[336,3072]{1,0:T(8,128)(2,1)} fusion(bf16[128,336]{1,0:T(8,128)(2,1)S(1)} %get-tuple-element.90, bf16[128,3072]{1,0:T(8,128)(2,1)S(1)} %get-tuple-element.89), kind=kOutput, calls=%fused_computation.2 | convolution fusion | flops 265273344 | bytes 2936832 | tf_op jit(solution)/shard_map/dot_general | solution.py:40
  35.8 0.9 %collective-permute-done.20.right_ref = bf16[32,1536]{1,0:T(8,128)(2,1)S(1)} collective-permute-done((bf16[32,1536]{1,0:T(8,128)(2,1)S(1)}, bf16[32,1536]{1,0:T(8,128)(2,1)S(1)}, u32[]{:S(2)}, u32[]{:S(2)}) %collective-permute-start.20) | collective-permute-done | bytes 98336 | tf_op jit(solution)/shard_map/ppermute | solution.py:290
  36.7 3.5 %collective-permute-start.21 = (bf16[32,1536]{1,0:T(8,128)(2,1)S(1)}, bf16[32,1536]{1,0:T(8,128)(2,1)S(1)}, u32[]{:S(2)}, u32[]{:S(2)}) collective-permute-start(bf16[32,1536]{1,0:T(8,128)(2,1)S(1)} %get-tuple-element.100), channel_id=1, source_target_pairs={{0,24},{4,28},{8,16},{12,20},{16,8},{20,12},{24,0},{28,4},{1,25},{... | collective-permute-start | bytes 294920 | tf_op jit(solution)/shard_map/ppermute | solution.py:297
  40.2 1.7 %collective-permute-start.22 = (bf16[32,1536]{1,0:T(8,128)(2,1)S(1)}, bf16[32,1536]{1,0:T(8,128)(2,1)S(1)}, u32[]{:S(2)}, u32[]{:S(2)}) collective-permute-start(bf16[32,1536]{1,0:T(8,128)(2,1)S(1)} %get-tuple-element.104), channel_id=1, source_target_pairs={{0,20},{4,16},{8,28},{12,24},{16,4},{20,0},{24,12},{28,8},{1,21},{... | collective-permute-start | bytes 294920 | tf_op jit(solution)/shard_map/ppermute | solution.py:297
  42.0 2.0 %convolution_convert_fusion.1 = bf16[336,3072]{1,0:T(8,128)(2,1)} fusion(bf16[128,336]{1,0:T(8,128)(2,1)S(1)} %get-tuple-element.101, bf16[128,3072]{1,0:T(8,128)(2,1)S(1)} %get-tuple-element.102), kind=kOutput, calls=%fused_computation.1 | convolution fusion | flops 265273344 | bytes 2936832 | tf_op jit(solution)/shard_map/dot_general | solution.py:40
  44.0 1.2 %collective-permute-done.21.refs_0_ = bf16[32,1536]{1,0:T(8,128)(2,1)S(1)} collective-permute-done((bf16[32,1536]{1,0:T(8,128)(2,1)S(1)}, bf16[32,1536]{1,0:T(8,128)(2,1)S(1)}, u32[]{:S(2)}, u32[]{:S(2)}) %collective-permute-start.21) | collective-permute-done | bytes 98336 | tf_op jit(solution)/shard_map/ppermute | solution.py:297
  45.2 1.1 %collective-permute-done.22.refs_1_ = bf16[32,1536]{1,0:T(8,128)(2,1)S(1)} collective-permute-done((bf16[32,1536]{1,0:T(8,128)(2,1)S(1)}, bf16[32,1536]{1,0:T(8,128)(2,1)S(1)}, u32[]{:S(2)}, u32[]{:S(2)}) %collective-permute-start.22) | collective-permute-done | bytes 98336 | tf_op jit(solution)/shard_map/ppermute | solution.py:297
  46.3 0.3 shard_map.110
  46.6 0.1 collective-permute-start.23
  46.7 1.4 %collective-permute-start.24 = (bf16[16,1536]{1,0:T(8,128)(2,1)S(1)}, bf16[16,1536]{1,0:T(8,128)(2,1)S(1)}, u32[]{:S(2)}, u32[]{:S(2)}) collective-permute-start(bf16[16,1536]{1,0:T(8,128)(2,1)S(1)} %get-tuple-element.107), channel_id=1, source_target_pairs={{0,2},{1,3},{2,0},{3,1},{4,6},{5,7},{6,4},{7,5},{8,10},{9,11},{10,... | collective-permute-start | bytes 147464 | tf_op jit(solution)/shard_map/ppermute | solution.py:290
  48.1 0.5 collective-permute-start.25
  48.5 2.0 %fusion = bf16[1,336,3072]{2,1,0:T(8,128)(2,1)} fusion(bf16[128,336]{1,0:T(8,128)(2,1)S(1)} %get-tuple-element.110, bf16[128,3072]{1,0:T(8,128)(2,1)S(1)} %get-tuple-element.102), kind=kOutput, calls=%fused_computation.3 | convolution fusion | flops 265273344 | bytes 2936832 | tf_op jit(solution)/shard_map/dot_general | solution.py:40
  50.6 0.3 collective-permute-done.24.chip_ref
  50.8 0.9 %collective-permute-done.25.both_ref = bf16[16,1536]{1,0:T(8,128)(2,1)S(1)} collective-permute-done((bf16[16,1536]{1,0:T(8,128)(2,1)S(1)}, bf16[16,1536]{1,0:T(8,128)(2,1)S(1)}, u32[]{:S(2)}, u32[]{:S(2)}) %collective-permute-start.25) | collective-permute-done | bytes 49184 | tf_op jit(solution)/shard_map/ppermute | solution.py:290
  51.8 0.7 %shard_map.111 = bf16[16,3072]{1,0:T(8,128)(2,1)} custom-call(bf16[16,1536]{1,0:T(8,128)(2,1)S(1)} %get-tuple-element.105.own_ref, bf16[16,1536]{1,0:T(8,128)(2,1)S(1)} %collective-permute-done.23.core_ref, bf16[16,1536]{1,0:T(8,128)(2,1)S(1)} %collective-permute-done.24.chip_ref, bf16[16,1536]{1,0:T(8,128)(2,1)S(1)} %collective-permute-done.25.both_ref), custom_call_target="tpu_custom_call" | custom-call | tf_op jit(solution)/shard_map/pallas_call | solution.py:109
  (17 shorter events, 0.1 us)
Async XLA Ops:
  1.7 6.0 %collective-permute-start = (bf16[16,1664]{1,0:T(8,128)(2,1)S(1)}, bf16[16,1664]{1,0:T(8,128)(2,1)S(1)}, u32[]{:S(2)}, u32[]{:S(2)}) collective-permute-start(bf16[16,1664]{1,0:T(8,128)(2,1)S(1)} %get-tuple-element.59), channel_id=1, source_target_pairs={{0,1},{1,0},{2,3},{3,2},{4,5},{5,4},{6,7},{7,6},{8,9},{9,8},{10,11... | collective-permute-start | bytes 159752 | tf_op jit(solution)/shard_map/ppermute | solution.py:290
  2.2 5.5 %collective-permute-start.1 = (bf16[16,1664]{1,0:T(8,128)(2,1)S(1)}, bf16[16,1664]{1,0:T(8,128)(2,1)S(1)}, u32[]{:S(2)}, u32[]{:S(2)}) collective-permute-start(bf16[16,1664]{1,0:T(8,128)(2,1)S(1)} %get-tuple-element.60), channel_id=1, source_target_pairs={{0,2},{1,3},{2,0},{3,1},{4,6},{5,7},{6,4},{7,5},{8,10},{9,11},{10,... | collective-permute-start | bytes 159752 | tf_op jit(solution)/shard_map/ppermute | solution.py:290
  4.8 3.8 %collective-permute-start.2 = (bf16[16,1664]{1,0:T(8,128)(2,1)S(1)}, bf16[16,1664]{1,0:T(8,128)(2,1)S(1)}, u32[]{:S(2)}, u32[]{:S(2)}) collective-permute-start(bf16[16,1664]{1,0:T(8,128)(2,1)S(1)} %get-tuple-element.61), channel_id=1, source_target_pairs={{0,3},{1,2},{2,1},{3,0},{4,7},{5,6},{6,5},{7,4},{8,11},{9,10},{10,... | collective-permute-start | bytes 159752 | tf_op jit(solution)/shard_map/ppermute | solution.py:290
  9.0 8.1 %collective-permute-start.9 = (bf16[32,1536]{1,0:T(8,128)(2,1)S(1)}, bf16[32,1536]{1,0:T(8,128)(2,1)S(1)}, u32[]{:S(2)}, u32[]{:S(2)}) collective-permute-start(bf16[32,1536]{1,0:T(8,128)(2,1)S(1)} %get-tuple-element.69.refs_3_), channel_id=1, source_target_pairs={{0,8},{4,12},{8,0},{12,4},{1,9},{5,13},{9,1},{13,5},{2,10},{6,14},... | collective-permute-start | bytes 294920 | tf_op jit(solution)/shard_map/ppermute | solution.py:290
  11.6 5.4 %collective-permute-start.17 = (bf16[32,1536]{1,0:T(8,128)(2,1)S(1)}, bf16[32,1536]{1,0:T(8,128)(2,1)S(1)}, u32[]{:S(2)}, u32[]{:S(2)}) collective-permute-start(bf16[32,1536]{1,0:T(8,128)(2,1)S(1)} %get-tuple-element.69.refs_3_), channel_id=1, source_target_pairs={{0,1},{1,0},{2,3},{3,2},{4,5},{5,4},{6,7},{7,6},{8,9},{9,8},{10,11... | collective-permute-start | bytes 294920 | tf_op jit(solution)/shard_map/ppermute | solution.py:290
  11.6 6.8 %collective-permute-start.6 = (bf16[32,1536]{1,0:T(8,128)(2,1)S(1)}, bf16[32,1536]{1,0:T(8,128)(2,1)S(1)}, u32[]{:S(2)}, u32[]{:S(2)}) collective-permute-start(bf16[32,1536]{1,0:T(8,128)(2,1)S(1)} %get-tuple-element.69.refs_3_), channel_id=1, source_target_pairs={{0,4},{4,0},{8,12},{12,8},{1,5},{5,1},{9,13},{13,9},{2,6},{6,2},{1... | collective-permute-start | bytes 294920 | tf_op jit(solution)/shard_map/ppermute | solution.py:290
  13.2 5.5 %collective-permute-start.12 = (bf16[32,1536]{1,0:T(8,128)(2,1)S(1)}, bf16[32,1536]{1,0:T(8,128)(2,1)S(1)}, u32[]{:S(2)}, u32[]{:S(2)}) collective-permute-start(bf16[32,1536]{1,0:T(8,128)(2,1)S(1)} %get-tuple-element.69.refs_3_), channel_id=1, source_target_pairs={{0,2},{1,3},{2,0},{3,1},{4,6},{5,7},{6,4},{7,5},{8,10},{9,11},{10,... | collective-permute-start | bytes 294920 | tf_op jit(solution)/shard_map/ppermute | solution.py:290
  14.3 6.6 %collective-permute-start.3 = (bf16[32,1536]{1,0:T(8,128)(2,1)S(1)}, bf16[32,1536]{1,0:T(8,128)(2,1)S(1)}, u32[]{:S(2)}, u32[]{:S(2)}) collective-permute-start(bf16[32,1536]{1,0:T(8,128)(2,1)S(1)} %get-tuple-element.69.refs_3_), channel_id=1, source_target_pairs={{0,12},{4,8},{8,4},{12,0},{1,13},{5,9},{9,5},{13,1},{2,14},{6,10},... | collective-permute-start | bytes 294920 | tf_op jit(solution)/shard_map/ppermute | solution.py:290
  17.0 4.8 %collective-permute-start.16 = (bf16[32,1536]{1,0:T(8,128)(2,1)S(1)}, bf16[32,1536]{1,0:T(8,128)(2,1)S(1)}, u32[]{:S(2)}, u32[]{:S(2)}) collective-permute-start(bf16[32,1536]{1,0:T(8,128)(2,1)S(1)} %collective-permute-done.9.refs_2_), channel_id=1, source_target_pairs={{0,1},{1,0},{2,3},{3,2},{4,5},{5,4},{6,7},{7,6},{8,9},{9,8},{10,11... | collective-permute-start | bytes 294920 | tf_op jit(solution)/shard_map/ppermute | solution.py:290
  17.0 5.6 %collective-permute-start.10 = (bf16[32,1536]{1,0:T(8,128)(2,1)S(1)}, bf16[32,1536]{1,0:T(8,128)(2,1)S(1)}, u32[]{:S(2)}, u32[]{:S(2)}) collective-permute-start(bf16[32,1536]{1,0:T(8,128)(2,1)S(1)} %collective-permute-done.9.refs_2_), channel_id=1, source_target_pairs={{0,2},{1,3},{2,0},{3,1},{4,6},{5,7},{6,4},{7,5},{8,10},{9,11},{10,... | collective-permute-start | bytes 294920 | tf_op jit(solution)/shard_map/ppermute | solution.py:290
  18.5 4.2 %collective-permute-start.15 = (bf16[32,1536]{1,0:T(8,128)(2,1)S(1)}, bf16[32,1536]{1,0:T(8,128)(2,1)S(1)}, u32[]{:S(2)}, u32[]{:S(2)}) collective-permute-start(bf16[32,1536]{1,0:T(8,128)(2,1)S(1)} %collective-permute-done.6.refs_1_), channel_id=1, source_target_pairs={{0,1},{1,0},{2,3},{3,2},{4,5},{5,4},{6,7},{7,6},{8,9},{9,8},{10,11... | collective-permute-start | bytes 294920 | tf_op jit(solution)/shard_map/ppermute | solution.py:290
  18.7 6.0 %collective-permute-start.7 = (bf16[32,1536]{1,0:T(8,128)(2,1)S(1)}, bf16[32,1536]{1,0:T(8,128)(2,1)S(1)}, u32[]{:S(2)}, u32[]{:S(2)}) collective-permute-start(bf16[32,1536]{1,0:T(8,128)(2,1)S(1)} %collective-permute-done.6.refs_1_), channel_id=1, source_target_pairs={{0,2},{1,3},{2,0},{3,1},{4,6},{5,7},{6,4},{7,5},{8,10},{9,11},{10,... | collective-permute-start | bytes 294920 | tf_op jit(solution)/shard_map/ppermute | solution.py:290
  20.8 5.6 %collective-permute-start.4 = (bf16[32,1536]{1,0:T(8,128)(2,1)S(1)}, bf16[32,1536]{1,0:T(8,128)(2,1)S(1)}, u32[]{:S(2)}, u32[]{:S(2)}) collective-permute-start(bf16[32,1536]{1,0:T(8,128)(2,1)S(1)} %collective-permute-done.3.refs_0_), channel_id=1, source_target_pairs={{0,2},{1,3},{2,0},{3,1},{4,6},{5,7},{6,4},{7,5},{8,10},{9,11},{10,... | collective-permute-start | bytes 294920 | tf_op jit(solution)/shard_map/ppermute | solution.py:290
  21.8 4.7 %collective-permute-start.14 = (bf16[32,1536]{1,0:T(8,128)(2,1)S(1)}, bf16[32,1536]{1,0:T(8,128)(2,1)S(1)}, u32[]{:S(2)}, u32[]{:S(2)}) collective-permute-start(bf16[32,1536]{1,0:T(8,128)(2,1)S(1)} %collective-permute-done.3.refs_0_), channel_id=1, source_target_pairs={{0,1},{1,0},{2,3},{3,2},{4,5},{5,4},{6,7},{7,6},{8,9},{9,8},{10,11... | collective-permute-start | bytes 294920 | tf_op jit(solution)/shard_map/ppermute | solution.py:290
  22.6 5.5 %collective-permute-start.13 = (bf16[32,1536]{1,0:T(8,128)(2,1)S(1)}, bf16[32,1536]{1,0:T(8,128)(2,1)S(1)}, u32[]{:S(2)}, u32[]{:S(2)}) collective-permute-start(bf16[32,1536]{1,0:T(8,128)(2,1)S(1)} %collective-permute-done.12.refs_11_), channel_id=1, source_target_pairs={{0,1},{1,0},{2,3},{3,2},{4,5},{5,4},{6,7},{7,6},{8,9},{9,8},{10,11... | collective-permute-start | bytes 294920 | tf_op jit(solution)/shard_map/ppermute | solution.py:290
  22.6 5.5 %collective-permute-start.11 = (bf16[32,1536]{1,0:T(8,128)(2,1)S(1)}, bf16[32,1536]{1,0:T(8,128)(2,1)S(1)}, u32[]{:S(2)}, u32[]{:S(2)}) collective-permute-start(bf16[32,1536]{1,0:T(8,128)(2,1)S(1)} %collective-permute-done.10.refs_10_), channel_id=1, source_target_pairs={{0,1},{1,0},{2,3},{3,2},{4,5},{5,4},{6,7},{7,6},{8,9},{9,8},{10,11... | collective-permute-start | bytes 294920 | tf_op jit(solution)/shard_map/ppermute | solution.py:290
  24.7 3.4 %collective-permute-start.8 = (bf16[32,1536]{1,0:T(8,128)(2,1)S(1)}, bf16[32,1536]{1,0:T(8,128)(2,1)S(1)}, u32[]{:S(2)}, u32[]{:S(2)}) collective-permute-start(bf16[32,1536]{1,0:T(8,128)(2,1)S(1)} %collective-permute-done.7.refs_9_), channel_id=1, source_target_pairs={{0,1},{1,0},{2,3},{3,2},{4,5},{5,4},{6,7},{7,6},{8,9},{9,8},{10,11... | collective-permute-start | bytes 294920 | tf_op jit(solution)/shard_map/ppermute | solution.py:290
  26.5 1.7 %collective-permute-start.5 = (bf16[32,1536]{1,0:T(8,128)(2,1)S(1)}, bf16[32,1536]{1,0:T(8,128)(2,1)S(1)}, u32[]{:S(2)}, u32[]{:S(2)}) collective-permute-start(bf16[32,1536]{1,0:T(8,128)(2,1)S(1)} %collective-permute-done.4.refs_8_), channel_id=1, source_target_pairs={{0,1},{1,0},{2,3},{3,2},{4,5},{5,4},{6,7},{7,6},{8,9},{9,8},{10,11... | collective-permute-start | bytes 294920 | tf_op jit(solution)/shard_map/ppermute | solution.py:290
  29.6 1.9 %collective-permute-start.18 = (bf16[128,1536]{1,0:T(8,128)(2,1)S(1)}, bf16[128,1536]{1,0:T(8,128)(2,1)S(1)}, u32[]{:S(2)}, u32[]{:S(2)}) collective-permute-start(bf16[128,1536]{1,0:T(8,128)(2,1)S(1)} %get-tuple-element.79), channel_id=1, source_target_pairs={{0,1},{1,0},{2,3},{3,2},{4,5},{5,4},{6,7},{7,6},{8,9},{9,8},{10,11... | collective-permute-start | bytes 1179656 | tf_op jit(solution)/shard_map/ppermute | solution.py:290
  31.6 5.1 %collective-permute-start.20 = (bf16[32,1536]{1,0:T(8,128)(2,1)S(1)}, bf16[32,1536]{1,0:T(8,128)(2,1)S(1)}, u32[]{:S(2)}, u32[]{:S(2)}) collective-permute-start(bf16[32,1536]{1,0:T(8,128)(2,1)S(1)} %get-tuple-element.94), channel_id=1, source_target_pairs={{0,4},{4,0},{8,12},{12,8},{1,5},{5,1},{9,13},{13,9},{2,6},{6,2},{1... | collective-permute-start | bytes 294920 | tf_op jit(solution)/shard_map/ppermute | solution.py:290
  32.3 12.9 %collective-permute-start.19 = (bf16[32,1664]{1,0:T(8,128)(2,1)S(1)}, bf16[32,1664]{1,0:T(8,128)(2,1)S(1)}, u32[]{:S(2)}, u32[]{:S(2)}) collective-permute-start(bf16[32,1664]{1,0:T(8,128)(2,1)S(1)} %get-tuple-element.81), channel_id=1, source_target_pairs={{0,16},{4,20},{8,24},{12,28},{16,0},{20,4},{24,8},{28,12},{1,17},{... | collective-permute-start | bytes 319496 | tf_op jit(solution)/shard_map/ppermute | solution.py:297
  36.7 8.5 %collective-permute-start.21 = (bf16[32,1536]{1,0:T(8,128)(2,1)S(1)}, bf16[32,1536]{1,0:T(8,128)(2,1)S(1)}, u32[]{:S(2)}, u32[]{:S(2)}) collective-permute-start(bf16[32,1536]{1,0:T(8,128)(2,1)S(1)} %get-tuple-element.100), channel_id=1, source_target_pairs={{0,24},{4,28},{8,16},{12,20},{16,8},{20,12},{24,0},{28,4},{1,25},{... | collective-permute-start | bytes 294920 | tf_op jit(solution)/shard_map/ppermute | solution.py:297
  40.2 6.1 %collective-permute-start.22 = (bf16[32,1536]{1,0:T(8,128)(2,1)S(1)}, bf16[32,1536]{1,0:T(8,128)(2,1)S(1)}, u32[]{:S(2)}, u32[]{:S(2)}) collective-permute-start(bf16[32,1536]{1,0:T(8,128)(2,1)S(1)} %get-tuple-element.104), channel_id=1, source_target_pairs={{0,20},{4,16},{8,28},{12,24},{16,4},{20,0},{24,12},{28,8},{1,21},{... | collective-permute-start | bytes 294920 | tf_op jit(solution)/shard_map/ppermute | solution.py:297
  46.6 4.0 %collective-permute-start.23 = (bf16[16,1536]{1,0:T(8,128)(2,1)S(1)}, bf16[16,1536]{1,0:T(8,128)(2,1)S(1)}, u32[]{:S(2)}, u32[]{:S(2)}) collective-permute-start(bf16[16,1536]{1,0:T(8,128)(2,1)S(1)} %get-tuple-element.106), channel_id=1, source_target_pairs={{0,1},{1,0},{2,3},{3,2},{4,5},{5,4},{6,7},{7,6},{8,9},{9,8},{10,11... | collective-permute-start | bytes 147464 | tf_op jit(solution)/shard_map/ppermute | solution.py:290
  46.7 4.2 %collective-permute-start.24 = (bf16[16,1536]{1,0:T(8,128)(2,1)S(1)}, bf16[16,1536]{1,0:T(8,128)(2,1)S(1)}, u32[]{:S(2)}, u32[]{:S(2)}) collective-permute-start(bf16[16,1536]{1,0:T(8,128)(2,1)S(1)} %get-tuple-element.107), channel_id=1, source_target_pairs={{0,2},{1,3},{2,0},{3,1},{4,6},{5,7},{6,4},{7,5},{8,10},{9,11},{10,... | collective-permute-start | bytes 147464 | tf_op jit(solution)/shard_map/ppermute | solution.py:290
  48.1 3.7 %collective-permute-start.25 = (bf16[16,1536]{1,0:T(8,128)(2,1)S(1)}, bf16[16,1536]{1,0:T(8,128)(2,1)S(1)}, u32[]{:S(2)}, u32[]{:S(2)}) collective-permute-start(bf16[16,1536]{1,0:T(8,128)(2,1)S(1)} %get-tuple-element.108), channel_id=1, source_target_pairs={{0,3},{1,2},{2,1},{3,0},{4,7},{5,6},{6,5},{7,4},{8,11},{9,10},{10,... | collective-permute-start | bytes 147464 | tf_op jit(solution)/shard_map/ppermute | solution.py:290

commit v7 on v6

--- a/solution.py
+++ b/solution.py
@@ -211,11 +211,18 @@
 
 
 def first_kernel(*refs):
-    weights, (x_ref, dz_ref, *sums) = refs[12:15], refs[15:]
-    for steps in range(3):
-        parts = add_quarter(steps, refs[4 * steps : 4 * steps + 4], x_ref, dz_ref, weights)
-        for out, part in zip(sums, parts):
-            out[...] = out[...] + part if steps else part
+    own, weights, (x_ref, dz_ref, *sums) = refs[:4], refs[4:7], refs[7:]
+    for out, part in zip(sums, add_quarter(0, own, x_ref, dz_ref, weights)):
+        out[...] = part
+
+
+def second_kernel(*refs):
+    core, chip, weights, olds = refs[:4], refs[4:8], refs[8:11], refs[13:16]
+    x_ref, dz_ref, *sums = refs[16:]
+    parts = add_quarter(1, core, x_ref, dz_ref, weights)
+    more = add_quarter(2, chip, x_ref, dz_ref, weights)
+    for out, old, part, other in zip(sums, olds, parts, more):
+        out[...] = old[...] + part + other
 
 
 def half_terms(other, gate_grad, up_grad, weights, half):
@@ -342,12 +349,23 @@
     diag = swap(slot_block, "dp", 3)
     near = swap(slot_block, "dp", 1)
     far = swap(slot_block, "dp", 2)
-    own = [diag, near, far, slot_block]
+    own = [far, diag, near, slot_block]
     chip = [swap(block, "et", 2) for block in own]
     core = [swap(block, "et", 1) for block in own]
+    wide, sums = [like((slots, width))] * 2, [like((slots, hidden), F32)] * 3
+    state = call(first_kernel, wide + sums, *own, *weights, vmem=32)
+    chip[0], state = lax.optimization_barrier((chip[0], state))
     both = [swap(block, "et", 1) for block in chip]
-    wide, sums = [like((slots, width))] * 2, [like((slots, hidden), F32)] * 3
-    state = call(first_kernel, wide + sums, *own, *core, *chip, *weights, vmem=32)
+    state = call(
+        second_kernel,
+        wide + sums,
+        *core,
+        *chip,
+        *weights,
+        *state,
+        vmem=32,
+        aliases={11 + i: i for i in range(5)},
+    )
     x, dz, act, gate_grad, up_grad, grads, away = call(
         third_kernel,
         wide + [like((slots, hidden))] * 3 + [like((2 * slots, hidden)), like((slots, half))],
@@ -366,7 +384,7 @@
         flops=4 * slots * hidden * half,
         vmem=32,
     )
-    to_last, to_near, to_far, home, first = call(
+    to_far, to_last, to_near, home, first = call(
         pair_kernel,
         [like((cap, half))] * 3 + [like((cap, half + FLAG)), like((8, 128), F32)],
         own_terms,

time: 52.6 us -> 53 us (level)
  waiting for transfers between devices: 14.3 us -> 15 us
    pallas_call x10 -> x11, Pallas kernels: 8.93 us -> 9.08 us  [call(): pl.pallas_call(kernel, out_shape=outs, in_specs=[space] * len(args), out_...]
  transfers between devices with their start and end apart: 26 -> 26, of which waited for: 12 -> 11; matrix products, arithmetic and copies ran while one was open for 12% -> 11% of each run, Pallas kernels for 10% -> 10%
where the time goes in v7:
time: 53 us; the launch traced here: 52.8 us
  starting transfers between devices  21.9 us (41%)
  waiting for transfers between devices  15 us (28%)
  Pallas kernels  9.08 us (17%)
  matrix products  6.07 us (11%)
  between operations  0.78 us (1%)
    ppermute x23, starting transfers between devices, swap(): return lax.ppermute(value, axis, spread(steps))  15.7 us
    ppermute x23, waiting for transfers between devices, swap(): return lax.ppermute(value, axis, spread(steps))  12.2 us
    pallas_call x11, Pallas kernels, call(): pl.pallas_call(kernel, out_shape=outs, in_specs=[space] * len(args), out_...  9.08 us
    ppermute x3, starting transfers between devices, hand(): return lax.ppermute(value, ('pipe', 'dp'), pairs)  6.18 us
    dot_general x3, matrix products, contract(): lax.dot_general(left, right, (((left_dim,), (right_dim,)), ((), ())), pre...  6.07 us
    ppermute x3, waiting for transfers between devices, hand(): return lax.ppermute(value, ('pipe', 'dp'), pairs)  2.84 us
  transfers between devices with their start and end apart: 26, of which 11 were waited for; matrix products, arithmetic and copies ran while one was open for 11% of the time, Pallas kernels for 10%

profile of v7, /device:TPU:0, one launch (start us, length us, event | category | flops | bytes accessed | tf_op | source)
XLA Modules:
  0.0 52.8 jit_solution(8634895757415956914)
XLA Ops:
  0.6 1.1 %shard_map.102 = (bf16[16,1664]{1,0:T(8,128)(2,1)S(1)}, bf16[16,1664]{1,0:T(8,128)(2,1)S(1)}, bf16[16,1664]{1,0:T(8,128)(2,1)S(1)}, bf16[16,1664]{1,0:T(8,128)(2,1)S(1)}) custom-call(bf16[16,3072]{1,0:T(8,128)(2,1)} %bitcast.27, bf16[16,3072]{1,0:T(8,128)(2,1)} %bitcast.28, s32[4,16]{1,0:T(4,128)} %bitcast.30, f32[4,16]{1,0:T(4,128)} %bitcast.31), custom_call_target="tpu_custom_call" | custom-call | bytes 410112 | tf_op jit(solution)/shard_map/pallas_call | solution.py:109
  1.7 0.5 collective-permute-start
  2.2 2.6 %collective-permute-start.1 = (bf16[16,1664]{1,0:T(8,128)(2,1)S(1)}, bf16[16,1664]{1,0:T(8,128)(2,1)S(1)}, u32[]{:S(2)}, u32[]{:S(2)}) collective-permute-start(bf16[16,1664]{1,0:T(8,128)(2,1)S(1)} %get-tuple-element.71), channel_id=1, source_target_pairs={{0,2},{1,3},{2,0},{3,1},{4,6},{5,7},{6,4},{7,5},{8,10},{9,11},{10,... | collective-permute-start | bytes 159752 | tf_op jit(solution)/shard_map/ppermute | solution.py:297
  4.8 0.1 collective-permute-start.2
  4.9 2.8 %shard_map.103 = (bf16[336,3072]{1,0:T(8,128)(2,1)S(1)}, bf16[336,3072]{1,0:T(8,128)(2,1)S(1)}, bf16[336,3072]{1,0:T(8,128)(2,1)S(1)}) custom-call(bf16[336,3072]{1,0:T(8,128)(2,1)} %bitcast.22, bf16[336,3072]{1,0:T(8,128)(2,1)} %bitcast.23, bf16[336,3072]{1,0:T(8,128)(2,1)} %bitcast.24), custom_call_target="tpu_custom_call" | custom-call | bytes 12386304 | tf_op jit(solution)/shard_map/pallas_call | solution.py:109
  7.7 0.0 collective-permute-done.refs_1_
  7.8 0.9 %collective-permute-done.2.refs_3_ = bf16[16,1664]{1,0:T(8,128)(2,1)S(1)} collective-permute-done((bf16[16,1664]{1,0:T(8,128)(2,1)S(1)}, bf16[16,1664]{1,0:T(8,128)(2,1)S(1)}, u32[]{:S(2)}, u32[]{:S(2)}) %collective-permute-start.2) | collective-permute-done | bytes 53280 | tf_op jit(solution)/shard_map/ppermute | solution.py:297
  8.6 0.3 shard_map.104
  9.0 2.7 %collective-permute-start.3 = (bf16[32,1536]{1,0:T(8,128)(2,1)S(1)}, bf16[32,1536]{1,0:T(8,128)(2,1)S(1)}, u32[]{:S(2)}, u32[]{:S(2)}) collective-permute-start(bf16[32,1536]{1,0:T(8,128)(2,1)S(1)} %get-tuple-element.80.refs_3_), channel_id=1, source_target_pairs={{0,8},{4,12},{8,0},{12,4},{1,9},{5,13},{9,1},{13,5},{2,10},{6,14},... | collective-permute-start | bytes 294920 | tf_op jit(solution)/shard_map/ppermute | solution.py:297
  11.6 1.6 %collective-permute-start.6 = (bf16[32,1536]{1,0:T(8,128)(2,1)S(1)}, bf16[32,1536]{1,0:T(8,128)(2,1)S(1)}, u32[]{:S(2)}, u32[]{:S(2)}) collective-permute-start(bf16[32,1536]{1,0:T(8,128)(2,1)S(1)} %get-tuple-element.80.refs_3_), channel_id=1, source_target_pairs={{0,4},{4,0},{8,12},{12,8},{1,5},{5,1},{9,13},{13,9},{2,6},{6,2},{1... | collective-permute-start | bytes 294920 | tf_op jit(solution)/shard_map/ppermute | solution.py:297
  13.2 0.2 collective-permute-start.5
  13.4 1.1 %collective-permute-start.12 = (bf16[32,1536]{1,0:T(8,128)(2,1)S(1)}, bf16[32,1536]{1,0:T(8,128)(2,1)S(1)}, u32[]{:S(2)}, u32[]{:S(2)}) collective-permute-start(bf16[32,1536]{1,0:T(8,128)(2,1)S(1)} %get-tuple-element.80.refs_3_), channel_id=1, source_target_pairs={{0,2},{1,3},{2,0},{3,1},{4,6},{5,7},{6,4},{7,5},{8,10},{9,11},{10,... | collective-permute-start | bytes 294920 | tf_op jit(solution)/shard_map/ppermute | solution.py:297
  14.5 3.6 %collective-permute-done.3.refs_0_ = bf16[32,1536]{1,0:T(8,128)(2,1)S(1)} collective-permute-done((bf16[32,1536]{1,0:T(8,128)(2,1)S(1)}, bf16[32,1536]{1,0:T(8,128)(2,1)S(1)}, u32[]{:S(2)}, u32[]{:S(2)}) %collective-permute-start.3) | collective-permute-done | bytes 98336 | tf_op jit(solution)/shard_map/ppermute | solution.py:297
  18.1 0.9 %collective-permute-start.4 = (bf16[32,1536]{1,0:T(8,128)(2,1)S(1)}, bf16[32,1536]{1,0:T(8,128)(2,1)S(1)}, u32[]{:S(2)}, u32[]{:S(2)}) collective-permute-start(bf16[32,1536]{1,0:T(8,128)(2,1)S(1)} %collective-permute-done.3.refs_0_), channel_id=1, source_target_pairs={{0,2},{1,3},{2,0},{3,1},{4,6},{5,7},{6,4},{7,5},{8,10},{9,11},{10,... | collective-permute-start | bytes 294920 | tf_op jit(solution)/shard_map/ppermute | solution.py:297
  19.0 1.1 %collective-permute-start.10 = (bf16[32,1536]{1,0:T(8,128)(2,1)S(1)}, bf16[32,1536]{1,0:T(8,128)(2,1)S(1)}, u32[]{:S(2)}, u32[]{:S(2)}) collective-permute-start(bf16[32,1536]{1,0:T(8,128)(2,1)S(1)} %collective-permute-done.6.refs_2_), channel_id=1, source_target_pairs={{0,2},{1,3},{2,0},{3,1},{4,6},{5,7},{6,4},{7,5},{8,10},{9,11},{10,... | collective-permute-start | bytes 294920 | tf_op jit(solution)/shard_map/ppermute | solution.py:297
  20.1 0.1 collective-permute-done.5.refs_1_
  20.2 1.2 %collective-permute-start.8 = (bf16[32,1536]{1,0:T(8,128)(2,1)S(1)}, bf16[32,1536]{1,0:T(8,128)(2,1)S(1)}, u32[]{:S(2)}, u32[]{:S(2)}) collective-permute-start(bf16[32,1536]{1,0:T(8,128)(2,1)S(1)} %collective-permute-done.5.refs_1_), channel_id=1, source_target_pairs={{0,2},{1,3},{2,0},{3,1},{4,6},{5,7},{6,4},{7,5},{8,10},{9,11},{10,... | collective-permute-start | bytes 294920 | tf_op jit(solution)/shard_map/ppermute | solution.py:297
  21.4 2.0 %collective-permute-done.4.refs_4_ = bf16[32,1536]{1,0:T(8,128)(2,1)S(1)} collective-permute-done((bf16[32,1536]{1,0:T(8,128)(2,1)S(1)}, bf16[32,1536]{1,0:T(8,128)(2,1)S(1)}, u32[]{:S(2)}, u32[]{:S(2)}) %collective-permute-start.4) | collective-permute-done | bytes 98336 | tf_op jit(solution)/shard_map/ppermute | solution.py:297
  23.4 0.6 %shard_map.105 = (bf16[128,3072]{1,0:T(8,128)(2,1)S(1)}, bf16[128,3072]{1,0:T(8,128)(2,1)S(1)}, f32[128,336]{1,0:T(8,128)S(1)}, f32[128,336]{1,0:T(8,128)S(1)}, f32[128,336]{1,0:T(8,128)S(1)}) custom-call(bf16[32,1536]{1,0:T(8,128)(2,1)S(1)} %collective-permute-done.3.refs_0_, bf16[32,1536]{1,0:T(8,128)(2,1)S(1)} %collective-permute-done.5.refs_1_, ...), custom_call_target="tpu_custom_call" | custom-call | tf_op jit(solution)/shard_map/pallas_call | solution.py:109
  24.1 0.6 %collective-permute-start.16 = (bf16[32,1536]{1,0:T(8,128)(2,1)S(1)}, bf16[32,1536]{1,0:T(8,128)(2,1)S(1)}, u32[]{:S(2)}, u32[]{:S(2)}) collective-permute-start(bf16[32,1536]{1,0:T(8,128)(2,1)S(1)} %collective-permute-done.6.refs_2_), channel_id=1, source_target_pairs={{0,1},{1,0},{2,3},{3,2},{4,5},{5,4},{6,7},{7,6},{8,9},{9,8},{10,11... | collective-permute-start | bytes 294920 | tf_op jit(solution)/shard_map/ppermute | solution.py:297
  24.6 0.9 %collective-permute-done.10.refs_6_ = bf16[32,1536]{1,0:T(8,128)(2,1)S(1)} collective-permute-done((bf16[32,1536]{1,0:T(8,128)(2,1)S(1)}, bf16[32,1536]{1,0:T(8,128)(2,1)S(1)}, u32[]{:S(2)}, u32[]{:S(2)}) %collective-permute-start.10) | collective-permute-done | bytes 98336 | tf_op jit(solution)/shard_map/ppermute | solution.py:297
  25.5 1.4 %collective-permute-done.8.refs_5_ = bf16[32,1536]{1,0:T(8,128)(2,1)S(1)} collective-permute-done((bf16[32,1536]{1,0:T(8,128)(2,1)S(1)}, bf16[32,1536]{1,0:T(8,128)(2,1)S(1)}, u32[]{:S(2)}, u32[]{:S(2)}) %collective-permute-start.8) | collective-permute-done | bytes 98336 | tf_op jit(solution)/shard_map/ppermute | solution.py:297
  26.9 0.5 collective-permute-start.11
  27.4 0.1 collective-permute-start.9
  27.5 1.2 %shard_map.106 = (bf16[128,3072]{1,0:T(8,128)(2,1)S(1)}, bf16[128,3072]{1,0:T(8,128)(2,1)S(1)}, f32[128,336]{1,0:T(8,128)S(1)}, f32[128,336]{1,0:T(8,128)S(1)}, f32[128,336]{1,0:T(8,128)S(1)}) custom-call(bf16[32,1536]{1,0:T(8,128)(2,1)S(1)} %collective-permute-done.14.refs_0_, ...), custom_call_target="tpu_custom_call", output_to_operand_aliasing={{0}: (11, {}), {1}: (12, {}), {2}: (13, {}), {3}: (14, {}),... | custom-call | tf_op jit(solution)/shard_map/pallas_call | solution.py:109
  28.7 0.0 collective-permute-done.9.refs_1_
  28.7 1.4 %shard_map.107 = (bf16[128,3072]{1,0:T(8,128)(2,1)S(1)}, bf16[128,3072]{1,0:T(8,128)(2,1)S(1)}, bf16[128,336]{1,0:T(8,128)(2,1)S(1)}, bf16[128,336]{1,0:T(8,128)...) custom-call(bf16[32,1536]{1,0:T(8,128)(2,1)S(1)} %collective-permute, ...), custom_call_target="tpu_custom_call", output_to_operand_aliasing={{0}: (7, {}), {1}: (8, {})} | custom-call | tf_op jit(solution)/shard_map/pallas_call | solution.py:109
  30.2 0.5 collective-permute-start.18
  30.7 0.6 %shard_map.108.own_ref = f32[128,1536]{1,0:T(8,128)S(1)} custom-call(bf16[256,336]{1,0:T(8,128)(2,1)S(1)} %get-tuple-element.100.grads_ref, bf16[336,3072]{1,0:T(8,128)(2,1)S(1)} %get-tuple-element.81.refs_4_.refs_8_.wg_ref, bf16[336,3072]{1,0:T(8,128)(2,1)S(1)} %get-tuple-element.82.refs_5_.refs_9_.wu_ref), custom_call_target="tpu_custom_call" | custom-call | flops 264241152 | bytes 5087232 | tf_op jit(solution)/shard_map/pallas_call | solution.py:109
  31.2 0.8 %collective-permute-done.18.other_ref = bf16[128,1536]{1,0:T(8,128)(2,1)S(1)} collective-permute-done((bf16[128,1536]{1,0:T(8,128)(2,1)S(1)}, bf16[128,1536]{1,0:T(8,128)(2,1)S(1)}, u32[]{:S(2)}, u32[]{:S(2)}) %collective-permute-start.18) | collective-permute-done | bytes 393248 | tf_op jit(solution)/shard_map/ppermute | solution.py:297
  32.0 0.1 shard_map.109
  32.1 0.2 collective-permute-start.20
  32.3 1.5 %collective-permute-start.19 = (bf16[32,1664]{1,0:T(8,128)(2,1)S(1)}, bf16[32,1664]{1,0:T(8,128)(2,1)S(1)}, u32[]{:S(2)}, u32[]{:S(2)}) collective-permute-start(bf16[32,1664]{1,0:T(8,128)(2,1)S(1)} %get-tuple-element.103), channel_id=1, source_target_pairs={{0,16},{4,20},{8,24},{12,28},{16,0},{20,4},{24,8},{28,12},{1,17},{... | collective-permute-start | bytes 319496 | tf_op jit(solution)/shard_map/ppermute | solution.py:304
  33.8 2.0 %convolution_convert_fusion.2 = bf16[336,3072]{1,0:T(8,128)(2,1)} fusion(bf16[128,336]{1,0:T(8,128)(2,1)S(1)} %get-tuple-element.112, bf16[128,3072]{1,0:T(8,128)(2,1)S(1)} %get-tuple-element.111), kind=kOutput, calls=%fused_computation.2 | convolution fusion | flops 265273344 | bytes 2936832 | tf_op jit(solution)/shard_map/dot_general | solution.py:40
  35.8 1.4 %collective-permute-done.20.right_ref = bf16[32,1536]{1,0:T(8,128)(2,1)S(1)} collective-permute-done((bf16[32,1536]{1,0:T(8,128)(2,1)S(1)}, bf16[32,1536]{1,0:T(8,128)(2,1)S(1)}, u32[]{:S(2)}, u32[]{:S(2)}) %collective-permute-start.20) | collective-permute-done | bytes 98336 | tf_op jit(solution)/shard_map/ppermute | solution.py:297
  37.2 3.0 %collective-permute-start.21 = (bf16[32,1536]{1,0:T(8,128)(2,1)S(1)}, bf16[32,1536]{1,0:T(8,128)(2,1)S(1)}, u32[]{:S(2)}, u32[]{:S(2)}) collective-permute-start(bf16[32,1536]{1,0:T(8,128)(2,1)S(1)} %get-tuple-element.122), channel_id=1, source_target_pairs={{0,24},{4,28},{8,16},{12,20},{16,8},{20,12},{24,0},{28,4},{1,25},{... | collective-permute-start | bytes 294920 | tf_op jit(solution)/shard_map/ppermute | solution.py:304
  40.2 1.7 %collective-permute-start.22 = (bf16[32,1536]{1,0:T(8,128)(2,1)S(1)}, bf16[32,1536]{1,0:T(8,128)(2,1)S(1)}, u32[]{:S(2)}, u32[]{:S(2)}) collective-permute-start(bf16[32,1536]{1,0:T(8,128)(2,1)S(1)} %get-tuple-element.126), channel_id=1, source_target_pairs={{0,20},{4,16},{8,28},{12,24},{16,4},{20,0},{24,12},{28,8},{1,21},{... | collective-permute-start | bytes 294920 | tf_op jit(solution)/shard_map/ppermute | solution.py:304
  41.9 2.0 %convolution_convert_fusion.1 = bf16[336,3072]{1,0:T(8,128)(2,1)} fusion(bf16[128,336]{1,0:T(8,128)(2,1)S(1)} %get-tuple-element.123, bf16[128,3072]{1,0:T(8,128)(2,1)S(1)} %get-tuple-element.124), kind=kOutput, calls=%fused_computation.1 | convolution fusion | flops 265273344 | bytes 2936832 | tf_op jit(solution)/shard_map/dot_general | solution.py:40
  44.0 1.5 %collective-permute-done.21.refs_0_ = bf16[32,1536]{1,0:T(8,128)(2,1)S(1)} collective-permute-done((bf16[32,1536]{1,0:T(8,128)(2,1)S(1)}, bf16[32,1536]{1,0:T(8,128)(2,1)S(1)}, u32[]{:S(2)}, u32[]{:S(2)}) %collective-permute-start.21) | collective-permute-done | bytes 98336 | tf_op jit(solution)/shard_map/ppermute | solution.py:304
  45.5 1.3 %collective-permute-done.22.refs_1_ = bf16[32,1536]{1,0:T(8,128)(2,1)S(1)} collective-permute-done((bf16[32,1536]{1,0:T(8,128)(2,1)S(1)}, bf16[32,1536]{1,0:T(8,128)(2,1)S(1)}, u32[]{:S(2)}, u32[]{:S(2)}) %collective-permute-start.22) | collective-permute-done | bytes 98336 | tf_op jit(solution)/shard_map/ppermute | solution.py:304
  46.8 0.3 shard_map.111
  47.1 0.1 collective-permute-start.23
  47.2 0.9 %collective-permute-start.24 = (bf16[16,1536]{1,0:T(8,128)(2,1)S(1)}, bf16[16,1536]{1,0:T(8,128)(2,1)S(1)}, u32[]{:S(2)}, u32[]{:S(2)}) collective-permute-start(bf16[16,1536]{1,0:T(8,128)(2,1)S(1)} %get-tuple-element.129), channel_id=1, source_target_pairs={{0,2},{1,3},{2,0},{3,1},{4,6},{5,7},{6,4},{7,5},{8,10},{9,11},{10,... | collective-permute-start | bytes 147464 | tf_op jit(solution)/shard_map/ppermute | solution.py:297
  48.1 0.9 %collective-permute-start.25 = (bf16[16,1536]{1,0:T(8,128)(2,1)S(1)}, bf16[16,1536]{1,0:T(8,128)(2,1)S(1)}, u32[]{:S(2)}, u32[]{:S(2)}) collective-permute-start(bf16[16,1536]{1,0:T(8,128)(2,1)S(1)} %get-tuple-element.130), channel_id=1, source_target_pairs={{0,3},{1,2},{2,1},{3,0},{4,7},{5,6},{6,5},{7,4},{8,11},{9,10},{10,... | collective-permute-start | bytes 147464 | tf_op jit(solution)/shard_map/ppermute | solution.py:297
  49.0 2.0 %fusion = bf16[1,336,3072]{2,1,0:T(8,128)(2,1)} fusion(bf16[128,336]{1,0:T(8,128)(2,1)S(1)} %get-tuple-element.132, bf16[128,3072]{1,0:T(8,128)(2,1)S(1)} %get-tuple-element.124), kind=kOutput, calls=%fused_computation.3 | convolution fusion | flops 265273344 | bytes 2936832 | tf_op jit(solution)/shard_map/dot_general | solution.py:40
  51.1 0.5 collective-permute-done.24.chip_ref
  51.6 0.6 %collective-permute-done.25.both_ref = bf16[16,1536]{1,0:T(8,128)(2,1)S(1)} collective-permute-done((bf16[16,1536]{1,0:T(8,128)(2,1)S(1)}, bf16[16,1536]{1,0:T(8,128)(2,1)S(1)}, u32[]{:S(2)}, u32[]{:S(2)}) %collective-permute-start.25) | collective-permute-done | bytes 49184 | tf_op jit(solution)/shard_map/ppermute | solution.py:297
  52.2 0.7 %shard_map.112 = bf16[16,3072]{1,0:T(8,128)(2,1)} custom-call(bf16[16,1536]{1,0:T(8,128)(2,1)S(1)} %get-tuple-element.127.own_ref, bf16[16,1536]{1,0:T(8,128)(2,1)S(1)} %collective-permute-done.23.core_ref, bf16[16,1536]{1,0:T(8,128)(2,1)S(1)} %collective-permute-done.24.chip_ref, bf16[16,1536]{1,0:T(8,128)(2,1)S(1)} %collective-permute-done.25.both_ref), custom_call_target="tpu_custom_call" | custom-call | tf_op jit(solution)/shard_map/pallas_call | solution.py:109
  (18 shorter events, 0.1 us)
Async XLA Ops:
  1.7 6.0 %collective-permute-start = (bf16[16,1664]{1,0:T(8,128)(2,1)S(1)}, bf16[16,1664]{1,0:T(8,128)(2,1)S(1)}, u32[]{:S(2)}, u32[]{:S(2)}) collective-permute-start(bf16[16,1664]{1,0:T(8,128)(2,1)S(1)} %get-tuple-element.70), channel_id=1, source_target_pairs={{0,1},{1,0},{2,3},{3,2},{4,5},{5,4},{6,7},{7,6},{8,9},{9,8},{10,11... | collective-permute-start | bytes 159752 | tf_op jit(solution)/shard_map/ppermute | solution.py:297
  2.2 5.5 %collective-permute-start.1 = (bf16[16,1664]{1,0:T(8,128)(2,1)S(1)}, bf16[16,1664]{1,0:T(8,128)(2,1)S(1)}, u32[]{:S(2)}, u32[]{:S(2)}) collective-permute-start(bf16[16,1664]{1,0:T(8,128)(2,1)S(1)} %get-tuple-element.71), channel_id=1, source_target_pairs={{0,2},{1,3},{2,0},{3,1},{4,6},{5,7},{6,4},{7,5},{8,10},{9,11},{10,... | collective-permute-start | bytes 159752 | tf_op jit(solution)/shard_map/ppermute | solution.py:297
  4.8 3.8 %collective-permute-start.2 = (bf16[16,1664]{1,0:T(8,128)(2,1)S(1)}, bf16[16,1664]{1,0:T(8,128)(2,1)S(1)}, u32[]{:S(2)}, u32[]{:S(2)}) collective-permute-start(bf16[16,1664]{1,0:T(8,128)(2,1)S(1)} %get-tuple-element.72), channel_id=1, source_target_pairs={{0,3},{1,2},{2,1},{3,0},{4,7},{5,6},{6,5},{7,4},{8,11},{9,10},{10,... | collective-permute-start | bytes 159752 | tf_op jit(solution)/shard_map/ppermute | solution.py:297
  9.0 9.1 %collective-permute-start.3 = (bf16[32,1536]{1,0:T(8,128)(2,1)S(1)}, bf16[32,1536]{1,0:T(8,128)(2,1)S(1)}, u32[]{:S(2)}, u32[]{:S(2)}) collective-permute-start(bf16[32,1536]{1,0:T(8,128)(2,1)S(1)} %get-tuple-element.80.refs_3_), channel_id=1, source_target_pairs={{0,8},{4,12},{8,0},{12,4},{1,9},{5,13},{9,1},{13,5},{2,10},{6,14},... | collective-permute-start | bytes 294920 | tf_op jit(solution)/shard_map/ppermute | solution.py:297
  11.6 7.4 %collective-permute-start.6 = (bf16[32,1536]{1,0:T(8,128)(2,1)S(1)}, bf16[32,1536]{1,0:T(8,128)(2,1)S(1)}, u32[]{:S(2)}, u32[]{:S(2)}) collective-permute-start(bf16[32,1536]{1,0:T(8,128)(2,1)S(1)} %get-tuple-element.80.refs_3_), channel_id=1, source_target_pairs={{0,4},{4,0},{8,12},{12,8},{1,5},{5,1},{9,13},{13,9},{2,6},{6,2},{1... | collective-permute-start | bytes 294920 | tf_op jit(solution)/shard_map/ppermute | solution.py:297
  13.2 7.0 %collective-permute-start.5 = (bf16[32,1536]{1,0:T(8,128)(2,1)S(1)}, bf16[32,1536]{1,0:T(8,128)(2,1)S(1)}, u32[]{:S(2)}, u32[]{:S(2)}) collective-permute-start(bf16[32,1536]{1,0:T(8,128)(2,1)S(1)} %get-tuple-element.80.refs_3_), channel_id=1, source_target_pairs={{0,12},{4,8},{8,4},{12,0},{1,13},{5,9},{9,5},{13,1},{2,14},{6,10},... | collective-permute-start | bytes 294920 | tf_op jit(solution)/shard_map/ppermute | solution.py:297
  13.4 7.9 %collective-permute-start.12 = (bf16[32,1536]{1,0:T(8,128)(2,1)S(1)}, bf16[32,1536]{1,0:T(8,128)(2,1)S(1)}, u32[]{:S(2)}, u32[]{:S(2)}) collective-permute-start(bf16[32,1536]{1,0:T(8,128)(2,1)S(1)} %get-tuple-element.80.refs_3_), channel_id=1, source_target_pairs={{0,2},{1,3},{2,0},{3,1},{4,6},{5,7},{6,4},{7,5},{8,10},{9,11},{10,... | collective-permute-start | bytes 294920 | tf_op jit(solution)/shard_map/ppermute | solution.py:297
  18.1 5.3 %collective-permute-start.4 = (bf16[32,1536]{1,0:T(8,128)(2,1)S(1)}, bf16[32,1536]{1,0:T(8,128)(2,1)S(1)}, u32[]{:S(2)}, u32[]{:S(2)}) collective-permute-start(bf16[32,1536]{1,0:T(8,128)(2,1)S(1)} %collective-permute-done.3.refs_0_), channel_id=1, source_target_pairs={{0,2},{1,3},{2,0},{3,1},{4,6},{5,7},{6,4},{7,5},{8,10},{9,11},{10,... | collective-permute-start | bytes 294920 | tf_op jit(solution)/shard_map/ppermute | solution.py:297
  19.0 5.1 %collective-permute-start.17 = (bf16[32,1536]{1,0:T(8,128)(2,1)S(1)}, bf16[32,1536]{1,0:T(8,128)(2,1)S(1)}, u32[]{:S(2)}, u32[]{:S(2)}) collective-permute-start(bf16[32,1536]{1,0:T(8,128)(2,1)S(1)} %get-tuple-element.80.refs_3_), channel_id=1, source_target_pairs={{0,1},{1,0},{2,3},{3,2},{4,5},{5,4},{6,7},{7,6},{8,9},{9,8},{10,11... | collective-permute-start | bytes 294920 | tf_op jit(solution)/shard_map/ppermute | solution.py:297
  19.0 6.5 %collective-permute-start.10 = (bf16[32,1536]{1,0:T(8,128)(2,1)S(1)}, bf16[32,1536]{1,0:T(8,128)(2,1)S(1)}, u32[]{:S(2)}, u32[]{:S(2)}) collective-permute-start(bf16[32,1536]{1,0:T(8,128)(2,1)S(1)} %collective-permute-done.6.refs_2_), channel_id=1, source_target_pairs={{0,2},{1,3},{2,0},{3,1},{4,6},{5,7},{6,4},{7,5},{8,10},{9,11},{10,... | collective-permute-start | bytes 294920 | tf_op jit(solution)/shard_map/ppermute | solution.py:297
  20.2 6.7 %collective-permute-start.8 = (bf16[32,1536]{1,0:T(8,128)(2,1)S(1)}, bf16[32,1536]{1,0:T(8,128)(2,1)S(1)}, u32[]{:S(2)}, u32[]{:S(2)}) collective-permute-start(bf16[32,1536]{1,0:T(8,128)(2,1)S(1)} %collective-permute-done.5.refs_1_), channel_id=1, source_target_pairs={{0,2},{1,3},{2,0},{3,1},{4,6},{5,7},{6,4},{7,5},{8,10},{9,11},{10,... | collective-permute-start | bytes 294920 | tf_op jit(solution)/shard_map/ppermute | solution.py:297
  21.4 5.6 %collective-permute-start.14 = (bf16[32,1536]{1,0:T(8,128)(2,1)S(1)}, bf16[32,1536]{1,0:T(8,128)(2,1)S(1)}, u32[]{:S(2)}, u32[]{:S(2)}) collective-permute-start(bf16[32,1536]{1,0:T(8,128)(2,1)S(1)} %collective-permute-done.3.refs_0_), channel_id=1, source_target_pairs={{0,1},{1,0},{2,3},{3,2},{4,5},{5,4},{6,7},{7,6},{8,9},{9,8},{10,11... | collective-permute-start | bytes 294920 | tf_op jit(solution)/shard_map/ppermute | solution.py:297
  23.4 4.0 %collective-permute-start.15 = (bf16[32,1536]{1,0:T(8,128)(2,1)S(1)}, bf16[32,1536]{1,0:T(8,128)(2,1)S(1)}, u32[]{:S(2)}, u32[]{:S(2)}) collective-permute-start(bf16[32,1536]{1,0:T(8,128)(2,1)S(1)} %collective-permute-done.5.refs_1_), channel_id=1, source_target_pairs={{0,1},{1,0},{2,3},{3,2},{4,5},{5,4},{6,7},{7,6},{8,9},{9,8},{10,11... | collective-permute-start | bytes 294920 | tf_op jit(solution)/shard_map/ppermute | solution.py:297
  24.1 3.4 %collective-permute-start.16 = (bf16[32,1536]{1,0:T(8,128)(2,1)S(1)}, bf16[32,1536]{1,0:T(8,128)(2,1)S(1)}, u32[]{:S(2)}, u32[]{:S(2)}) collective-permute-start(bf16[32,1536]{1,0:T(8,128)(2,1)S(1)} %collective-permute-done.6.refs_2_), channel_id=1, source_target_pairs={{0,1},{1,0},{2,3},{3,2},{4,5},{5,4},{6,7},{7,6},{8,9},{9,8},{10,11... | collective-permute-start | bytes 294920 | tf_op jit(solution)/shard_map/ppermute | solution.py:297
  25.5 3.2 %collective-permute-start.13 = (bf16[32,1536]{1,0:T(8,128)(2,1)S(1)}, bf16[32,1536]{1,0:T(8,128)(2,1)S(1)}, u32[]{:S(2)}, u32[]{:S(2)}) collective-permute-start(bf16[32,1536]{1,0:T(8,128)(2,1)S(1)} %collective-permute-done.12.refs_7_), channel_id=1, source_target_pairs={{0,1},{1,0},{2,3},{3,2},{4,5},{5,4},{6,7},{7,6},{8,9},{9,8},{10,11... | collective-permute-start | bytes 294920 | tf_op jit(solution)/shard_map/ppermute | solution.py:297
  26.9 1.8 %collective-permute-start.7 = (bf16[32,1536]{1,0:T(8,128)(2,1)S(1)}, bf16[32,1536]{1,0:T(8,128)(2,1)S(1)}, u32[]{:S(2)}, u32[]{:S(2)}) collective-permute-start(bf16[32,1536]{1,0:T(8,128)(2,1)S(1)} %collective-permute-done.4.refs_4_), channel_id=1, source_target_pairs={{0,1},{1,0},{2,3},{3,2},{4,5},{5,4},{6,7},{7,6},{8,9},{9,8},{10,11... | collective-permute-start | bytes 294920 | tf_op jit(solution)/shard_map/ppermute | solution.py:297
  26.9 1.8 %collective-permute-start.11 = (bf16[32,1536]{1,0:T(8,128)(2,1)S(1)}, bf16[32,1536]{1,0:T(8,128)(2,1)S(1)}, u32[]{:S(2)}, u32[]{:S(2)}) collective-permute-start(bf16[32,1536]{1,0:T(8,128)(2,1)S(1)} %collective-permute-done.10.refs_6_), channel_id=1, source_target_pairs={{0,1},{1,0},{2,3},{3,2},{4,5},{5,4},{6,7},{7,6},{8,9},{9,8},{10,11... | collective-permute-start | bytes 294920 | tf_op jit(solution)/shard_map/ppermute | solution.py:297
  27.4 1.3 %collective-permute-start.9 = (bf16[32,1536]{1,0:T(8,128)(2,1)S(1)}, bf16[32,1536]{1,0:T(8,128)(2,1)S(1)}, u32[]{:S(2)}, u32[]{:S(2)}) collective-permute-start(bf16[32,1536]{1,0:T(8,128)(2,1)S(1)} %collective-permute-done.8.refs_5_), channel_id=1, source_target_pairs={{0,1},{1,0},{2,3},{3,2},{4,5},{5,4},{6,7},{7,6},{8,9},{9,8},{10,11... | collective-permute-start | bytes 294920 | tf_op jit(solution)/shard_map/ppermute | solution.py:297
  30.2 1.8 %collective-permute-start.18 = (bf16[128,1536]{1,0:T(8,128)(2,1)S(1)}, bf16[128,1536]{1,0:T(8,128)(2,1)S(1)}, u32[]{:S(2)}, u32[]{:S(2)}) collective-permute-start(bf16[128,1536]{1,0:T(8,128)(2,1)S(1)} %get-tuple-element.101), channel_id=1, source_target_pairs={{0,1},{1,0},{2,3},{3,2},{4,5},{5,4},{6,7},{7,6},{8,9},{9,8},{10,11... | collective-permute-start | bytes 1179656 | tf_op jit(solution)/shard_map/ppermute | solution.py:297
  32.1 5.1 %collective-permute-start.20 = (bf16[32,1536]{1,0:T(8,128)(2,1)S(1)}, bf16[32,1536]{1,0:T(8,128)(2,1)S(1)}, u32[]{:S(2)}, u32[]{:S(2)}) collective-permute-start(bf16[32,1536]{1,0:T(8,128)(2,1)S(1)} %get-tuple-element.116), channel_id=1, source_target_pairs={{0,4},{4,0},{8,12},{12,8},{1,5},{5,1},{9,13},{13,9},{2,6},{6,2},{1... | collective-permute-start | bytes 294920 | tf_op jit(solution)/shard_map/ppermute | solution.py:297
  32.3 13.2 %collective-permute-start.19 = (bf16[32,1664]{1,0:T(8,128)(2,1)S(1)}, bf16[32,1664]{1,0:T(8,128)(2,1)S(1)}, u32[]{:S(2)}, u32[]{:S(2)}) collective-permute-start(bf16[32,1664]{1,0:T(8,128)(2,1)S(1)} %get-tuple-element.103), channel_id=1, source_target_pairs={{0,16},{4,20},{8,24},{12,28},{16,0},{20,4},{24,8},{28,12},{1,17},{... | collective-permute-start | bytes 319496 | tf_op jit(solution)/shard_map/ppermute | solution.py:304
  37.2 8.2 %collective-permute-start.21 = (bf16[32,1536]{1,0:T(8,128)(2,1)S(1)}, bf16[32,1536]{1,0:T(8,128)(2,1)S(1)}, u32[]{:S(2)}, u32[]{:S(2)}) collective-permute-start(bf16[32,1536]{1,0:T(8,128)(2,1)S(1)} %get-tuple-element.122), channel_id=1, source_target_pairs={{0,24},{4,28},{8,16},{12,20},{16,8},{20,12},{24,0},{28,4},{1,25},{... | collective-permute-start | bytes 294920 | tf_op jit(solution)/shard_map/ppermute | solution.py:304
  40.2 6.6 %collective-permute-start.22 = (bf16[32,1536]{1,0:T(8,128)(2,1)S(1)}, bf16[32,1536]{1,0:T(8,128)(2,1)S(1)}, u32[]{:S(2)}, u32[]{:S(2)}) collective-permute-start(bf16[32,1536]{1,0:T(8,128)(2,1)S(1)} %get-tuple-element.126), channel_id=1, source_target_pairs={{0,20},{4,16},{8,28},{12,24},{16,4},{20,0},{24,12},{28,8},{1,21},{... | collective-permute-start | bytes 294920 | tf_op jit(solution)/shard_map/ppermute | solution.py:304
  47.1 4.0 %collective-permute-start.23 = (bf16[16,1536]{1,0:T(8,128)(2,1)S(1)}, bf16[16,1536]{1,0:T(8,128)(2,1)S(1)}, u32[]{:S(2)}, u32[]{:S(2)}) collective-permute-start(bf16[16,1536]{1,0:T(8,128)(2,1)S(1)} %get-tuple-element.128), channel_id=1, source_target_pairs={{0,1},{1,0},{2,3},{3,2},{4,5},{5,4},{6,7},{7,6},{8,9},{9,8},{10,11... | collective-permute-start | bytes 147464 | tf_op jit(solution)/shard_map/ppermute | solution.py:297
  47.2 4.4 %collective-permute-start.24 = (bf16[16,1536]{1,0:T(8,128)(2,1)S(1)}, bf16[16,1536]{1,0:T(8,128)(2,1)S(1)}, u32[]{:S(2)}, u32[]{:S(2)}) collective-permute-start(bf16[16,1536]{1,0:T(8,128)(2,1)S(1)} %get-tuple-element.129), channel_id=1, source_target_pairs={{0,2},{1,3},{2,0},{3,1},{4,6},{5,7},{6,4},{7,5},{8,10},{9,11},{10,... | collective-permute-start | bytes 147464 | tf_op jit(solution)/shard_map/ppermute | solution.py:297
  48.1 4.0 %collective-permute-start.25 = (bf16[16,1536]{1,0:T(8,128)(2,1)S(1)}, bf16[16,1536]{1,0:T(8,128)(2,1)S(1)}, u32[]{:S(2)}, u32[]{:S(2)}) collective-permute-start(bf16[16,1536]{1,0:T(8,128)(2,1)S(1)} %get-tuple-element.130), channel_id=1, source_target_pairs={{0,3},{1,2},{2,1},{3,0},{4,7},{5,6},{6,5},{7,4},{8,11},{9,10},{10,... | collective-permute-start | bytes 147464 | tf_op jit(solution)/shard_map/ppermute | solution.py:297

commit v8 on v4

--- a/solution.py
+++ b/solution.py
@@ -257,9 +257,8 @@
     outs[3][:, half:] = pick_ref[...]
 
 
-def add_kernel(left_ref, right_ref, near_ref, out_ref, pass_ref, ready_ref):
+def add_kernel(left_ref, right_ref, out_ref, ready_ref):
     out_ref[...] = (left_ref[...].astype(F32) + right_ref[...].astype(F32)).astype(BF16)
-    pass_ref[...] = near_ref[...]
     ready_ref[...] = jnp.zeros_like(ready_ref)
 
 
@@ -373,12 +372,9 @@
     )
     from_last = swap(to_last, "dp", 1)
     home = hand(home, pipe_size, 0)
-    to_far, to_near, ready = call(
-        add_kernel,
-        [like((cap, half))] * 2 + [like((8, 128), F32)],
-        to_far,
-        from_last,
-        to_near,
+    from_near = hand(to_near, pipe_size, 1)
+    to_far, ready = call(
+        add_kernel, [like((cap, half)), like((8, 128), F32)], to_far, from_last
     )
     x, dz, act, gate_grad, up_grad, ready = lax.optimization_barrier(
         (x, dz, act, gate_grad, up_grad, ready)
@@ -386,7 +382,6 @@
     grad_gate = contract(gate_grad, x, 0, 0).astype(BF16)
     grad_up = contract(up_grad, x, 0, 0).astype(BF16)
     from_far = hand(to_far, pipe_size, 2)
-    from_near = hand(to_near, pipe_size, 1)
     from_far, grad_gate, grad_up = lax.optimization_barrier((from_far, grad_gate, grad_up))
     by_token = call(
         expand_kernel,

time: 52.6 us -> 51.3 us (0.975)
  waiting for transfers between devices: 14.3 us -> 13.6 us
    ppermute x23, waiting for transfers between devices: 14 us -> 13.1 us  [swap(): return lax.ppermute(value, axis, spread(steps))]
    ppermute x3, starting transfers between devices: 6.7 us -> 6.13 us  [hand(): return lax.ppermute(value, ('pipe', 'dp'), pairs)]
where the time goes in v8:
time: 51.3 us; the launch traced here: 51.2 us
  starting transfers between devices  21.8 us (42%)
  waiting for transfers between devices  13.6 us (27%)
  Pallas kernels  8.94 us (17%)
  matrix products  6.07 us (12%)
  between operations  0.77 us (2%)
    ppermute x23, starting transfers between devices, swap(): return lax.ppermute(value, axis, spread(steps))  15.6 us
    ppermute x23, waiting for transfers between devices, swap(): return lax.ppermute(value, axis, spread(steps))  13.1 us
    pallas_call x10, Pallas kernels, call(): pl.pallas_call(kernel, out_shape=outs, in_specs=[space] * len(args), out_...  8.94 us
    ppermute x3, starting transfers between devices, hand(): return lax.ppermute(value, ('pipe', 'dp'), pairs)  6.13 us
    dot_general x3, matrix products, contract(): lax.dot_general(left, right, (((left_dim,), (right_dim,)), ((), ())), pre...  6.07 us
  transfers between devices with their start and end apart: 26, of which 11 were waited for; matrix products, arithmetic and copies ran while one was open for 12% of the time, Pallas kernels for 10%

profile of v8, /device:TPU:0, one launch (start us, length us, event | category | flops | bytes accessed | tf_op | source)
XLA Modules:
  0.0 51.2 jit_solution(4277878628275281722)
XLA Ops:
  0.6 1.1 %shard_map.102 = (bf16[16,1664]{1,0:T(8,128)(2,1)S(1)}, bf16[16,1664]{1,0:T(8,128)(2,1)S(1)}, bf16[16,1664]{1,0:T(8,128)(2,1)S(1)}, bf16[16,1664]{1,0:T(8,128)(2,1)S(1)}) custom-call(bf16[16,3072]{1,0:T(8,128)(2,1)} %bitcast.27, bf16[16,3072]{1,0:T(8,128)(2,1)} %bitcast.28, s32[4,16]{1,0:T(4,128)} %bitcast.30, f32[4,16]{1,0:T(4,128)} %bitcast.31), custom_call_target="tpu_custom_call" | custom-call | bytes 410112 | tf_op jit(solution)/shard_map/pallas_call | solution.py:109
  1.7 0.5 %collective-permute-start = (bf16[16,1664]{1,0:T(8,128)(2,1)S(1)}, bf16[16,1664]{1,0:T(8,128)(2,1)S(1)}, u32[]{:S(2)}, u32[]{:S(2)}) collective-permute-start(bf16[16,1664]{1,0:T(8,128)(2,1)S(1)} %get-tuple-element.52), channel_id=1, source_target_pairs={{0,1},{1,0},{2,3},{3,2},{4,5},{5,4},{6,7},{7,6},{8,9},{9,8},{10,11... | collective-permute-start | bytes 159752 | tf_op jit(solution)/shard_map/ppermute | solution.py:287
  2.2 2.6 %collective-permute-start.1 = (bf16[16,1664]{1,0:T(8,128)(2,1)S(1)}, bf16[16,1664]{1,0:T(8,128)(2,1)S(1)}, u32[]{:S(2)}, u32[]{:S(2)}) collective-permute-start(bf16[16,1664]{1,0:T(8,128)(2,1)S(1)} %get-tuple-element.53), channel_id=1, source_target_pairs={{0,2},{1,3},{2,0},{3,1},{4,6},{5,7},{6,4},{7,5},{8,10},{9,11},{10,... | collective-permute-start | bytes 159752 | tf_op jit(solution)/shard_map/ppermute | solution.py:287
  4.8 0.1 collective-permute-start.2
  4.9 2.8 %shard_map.103 = (bf16[336,3072]{1,0:T(8,128)(2,1)S(1)}, bf16[336,3072]{1,0:T(8,128)(2,1)S(1)}, bf16[336,3072]{1,0:T(8,128)(2,1)S(1)}) custom-call(bf16[336,3072]{1,0:T(8,128)(2,1)} %bitcast.22, bf16[336,3072]{1,0:T(8,128)(2,1)} %bitcast.23, bf16[336,3072]{1,0:T(8,128)(2,1)} %bitcast.24), custom_call_target="tpu_custom_call" | custom-call | bytes 12386304 | tf_op jit(solution)/shard_map/pallas_call | solution.py:109
  7.8 0.9 %collective-permute-done.2.refs_3_ = bf16[16,1664]{1,0:T(8,128)(2,1)S(1)} collective-permute-done((bf16[16,1664]{1,0:T(8,128)(2,1)S(1)}, bf16[16,1664]{1,0:T(8,128)(2,1)S(1)}, u32[]{:S(2)}, u32[]{:S(2)}) %collective-permute-start.2) | collective-permute-done | bytes 53280 | tf_op jit(solution)/shard_map/ppermute | solution.py:287
  8.6 0.3 shard_map.104
  9.0 2.7 %collective-permute-start.9 = (bf16[32,1536]{1,0:T(8,128)(2,1)S(1)}, bf16[32,1536]{1,0:T(8,128)(2,1)S(1)}, u32[]{:S(2)}, u32[]{:S(2)}) collective-permute-start(bf16[32,1536]{1,0:T(8,128)(2,1)S(1)} %get-tuple-element.62.refs_3_), channel_id=1, source_target_pairs={{0,8},{4,12},{8,0},{12,4},{1,9},{5,13},{9,1},{13,5},{2,10},{6,14},... | collective-permute-start | bytes 294920 | tf_op jit(solution)/shard_map/ppermute | solution.py:287
  11.6 1.6 %collective-permute-start.6 = (bf16[32,1536]{1,0:T(8,128)(2,1)S(1)}, bf16[32,1536]{1,0:T(8,128)(2,1)S(1)}, u32[]{:S(2)}, u32[]{:S(2)}) collective-permute-start(bf16[32,1536]{1,0:T(8,128)(2,1)S(1)} %get-tuple-element.62.refs_3_), channel_id=1, source_target_pairs={{0,4},{4,0},{8,12},{12,8},{1,5},{5,1},{9,13},{13,9},{2,6},{6,2},{1... | collective-permute-start | bytes 294920 | tf_op jit(solution)/shard_map/ppermute | solution.py:287
  13.2 1.1 %collective-permute-start.12 = (bf16[32,1536]{1,0:T(8,128)(2,1)S(1)}, bf16[32,1536]{1,0:T(8,128)(2,1)S(1)}, u32[]{:S(2)}, u32[]{:S(2)}) collective-permute-start(bf16[32,1536]{1,0:T(8,128)(2,1)S(1)} %get-tuple-element.62.refs_3_), channel_id=1, source_target_pairs={{0,2},{1,3},{2,0},{3,1},{4,6},{5,7},{6,4},{7,5},{8,10},{9,11},{10,... | collective-permute-start | bytes 294920 | tf_op jit(solution)/shard_map/ppermute | solution.py:287
  14.3 0.2 collective-permute-start.3
  14.5 2.5 %collective-permute-done.9.refs_2_ = bf16[32,1536]{1,0:T(8,128)(2,1)S(1)} collective-permute-done((bf16[32,1536]{1,0:T(8,128)(2,1)S(1)}, bf16[32,1536]{1,0:T(8,128)(2,1)S(1)}, u32[]{:S(2)}, u32[]{:S(2)}) %collective-permute-start.9) | collective-permute-done | bytes 98336 | tf_op jit(solution)/shard_map/ppermute | solution.py:287
  17.0 0.0 collective-permute-start.16
  17.0 0.0 collective-permute-done.17.refs_7_
  17.0 1.4 %collective-permute-start.10 = (bf16[32,1536]{1,0:T(8,128)(2,1)S(1)}, bf16[32,1536]{1,0:T(8,128)(2,1)S(1)}, u32[]{:S(2)}, u32[]{:S(2)}) collective-permute-start(bf16[32,1536]{1,0:T(8,128)(2,1)S(1)} %collective-permute-done.9.refs_2_), channel_id=1, source_target_pairs={{0,2},{1,3},{2,0},{3,1},{4,6},{5,7},{6,4},{7,5},{8,10},{9,11},{10,... | collective-permute-start | bytes 294920 | tf_op jit(solution)/shard_map/ppermute | solution.py:287
  18.5 0.0 collective-permute-done.6.refs_1_
  18.5 0.2 collective-permute-start.15
  18.7 0.6 %collective-permute-start.7 = (bf16[32,1536]{1,0:T(8,128)(2,1)S(1)}, bf16[32,1536]{1,0:T(8,128)(2,1)S(1)}, u32[]{:S(2)}, u32[]{:S(2)}) collective-permute-start(bf16[32,1536]{1,0:T(8,128)(2,1)S(1)} %collective-permute-done.6.refs_1_), channel_id=1, source_target_pairs={{0,2},{1,3},{2,0},{3,1},{4,6},{5,7},{6,4},{7,5},{8,10},{9,11},{10,... | collective-permute-start | bytes 294920 | tf_op jit(solution)/shard_map/ppermute | solution.py:287
  19.3 1.5 %collective-permute-done.3.refs_0_ = bf16[32,1536]{1,0:T(8,128)(2,1)S(1)} collective-permute-done((bf16[32,1536]{1,0:T(8,128)(2,1)S(1)}, bf16[32,1536]{1,0:T(8,128)(2,1)S(1)}, u32[]{:S(2)}, u32[]{:S(2)}) %collective-permute-start.3) | collective-permute-done | bytes 98336 | tf_op jit(solution)/shard_map/ppermute | solution.py:287
  20.8 0.9 %collective-permute-start.4 = (bf16[32,1536]{1,0:T(8,128)(2,1)S(1)}, bf16[32,1536]{1,0:T(8,128)(2,1)S(1)}, u32[]{:S(2)}, u32[]{:S(2)}) collective-permute-start(bf16[32,1536]{1,0:T(8,128)(2,1)S(1)} %collective-permute-done.3.refs_0_), channel_id=1, source_target_pairs={{0,2},{1,3},{2,0},{3,1},{4,6},{5,7},{6,4},{7,5},{8,10},{9,11},{10,... | collective-permute-start | bytes 294920 | tf_op jit(solution)/shard_map/ppermute | solution.py:287
  21.8 0.0 collective-permute-start.14
  21.8 0.8 %collective-permute-done.10.refs_10_ = bf16[32,1536]{1,0:T(8,128)(2,1)S(1)} collective-permute-done((bf16[32,1536]{1,0:T(8,128)(2,1)S(1)}, bf16[32,1536]{1,0:T(8,128)(2,1)S(1)}, u32[]{:S(2)}, u32[]{:S(2)}) %collective-permute-start.10) | collective-permute-done | bytes 98336 | tf_op jit(solution)/shard_map/ppermute | solution.py:287
  22.6 0.0 collective-permute-done.15.refs_5_
  22.6 0.5 collective-permute-start.11
  23.2 1.6 %collective-permute-done.7.refs_9_ = bf16[32,1536]{1,0:T(8,128)(2,1)S(1)} collective-permute-done((bf16[32,1536]{1,0:T(8,128)(2,1)S(1)}, bf16[32,1536]{1,0:T(8,128)(2,1)S(1)}, u32[]{:S(2)}, u32[]{:S(2)}) %collective-permute-start.7) | collective-permute-done | bytes 98336 | tf_op jit(solution)/shard_map/ppermute | solution.py:287
  24.7 1.7 %collective-permute-done.4.refs_8_ = bf16[32,1536]{1,0:T(8,128)(2,1)S(1)} collective-permute-done((bf16[32,1536]{1,0:T(8,128)(2,1)S(1)}, bf16[32,1536]{1,0:T(8,128)(2,1)S(1)}, u32[]{:S(2)}, u32[]{:S(2)}) %collective-permute-start.4) | collective-permute-done | bytes 98336 | tf_op jit(solution)/shard_map/ppermute | solution.py:287
  26.5 1.6 %shard_map.105 = (bf16[128,3072]{1,0:T(8,128)(2,1)S(1)}, bf16[128,3072]{1,0:T(8,128)(2,1)S(1)}, f32[128,336]{1,0:T(8,128)S(1)}, f32[128,336]{1,0:T(8,128)S(1)}, f32[128,336]{1,0:T(8,128)S(1)}) custom-call(bf16[32,1536]{1,0:T(8,128)(2,1)S(1)} %collective-permute-done.3.refs_0_, bf16[32,1536]{1,0:T(8,128)(2,1)S(1)} %collective-permute-done.6.refs_1_, ...), custom_call_target="tpu_custom_call" | custom-call | tf_op jit(solution)/shard_map/pallas_call | solution.py:109
  28.1 1.4 %shard_map.106 = (bf16[128,3072]{1,0:T(8,128)(2,1)S(1)}, bf16[128,3072]{1,0:T(8,128)(2,1)S(1)}, bf16[128,336]{1,0:T(8,128)(2,1)S(1)}, bf16[128,336]{1,0:T(8,128)...) custom-call(bf16[32,1536]{1,0:T(8,128)(2,1)S(1)} %collective-permute, ...), custom_call_target="tpu_custom_call", output_to_operand_aliasing={{0}: (7, {}), {1}: (8, {})} | custom-call | tf_op jit(solution)/shard_map/pallas_call | solution.py:109
  29.6 0.6 %collective-permute-start.18 = (bf16[128,1536]{1,0:T(8,128)(2,1)S(1)}, bf16[128,1536]{1,0:T(8,128)(2,1)S(1)}, u32[]{:S(2)}, u32[]{:S(2)}) collective-permute-start(bf16[128,1536]{1,0:T(8,128)(2,1)S(1)} %get-tuple-element.72), channel_id=1, source_target_pairs={{0,1},{1,0},{2,3},{3,2},{4,5},{5,4},{6,7},{7,6},{8,9},{9,8},{10,11... | collective-permute-start | bytes 1179656 | tf_op jit(solution)/shard_map/ppermute | solution.py:287
  30.1 0.6 %shard_map.107.own_ref = f32[128,1536]{1,0:T(8,128)S(1)} custom-call(bf16[256,336]{1,0:T(8,128)(2,1)S(1)} %get-tuple-element.71.grads_ref, bf16[336,3072]{1,0:T(8,128)(2,1)S(1)} %get-tuple-element.63.refs_12_.refs_4_.wg_ref, bf16[336,3072]{1,0:T(8,128)(2,1)S(1)} %get-tuple-element.64.refs_13_.refs_5_.wu_ref), custom_call_target="tpu_custom_call" | custom-call | flops 264241152 | bytes 5087232 | tf_op jit(solution)/shard_map/pallas_call | solution.py:109
  30.7 0.8 %collective-permute-done.18.other_ref = bf16[128,1536]{1,0:T(8,128)(2,1)S(1)} collective-permute-done((bf16[128,1536]{1,0:T(8,128)(2,1)S(1)}, bf16[128,1536]{1,0:T(8,128)(2,1)S(1)}, u32[]{:S(2)}, u32[]{:S(2)}) %collective-permute-start.18) | collective-permute-done | bytes 393248 | tf_op jit(solution)/shard_map/ppermute | solution.py:287
  31.5 0.1 shard_map.108
  31.6 0.7 %collective-permute-start.20 = (bf16[32,1536]{1,0:T(8,128)(2,1)S(1)}, bf16[32,1536]{1,0:T(8,128)(2,1)S(1)}, u32[]{:S(2)}, u32[]{:S(2)}) collective-permute-start(bf16[32,1536]{1,0:T(8,128)(2,1)S(1)} %get-tuple-element.81), channel_id=1, source_target_pairs={{0,4},{4,0},{8,12},{12,8},{1,5},{5,1},{9,13},{13,9},{2,6},{6,2},{1... | collective-permute-start | bytes 294920 | tf_op jit(solution)/shard_map/ppermute | solution.py:287
  32.3 2.3 %collective-permute-start.22 = (bf16[32,1536]{1,0:T(8,128)(2,1)S(1)}, bf16[32,1536]{1,0:T(8,128)(2,1)S(1)}, u32[]{:S(2)}, u32[]{:S(2)}) collective-permute-start(bf16[32,1536]{1,0:T(8,128)(2,1)S(1)} %get-tuple-element.89), channel_id=1, source_target_pairs={{0,20},{4,16},{8,28},{12,24},{16,4},{20,0},{24,12},{28,8},{1,21},{... | collective-permute-start | bytes 294920 | tf_op jit(solution)/shard_map/ppermute | solution.py:294
  34.6 0.5 %collective-permute-start.19 = (bf16[32,1664]{1,0:T(8,128)(2,1)S(1)}, bf16[32,1664]{1,0:T(8,128)(2,1)S(1)}, u32[]{:S(2)}, u32[]{:S(2)}) collective-permute-start(bf16[32,1664]{1,0:T(8,128)(2,1)S(1)} %get-tuple-element.74), channel_id=1, source_target_pairs={{0,16},{4,20},{8,24},{12,28},{16,0},{20,4},{24,8},{28,12},{1,17},{... | collective-permute-start | bytes 319496 | tf_op jit(solution)/shard_map/ppermute | solution.py:294
  35.1 2.1 %collective-permute-done.20.right_ref = bf16[32,1536]{1,0:T(8,128)(2,1)S(1)} collective-permute-done((bf16[32,1536]{1,0:T(8,128)(2,1)S(1)}, bf16[32,1536]{1,0:T(8,128)(2,1)S(1)}, u32[]{:S(2)}, u32[]{:S(2)}) %collective-permute-start.20) | collective-permute-done | bytes 98336 | tf_op jit(solution)/shard_map/ppermute | solution.py:287
  37.3 3.3 %collective-permute-start.21 = (bf16[32,1536]{1,0:T(8,128)(2,1)S(1)}, bf16[32,1536]{1,0:T(8,128)(2,1)S(1)}, u32[]{:S(2)}, u32[]{:S(2)}) collective-permute-start(bf16[32,1536]{1,0:T(8,128)(2,1)S(1)} %get-tuple-element.84), channel_id=1, source_target_pairs={{0,24},{4,28},{8,16},{12,20},{16,8},{20,12},{24,0},{28,4},{1,25},{... | collective-permute-start | bytes 294920 | tf_op jit(solution)/shard_map/ppermute | solution.py:294
  40.5 2.0 %convolution_convert_fusion.2 = bf16[336,3072]{1,0:T(8,128)(2,1)} fusion(bf16[128,336]{1,0:T(8,128)(2,1)S(1)} %get-tuple-element.85, bf16[128,3072]{1,0:T(8,128)(2,1)S(1)} %get-tuple-element.86), kind=kOutput, calls=%fused_computation.2 | convolution fusion | flops 265273344 | bytes 2936832 | tf_op jit(solution)/shard_map/dot_general | solution.py:40
  42.6 2.0 %convolution_convert_fusion.1 = bf16[336,3072]{1,0:T(8,128)(2,1)} fusion(bf16[128,336]{1,0:T(8,128)(2,1)S(1)} %get-tuple-element.87, bf16[128,3072]{1,0:T(8,128)(2,1)S(1)} %get-tuple-element.86), kind=kOutput, calls=%fused_computation.1 | convolution fusion | flops 265273344 | bytes 2936832 | tf_op jit(solution)/shard_map/dot_general | solution.py:40
  44.6 0.5 collective-permute-done.21.refs_0_
  45.1 0.3 shard_map.110
  45.4 0.1 collective-permute-start.23
  45.5 1.3 %collective-permute-start.24 = (bf16[16,1536]{1,0:T(8,128)(2,1)S(1)}, bf16[16,1536]{1,0:T(8,128)(2,1)S(1)}, u32[]{:S(2)}, u32[]{:S(2)}) collective-permute-start(bf16[16,1536]{1,0:T(8,128)(2,1)S(1)} %get-tuple-element.92), channel_id=1, source_target_pairs={{0,2},{1,3},{2,0},{3,1},{4,6},{5,7},{6,4},{7,5},{8,10},{9,11},{10,... | collective-permute-start | bytes 147464 | tf_op jit(solution)/shard_map/ppermute | solution.py:287
  46.8 0.5 %collective-permute-start.25 = (bf16[16,1536]{1,0:T(8,128)(2,1)S(1)}, bf16[16,1536]{1,0:T(8,128)(2,1)S(1)}, u32[]{:S(2)}, u32[]{:S(2)}) collective-permute-start(bf16[16,1536]{1,0:T(8,128)(2,1)S(1)} %get-tuple-element.93), channel_id=1, source_target_pairs={{0,3},{1,2},{2,1},{3,0},{4,7},{5,6},{6,5},{7,4},{8,11},{9,10},{10,... | collective-permute-start | bytes 147464 | tf_op jit(solution)/shard_map/ppermute | solution.py:287
  47.4 2.0 %fusion = bf16[1,336,3072]{2,1,0:T(8,128)(2,1)} fusion(bf16[128,336]{1,0:T(8,128)(2,1)S(1)} %get-tuple-element.96, bf16[128,3072]{1,0:T(8,128)(2,1)S(1)} %get-tuple-element.97), kind=kOutput, calls=%fused_computation.3 | convolution fusion | flops 265273344 | bytes 2936832 | tf_op jit(solution)/shard_map/dot_general | solution.py:40
  49.4 0.3 collective-permute-done.24.chip_ref
  49.6 0.9 %collective-permute-done.25.both_ref = bf16[16,1536]{1,0:T(8,128)(2,1)S(1)} collective-permute-done((bf16[16,1536]{1,0:T(8,128)(2,1)S(1)}, bf16[16,1536]{1,0:T(8,128)(2,1)S(1)}, u32[]{:S(2)}, u32[]{:S(2)}) %collective-permute-start.25) | collective-permute-done | bytes 49184 | tf_op jit(solution)/shard_map/ppermute | solution.py:287
  50.5 0.7 %shard_map.111 = bf16[16,3072]{1,0:T(8,128)(2,1)} custom-call(bf16[16,1536]{1,0:T(8,128)(2,1)S(1)} %get-tuple-element.90.own_ref, bf16[16,1536]{1,0:T(8,128)(2,1)S(1)} %collective-permute-done.23.core_ref, bf16[16,1536]{1,0:T(8,128)(2,1)S(1)} %collective-permute-done.24.chip_ref, bf16[16,1536]{1,0:T(8,128)(2,1)S(1)} %collective-permute-done.25.both_ref), custom_call_target="tpu_custom_call" | custom-call | tf_op jit(solution)/shard_map/pallas_call | solution.py:109
  (17 shorter events, 0.1 us)
Async XLA Ops:
  1.7 6.0 %collective-permute-start = (bf16[16,1664]{1,0:T(8,128)(2,1)S(1)}, bf16[16,1664]{1,0:T(8,128)(2,1)S(1)}, u32[]{:S(2)}, u32[]{:S(2)}) collective-permute-start(bf16[16,1664]{1,0:T(8,128)(2,1)S(1)} %get-tuple-element.52), channel_id=1, source_target_pairs={{0,1},{1,0},{2,3},{3,2},{4,5},{5,4},{6,7},{7,6},{8,9},{9,8},{10,11... | collective-permute-start | bytes 159752 | tf_op jit(solution)/shard_map/ppermute | solution.py:287
  2.2 5.5 %collective-permute-start.1 = (bf16[16,1664]{1,0:T(8,128)(2,1)S(1)}, bf16[16,1664]{1,0:T(8,128)(2,1)S(1)}, u32[]{:S(2)}, u32[]{:S(2)}) collective-permute-start(bf16[16,1664]{1,0:T(8,128)(2,1)S(1)} %get-tuple-element.53), channel_id=1, source_target_pairs={{0,2},{1,3},{2,0},{3,1},{4,6},{5,7},{6,4},{7,5},{8,10},{9,11},{10,... | collective-permute-start | bytes 159752 | tf_op jit(solution)/shard_map/ppermute | solution.py:287
  4.8 3.8 %collective-permute-start.2 = (bf16[16,1664]{1,0:T(8,128)(2,1)S(1)}, bf16[16,1664]{1,0:T(8,128)(2,1)S(1)}, u32[]{:S(2)}, u32[]{:S(2)}) collective-permute-start(bf16[16,1664]{1,0:T(8,128)(2,1)S(1)} %get-tuple-element.54), channel_id=1, source_target_pairs={{0,3},{1,2},{2,1},{3,0},{4,7},{5,6},{6,5},{7,4},{8,11},{9,10},{10,... | collective-permute-start | bytes 159752 | tf_op jit(solution)/shard_map/ppermute | solution.py:287
  9.0 8.1 %collective-permute-start.9 = (bf16[32,1536]{1,0:T(8,128)(2,1)S(1)}, bf16[32,1536]{1,0:T(8,128)(2,1)S(1)}, u32[]{:S(2)}, u32[]{:S(2)}) collective-permute-start(bf16[32,1536]{1,0:T(8,128)(2,1)S(1)} %get-tuple-element.62.refs_3_), channel_id=1, source_target_pairs={{0,8},{4,12},{8,0},{12,4},{1,9},{5,13},{9,1},{13,5},{2,10},{6,14},... | collective-permute-start | bytes 294920 | tf_op jit(solution)/shard_map/ppermute | solution.py:287
  11.6 5.4 %collective-permute-start.17 = (bf16[32,1536]{1,0:T(8,128)(2,1)S(1)}, bf16[32,1536]{1,0:T(8,128)(2,1)S(1)}, u32[]{:S(2)}, u32[]{:S(2)}) collective-permute-start(bf16[32,1536]{1,0:T(8,128)(2,1)S(1)} %get-tuple-element.62.refs_3_), channel_id=1, source_target_pairs={{0,1},{1,0},{2,3},{3,2},{4,5},{5,4},{6,7},{7,6},{8,9},{9,8},{10,11... | collective-permute-start | bytes 294920 | tf_op jit(solution)/shard_map/ppermute | solution.py:287
  11.6 6.8 %collective-permute-start.6 = (bf16[32,1536]{1,0:T(8,128)(2,1)S(1)}, bf16[32,1536]{1,0:T(8,128)(2,1)S(1)}, u32[]{:S(2)}, u32[]{:S(2)}) collective-permute-start(bf16[32,1536]{1,0:T(8,128)(2,1)S(1)} %get-tuple-element.62.refs_3_), channel_id=1, source_target_pairs={{0,4},{4,0},{8,12},{12,8},{1,5},{5,1},{9,13},{13,9},{2,6},{6,2},{1... | collective-permute-start | bytes 294920 | tf_op jit(solution)/shard_map/ppermute | solution.py:287
  13.2 5.5 %collective-permute-start.12 = (bf16[32,1536]{1,0:T(8,128)(2,1)S(1)}, bf16[32,1536]{1,0:T(8,128)(2,1)S(1)}, u32[]{:S(2)}, u32[]{:S(2)}) collective-permute-start(bf16[32,1536]{1,0:T(8,128)(2,1)S(1)} %get-tuple-element.62.refs_3_), channel_id=1, source_target_pairs={{0,2},{1,3},{2,0},{3,1},{4,6},{5,7},{6,4},{7,5},{8,10},{9,11},{10,... | collective-permute-start | bytes 294920 | tf_op jit(solution)/shard_map/ppermute | solution.py:287
  14.3 6.6 %collective-permute-start.3 = (bf16[32,1536]{1,0:T(8,128)(2,1)S(1)}, bf16[32,1536]{1,0:T(8,128)(2,1)S(1)}, u32[]{:S(2)}, u32[]{:S(2)}) collective-permute-start(bf16[32,1536]{1,0:T(8,128)(2,1)S(1)} %get-tuple-element.62.refs_3_), channel_id=1, source_target_pairs={{0,12},{4,8},{8,4},{12,0},{1,13},{5,9},{9,5},{13,1},{2,14},{6,10},... | collective-permute-start | bytes 294920 | tf_op jit(solution)/shard_map/ppermute | solution.py:287
  17.0 4.8 %collective-permute-start.16 = (bf16[32,1536]{1,0:T(8,128)(2,1)S(1)}, bf16[32,1536]{1,0:T(8,128)(2,1)S(1)}, u32[]{:S(2)}, u32[]{:S(2)}) collective-permute-start(bf16[32,1536]{1,0:T(8,128)(2,1)S(1)} %collective-permute-done.9.refs_2_), channel_id=1, source_target_pairs={{0,1},{1,0},{2,3},{3,2},{4,5},{5,4},{6,7},{7,6},{8,9},{9,8},{10,11... | collective-permute-start | bytes 294920 | tf_op jit(solution)/shard_map/ppermute | solution.py:287
  17.0 5.6 %collective-permute-start.10 = (bf16[32,1536]{1,0:T(8,128)(2,1)S(1)}, bf16[32,1536]{1,0:T(8,128)(2,1)S(1)}, u32[]{:S(2)}, u32[]{:S(2)}) collective-permute-start(bf16[32,1536]{1,0:T(8,128)(2,1)S(1)} %collective-permute-done.9.refs_2_), channel_id=1, source_target_pairs={{0,2},{1,3},{2,0},{3,1},{4,6},{5,7},{6,4},{7,5},{8,10},{9,11},{10,... | collective-permute-start | bytes 294920 | tf_op jit(solution)/shard_map/ppermute | solution.py:287
  18.5 4.2 %collective-permute-start.15 = (bf16[32,1536]{1,0:T(8,128)(2,1)S(1)}, bf16[32,1536]{1,0:T(8,128)(2,1)S(1)}, u32[]{:S(2)}, u32[]{:S(2)}) collective-permute-start(bf16[32,1536]{1,0:T(8,128)(2,1)S(1)} %collective-permute-done.6.refs_1_), channel_id=1, source_target_pairs={{0,1},{1,0},{2,3},{3,2},{4,5},{5,4},{6,7},{7,6},{8,9},{9,8},{10,11... | collective-permute-start | bytes 294920 | tf_op jit(solution)/shard_map/ppermute | solution.py:287
  18.7 6.0 %collective-permute-start.7 = (bf16[32,1536]{1,0:T(8,128)(2,1)S(1)}, bf16[32,1536]{1,0:T(8,128)(2,1)S(1)}, u32[]{:S(2)}, u32[]{:S(2)}) collective-permute-start(bf16[32,1536]{1,0:T(8,128)(2,1)S(1)} %collective-permute-done.6.refs_1_), channel_id=1, source_target_pairs={{0,2},{1,3},{2,0},{3,1},{4,6},{5,7},{6,4},{7,5},{8,10},{9,11},{10,... | collective-permute-start | bytes 294920 | tf_op jit(solution)/shard_map/ppermute | solution.py:287
  20.8 5.6 %collective-permute-start.4 = (bf16[32,1536]{1,0:T(8,128)(2,1)S(1)}, bf16[32,1536]{1,0:T(8,128)(2,1)S(1)}, u32[]{:S(2)}, u32[]{:S(2)}) collective-permute-start(bf16[32,1536]{1,0:T(8,128)(2,1)S(1)} %collective-permute-done.3.refs_0_), channel_id=1, source_target_pairs={{0,2},{1,3},{2,0},{3,1},{4,6},{5,7},{6,4},{7,5},{8,10},{9,11},{10,... | collective-permute-start | bytes 294920 | tf_op jit(solution)/shard_map/ppermute | solution.py:287
  21.8 4.7 %collective-permute-start.14 = (bf16[32,1536]{1,0:T(8,128)(2,1)S(1)}, bf16[32,1536]{1,0:T(8,128)(2,1)S(1)}, u32[]{:S(2)}, u32[]{:S(2)}) collective-permute-start(bf16[32,1536]{1,0:T(8,128)(2,1)S(1)} %collective-permute-done.3.refs_0_), channel_id=1, source_target_pairs={{0,1},{1,0},{2,3},{3,2},{4,5},{5,4},{6,7},{7,6},{8,9},{9,8},{10,11... | collective-permute-start | bytes 294920 | tf_op jit(solution)/shard_map/ppermute | solution.py:287
  22.6 5.5 %collective-permute-start.13 = (bf16[32,1536]{1,0:T(8,128)(2,1)S(1)}, bf16[32,1536]{1,0:T(8,128)(2,1)S(1)}, u32[]{:S(2)}, u32[]{:S(2)}) collective-permute-start(bf16[32,1536]{1,0:T(8,128)(2,1)S(1)} %collective-permute-done.12.refs_11_), channel_id=1, source_target_pairs={{0,1},{1,0},{2,3},{3,2},{4,5},{5,4},{6,7},{7,6},{8,9},{9,8},{10,11... | collective-permute-start | bytes 294920 | tf_op jit(solution)/shard_map/ppermute | solution.py:287
  22.6 5.5 %collective-permute-start.11 = (bf16[32,1536]{1,0:T(8,128)(2,1)S(1)}, bf16[32,1536]{1,0:T(8,128)(2,1)S(1)}, u32[]{:S(2)}, u32[]{:S(2)}) collective-permute-start(bf16[32,1536]{1,0:T(8,128)(2,1)S(1)} %collective-permute-done.10.refs_10_), channel_id=1, source_target_pairs={{0,1},{1,0},{2,3},{3,2},{4,5},{5,4},{6,7},{7,6},{8,9},{9,8},{10,11... | collective-permute-start | bytes 294920 | tf_op jit(solution)/shard_map/ppermute | solution.py:287
  24.7 3.4 %collective-permute-start.8 = (bf16[32,1536]{1,0:T(8,128)(2,1)S(1)}, bf16[32,1536]{1,0:T(8,128)(2,1)S(1)}, u32[]{:S(2)}, u32[]{:S(2)}) collective-permute-start(bf16[32,1536]{1,0:T(8,128)(2,1)S(1)} %collective-permute-done.7.refs_9_), channel_id=1, source_target_pairs={{0,1},{1,0},{2,3},{3,2},{4,5},{5,4},{6,7},{7,6},{8,9},{9,8},{10,11... | collective-permute-start | bytes 294920 | tf_op jit(solution)/shard_map/ppermute | solution.py:287
  26.5 1.7 %collective-permute-start.5 = (bf16[32,1536]{1,0:T(8,128)(2,1)S(1)}, bf16[32,1536]{1,0:T(8,128)(2,1)S(1)}, u32[]{:S(2)}, u32[]{:S(2)}) collective-permute-start(bf16[32,1536]{1,0:T(8,128)(2,1)S(1)} %collective-permute-done.4.refs_8_), channel_id=1, source_target_pairs={{0,1},{1,0},{2,3},{3,2},{4,5},{5,4},{6,7},{7,6},{8,9},{9,8},{10,11... | collective-permute-start | bytes 294920 | tf_op jit(solution)/shard_map/ppermute | solution.py:287
  29.6 1.9 %collective-permute-start.18 = (bf16[128,1536]{1,0:T(8,128)(2,1)S(1)}, bf16[128,1536]{1,0:T(8,128)(2,1)S(1)}, u32[]{:S(2)}, u32[]{:S(2)}) collective-permute-start(bf16[128,1536]{1,0:T(8,128)(2,1)S(1)} %get-tuple-element.72), channel_id=1, source_target_pairs={{0,1},{1,0},{2,3},{3,2},{4,5},{5,4},{6,7},{7,6},{8,9},{9,8},{10,11... | collective-permute-start | bytes 1179656 | tf_op jit(solution)/shard_map/ppermute | solution.py:287
  31.6 5.7 %collective-permute-start.20 = (bf16[32,1536]{1,0:T(8,128)(2,1)S(1)}, bf16[32,1536]{1,0:T(8,128)(2,1)S(1)}, u32[]{:S(2)}, u32[]{:S(2)}) collective-permute-start(bf16[32,1536]{1,0:T(8,128)(2,1)S(1)} %get-tuple-element.81), channel_id=1, source_target_pairs={{0,4},{4,0},{8,12},{12,8},{1,5},{5,1},{9,13},{13,9},{2,6},{6,2},{1... | collective-permute-start | bytes 294920 | tf_op jit(solution)/shard_map/ppermute | solution.py:287
  32.3 12.8 %collective-permute-start.22 = (bf16[32,1536]{1,0:T(8,128)(2,1)S(1)}, bf16[32,1536]{1,0:T(8,128)(2,1)S(1)}, u32[]{:S(2)}, u32[]{:S(2)}) collective-permute-start(bf16[32,1536]{1,0:T(8,128)(2,1)S(1)} %get-tuple-element.89), channel_id=1, source_target_pairs={{0,20},{4,16},{8,28},{12,24},{16,4},{20,0},{24,12},{28,8},{1,21},{... | collective-permute-start | bytes 294920 | tf_op jit(solution)/shard_map/ppermute | solution.py:294
  34.6 10.5 %collective-permute-start.19 = (bf16[32,1664]{1,0:T(8,128)(2,1)S(1)}, bf16[32,1664]{1,0:T(8,128)(2,1)S(1)}, u32[]{:S(2)}, u32[]{:S(2)}) collective-permute-start(bf16[32,1664]{1,0:T(8,128)(2,1)S(1)} %get-tuple-element.74), channel_id=1, source_target_pairs={{0,16},{4,20},{8,24},{12,28},{16,0},{20,4},{24,8},{28,12},{1,17},{... | collective-permute-start | bytes 319496 | tf_op jit(solution)/shard_map/ppermute | solution.py:294
  37.3 7.8 %collective-permute-start.21 = (bf16[32,1536]{1,0:T(8,128)(2,1)S(1)}, bf16[32,1536]{1,0:T(8,128)(2,1)S(1)}, u32[]{:S(2)}, u32[]{:S(2)}) collective-permute-start(bf16[32,1536]{1,0:T(8,128)(2,1)S(1)} %get-tuple-element.84), channel_id=1, source_target_pairs={{0,24},{4,28},{8,16},{12,20},{16,8},{20,12},{24,0},{28,4},{1,25},{... | collective-permute-start | bytes 294920 | tf_op jit(solution)/shard_map/ppermute | solution.py:294
  45.4 4.0 %collective-permute-start.23 = (bf16[16,1536]{1,0:T(8,128)(2,1)S(1)}, bf16[16,1536]{1,0:T(8,128)(2,1)S(1)}, u32[]{:S(2)}, u32[]{:S(2)}) collective-permute-start(bf16[16,1536]{1,0:T(8,128)(2,1)S(1)} %get-tuple-element.91), channel_id=1, source_target_pairs={{0,1},{1,0},{2,3},{3,2},{4,5},{5,4},{6,7},{7,6},{8,9},{9,8},{10,11... | collective-permute-start | bytes 147464 | tf_op jit(solution)/shard_map/ppermute | solution.py:287
  45.5 4.2 %collective-permute-start.24 = (bf16[16,1536]{1,0:T(8,128)(2,1)S(1)}, bf16[16,1536]{1,0:T(8,128)(2,1)S(1)}, u32[]{:S(2)}, u32[]{:S(2)}) collective-permute-start(bf16[16,1536]{1,0:T(8,128)(2,1)S(1)} %get-tuple-element.92), channel_id=1, source_target_pairs={{0,2},{1,3},{2,0},{3,1},{4,6},{5,7},{6,4},{7,5},{8,10},{9,11},{10,... | collective-permute-start | bytes 147464 | tf_op jit(solution)/shard_map/ppermute | solution.py:287
  46.8 3.7 %collective-permute-start.25 = (bf16[16,1536]{1,0:T(8,128)(2,1)S(1)}, bf16[16,1536]{1,0:T(8,128)(2,1)S(1)}, u32[]{:S(2)}, u32[]{:S(2)}) collective-permute-start(bf16[16,1536]{1,0:T(8,128)(2,1)S(1)} %get-tuple-element.93), channel_id=1, source_target_pairs={{0,3},{1,2},{2,1},{3,0},{4,7},{5,6},{6,5},{7,4},{8,11},{9,10},{10,... | collective-permute-start | bytes 147464 | tf_op jit(solution)/shard_map/ppermute | solution.py:287

commit v9 on v8

--- a/solution.py
+++ b/solution.py
@@ -339,7 +339,7 @@
     diag = swap(slot_block, "dp", 3)
     near = swap(slot_block, "dp", 1)
     far = swap(slot_block, "dp", 2)
-    own = [diag, near, far, slot_block]
+    own = [diag, far, near, slot_block]
     chip = [swap(block, "et", 2) for block in own]
     core = [swap(block, "et", 1) for block in own]
     both = [swap(block, "et", 1) for block in chip]
@@ -363,7 +363,7 @@
         flops=4 * slots * hidden * half,
         vmem=32,
     )
-    to_last, to_near, to_far, home = call(
+    to_last, to_far, to_near, home = call(
         pair_kernel,
         [like((cap, half))] * 3 + [like((cap, half + FLAG))],
         own_terms,

time: 51.3 us -> 53.2 us (1.037)
  waiting for transfers between devices: 13.6 us -> 16.8 us
  starting transfers between devices: 21.8 us -> 20.5 us
    ppermute x23, waiting for transfers between devices: 13.1 us -> 15.3 us  [swap(): return lax.ppermute(value, axis, spread(steps))]
    ppermute x3, waiting for transfers between devices: 0.51 us -> 1.5 us  [hand(): return lax.ppermute(value, ('pipe', 'dp'), pairs)]
    ppermute x23, starting transfers between devices: 15.6 us -> 14.9 us  [swap(): return lax.ppermute(value, axis, spread(steps))]
    ppermute x3, starting transfers between devices: 6.13 us -> 5.58 us  [hand(): return lax.ppermute(value, ('pipe', 'dp'), pairs)]
  transfers between devices with their start and end apart: 26 -> 26, of which waited for: 11 -> 9; matrix products, arithmetic and copies ran while one was open for 12% -> 11% of each run, Pallas kernels for 10% -> 10%
where the time goes in v9:
time: 53.2 us; the launch traced here: 53.1 us
  starting transfers between devices  20.5 us (39%)
  waiting for transfers between devices  16.8 us (32%)
  Pallas kernels  8.93 us (17%)
  matrix products  6.06 us (11%)
  between operations  0.78 us (1%)
    ppermute x23, waiting for transfers between devices, swap(): return lax.ppermute(value, axis, spread(steps))  15.3 us
    ppermute x23, starting transfers between devices, swap(): return lax.ppermute(value, axis, spread(steps))  14.9 us
    pallas_call x10, Pallas kernels, call(): pl.pallas_call(kernel, out_shape=outs, in_specs=[space] * len(args), out_...  8.93 us
    dot_general x3, matrix products, contract(): lax.dot_general(left, right, (((left_dim,), (right_dim,)), ((), ())), pre...  6.06 us
    ppermute x3, starting transfers between devices, hand(): return lax.ppermute(value, ('pipe', 'dp'), pairs)  5.58 us
    ppermute x3, waiting for transfers between devices, hand(): return lax.ppermute(value, ('pipe', 'dp'), pairs)  1.5 us
  transfers between devices with their start and end apart: 26, of which 9 were waited for; matrix products, arithmetic and copies ran while one was open for 11% of the time, Pallas kernels for 10%

profile of v9, /device:TPU:0, one launch (start us, length us, event | category | flops | bytes accessed | tf_op | source)
XLA Modules:
  0.0 53.1 jit_solution(5030108264521047820)
XLA Ops:
  0.6 1.1 %shard_map.102 = (bf16[16,1664]{1,0:T(8,128)(2,1)S(1)}, bf16[16,1664]{1,0:T(8,128)(2,1)S(1)}, bf16[16,1664]{1,0:T(8,128)(2,1)S(1)}, bf16[16,1664]{1,0:T(8,128)(2,1)S(1)}) custom-call(bf16[16,3072]{1,0:T(8,128)(2,1)} %bitcast.27, bf16[16,3072]{1,0:T(8,128)(2,1)} %bitcast.28, s32[4,16]{1,0:T(4,128)} %bitcast.30, f32[4,16]{1,0:T(4,128)} %bitcast.31), custom_call_target="tpu_custom_call" | custom-call | bytes 410112 | tf_op jit(solution)/shard_map/pallas_call | solution.py:109
  1.7 0.5 collective-permute-start
  2.2 2.6 %collective-permute-start.1 = (bf16[16,1664]{1,0:T(8,128)(2,1)S(1)}, bf16[16,1664]{1,0:T(8,128)(2,1)S(1)}, u32[]{:S(2)}, u32[]{:S(2)}) collective-permute-start(bf16[16,1664]{1,0:T(8,128)(2,1)S(1)} %get-tuple-element.53), channel_id=1, source_target_pairs={{0,2},{1,3},{2,0},{3,1},{4,6},{5,7},{6,4},{7,5},{8,10},{9,11},{10,... | collective-permute-start | bytes 159752 | tf_op jit(solution)/shard_map/ppermute | solution.py:287
  4.8 0.1 collective-permute-start.2
  4.9 2.8 %shard_map.103 = (bf16[336,3072]{1,0:T(8,128)(2,1)S(1)}, bf16[336,3072]{1,0:T(8,128)(2,1)S(1)}, bf16[336,3072]{1,0:T(8,128)(2,1)S(1)}) custom-call(bf16[336,3072]{1,0:T(8,128)(2,1)} %bitcast.22, bf16[336,3072]{1,0:T(8,128)(2,1)} %bitcast.23, bf16[336,3072]{1,0:T(8,128)(2,1)} %bitcast.24), custom_call_target="tpu_custom_call" | custom-call | bytes 12386304 | tf_op jit(solution)/shard_map/pallas_call | solution.py:109
  7.7 0.0 collective-permute-done.refs_1_
  7.8 0.9 %collective-permute-done.2.refs_3_ = bf16[16,1664]{1,0:T(8,128)(2,1)S(1)} collective-permute-done((bf16[16,1664]{1,0:T(8,128)(2,1)S(1)}, bf16[16,1664]{1,0:T(8,128)(2,1)S(1)}, u32[]{:S(2)}, u32[]{:S(2)}) %collective-permute-start.2) | collective-permute-done | bytes 53280 | tf_op jit(solution)/shard_map/ppermute | solution.py:287
  8.6 0.3 shard_map.104
  9.0 1.6 %collective-permute-start.9 = (bf16[32,1536]{1,0:T(8,128)(2,1)S(1)}, bf16[32,1536]{1,0:T(8,128)(2,1)S(1)}, u32[]{:S(2)}, u32[]{:S(2)}) collective-permute-start(bf16[32,1536]{1,0:T(8,128)(2,1)S(1)} %get-tuple-element.62.refs_3_), channel_id=1, source_target_pairs={{0,4},{4,0},{8,12},{12,8},{1,5},{5,1},{9,13},{13,9},{2,6},{6,2},{1... | collective-permute-start | bytes 294920 | tf_op jit(solution)/shard_map/ppermute | solution.py:287
  10.6 2.6 %collective-permute-start.6 = (bf16[32,1536]{1,0:T(8,128)(2,1)S(1)}, bf16[32,1536]{1,0:T(8,128)(2,1)S(1)}, u32[]{:S(2)}, u32[]{:S(2)}) collective-permute-start(bf16[32,1536]{1,0:T(8,128)(2,1)S(1)} %get-tuple-element.62.refs_3_), channel_id=1, source_target_pairs={{0,8},{4,12},{8,0},{12,4},{1,9},{5,13},{9,1},{13,5},{2,10},{6,14},... | collective-permute-start | bytes 294920 | tf_op jit(solution)/shard_map/ppermute | solution.py:287
  13.2 1.1 %collective-permute-start.12 = (bf16[32,1536]{1,0:T(8,128)(2,1)S(1)}, bf16[32,1536]{1,0:T(8,128)(2,1)S(1)}, u32[]{:S(2)}, u32[]{:S(2)}) collective-permute-start(bf16[32,1536]{1,0:T(8,128)(2,1)S(1)} %get-tuple-element.62.refs_3_), channel_id=1, source_target_pairs={{0,2},{1,3},{2,0},{3,1},{4,6},{5,7},{6,4},{7,5},{8,10},{9,11},{10,... | collective-permute-start | bytes 294920 | tf_op jit(solution)/shard_map/ppermute | solution.py:287
  14.3 0.2 collective-permute-start.3
  14.5 0.0 collective-permute-done.9.refs_2_
  14.5 0.0 collective-permute-start.16
  14.5 1.0 %collective-permute-start.10 = (bf16[32,1536]{1,0:T(8,128)(2,1)S(1)}, bf16[32,1536]{1,0:T(8,128)(2,1)S(1)}, u32[]{:S(2)}, u32[]{:S(2)}) collective-permute-start(bf16[32,1536]{1,0:T(8,128)(2,1)S(1)} %collective-permute-done.9.refs_2_), channel_id=1, source_target_pairs={{0,2},{1,3},{2,0},{3,1},{4,6},{5,7},{6,4},{7,5},{8,10},{9,11},{10,... | collective-permute-start | bytes 294920 | tf_op jit(solution)/shard_map/ppermute | solution.py:287
  15.5 5.8 %collective-permute-done.6.refs_1_ = bf16[32,1536]{1,0:T(8,128)(2,1)S(1)} collective-permute-done((bf16[32,1536]{1,0:T(8,128)(2,1)S(1)}, bf16[32,1536]{1,0:T(8,128)(2,1)S(1)}, u32[]{:S(2)}, u32[]{:S(2)}) %collective-permute-start.6) | collective-permute-done | bytes 98336 | tf_op jit(solution)/shard_map/ppermute | solution.py:287
  21.3 0.0 collective-permute-start.15
  21.3 0.0 collective-permute-done.12.refs_11_
  21.3 1.1 %collective-permute-start.7 = (bf16[32,1536]{1,0:T(8,128)(2,1)S(1)}, bf16[32,1536]{1,0:T(8,128)(2,1)S(1)}, u32[]{:S(2)}, u32[]{:S(2)}) collective-permute-start(bf16[32,1536]{1,0:T(8,128)(2,1)S(1)} %collective-permute-done.6.refs_1_), channel_id=1, source_target_pairs={{0,2},{1,3},{2,0},{3,1},{4,6},{5,7},{6,4},{7,5},{8,10},{9,11},{10,... | collective-permute-start | bytes 294920 | tf_op jit(solution)/shard_map/ppermute | solution.py:287
  22.4 0.0 collective-permute-done.3.refs_0_
  22.4 0.9 %collective-permute-start.4 = (bf16[32,1536]{1,0:T(8,128)(2,1)S(1)}, bf16[32,1536]{1,0:T(8,128)(2,1)S(1)}, u32[]{:S(2)}, u32[]{:S(2)}) collective-permute-start(bf16[32,1536]{1,0:T(8,128)(2,1)S(1)} %collective-permute-done.3.refs_0_), channel_id=1, source_target_pairs={{0,2},{1,3},{2,0},{3,1},{4,6},{5,7},{6,4},{7,5},{8,10},{9,11},{10,... | collective-permute-start | bytes 294920 | tf_op jit(solution)/shard_map/ppermute | solution.py:287
  23.4 0.0 collective-permute-done.16.refs_6_
  23.4 0.5 collective-permute-start.13
  23.9 0.1 collective-permute-start.11
  23.9 3.0 %collective-permute-done.7.refs_9_ = bf16[32,1536]{1,0:T(8,128)(2,1)S(1)} collective-permute-done((bf16[32,1536]{1,0:T(8,128)(2,1)S(1)}, bf16[32,1536]{1,0:T(8,128)(2,1)S(1)}, u32[]{:S(2)}, u32[]{:S(2)}) %collective-permute-start.7) | collective-permute-done | bytes 98336 | tf_op jit(solution)/shard_map/ppermute | solution.py:287
  26.9 1.7 %collective-permute-done.4.refs_8_ = bf16[32,1536]{1,0:T(8,128)(2,1)S(1)} collective-permute-done((bf16[32,1536]{1,0:T(8,128)(2,1)S(1)}, bf16[32,1536]{1,0:T(8,128)(2,1)S(1)}, u32[]{:S(2)}, u32[]{:S(2)}) %collective-permute-start.4) | collective-permute-done | bytes 98336 | tf_op jit(solution)/shard_map/ppermute | solution.py:287
  28.6 1.6 %shard_map.105 = (bf16[128,3072]{1,0:T(8,128)(2,1)S(1)}, bf16[128,3072]{1,0:T(8,128)(2,1)S(1)}, f32[128,336]{1,0:T(8,128)S(1)}, f32[128,336]{1,0:T(8,128)S(1)}, f32[128,336]{1,0:T(8,128)S(1)}) custom-call(bf16[32,1536]{1,0:T(8,128)(2,1)S(1)} %collective-permute-done.3.refs_0_, bf16[32,1536]{1,0:T(8,128)(2,1)S(1)} %collective-permute-done.6.refs_1_, ...), custom_call_target="tpu_custom_call" | custom-call | tf_op jit(solution)/shard_map/pallas_call | solution.py:109
  30.3 1.4 %shard_map.106 = (bf16[128,3072]{1,0:T(8,128)(2,1)S(1)}, bf16[128,3072]{1,0:T(8,128)(2,1)S(1)}, bf16[128,336]{1,0:T(8,128)(2,1)S(1)}, bf16[128,336]{1,0:T(8,128)...) custom-call(bf16[32,1536]{1,0:T(8,128)(2,1)S(1)} %collective-permute, ...), custom_call_target="tpu_custom_call", output_to_operand_aliasing={{0}: (7, {}), {1}: (8, {})} | custom-call | tf_op jit(solution)/shard_map/pallas_call | solution.py:109
  31.8 0.6 %collective-permute-start.18 = (bf16[128,1536]{1,0:T(8,128)(2,1)S(1)}, bf16[128,1536]{1,0:T(8,128)(2,1)S(1)}, u32[]{:S(2)}, u32[]{:S(2)}) collective-permute-start(bf16[128,1536]{1,0:T(8,128)(2,1)S(1)} %get-tuple-element.72), channel_id=1, source_target_pairs={{0,1},{1,0},{2,3},{3,2},{4,5},{5,4},{6,7},{7,6},{8,9},{9,8},{10,11... | collective-permute-start | bytes 1179656 | tf_op jit(solution)/shard_map/ppermute | solution.py:287
  32.3 0.6 %shard_map.107.own_ref = f32[128,1536]{1,0:T(8,128)S(1)} custom-call(bf16[256,336]{1,0:T(8,128)(2,1)S(1)} %get-tuple-element.71.grads_ref, bf16[336,3072]{1,0:T(8,128)(2,1)S(1)} %get-tuple-element.63.refs_12_.refs_4_.wg_ref, bf16[336,3072]{1,0:T(8,128)(2,1)S(1)} %get-tuple-element.64.refs_13_.refs_5_.wu_ref), custom_call_target="tpu_custom_call" | custom-call | flops 264241152 | bytes 5087232 | tf_op jit(solution)/shard_map/pallas_call | solution.py:109
  32.9 0.8 %collective-permute-done.18.other_ref = bf16[128,1536]{1,0:T(8,128)(2,1)S(1)} collective-permute-done((bf16[128,1536]{1,0:T(8,128)(2,1)S(1)}, bf16[128,1536]{1,0:T(8,128)(2,1)S(1)}, u32[]{:S(2)}, u32[]{:S(2)}) %collective-permute-start.18) | collective-permute-done | bytes 393248 | tf_op jit(solution)/shard_map/ppermute | solution.py:287
  33.7 0.1 shard_map.108
  33.7 0.1 collective-permute-start.20
  33.8 3.0 %collective-permute-start.22 = (bf16[32,1536]{1,0:T(8,128)(2,1)S(1)}, bf16[32,1536]{1,0:T(8,128)(2,1)S(1)}, u32[]{:S(2)}, u32[]{:S(2)}) collective-permute-start(bf16[32,1536]{1,0:T(8,128)(2,1)S(1)} %get-tuple-element.89), channel_id=1, source_target_pairs={{0,20},{4,16},{8,28},{12,24},{16,4},{20,0},{24,12},{28,8},{1,21},{... | collective-permute-start | bytes 294920 | tf_op jit(solution)/shard_map/ppermute | solution.py:294
  36.8 0.5 %collective-permute-start.19 = (bf16[32,1664]{1,0:T(8,128)(2,1)S(1)}, bf16[32,1664]{1,0:T(8,128)(2,1)S(1)}, u32[]{:S(2)}, u32[]{:S(2)}) collective-permute-start(bf16[32,1664]{1,0:T(8,128)(2,1)S(1)} %get-tuple-element.74), channel_id=1, source_target_pairs={{0,16},{4,20},{8,24},{12,28},{16,0},{20,4},{24,8},{28,12},{1,17},{... | collective-permute-start | bytes 319496 | tf_op jit(solution)/shard_map/ppermute | solution.py:294
  37.3 2.1 %collective-permute-done.20.right_ref = bf16[32,1536]{1,0:T(8,128)(2,1)S(1)} collective-permute-done((bf16[32,1536]{1,0:T(8,128)(2,1)S(1)}, bf16[32,1536]{1,0:T(8,128)(2,1)S(1)}, u32[]{:S(2)}, u32[]{:S(2)}) %collective-permute-start.20) | collective-permute-done | bytes 98336 | tf_op jit(solution)/shard_map/ppermute | solution.py:287
  39.5 2.1 %collective-permute-start.21 = (bf16[32,1536]{1,0:T(8,128)(2,1)S(1)}, bf16[32,1536]{1,0:T(8,128)(2,1)S(1)}, u32[]{:S(2)}, u32[]{:S(2)}) collective-permute-start(bf16[32,1536]{1,0:T(8,128)(2,1)S(1)} %get-tuple-element.84), channel_id=1, source_target_pairs={{0,24},{4,28},{8,16},{12,20},{16,8},{20,12},{24,0},{28,4},{1,25},{... | collective-permute-start | bytes 294920 | tf_op jit(solution)/shard_map/ppermute | solution.py:294
  41.6 2.0 %convolution_convert_fusion.2 = bf16[336,3072]{1,0:T(8,128)(2,1)} fusion(bf16[128,336]{1,0:T(8,128)(2,1)S(1)} %get-tuple-element.85, bf16[128,3072]{1,0:T(8,128)(2,1)S(1)} %get-tuple-element.86), kind=kOutput, calls=%fused_computation.2 | convolution fusion | flops 265273344 | bytes 2936832 | tf_op jit(solution)/shard_map/dot_general | solution.py:40
  43.6 2.0 %convolution_convert_fusion.1 = bf16[336,3072]{1,0:T(8,128)(2,1)} fusion(bf16[128,336]{1,0:T(8,128)(2,1)S(1)} %get-tuple-element.87, bf16[128,3072]{1,0:T(8,128)(2,1)S(1)} %get-tuple-element.86), kind=kOutput, calls=%fused_computation.1 | convolution fusion | flops 265273344 | bytes 2936832 | tf_op jit(solution)/shard_map/dot_general | solution.py:40
  45.6 1.5 %collective-permute-done.21.refs_0_ = bf16[32,1536]{1,0:T(8,128)(2,1)S(1)} collective-permute-done((bf16[32,1536]{1,0:T(8,128)(2,1)S(1)}, bf16[32,1536]{1,0:T(8,128)(2,1)S(1)}, u32[]{:S(2)}, u32[]{:S(2)}) %collective-permute-start.21) | collective-permute-done | bytes 98336 | tf_op jit(solution)/shard_map/ppermute | solution.py:294
  47.1 0.3 shard_map.110
  47.4 0.1 collective-permute-start.23
  47.5 1.1 %collective-permute-start.24 = (bf16[16,1536]{1,0:T(8,128)(2,1)S(1)}, bf16[16,1536]{1,0:T(8,128)(2,1)S(1)}, u32[]{:S(2)}, u32[]{:S(2)}) collective-permute-start(bf16[16,1536]{1,0:T(8,128)(2,1)S(1)} %get-tuple-element.92), channel_id=1, source_target_pairs={{0,2},{1,3},{2,0},{3,1},{4,6},{5,7},{6,4},{7,5},{8,10},{9,11},{10,... | collective-permute-start | bytes 147464 | tf_op jit(solution)/shard_map/ppermute | solution.py:287
  48.6 0.7 %collective-permute-start.25 = (bf16[16,1536]{1,0:T(8,128)(2,1)S(1)}, bf16[16,1536]{1,0:T(8,128)(2,1)S(1)}, u32[]{:S(2)}, u32[]{:S(2)}) collective-permute-start(bf16[16,1536]{1,0:T(8,128)(2,1)S(1)} %get-tuple-element.93), channel_id=1, source_target_pairs={{0,3},{1,2},{2,1},{3,0},{4,7},{5,6},{6,5},{7,4},{8,11},{9,10},{10,... | collective-permute-start | bytes 147464 | tf_op jit(solution)/shard_map/ppermute | solution.py:287
  49.4 2.0 %fusion = bf16[1,336,3072]{2,1,0:T(8,128)(2,1)} fusion(bf16[128,336]{1,0:T(8,128)(2,1)S(1)} %get-tuple-element.96, bf16[128,3072]{1,0:T(8,128)(2,1)S(1)} %get-tuple-element.97), kind=kOutput, calls=%fused_computation.3 | convolution fusion | flops 265273344 | bytes 2936832 | tf_op jit(solution)/shard_map/dot_general | solution.py:40
  51.4 0.4 collective-permute-done.24.chip_ref
  51.8 0.6 %collective-permute-done.25.both_ref = bf16[16,1536]{1,0:T(8,128)(2,1)S(1)} collective-permute-done((bf16[16,1536]{1,0:T(8,128)(2,1)S(1)}, bf16[16,1536]{1,0:T(8,128)(2,1)S(1)}, u32[]{:S(2)}, u32[]{:S(2)}) %collective-permute-start.25) | collective-permute-done | bytes 49184 | tf_op jit(solution)/shard_map/ppermute | solution.py:287
  52.4 0.7 %shard_map.111 = bf16[16,3072]{1,0:T(8,128)(2,1)} custom-call(bf16[16,1536]{1,0:T(8,128)(2,1)S(1)} %get-tuple-element.90.own_ref, bf16[16,1536]{1,0:T(8,128)(2,1)S(1)} %collective-permute-done.23.core_ref, bf16[16,1536]{1,0:T(8,128)(2,1)S(1)} %collective-permute-done.24.chip_ref, bf16[16,1536]{1,0:T(8,128)(2,1)S(1)} %collective-permute-done.25.both_ref), custom_call_target="tpu_custom_call" | custom-call | tf_op jit(solution)/shard_map/pallas_call | solution.py:109
  (17 shorter events, 0.1 us)
Async XLA Ops:
  1.7 6.0 %collective-permute-start = (bf16[16,1664]{1,0:T(8,128)(2,1)S(1)}, bf16[16,1664]{1,0:T(8,128)(2,1)S(1)}, u32[]{:S(2)}, u32[]{:S(2)}) collective-permute-start(bf16[16,1664]{1,0:T(8,128)(2,1)S(1)} %get-tuple-element.52), channel_id=1, source_target_pairs={{0,1},{1,0},{2,3},{3,2},{4,5},{5,4},{6,7},{7,6},{8,9},{9,8},{10,11... | collective-permute-start | bytes 159752 | tf_op jit(solution)/shard_map/ppermute | solution.py:287
  2.2 5.5 %collective-permute-start.1 = (bf16[16,1664]{1,0:T(8,128)(2,1)S(1)}, bf16[16,1664]{1,0:T(8,128)(2,1)S(1)}, u32[]{:S(2)}, u32[]{:S(2)}) collective-permute-start(bf16[16,1664]{1,0:T(8,128)(2,1)S(1)} %get-tuple-element.53), channel_id=1, source_target_pairs={{0,2},{1,3},{2,0},{3,1},{4,6},{5,7},{6,4},{7,5},{8,10},{9,11},{10,... | collective-permute-start | bytes 159752 | tf_op jit(solution)/shard_map/ppermute | solution.py:287
  4.8 3.8 %collective-permute-start.2 = (bf16[16,1664]{1,0:T(8,128)(2,1)S(1)}, bf16[16,1664]{1,0:T(8,128)(2,1)S(1)}, u32[]{:S(2)}, u32[]{:S(2)}) collective-permute-start(bf16[16,1664]{1,0:T(8,128)(2,1)S(1)} %get-tuple-element.54), channel_id=1, source_target_pairs={{0,3},{1,2},{2,1},{3,0},{4,7},{5,6},{6,5},{7,4},{8,11},{9,10},{10,... | collective-permute-start | bytes 159752 | tf_op jit(solution)/shard_map/ppermute | solution.py:287
  9.0 5.5 %collective-permute-start.9 = (bf16[32,1536]{1,0:T(8,128)(2,1)S(1)}, bf16[32,1536]{1,0:T(8,128)(2,1)S(1)}, u32[]{:S(2)}, u32[]{:S(2)}) collective-permute-start(bf16[32,1536]{1,0:T(8,128)(2,1)S(1)} %get-tuple-element.62.refs_3_), channel_id=1, source_target_pairs={{0,4},{4,0},{8,12},{12,8},{1,5},{5,1},{9,13},{13,9},{2,6},{6,2},{1... | collective-permute-start | bytes 294920 | tf_op jit(solution)/shard_map/ppermute | solution.py:287
  10.6 3.9 %collective-permute-start.17 = (bf16[32,1536]{1,0:T(8,128)(2,1)S(1)}, bf16[32,1536]{1,0:T(8,128)(2,1)S(1)}, u32[]{:S(2)}, u32[]{:S(2)}) collective-permute-start(bf16[32,1536]{1,0:T(8,128)(2,1)S(1)} %get-tuple-element.62.refs_3_), channel_id=1, source_target_pairs={{0,1},{1,0},{2,3},{3,2},{4,5},{5,4},{6,7},{7,6},{8,9},{9,8},{10,11... | collective-permute-start | bytes 294920 | tf_op jit(solution)/shard_map/ppermute | solution.py:287
  10.6 10.7 %collective-permute-start.6 = (bf16[32,1536]{1,0:T(8,128)(2,1)S(1)}, bf16[32,1536]{1,0:T(8,128)(2,1)S(1)}, u32[]{:S(2)}, u32[]{:S(2)}) collective-permute-start(bf16[32,1536]{1,0:T(8,128)(2,1)S(1)} %get-tuple-element.62.refs_3_), channel_id=1, source_target_pairs={{0,8},{4,12},{8,0},{12,4},{1,9},{5,13},{9,1},{13,5},{2,10},{6,14},... | collective-permute-start | bytes 294920 | tf_op jit(solution)/shard_map/ppermute | solution.py:287
  13.2 8.1 %collective-permute-start.12 = (bf16[32,1536]{1,0:T(8,128)(2,1)S(1)}, bf16[32,1536]{1,0:T(8,128)(2,1)S(1)}, u32[]{:S(2)}, u32[]{:S(2)}) collective-permute-start(bf16[32,1536]{1,0:T(8,128)(2,1)S(1)} %get-tuple-element.62.refs_3_), channel_id=1, source_target_pairs={{0,2},{1,3},{2,0},{3,1},{4,6},{5,7},{6,4},{7,5},{8,10},{9,11},{10,... | collective-permute-start | bytes 294920 | tf_op jit(solution)/shard_map/ppermute | solution.py:287
  14.3 8.1 %collective-permute-start.3 = (bf16[32,1536]{1,0:T(8,128)(2,1)S(1)}, bf16[32,1536]{1,0:T(8,128)(2,1)S(1)}, u32[]{:S(2)}, u32[]{:S(2)}) collective-permute-start(bf16[32,1536]{1,0:T(8,128)(2,1)S(1)} %get-tuple-element.62.refs_3_), channel_id=1, source_target_pairs={{0,12},{4,8},{8,4},{12,0},{1,13},{5,9},{9,5},{13,1},{2,14},{6,10},... | collective-permute-start | bytes 294920 | tf_op jit(solution)/shard_map/ppermute | solution.py:287
  14.5 8.8 %collective-permute-start.16 = (bf16[32,1536]{1,0:T(8,128)(2,1)S(1)}, bf16[32,1536]{1,0:T(8,128)(2,1)S(1)}, u32[]{:S(2)}, u32[]{:S(2)}) collective-permute-start(bf16[32,1536]{1,0:T(8,128)(2,1)S(1)} %collective-permute-done.9.refs_2_), channel_id=1, source_target_pairs={{0,1},{1,0},{2,3},{3,2},{4,5},{5,4},{6,7},{7,6},{8,9},{9,8},{10,11... | collective-permute-start | bytes 294920 | tf_op jit(solution)/shard_map/ppermute | solution.py:287
  14.5 8.8 %collective-permute-start.10 = (bf16[32,1536]{1,0:T(8,128)(2,1)S(1)}, bf16[32,1536]{1,0:T(8,128)(2,1)S(1)}, u32[]{:S(2)}, u32[]{:S(2)}) collective-permute-start(bf16[32,1536]{1,0:T(8,128)(2,1)S(1)} %collective-permute-done.9.refs_2_), channel_id=1, source_target_pairs={{0,2},{1,3},{2,0},{3,1},{4,6},{5,7},{6,4},{7,5},{8,10},{9,11},{10,... | collective-permute-start | bytes 294920 | tf_op jit(solution)/shard_map/ppermute | solution.py:287
  21.3 2.6 %collective-permute-start.15 = (bf16[32,1536]{1,0:T(8,128)(2,1)S(1)}, bf16[32,1536]{1,0:T(8,128)(2,1)S(1)}, u32[]{:S(2)}, u32[]{:S(2)}) collective-permute-start(bf16[32,1536]{1,0:T(8,128)(2,1)S(1)} %collective-permute-done.6.refs_1_), channel_id=1, source_target_pairs={{0,1},{1,0},{2,3},{3,2},{4,5},{5,4},{6,7},{7,6},{8,9},{9,8},{10,11... | collective-permute-start | bytes 294920 | tf_op jit(solution)/shard_map/ppermute | solution.py:287
  21.3 5.6 %collective-permute-start.7 = (bf16[32,1536]{1,0:T(8,128)(2,1)S(1)}, bf16[32,1536]{1,0:T(8,128)(2,1)S(1)}, u32[]{:S(2)}, u32[]{:S(2)}) collective-permute-start(bf16[32,1536]{1,0:T(8,128)(2,1)S(1)} %collective-permute-done.6.refs_1_), channel_id=1, source_target_pairs={{0,2},{1,3},{2,0},{3,1},{4,6},{5,7},{6,4},{7,5},{8,10},{9,11},{10,... | collective-permute-start | bytes 294920 | tf_op jit(solution)/shard_map/ppermute | solution.py:287
  22.4 6.2 %collective-permute-start.4 = (bf16[32,1536]{1,0:T(8,128)(2,1)S(1)}, bf16[32,1536]{1,0:T(8,128)(2,1)S(1)}, u32[]{:S(2)}, u32[]{:S(2)}) collective-permute-start(bf16[32,1536]{1,0:T(8,128)(2,1)S(1)} %collective-permute-done.3.refs_0_), channel_id=1, source_target_pairs={{0,2},{1,3},{2,0},{3,1},{4,6},{5,7},{6,4},{7,5},{8,10},{9,11},{10,... | collective-permute-start | bytes 294920 | tf_op jit(solution)/shard_map/ppermute | solution.py:287
  23.4 5.3 %collective-permute-start.14 = (bf16[32,1536]{1,0:T(8,128)(2,1)S(1)}, bf16[32,1536]{1,0:T(8,128)(2,1)S(1)}, u32[]{:S(2)}, u32[]{:S(2)}) collective-permute-start(bf16[32,1536]{1,0:T(8,128)(2,1)S(1)} %collective-permute-done.3.refs_0_), channel_id=1, source_target_pairs={{0,1},{1,0},{2,3},{3,2},{4,5},{5,4},{6,7},{7,6},{8,9},{9,8},{10,11... | collective-permute-start | bytes 294920 | tf_op jit(solution)/shard_map/ppermute | solution.py:287
  23.4 6.9 %collective-permute-start.13 = (bf16[32,1536]{1,0:T(8,128)(2,1)S(1)}, bf16[32,1536]{1,0:T(8,128)(2,1)S(1)}, u32[]{:S(2)}, u32[]{:S(2)}) collective-permute-start(bf16[32,1536]{1,0:T(8,128)(2,1)S(1)} %collective-permute-done.12.refs_11_), channel_id=1, source_target_pairs={{0,1},{1,0},{2,3},{3,2},{4,5},{5,4},{6,7},{7,6},{8,9},{9,8},{10,11... | collective-permute-start | bytes 294920 | tf_op jit(solution)/shard_map/ppermute | solution.py:287
  23.9 6.4 %collective-permute-start.11 = (bf16[32,1536]{1,0:T(8,128)(2,1)S(1)}, bf16[32,1536]{1,0:T(8,128)(2,1)S(1)}, u32[]{:S(2)}, u32[]{:S(2)}) collective-permute-start(bf16[32,1536]{1,0:T(8,128)(2,1)S(1)} %collective-permute-done.10.refs_10_), channel_id=1, source_target_pairs={{0,1},{1,0},{2,3},{3,2},{4,5},{5,4},{6,7},{7,6},{8,9},{9,8},{10,11... | collective-permute-start | bytes 294920 | tf_op jit(solution)/shard_map/ppermute | solution.py:287
  26.9 3.4 %collective-permute-start.8 = (bf16[32,1536]{1,0:T(8,128)(2,1)S(1)}, bf16[32,1536]{1,0:T(8,128)(2,1)S(1)}, u32[]{:S(2)}, u32[]{:S(2)}) collective-permute-start(bf16[32,1536]{1,0:T(8,128)(2,1)S(1)} %collective-permute-done.7.refs_9_), channel_id=1, source_target_pairs={{0,1},{1,0},{2,3},{3,2},{4,5},{5,4},{6,7},{7,6},{8,9},{9,8},{10,11... | collective-permute-start | bytes 294920 | tf_op jit(solution)/shard_map/ppermute | solution.py:287
  28.6 1.7 %collective-permute-start.5 = (bf16[32,1536]{1,0:T(8,128)(2,1)S(1)}, bf16[32,1536]{1,0:T(8,128)(2,1)S(1)}, u32[]{:S(2)}, u32[]{:S(2)}) collective-permute-start(bf16[32,1536]{1,0:T(8,128)(2,1)S(1)} %collective-permute-done.4.refs_8_), channel_id=1, source_target_pairs={{0,1},{1,0},{2,3},{3,2},{4,5},{5,4},{6,7},{7,6},{8,9},{9,8},{10,11... | collective-permute-start | bytes 294920 | tf_op jit(solution)/shard_map/ppermute | solution.py:287
  31.8 1.9 %collective-permute-start.18 = (bf16[128,1536]{1,0:T(8,128)(2,1)S(1)}, bf16[128,1536]{1,0:T(8,128)(2,1)S(1)}, u32[]{:S(2)}, u32[]{:S(2)}) collective-permute-start(bf16[128,1536]{1,0:T(8,128)(2,1)S(1)} %get-tuple-element.72), channel_id=1, source_target_pairs={{0,1},{1,0},{2,3},{3,2},{4,5},{5,4},{6,7},{7,6},{8,9},{9,8},{10,11... | collective-permute-start | bytes 1179656 | tf_op jit(solution)/shard_map/ppermute | solution.py:287
  33.7 5.7 %collective-permute-start.20 = (bf16[32,1536]{1,0:T(8,128)(2,1)S(1)}, bf16[32,1536]{1,0:T(8,128)(2,1)S(1)}, u32[]{:S(2)}, u32[]{:S(2)}) collective-permute-start(bf16[32,1536]{1,0:T(8,128)(2,1)S(1)} %get-tuple-element.81), channel_id=1, source_target_pairs={{0,4},{4,0},{8,12},{12,8},{1,5},{5,1},{9,13},{13,9},{2,6},{6,2},{1... | collective-permute-start | bytes 294920 | tf_op jit(solution)/shard_map/ppermute | solution.py:287
  33.8 13.3 %collective-permute-start.22 = (bf16[32,1536]{1,0:T(8,128)(2,1)S(1)}, bf16[32,1536]{1,0:T(8,128)(2,1)S(1)}, u32[]{:S(2)}, u32[]{:S(2)}) collective-permute-start(bf16[32,1536]{1,0:T(8,128)(2,1)S(1)} %get-tuple-element.89), channel_id=1, source_target_pairs={{0,20},{4,16},{8,28},{12,24},{16,4},{20,0},{24,12},{28,8},{1,21},{... | collective-permute-start | bytes 294920 | tf_op jit(solution)/shard_map/ppermute | solution.py:294
  36.8 10.3 %collective-permute-start.19 = (bf16[32,1664]{1,0:T(8,128)(2,1)S(1)}, bf16[32,1664]{1,0:T(8,128)(2,1)S(1)}, u32[]{:S(2)}, u32[]{:S(2)}) collective-permute-start(bf16[32,1664]{1,0:T(8,128)(2,1)S(1)} %get-tuple-element.74), channel_id=1, source_target_pairs={{0,16},{4,20},{8,24},{12,28},{16,0},{20,4},{24,8},{28,12},{1,17},{... | collective-permute-start | bytes 319496 | tf_op jit(solution)/shard_map/ppermute | solution.py:294
  39.5 7.6 %collective-permute-start.21 = (bf16[32,1536]{1,0:T(8,128)(2,1)S(1)}, bf16[32,1536]{1,0:T(8,128)(2,1)S(1)}, u32[]{:S(2)}, u32[]{:S(2)}) collective-permute-start(bf16[32,1536]{1,0:T(8,128)(2,1)S(1)} %get-tuple-element.84), channel_id=1, source_target_pairs={{0,24},{4,28},{8,16},{12,20},{16,8},{20,12},{24,0},{28,4},{1,25},{... | collective-permute-start | bytes 294920 | tf_op jit(solution)/shard_map/ppermute | solution.py:294
  47.4 4.0 %collective-permute-start.23 = (bf16[16,1536]{1,0:T(8,128)(2,1)S(1)}, bf16[16,1536]{1,0:T(8,128)(2,1)S(1)}, u32[]{:S(2)}, u32[]{:S(2)}) collective-permute-start(bf16[16,1536]{1,0:T(8,128)(2,1)S(1)} %get-tuple-element.91), channel_id=1, source_target_pairs={{0,1},{1,0},{2,3},{3,2},{4,5},{5,4},{6,7},{7,6},{8,9},{9,8},{10,11... | collective-permute-start | bytes 147464 | tf_op jit(solution)/shard_map/ppermute | solution.py:287
  47.5 4.3 %collective-permute-start.24 = (bf16[16,1536]{1,0:T(8,128)(2,1)S(1)}, bf16[16,1536]{1,0:T(8,128)(2,1)S(1)}, u32[]{:S(2)}, u32[]{:S(2)}) collective-permute-start(bf16[16,1536]{1,0:T(8,128)(2,1)S(1)} %get-tuple-element.92), channel_id=1, source_target_pairs={{0,2},{1,3},{2,0},{3,1},{4,6},{5,7},{6,4},{7,5},{8,10},{9,11},{10,... | collective-permute-start | bytes 147464 | tf_op jit(solution)/shard_map/ppermute | solution.py:287
  48.6 3.8 %collective-permute-start.25 = (bf16[16,1536]{1,0:T(8,128)(2,1)S(1)}, bf16[16,1536]{1,0:T(8,128)(2,1)S(1)}, u32[]{:S(2)}, u32[]{:S(2)}) collective-permute-start(bf16[16,1536]{1,0:T(8,128)(2,1)S(1)} %get-tuple-element.93), channel_id=1, source_target_pairs={{0,3},{1,2},{2,1},{3,0},{4,7},{5,6},{6,5},{7,4},{8,11},{9,10},{10,... | collective-permute-start | bytes 147464 | tf_op jit(solution)/shard_map/ppermute | solution.py:287

commit v10 on v9

--- a/solution.py
+++ b/solution.py
@@ -336,10 +336,10 @@
         *arrived,
         scratch=[pltpu.VMEM((4 * rows, 2 * piece + FLAG), BF16)],
     )
-    diag = swap(slot_block, "dp", 3)
     near = swap(slot_block, "dp", 1)
     far = swap(slot_block, "dp", 2)
-    own = [diag, far, near, slot_block]
+    last = swap(far, "dp", 1)
+    own = [near, last, far, slot_block]
     chip = [swap(block, "et", 2) for block in own]
     core = [swap(block, "et", 1) for block in own]
     both = [swap(block, "et", 1) for block in chip]
@@ -363,7 +363,7 @@
         flops=4 * slots * hidden * half,
         vmem=32,
     )
-    to_last, to_far, to_near, home = call(
+    to_near, to_last, to_far, home = call(
         pair_kernel,
         [like((cap, half))] * 3 + [like((cap, half + FLAG))],
         own_terms,

time: 53.2 us -> 52.5 us (0.987)
  waiting for transfers between devices: 16.8 us -> 12.5 us
  starting transfers between devices: 20.5 us -> 24 us
    ppermute x23, waiting for transfers between devices: 15.3 us -> 12.5 us  [swap(): return lax.ppermute(value, axis, spread(steps))]
    ppermute x23, starting transfers between devices: 14.9 us -> 17.1 us  [swap(): return lax.ppermute(value, axis, spread(steps))]
    ppermute x3, waiting for transfers between devices: 1.5 us -> 0.06 us  [hand(): return lax.ppermute(value, ('pipe', 'dp'), pairs)]
    ppermute x3, starting transfers between devices: 5.58 us -> 6.95 us  [hand(): return lax.ppermute(value, ('pipe', 'dp'), pairs)]
  transfers between devices with their start and end apart: 26 -> 26, of which waited for: 9 -> 11; matrix products, arithmetic and copies ran while one was open for 11% -> 12% of each run, Pallas kernels for 10% -> 10%
where the time goes in v10:
time: 52.5 us; the launch traced here: 52.3 us
  starting transfers between devices  24 us (46%)
  waiting for transfers between devices  12.5 us (24%)
  Pallas kernels  8.93 us (17%)
  matrix products  6.07 us (12%)
  between operations  0.77 us (1%)
    ppermute x23, starting transfers between devices, swap(): return lax.ppermute(value, axis, spread(steps))  17.1 us
    ppermute x23, waiting for transfers between devices, swap(): return lax.ppermute(value, axis, spread(steps))  12.5 us
    pallas_call x10, Pallas kernels, call(): pl.pallas_call(kernel, out_shape=outs, in_specs=[space] * len(args), out_...  8.93 us
    ppermute x3, starting transfers between devices, hand(): return lax.ppermute(value, ('pipe', 'dp'), pairs)  6.95 us
    dot_general x3, matrix products, contract(): lax.dot_general(left, right, (((left_dim,), (right_dim,)), ((), ())), pre...  6.07 us
  transfers between devices with their start and end apart: 26, of which 11 were waited for; matrix products, arithmetic and copies ran while one was open for 12% of the time, Pallas kernels for 10%

profile of v10, /device:TPU:0, one launch (start us, length us, event | category | flops | bytes accessed | tf_op | source)
XLA Modules:
  0.0 52.3 jit_solution(13391043286199445767)
XLA Ops:
  0.6 1.1 %shard_map.102 = (bf16[16,1664]{1,0:T(8,128)(2,1)S(1)}, bf16[16,1664]{1,0:T(8,128)(2,1)S(1)}, bf16[16,1664]{1,0:T(8,128)(2,1)S(1)}, bf16[16,1664]{1,0:T(8,128)(2,1)S(1)}) custom-call(bf16[16,3072]{1,0:T(8,128)(2,1)} %bitcast.27, bf16[16,3072]{1,0:T(8,128)(2,1)} %bitcast.28, s32[4,16]{1,0:T(4,128)} %bitcast.30, f32[4,16]{1,0:T(4,128)} %bitcast.31), custom_call_target="tpu_custom_call" | custom-call | bytes 410112 | tf_op jit(solution)/shard_map/pallas_call | solution.py:109
  1.7 0.5 collective-permute-start
  2.2 2.6 %collective-permute-start.1 = (bf16[16,1664]{1,0:T(8,128)(2,1)S(1)}, bf16[16,1664]{1,0:T(8,128)(2,1)S(1)}, u32[]{:S(2)}, u32[]{:S(2)}) collective-permute-start(bf16[16,1664]{1,0:T(8,128)(2,1)S(1)} %get-tuple-element.53), channel_id=1, source_target_pairs={{0,2},{1,3},{2,0},{3,1},{4,6},{5,7},{6,4},{7,5},{8,10},{9,11},{10,... | collective-permute-start | bytes 159752 | tf_op jit(solution)/shard_map/ppermute | solution.py:287
  4.8 0.1 collective-permute-start.2
  4.9 2.8 %shard_map.103 = (bf16[336,3072]{1,0:T(8,128)(2,1)S(1)}, bf16[336,3072]{1,0:T(8,128)(2,1)S(1)}, bf16[336,3072]{1,0:T(8,128)(2,1)S(1)}) custom-call(bf16[336,3072]{1,0:T(8,128)(2,1)} %bitcast.22, bf16[336,3072]{1,0:T(8,128)(2,1)} %bitcast.23, bf16[336,3072]{1,0:T(8,128)(2,1)} %bitcast.24), custom_call_target="tpu_custom_call" | custom-call | bytes 12386304 | tf_op jit(solution)/shard_map/pallas_call | solution.py:109
  7.7 0.0 collective-permute-done.1.refs_2_
  7.8 0.9 %collective-permute-done.2.refs_3_ = bf16[16,1664]{1,0:T(8,128)(2,1)S(1)} collective-permute-done((bf16[16,1664]{1,0:T(8,128)(2,1)S(1)}, bf16[16,1664]{1,0:T(8,128)(2,1)S(1)}, u32[]{:S(2)}, u32[]{:S(2)}) %collective-permute-start.2) | collective-permute-done | bytes 53280 | tf_op jit(solution)/shard_map/ppermute | solution.py:287
  8.6 0.3 shard_map.104
  9.0 2.7 %collective-permute-start.6 = (bf16[32,1536]{1,0:T(8,128)(2,1)S(1)}, bf16[32,1536]{1,0:T(8,128)(2,1)S(1)}, u32[]{:S(2)}, u32[]{:S(2)}) collective-permute-start(bf16[32,1536]{1,0:T(8,128)(2,1)S(1)} %get-tuple-element.62.refs_3_), channel_id=1, source_target_pairs={{0,8},{4,12},{8,0},{12,4},{1,9},{5,13},{9,1},{13,5},{2,10},{6,14},... | collective-permute-start | bytes 294920 | tf_op jit(solution)/shard_map/ppermute | solution.py:287
  11.6 1.6 %collective-permute-start.3 = (bf16[32,1536]{1,0:T(8,128)(2,1)S(1)}, bf16[32,1536]{1,0:T(8,128)(2,1)S(1)}, u32[]{:S(2)}, u32[]{:S(2)}) collective-permute-start(bf16[32,1536]{1,0:T(8,128)(2,1)S(1)} %get-tuple-element.62.refs_3_), channel_id=1, source_target_pairs={{0,4},{4,0},{8,12},{12,8},{1,5},{5,1},{9,13},{13,9},{2,6},{6,2},{1... | collective-permute-start | bytes 294920 | tf_op jit(solution)/shard_map/ppermute | solution.py:287
  13.2 1.1 %collective-permute-start.12 = (bf16[32,1536]{1,0:T(8,128)(2,1)S(1)}, bf16[32,1536]{1,0:T(8,128)(2,1)S(1)}, u32[]{:S(2)}, u32[]{:S(2)}) collective-permute-start(bf16[32,1536]{1,0:T(8,128)(2,1)S(1)} %get-tuple-element.62.refs_3_), channel_id=1, source_target_pairs={{0,2},{1,3},{2,0},{3,1},{4,6},{5,7},{6,4},{7,5},{8,10},{9,11},{10,... | collective-permute-start | bytes 294920 | tf_op jit(solution)/shard_map/ppermute | solution.py:287
  14.3 2.7 %collective-permute-done.6.refs_2_ = bf16[32,1536]{1,0:T(8,128)(2,1)S(1)} collective-permute-done((bf16[32,1536]{1,0:T(8,128)(2,1)S(1)}, bf16[32,1536]{1,0:T(8,128)(2,1)S(1)}, u32[]{:S(2)}, u32[]{:S(2)}) %collective-permute-start.6) | collective-permute-done | bytes 98336 | tf_op jit(solution)/shard_map/ppermute | solution.py:287
  17.0 0.6 %collective-permute-start.7 = (bf16[32,1536]{1,0:T(8,128)(2,1)S(1)}, bf16[32,1536]{1,0:T(8,128)(2,1)S(1)}, u32[]{:S(2)}, u32[]{:S(2)}) collective-permute-start(bf16[32,1536]{1,0:T(8,128)(2,1)S(1)} %collective-permute-done.6.refs_2_), channel_id=1, source_target_pairs={{0,4},{4,0},{8,12},{12,8},{1,5},{5,1},{9,13},{13,9},{2,6},{6,2},{1... | collective-permute-start | bytes 294920 | tf_op jit(solution)/shard_map/ppermute | solution.py:287
  17.6 0.0 collective-permute-start.16
  17.6 0.0 collective-permute-done.17.refs_7_
  17.6 1.2 %collective-permute-start.10 = (bf16[32,1536]{1,0:T(8,128)(2,1)S(1)}, bf16[32,1536]{1,0:T(8,128)(2,1)S(1)}, u32[]{:S(2)}, u32[]{:S(2)}) collective-permute-start(bf16[32,1536]{1,0:T(8,128)(2,1)S(1)} %collective-permute-done.6.refs_2_), channel_id=1, source_target_pairs={{0,2},{1,3},{2,0},{3,1},{4,6},{5,7},{6,4},{7,5},{8,10},{9,11},{10,... | collective-permute-start | bytes 294920 | tf_op jit(solution)/shard_map/ppermute | solution.py:287
  18.8 0.0 collective-permute-done.3.refs_0_
  18.8 0.2 collective-permute-start.14
  19.0 0.8 %collective-permute-start.4 = (bf16[32,1536]{1,0:T(8,128)(2,1)S(1)}, bf16[32,1536]{1,0:T(8,128)(2,1)S(1)}, u32[]{:S(2)}, u32[]{:S(2)}) collective-permute-start(bf16[32,1536]{1,0:T(8,128)(2,1)S(1)} %collective-permute-done.3.refs_0_), channel_id=1, source_target_pairs={{0,2},{1,3},{2,0},{3,1},{4,6},{5,7},{6,4},{7,5},{8,10},{9,11},{10,... | collective-permute-start | bytes 294920 | tf_op jit(solution)/shard_map/ppermute | solution.py:287
  19.9 1.8 %collective-permute-done.7.refs_1_ = bf16[32,1536]{1,0:T(8,128)(2,1)S(1)} collective-permute-done((bf16[32,1536]{1,0:T(8,128)(2,1)S(1)}, bf16[32,1536]{1,0:T(8,128)(2,1)S(1)}, u32[]{:S(2)}, u32[]{:S(2)}) %collective-permute-start.7) | collective-permute-done | bytes 98336 | tf_op jit(solution)/shard_map/ppermute | solution.py:287
  21.6 1.2 %collective-permute-start.8 = (bf16[32,1536]{1,0:T(8,128)(2,1)S(1)}, bf16[32,1536]{1,0:T(8,128)(2,1)S(1)}, u32[]{:S(2)}, u32[]{:S(2)}) collective-permute-start(bf16[32,1536]{1,0:T(8,128)(2,1)S(1)} %collective-permute-done.7.refs_1_), channel_id=1, source_target_pairs={{0,2},{1,3},{2,0},{3,1},{4,6},{5,7},{6,4},{7,5},{8,10},{9,11},{10,... | collective-permute-start | bytes 294920 | tf_op jit(solution)/shard_map/ppermute | solution.py:287
  22.8 0.4 collective-permute-done.10.refs_10_
  23.2 0.2 collective-permute-start.13
  23.3 0.4 collective-permute-start.11
  23.7 1.6 %collective-permute-done.4.refs_8_ = bf16[32,1536]{1,0:T(8,128)(2,1)S(1)} collective-permute-done((bf16[32,1536]{1,0:T(8,128)(2,1)S(1)}, bf16[32,1536]{1,0:T(8,128)(2,1)S(1)}, u32[]{:S(2)}, u32[]{:S(2)}) %collective-permute-start.4) | collective-permute-done | bytes 98336 | tf_op jit(solution)/shard_map/ppermute | solution.py:287
  25.3 1.7 %collective-permute-done.8.refs_9_ = bf16[32,1536]{1,0:T(8,128)(2,1)S(1)} collective-permute-done((bf16[32,1536]{1,0:T(8,128)(2,1)S(1)}, bf16[32,1536]{1,0:T(8,128)(2,1)S(1)}, u32[]{:S(2)}, u32[]{:S(2)}) %collective-permute-start.8) | collective-permute-done | bytes 98336 | tf_op jit(solution)/shard_map/ppermute | solution.py:287
  27.0 1.6 %shard_map.105 = (bf16[128,3072]{1,0:T(8,128)(2,1)S(1)}, bf16[128,3072]{1,0:T(8,128)(2,1)S(1)}, f32[128,336]{1,0:T(8,128)S(1)}, f32[128,336]{1,0:T(8,128)S(1)}, f32[128,336]{1,0:T(8,128)S(1)}) custom-call(bf16[32,1536]{1,0:T(8,128)(2,1)S(1)} %collective-permute-done.3.refs_0_, bf16[32,1536]{1,0:T(8,128)(2,1)S(1)} %collective-permute-done.7.refs_1_, ...), custom_call_target="tpu_custom_call" | custom-call | tf_op jit(solution)/shard_map/pallas_call | solution.py:109
  28.7 1.4 %shard_map.106 = (bf16[128,3072]{1,0:T(8,128)(2,1)S(1)}, bf16[128,3072]{1,0:T(8,128)(2,1)S(1)}, bf16[128,336]{1,0:T(8,128)(2,1)S(1)}, bf16[128,336]{1,0:T(8,128)...) custom-call(bf16[32,1536]{1,0:T(8,128)(2,1)S(1)} %collective-permute, ...), custom_call_target="tpu_custom_call", output_to_operand_aliasing={{0}: (7, {}), {1}: (8, {})} | custom-call | tf_op jit(solution)/shard_map/pallas_call | solution.py:109
  30.1 0.6 %collective-permute-start.18 = (bf16[128,1536]{1,0:T(8,128)(2,1)S(1)}, bf16[128,1536]{1,0:T(8,128)(2,1)S(1)}, u32[]{:S(2)}, u32[]{:S(2)}) collective-permute-start(bf16[128,1536]{1,0:T(8,128)(2,1)S(1)} %get-tuple-element.72), channel_id=1, source_target_pairs={{0,1},{1,0},{2,3},{3,2},{4,5},{5,4},{6,7},{7,6},{8,9},{9,8},{10,11... | collective-permute-start | bytes 1179656 | tf_op jit(solution)/shard_map/ppermute | solution.py:287
  30.7 0.6 %shard_map.107.own_ref = f32[128,1536]{1,0:T(8,128)S(1)} custom-call(bf16[256,336]{1,0:T(8,128)(2,1)S(1)} %get-tuple-element.71.grads_ref, bf16[336,3072]{1,0:T(8,128)(2,1)S(1)} %get-tuple-element.63.refs_12_.refs_4_.wg_ref, bf16[336,3072]{1,0:T(8,128)(2,1)S(1)} %get-tuple-element.64.refs_13_.refs_5_.wu_ref), custom_call_target="tpu_custom_call" | custom-call | flops 264241152 | bytes 5087232 | tf_op jit(solution)/shard_map/pallas_call | solution.py:109
  31.3 0.8 %collective-permute-done.18.other_ref = bf16[128,1536]{1,0:T(8,128)(2,1)S(1)} collective-permute-done((bf16[128,1536]{1,0:T(8,128)(2,1)S(1)}, bf16[128,1536]{1,0:T(8,128)(2,1)S(1)}, u32[]{:S(2)}, u32[]{:S(2)}) %collective-permute-start.18) | collective-permute-done | bytes 393248 | tf_op jit(solution)/shard_map/ppermute | solution.py:287
  32.1 0.1 shard_map.108
  32.1 1.5 %collective-permute-start.20 = (bf16[32,1536]{1,0:T(8,128)(2,1)S(1)}, bf16[32,1536]{1,0:T(8,128)(2,1)S(1)}, u32[]{:S(2)}, u32[]{:S(2)}) collective-permute-start(bf16[32,1536]{1,0:T(8,128)(2,1)S(1)} %get-tuple-element.81), channel_id=1, source_target_pairs={{0,4},{4,0},{8,12},{12,8},{1,5},{5,1},{9,13},{13,9},{2,6},{6,2},{1... | collective-permute-start | bytes 294920 | tf_op jit(solution)/shard_map/ppermute | solution.py:287
  33.7 1.5 %collective-permute-start.22 = (bf16[32,1536]{1,0:T(8,128)(2,1)S(1)}, bf16[32,1536]{1,0:T(8,128)(2,1)S(1)}, u32[]{:S(2)}, u32[]{:S(2)}) collective-permute-start(bf16[32,1536]{1,0:T(8,128)(2,1)S(1)} %get-tuple-element.89), channel_id=1, source_target_pairs={{0,20},{4,16},{8,28},{12,24},{16,4},{20,0},{24,12},{28,8},{1,21},{... | collective-permute-start | bytes 294920 | tf_op jit(solution)/shard_map/ppermute | solution.py:294
  35.2 0.5 %collective-permute-start.19 = (bf16[32,1664]{1,0:T(8,128)(2,1)S(1)}, bf16[32,1664]{1,0:T(8,128)(2,1)S(1)}, u32[]{:S(2)}, u32[]{:S(2)}) collective-permute-start(bf16[32,1664]{1,0:T(8,128)(2,1)S(1)} %get-tuple-element.74), channel_id=1, source_target_pairs={{0,16},{4,20},{8,24},{12,28},{16,0},{20,4},{24,8},{28,12},{1,17},{... | collective-permute-start | bytes 319496 | tf_op jit(solution)/shard_map/ppermute | solution.py:294
  35.7 1.6 %collective-permute-done.20.right_ref = bf16[32,1536]{1,0:T(8,128)(2,1)S(1)} collective-permute-done((bf16[32,1536]{1,0:T(8,128)(2,1)S(1)}, bf16[32,1536]{1,0:T(8,128)(2,1)S(1)}, u32[]{:S(2)}, u32[]{:S(2)}) %collective-permute-start.20) | collective-permute-done | bytes 98336 | tf_op jit(solution)/shard_map/ppermute | solution.py:287
  37.3 4.9 %collective-permute-start.21 = (bf16[32,1536]{1,0:T(8,128)(2,1)S(1)}, bf16[32,1536]{1,0:T(8,128)(2,1)S(1)}, u32[]{:S(2)}, u32[]{:S(2)}) collective-permute-start(bf16[32,1536]{1,0:T(8,128)(2,1)S(1)} %get-tuple-element.84), channel_id=1, source_target_pairs={{0,24},{4,28},{8,16},{12,20},{16,8},{20,12},{24,0},{28,4},{1,25},{... | collective-permute-start | bytes 294920 | tf_op jit(solution)/shard_map/ppermute | solution.py:294
  42.2 2.0 %convolution_convert_fusion.2 = bf16[336,3072]{1,0:T(8,128)(2,1)} fusion(bf16[128,336]{1,0:T(8,128)(2,1)S(1)} %get-tuple-element.85, bf16[128,3072]{1,0:T(8,128)(2,1)S(1)} %get-tuple-element.86), kind=kOutput, calls=%fused_computation.2 | convolution fusion | flops 265273344 | bytes 2936832 | tf_op jit(solution)/shard_map/dot_general | solution.py:40
  44.2 2.0 %convolution_convert_fusion.1 = bf16[336,3072]{1,0:T(8,128)(2,1)} fusion(bf16[128,336]{1,0:T(8,128)(2,1)S(1)} %get-tuple-element.87, bf16[128,3072]{1,0:T(8,128)(2,1)S(1)} %get-tuple-element.86), kind=kOutput, calls=%fused_computation.1 | convolution fusion | flops 265273344 | bytes 2936832 | tf_op jit(solution)/shard_map/dot_general | solution.py:40
  46.2 0.1 collective-permute-done.21.refs_0_
  46.3 0.3 shard_map.110
  46.6 0.1 collective-permute-start.23
  46.7 1.3 %collective-permute-start.24 = (bf16[16,1536]{1,0:T(8,128)(2,1)S(1)}, bf16[16,1536]{1,0:T(8,128)(2,1)S(1)}, u32[]{:S(2)}, u32[]{:S(2)}) collective-permute-start(bf16[16,1536]{1,0:T(8,128)(2,1)S(1)} %get-tuple-element.92), channel_id=1, source_target_pairs={{0,2},{1,3},{2,0},{3,1},{4,6},{5,7},{6,4},{7,5},{8,10},{9,11},{10,... | collective-permute-start | bytes 147464 | tf_op jit(solution)/shard_map/ppermute | solution.py:287
  48.0 0.6 %collective-permute-start.25 = (bf16[16,1536]{1,0:T(8,128)(2,1)S(1)}, bf16[16,1536]{1,0:T(8,128)(2,1)S(1)}, u32[]{:S(2)}, u32[]{:S(2)}) collective-permute-start(bf16[16,1536]{1,0:T(8,128)(2,1)S(1)} %get-tuple-element.93), channel_id=1, source_target_pairs={{0,3},{1,2},{2,1},{3,0},{4,7},{5,6},{6,5},{7,4},{8,11},{9,10},{10,... | collective-permute-start | bytes 147464 | tf_op jit(solution)/shard_map/ppermute | solution.py:287
  48.6 2.0 %fusion = bf16[1,336,3072]{2,1,0:T(8,128)(2,1)} fusion(bf16[128,336]{1,0:T(8,128)(2,1)S(1)} %get-tuple-element.96, bf16[128,3072]{1,0:T(8,128)(2,1)S(1)} %get-tuple-element.97), kind=kOutput, calls=%fused_computation.3 | convolution fusion | flops 265273344 | bytes 2936832 | tf_op jit(solution)/shard_map/dot_general | solution.py:40
  50.6 0.3 collective-permute-done.24.chip_ref
  50.9 0.8 %collective-permute-done.25.both_ref = bf16[16,1536]{1,0:T(8,128)(2,1)S(1)} collective-permute-done((bf16[16,1536]{1,0:T(8,128)(2,1)S(1)}, bf16[16,1536]{1,0:T(8,128)(2,1)S(1)}, u32[]{:S(2)}, u32[]{:S(2)}) %collective-permute-start.25) | collective-permute-done | bytes 49184 | tf_op jit(solution)/shard_map/ppermute | solution.py:287
  51.7 0.7 %shard_map.111 = bf16[16,3072]{1,0:T(8,128)(2,1)} custom-call(bf16[16,1536]{1,0:T(8,128)(2,1)S(1)} %get-tuple-element.90.own_ref, bf16[16,1536]{1,0:T(8,128)(2,1)S(1)} %collective-permute-done.23.core_ref, bf16[16,1536]{1,0:T(8,128)(2,1)S(1)} %collective-permute-done.24.chip_ref, bf16[16,1536]{1,0:T(8,128)(2,1)S(1)} %collective-permute-done.25.both_ref), custom_call_target="tpu_custom_call" | custom-call | tf_op jit(solution)/shard_map/pallas_call | solution.py:109
  (17 shorter events, 0.1 us)
Async XLA Ops:
  1.7 6.0 %collective-permute-start = (bf16[16,1664]{1,0:T(8,128)(2,1)S(1)}, bf16[16,1664]{1,0:T(8,128)(2,1)S(1)}, u32[]{:S(2)}, u32[]{:S(2)}) collective-permute-start(bf16[16,1664]{1,0:T(8,128)(2,1)S(1)} %get-tuple-element.52), channel_id=1, source_target_pairs={{0,1},{1,0},{2,3},{3,2},{4,5},{5,4},{6,7},{7,6},{8,9},{9,8},{10,11... | collective-permute-start | bytes 159752 | tf_op jit(solution)/shard_map/ppermute | solution.py:287
  2.2 5.5 %collective-permute-start.1 = (bf16[16,1664]{1,0:T(8,128)(2,1)S(1)}, bf16[16,1664]{1,0:T(8,128)(2,1)S(1)}, u32[]{:S(2)}, u32[]{:S(2)}) collective-permute-start(bf16[16,1664]{1,0:T(8,128)(2,1)S(1)} %get-tuple-element.53), channel_id=1, source_target_pairs={{0,2},{1,3},{2,0},{3,1},{4,6},{5,7},{6,4},{7,5},{8,10},{9,11},{10,... | collective-permute-start | bytes 159752 | tf_op jit(solution)/shard_map/ppermute | solution.py:287
  4.8 3.8 %collective-permute-start.2 = (bf16[16,1664]{1,0:T(8,128)(2,1)S(1)}, bf16[16,1664]{1,0:T(8,128)(2,1)S(1)}, u32[]{:S(2)}, u32[]{:S(2)}) collective-permute-start(bf16[16,1664]{1,0:T(8,128)(2,1)S(1)} %get-tuple-element.54), channel_id=1, source_target_pairs={{0,3},{1,2},{2,1},{3,0},{4,7},{5,6},{6,5},{7,4},{8,11},{9,10},{10,... | collective-permute-start | bytes 159752 | tf_op jit(solution)/shard_map/ppermute | solution.py:287
  9.0 8.0 %collective-permute-start.6 = (bf16[32,1536]{1,0:T(8,128)(2,1)S(1)}, bf16[32,1536]{1,0:T(8,128)(2,1)S(1)}, u32[]{:S(2)}, u32[]{:S(2)}) collective-permute-start(bf16[32,1536]{1,0:T(8,128)(2,1)S(1)} %get-tuple-element.62.refs_3_), channel_id=1, source_target_pairs={{0,8},{4,12},{8,0},{12,4},{1,9},{5,13},{9,1},{13,5},{2,10},{6,14},... | collective-permute-start | bytes 294920 | tf_op jit(solution)/shard_map/ppermute | solution.py:287
  11.6 6.0 %collective-permute-start.17 = (bf16[32,1536]{1,0:T(8,128)(2,1)S(1)}, bf16[32,1536]{1,0:T(8,128)(2,1)S(1)}, u32[]{:S(2)}, u32[]{:S(2)}) collective-permute-start(bf16[32,1536]{1,0:T(8,128)(2,1)S(1)} %get-tuple-element.62.refs_3_), channel_id=1, source_target_pairs={{0,1},{1,0},{2,3},{3,2},{4,5},{5,4},{6,7},{7,6},{8,9},{9,8},{10,11... | collective-permute-start | bytes 294920 | tf_op jit(solution)/shard_map/ppermute | solution.py:287
  11.6 7.2 %collective-permute-start.3 = (bf16[32,1536]{1,0:T(8,128)(2,1)S(1)}, bf16[32,1536]{1,0:T(8,128)(2,1)S(1)}, u32[]{:S(2)}, u32[]{:S(2)}) collective-permute-start(bf16[32,1536]{1,0:T(8,128)(2,1)S(1)} %get-tuple-element.62.refs_3_), channel_id=1, source_target_pairs={{0,4},{4,0},{8,12},{12,8},{1,5},{5,1},{9,13},{13,9},{2,6},{6,2},{1... | collective-permute-start | bytes 294920 | tf_op jit(solution)/shard_map/ppermute | solution.py:287
  13.2 5.8 %collective-permute-start.12 = (bf16[32,1536]{1,0:T(8,128)(2,1)S(1)}, bf16[32,1536]{1,0:T(8,128)(2,1)S(1)}, u32[]{:S(2)}, u32[]{:S(2)}) collective-permute-start(bf16[32,1536]{1,0:T(8,128)(2,1)S(1)} %get-tuple-element.62.refs_3_), channel_id=1, source_target_pairs={{0,2},{1,3},{2,0},{3,1},{4,6},{5,7},{6,4},{7,5},{8,10},{9,11},{10,... | collective-permute-start | bytes 294920 | tf_op jit(solution)/shard_map/ppermute | solution.py:287
  17.0 4.6 %collective-permute-start.7 = (bf16[32,1536]{1,0:T(8,128)(2,1)S(1)}, bf16[32,1536]{1,0:T(8,128)(2,1)S(1)}, u32[]{:S(2)}, u32[]{:S(2)}) collective-permute-start(bf16[32,1536]{1,0:T(8,128)(2,1)S(1)} %collective-permute-done.6.refs_2_), channel_id=1, source_target_pairs={{0,4},{4,0},{8,12},{12,8},{1,5},{5,1},{9,13},{13,9},{2,6},{6,2},{1... | collective-permute-start | bytes 294920 | tf_op jit(solution)/shard_map/ppermute | solution.py:287
  17.6 5.2 %collective-permute-start.16 = (bf16[32,1536]{1,0:T(8,128)(2,1)S(1)}, bf16[32,1536]{1,0:T(8,128)(2,1)S(1)}, u32[]{:S(2)}, u32[]{:S(2)}) collective-permute-start(bf16[32,1536]{1,0:T(8,128)(2,1)S(1)} %collective-permute-done.6.refs_2_), channel_id=1, source_target_pairs={{0,1},{1,0},{2,3},{3,2},{4,5},{5,4},{6,7},{7,6},{8,9},{9,8},{10,11... | collective-permute-start | bytes 294920 | tf_op jit(solution)/shard_map/ppermute | solution.py:287
  17.6 5.6 %collective-permute-start.10 = (bf16[32,1536]{1,0:T(8,128)(2,1)S(1)}, bf16[32,1536]{1,0:T(8,128)(2,1)S(1)}, u32[]{:S(2)}, u32[]{:S(2)}) collective-permute-start(bf16[32,1536]{1,0:T(8,128)(2,1)S(1)} %collective-permute-done.6.refs_2_), channel_id=1, source_target_pairs={{0,2},{1,3},{2,0},{3,1},{4,6},{5,7},{6,4},{7,5},{8,10},{9,11},{10,... | collective-permute-start | bytes 294920 | tf_op jit(solution)/shard_map/ppermute | solution.py:287
  18.8 4.6 %collective-permute-start.14 = (bf16[32,1536]{1,0:T(8,128)(2,1)S(1)}, bf16[32,1536]{1,0:T(8,128)(2,1)S(1)}, u32[]{:S(2)}, u32[]{:S(2)}) collective-permute-start(bf16[32,1536]{1,0:T(8,128)(2,1)S(1)} %collective-permute-done.3.refs_0_), channel_id=1, source_target_pairs={{0,1},{1,0},{2,3},{3,2},{4,5},{5,4},{6,7},{7,6},{8,9},{9,8},{10,11... | collective-permute-start | bytes 294920 | tf_op jit(solution)/shard_map/ppermute | solution.py:287
  19.0 6.3 %collective-permute-start.4 = (bf16[32,1536]{1,0:T(8,128)(2,1)S(1)}, bf16[32,1536]{1,0:T(8,128)(2,1)S(1)}, u32[]{:S(2)}, u32[]{:S(2)}) collective-permute-start(bf16[32,1536]{1,0:T(8,128)(2,1)S(1)} %collective-permute-done.3.refs_0_), channel_id=1, source_target_pairs={{0,2},{1,3},{2,0},{3,1},{4,6},{5,7},{6,4},{7,5},{8,10},{9,11},{10,... | collective-permute-start | bytes 294920 | tf_op jit(solution)/shard_map/ppermute | solution.py:287
  21.6 5.4 %collective-permute-start.8 = (bf16[32,1536]{1,0:T(8,128)(2,1)S(1)}, bf16[32,1536]{1,0:T(8,128)(2,1)S(1)}, u32[]{:S(2)}, u32[]{:S(2)}) collective-permute-start(bf16[32,1536]{1,0:T(8,128)(2,1)S(1)} %collective-permute-done.7.refs_1_), channel_id=1, source_target_pairs={{0,2},{1,3},{2,0},{3,1},{4,6},{5,7},{6,4},{7,5},{8,10},{9,11},{10,... | collective-permute-start | bytes 294920 | tf_op jit(solution)/shard_map/ppermute | solution.py:287
  22.8 4.2 %collective-permute-start.15 = (bf16[32,1536]{1,0:T(8,128)(2,1)S(1)}, bf16[32,1536]{1,0:T(8,128)(2,1)S(1)}, u32[]{:S(2)}, u32[]{:S(2)}) collective-permute-start(bf16[32,1536]{1,0:T(8,128)(2,1)S(1)} %collective-permute-done.7.refs_1_), channel_id=1, source_target_pairs={{0,1},{1,0},{2,3},{3,2},{4,5},{5,4},{6,7},{7,6},{8,9},{9,8},{10,11... | collective-permute-start | bytes 294920 | tf_op jit(solution)/shard_map/ppermute | solution.py:287
  23.2 5.5 %collective-permute-start.13 = (bf16[32,1536]{1,0:T(8,128)(2,1)S(1)}, bf16[32,1536]{1,0:T(8,128)(2,1)S(1)}, u32[]{:S(2)}, u32[]{:S(2)}) collective-permute-start(bf16[32,1536]{1,0:T(8,128)(2,1)S(1)} %collective-permute-done.12.refs_11_), channel_id=1, source_target_pairs={{0,1},{1,0},{2,3},{3,2},{4,5},{5,4},{6,7},{7,6},{8,9},{9,8},{10,11... | collective-permute-start | bytes 294920 | tf_op jit(solution)/shard_map/ppermute | solution.py:287
  23.3 5.3 %collective-permute-start.11 = (bf16[32,1536]{1,0:T(8,128)(2,1)S(1)}, bf16[32,1536]{1,0:T(8,128)(2,1)S(1)}, u32[]{:S(2)}, u32[]{:S(2)}) collective-permute-start(bf16[32,1536]{1,0:T(8,128)(2,1)S(1)} %collective-permute-done.10.refs_10_), channel_id=1, source_target_pairs={{0,1},{1,0},{2,3},{3,2},{4,5},{5,4},{6,7},{7,6},{8,9},{9,8},{10,11... | collective-permute-start | bytes 294920 | tf_op jit(solution)/shard_map/ppermute | solution.py:287
  25.3 3.4 %collective-permute-start.5 = (bf16[32,1536]{1,0:T(8,128)(2,1)S(1)}, bf16[32,1536]{1,0:T(8,128)(2,1)S(1)}, u32[]{:S(2)}, u32[]{:S(2)}) collective-permute-start(bf16[32,1536]{1,0:T(8,128)(2,1)S(1)} %collective-permute-done.4.refs_8_), channel_id=1, source_target_pairs={{0,1},{1,0},{2,3},{3,2},{4,5},{5,4},{6,7},{7,6},{8,9},{9,8},{10,11... | collective-permute-start | bytes 294920 | tf_op jit(solution)/shard_map/ppermute | solution.py:287
  27.0 1.7 %collective-permute-start.9 = (bf16[32,1536]{1,0:T(8,128)(2,1)S(1)}, bf16[32,1536]{1,0:T(8,128)(2,1)S(1)}, u32[]{:S(2)}, u32[]{:S(2)}) collective-permute-start(bf16[32,1536]{1,0:T(8,128)(2,1)S(1)} %collective-permute-done.8.refs_9_), channel_id=1, source_target_pairs={{0,1},{1,0},{2,3},{3,2},{4,5},{5,4},{6,7},{7,6},{8,9},{9,8},{10,11... | collective-permute-start | bytes 294920 | tf_op jit(solution)/shard_map/ppermute | solution.py:287
  30.1 1.9 %collective-permute-start.18 = (bf16[128,1536]{1,0:T(8,128)(2,1)S(1)}, bf16[128,1536]{1,0:T(8,128)(2,1)S(1)}, u32[]{:S(2)}, u32[]{:S(2)}) collective-permute-start(bf16[128,1536]{1,0:T(8,128)(2,1)S(1)} %get-tuple-element.72), channel_id=1, source_target_pairs={{0,1},{1,0},{2,3},{3,2},{4,5},{5,4},{6,7},{7,6},{8,9},{9,8},{10,11... | collective-permute-start | bytes 1179656 | tf_op jit(solution)/shard_map/ppermute | solution.py:287
  32.1 5.1 %collective-permute-start.20 = (bf16[32,1536]{1,0:T(8,128)(2,1)S(1)}, bf16[32,1536]{1,0:T(8,128)(2,1)S(1)}, u32[]{:S(2)}, u32[]{:S(2)}) collective-permute-start(bf16[32,1536]{1,0:T(8,128)(2,1)S(1)} %get-tuple-element.81), channel_id=1, source_target_pairs={{0,4},{4,0},{8,12},{12,8},{1,5},{5,1},{9,13},{13,9},{2,6},{6,2},{1... | collective-permute-start | bytes 294920 | tf_op jit(solution)/shard_map/ppermute | solution.py:287
  33.7 12.7 %collective-permute-start.22 = (bf16[32,1536]{1,0:T(8,128)(2,1)S(1)}, bf16[32,1536]{1,0:T(8,128)(2,1)S(1)}, u32[]{:S(2)}, u32[]{:S(2)}) collective-permute-start(bf16[32,1536]{1,0:T(8,128)(2,1)S(1)} %get-tuple-element.89), channel_id=1, source_target_pairs={{0,20},{4,16},{8,28},{12,24},{16,4},{20,0},{24,12},{28,8},{1,21},{... | collective-permute-start | bytes 294920 | tf_op jit(solution)/shard_map/ppermute | solution.py:294
  35.2 11.2 %collective-permute-start.19 = (bf16[32,1664]{1,0:T(8,128)(2,1)S(1)}, bf16[32,1664]{1,0:T(8,128)(2,1)S(1)}, u32[]{:S(2)}, u32[]{:S(2)}) collective-permute-start(bf16[32,1664]{1,0:T(8,128)(2,1)S(1)} %get-tuple-element.74), channel_id=1, source_target_pairs={{0,16},{4,20},{8,24},{12,28},{16,0},{20,4},{24,8},{28,12},{1,17},{... | collective-permute-start | bytes 319496 | tf_op jit(solution)/shard_map/ppermute | solution.py:294
  37.3 9.0 %collective-permute-start.21 = (bf16[32,1536]{1,0:T(8,128)(2,1)S(1)}, bf16[32,1536]{1,0:T(8,128)(2,1)S(1)}, u32[]{:S(2)}, u32[]{:S(2)}) collective-permute-start(bf16[32,1536]{1,0:T(8,128)(2,1)S(1)} %get-tuple-element.84), channel_id=1, source_target_pairs={{0,24},{4,28},{8,16},{12,20},{16,8},{20,12},{24,0},{28,4},{1,25},{... | collective-permute-start | bytes 294920 | tf_op jit(solution)/shard_map/ppermute | solution.py:294
  46.6 4.0 %collective-permute-start.23 = (bf16[16,1536]{1,0:T(8,128)(2,1)S(1)}, bf16[16,1536]{1,0:T(8,128)(2,1)S(1)}, u32[]{:S(2)}, u32[]{:S(2)}) collective-permute-start(bf16[16,1536]{1,0:T(8,128)(2,1)S(1)} %get-tuple-element.91), channel_id=1, source_target_pairs={{0,1},{1,0},{2,3},{3,2},{4,5},{5,4},{6,7},{7,6},{8,9},{9,8},{10,11... | collective-permute-start | bytes 147464 | tf_op jit(solution)/shard_map/ppermute | solution.py:287
  46.7 4.2 %collective-permute-start.24 = (bf16[16,1536]{1,0:T(8,128)(2,1)S(1)}, bf16[16,1536]{1,0:T(8,128)(2,1)S(1)}, u32[]{:S(2)}, u32[]{:S(2)}) collective-permute-start(bf16[16,1536]{1,0:T(8,128)(2,1)S(1)} %get-tuple-element.92), channel_id=1, source_target_pairs={{0,2},{1,3},{2,0},{3,1},{4,6},{5,7},{6,4},{7,5},{8,10},{9,11},{10,... | collective-permute-start | bytes 147464 | tf_op jit(solution)/shard_map/ppermute | solution.py:287
  48.0 3.7 %collective-permute-start.25 = (bf16[16,1536]{1,0:T(8,128)(2,1)S(1)}, bf16[16,1536]{1,0:T(8,128)(2,1)S(1)}, u32[]{:S(2)}, u32[]{:S(2)}) collective-permute-start(bf16[16,1536]{1,0:T(8,128)(2,1)S(1)} %get-tuple-element.93), channel_id=1, source_target_pairs={{0,3},{1,2},{2,1},{3,0},{4,7},{5,6},{6,5},{7,4},{8,11},{9,10},{10,... | collective-permute-start | bytes 147464 | tf_op jit(solution)/shard_map/ppermute | solution.py:287

commit v11 on v8

--- a/solution.py
+++ b/solution.py
@@ -178,7 +178,7 @@
     data = wide - FLAG
     cap = slots_ref.shape[0]
     e = lax.axis_index("et")
-    for steps, part in enumerate(parts):
+    for steps, part in zip((0, 2, 3, 1), parts):
         all_rows[pl.ds(pl.multiple_of((e ^ steps) * rows, 16), rows), :] = part[...]
     flags = all_rows[:, data:]
     before = lax.broadcasted_iota(jnp.int32, (tokens, tokens), 0)
@@ -254,7 +254,8 @@
     for k, out in enumerate(outs):
         rows = pl.ds(k * cap, cap)
         out[:, :half] = (own_ref[rows, :] + other_ref[rows, :].astype(F32)).astype(BF16)
-    outs[3][:, half:] = pick_ref[...]
+    for out in outs[1::2]:
+        out[:, half:] = pick_ref[...]
 
 
 def add_kernel(left_ref, right_ref, out_ref, ready_ref):
@@ -268,7 +269,7 @@
     e = lax.axis_index("et")
     total = own_ref[:, :half].astype(F32)
     for other in others:
-        total += other[...].astype(F32)
+        total += other[:, :half].astype(F32)
     tokens_ref[...] = contract(own_ref[:, half:], total.astype(BF16), 0, 0).astype(BF16)
     for steps, out in enumerate(outs):
         out[...] = tokens_ref[pl.ds(pl.multiple_of((e ^ steps) * rows, 16), rows), :]
@@ -319,7 +320,7 @@
         ],
         space=HBM,
     )
-    arrived = [packed[0]] + [swap(packed[s], "et", s) for s in (1, 2, 3)]
+    arrived = [packed[0]] + [swap(packed[s], "et", s) for s in (2, 3, 1)]
     weights = call(
         stage_kernel,
         [like((hidden, width))] * 3,
@@ -365,7 +366,7 @@
     )
     to_last, to_near, to_far, home = call(
         pair_kernel,
-        [like((cap, half))] * 3 + [like((cap, half + FLAG))],
+        [like((cap, half)), like((cap, half + FLAG)), like((cap, half)), like((cap, half + FLAG))],
         own_terms,
         theirs,
         pick,

time: 51.3 us -> 51.3 us (level)
  starting transfers between devices: 21.8 us -> 22.6 us
  waiting for transfers between devices: 13.6 us -> 12.8 us
    ppermute x23, waiting for transfers between devices: 13.1 us -> 12 us  [swap(): return lax.ppermute(value, axis, spread(steps))]
    ppermute x23, starting transfers between devices: 15.6 us -> 16.4 us  [swap(): return lax.ppermute(value, axis, spread(steps))]
where the time goes in v11:
time: 51.3 us; the launch traced here: 51.2 us
  starting transfers between devices  22.6 us (44%)
  waiting for transfers between devices  12.8 us (25%)
  Pallas kernels  8.93 us (17%)
  matrix products  6.07 us (12%)
  between operations  0.76 us (1%)
    ppermute x23, starting transfers between devices, swap(): return lax.ppermute(value, axis, spread(steps))  16.4 us
    ppermute x23, waiting for transfers between devices, swap(): return lax.ppermute(value, axis, spread(steps))  12 us
    pallas_call x10, Pallas kernels, call(): pl.pallas_call(kernel, out_shape=outs, in_specs=[space] * len(args), out_...  8.93 us
    ppermute x3, starting transfers between devices, hand(): return lax.ppermute(value, ('pipe', 'dp'), pairs)  6.17 us
    dot_general x3, matrix products, contract(): lax.dot_general(left, right, (((left_dim,), (right_dim,)), ((), ())), pre...  6.07 us
  transfers between devices with their start and end apart: 26, of which 11 were waited for; matrix products, arithmetic and copies ran while one was open for 12% of the time, Pallas kernels for 10%

profile of v11, /device:TPU:0, one launch (start us, length us, event | category | flops | bytes accessed | tf_op | source)
XLA Modules:
  0.0 51.2 jit_solution(10911020836102962470)
XLA Ops:
  0.6 1.1 %shard_map.102 = (bf16[16,1664]{1,0:T(8,128)(2,1)S(1)}, bf16[16,1664]{1,0:T(8,128)(2,1)S(1)}, bf16[16,1664]{1,0:T(8,128)(2,1)S(1)}, bf16[16,1664]{1,0:T(8,128)(2,1)S(1)}) custom-call(bf16[16,3072]{1,0:T(8,128)(2,1)} %bitcast.27, bf16[16,3072]{1,0:T(8,128)(2,1)} %bitcast.28, s32[4,16]{1,0:T(4,128)} %bitcast.30, f32[4,16]{1,0:T(4,128)} %bitcast.31), custom_call_target="tpu_custom_call" | custom-call | bytes 410112 | tf_op jit(solution)/shard_map/pallas_call | solution.py:109
  1.7 3.0 %collective-permute-start = (bf16[16,1664]{1,0:T(8,128)(2,1)S(1)}, bf16[16,1664]{1,0:T(8,128)(2,1)S(1)}, u32[]{:S(2)}, u32[]{:S(2)}) collective-permute-start(bf16[16,1664]{1,0:T(8,128)(2,1)S(1)} %get-tuple-element.52), channel_id=1, source_target_pairs={{0,2},{1,3},{2,0},{3,1},{4,6},{5,7},{6,4},{7,5},{8,10},{9,11},{10,... | collective-permute-start | bytes 159752 | tf_op jit(solution)/shard_map/ppermute | solution.py:288
  4.7 0.0 collective-permute-start.1
  4.8 0.2 collective-permute-start.2
  4.9 2.8 %shard_map.103 = (bf16[336,3072]{1,0:T(8,128)(2,1)S(1)}, bf16[336,3072]{1,0:T(8,128)(2,1)S(1)}, bf16[336,3072]{1,0:T(8,128)(2,1)S(1)}) custom-call(bf16[336,3072]{1,0:T(8,128)(2,1)} %bitcast.22, bf16[336,3072]{1,0:T(8,128)(2,1)} %bitcast.23, bf16[336,3072]{1,0:T(8,128)(2,1)} %bitcast.24), custom_call_target="tpu_custom_call" | custom-call | bytes 12386304 | tf_op jit(solution)/shard_map/pallas_call | solution.py:109
  7.8 0.0 collective-permute-done.refs_1_
  7.8 0.8 %collective-permute-done.1.refs_2_ = bf16[16,1664]{1,0:T(8,128)(2,1)S(1)} collective-permute-done((bf16[16,1664]{1,0:T(8,128)(2,1)S(1)}, bf16[16,1664]{1,0:T(8,128)(2,1)S(1)}, u32[]{:S(2)}, u32[]{:S(2)}) %collective-permute-start.1) | collective-permute-done | bytes 53280 | tf_op jit(solution)/shard_map/ppermute | solution.py:288
  8.6 0.0 collective-permute-done.2.refs_3_
  8.6 0.4 shard_map.104
  9.0 2.7 %collective-permute-start.9 = (bf16[32,1536]{1,0:T(8,128)(2,1)S(1)}, bf16[32,1536]{1,0:T(8,128)(2,1)S(1)}, u32[]{:S(2)}, u32[]{:S(2)}) collective-permute-start(bf16[32,1536]{1,0:T(8,128)(2,1)S(1)} %get-tuple-element.62.refs_3_), channel_id=1, source_target_pairs={{0,8},{4,12},{8,0},{12,4},{1,9},{5,13},{9,1},{13,5},{2,10},{6,14},... | collective-permute-start | bytes 294920 | tf_op jit(solution)/shard_map/ppermute | solution.py:288
  11.6 0.0 collective-permute-start.17
  11.6 1.6 %collective-permute-start.6 = (bf16[32,1536]{1,0:T(8,128)(2,1)S(1)}, bf16[32,1536]{1,0:T(8,128)(2,1)S(1)}, u32[]{:S(2)}, u32[]{:S(2)}) collective-permute-start(bf16[32,1536]{1,0:T(8,128)(2,1)S(1)} %get-tuple-element.62.refs_3_), channel_id=1, source_target_pairs={{0,4},{4,0},{8,12},{12,8},{1,5},{5,1},{9,13},{13,9},{2,6},{6,2},{1... | collective-permute-start | bytes 294920 | tf_op jit(solution)/shard_map/ppermute | solution.py:288
  13.2 1.1 %collective-permute-start.12 = (bf16[32,1536]{1,0:T(8,128)(2,1)S(1)}, bf16[32,1536]{1,0:T(8,128)(2,1)S(1)}, u32[]{:S(2)}, u32[]{:S(2)}) collective-permute-start(bf16[32,1536]{1,0:T(8,128)(2,1)S(1)} %get-tuple-element.62.refs_3_), channel_id=1, source_target_pairs={{0,2},{1,3},{2,0},{3,1},{4,6},{5,7},{6,4},{7,5},{8,10},{9,11},{10,... | collective-permute-start | bytes 294920 | tf_op jit(solution)/shard_map/ppermute | solution.py:288
  14.4 0.2 collective-permute-start.3
  14.6 2.0 %collective-permute-done.9.refs_2_ = bf16[32,1536]{1,0:T(8,128)(2,1)S(1)} collective-permute-done((bf16[32,1536]{1,0:T(8,128)(2,1)S(1)}, bf16[32,1536]{1,0:T(8,128)(2,1)S(1)}, u32[]{:S(2)}, u32[]{:S(2)}) %collective-permute-start.9) | collective-permute-done | bytes 98336 | tf_op jit(solution)/shard_map/ppermute | solution.py:288
  16.6 0.0 collective-permute-start.16
  16.6 1.4 %collective-permute-start.10 = (bf16[32,1536]{1,0:T(8,128)(2,1)S(1)}, bf16[32,1536]{1,0:T(8,128)(2,1)S(1)}, u32[]{:S(2)}, u32[]{:S(2)}) collective-permute-start(bf16[32,1536]{1,0:T(8,128)(2,1)S(1)} %collective-permute-done.9.refs_2_), channel_id=1, source_target_pairs={{0,2},{1,3},{2,0},{3,1},{4,6},{5,7},{6,4},{7,5},{8,10},{9,11},{10,... | collective-permute-start | bytes 294920 | tf_op jit(solution)/shard_map/ppermute | solution.py:288
  18.0 0.2 collective-permute-start.15
  18.2 1.0 %collective-permute-start.7 = (bf16[32,1536]{1,0:T(8,128)(2,1)S(1)}, bf16[32,1536]{1,0:T(8,128)(2,1)S(1)}, u32[]{:S(2)}, u32[]{:S(2)}) collective-permute-start(bf16[32,1536]{1,0:T(8,128)(2,1)S(1)} %collective-permute-done.6.refs_1_), channel_id=1, source_target_pairs={{0,2},{1,3},{2,0},{3,1},{4,6},{5,7},{6,4},{7,5},{8,10},{9,11},{10,... | collective-permute-start | bytes 294920 | tf_op jit(solution)/shard_map/ppermute | solution.py:288
  19.3 1.6 %collective-permute-done.3.refs_0_ = bf16[32,1536]{1,0:T(8,128)(2,1)S(1)} collective-permute-done((bf16[32,1536]{1,0:T(8,128)(2,1)S(1)}, bf16[32,1536]{1,0:T(8,128)(2,1)S(1)}, u32[]{:S(2)}, u32[]{:S(2)}) %collective-permute-start.3) | collective-permute-done | bytes 98336 | tf_op jit(solution)/shard_map/ppermute | solution.py:288
  20.9 0.9 %collective-permute-start.4 = (bf16[32,1536]{1,0:T(8,128)(2,1)S(1)}, bf16[32,1536]{1,0:T(8,128)(2,1)S(1)}, u32[]{:S(2)}, u32[]{:S(2)}) collective-permute-start(bf16[32,1536]{1,0:T(8,128)(2,1)S(1)} %collective-permute-done.3.refs_0_), channel_id=1, source_target_pairs={{0,2},{1,3},{2,0},{3,1},{4,6},{5,7},{6,4},{7,5},{8,10},{9,11},{10,... | collective-permute-start | bytes 294920 | tf_op jit(solution)/shard_map/ppermute | solution.py:288
  21.8 0.4 collective-permute-done.10.refs_10_
  22.2 0.1 collective-permute-start.13
  22.3 0.4 collective-permute-start.11
  22.7 1.6 %collective-permute-done.7.refs_9_ = bf16[32,1536]{1,0:T(8,128)(2,1)S(1)} collective-permute-done((bf16[32,1536]{1,0:T(8,128)(2,1)S(1)}, bf16[32,1536]{1,0:T(8,128)(2,1)S(1)}, u32[]{:S(2)}, u32[]{:S(2)}) %collective-permute-start.7) | collective-permute-done | bytes 98336 | tf_op jit(solution)/shard_map/ppermute | solution.py:288
  24.3 1.7 %collective-permute-done.4.refs_8_ = bf16[32,1536]{1,0:T(8,128)(2,1)S(1)} collective-permute-done((bf16[32,1536]{1,0:T(8,128)(2,1)S(1)}, bf16[32,1536]{1,0:T(8,128)(2,1)S(1)}, u32[]{:S(2)}, u32[]{:S(2)}) %collective-permute-start.4) | collective-permute-done | bytes 98336 | tf_op jit(solution)/shard_map/ppermute | solution.py:288
  26.0 1.6 %shard_map.105 = (bf16[128,3072]{1,0:T(8,128)(2,1)S(1)}, bf16[128,3072]{1,0:T(8,128)(2,1)S(1)}, f32[128,336]{1,0:T(8,128)S(1)}, f32[128,336]{1,0:T(8,128)S(1)}, f32[128,336]{1,0:T(8,128)S(1)}) custom-call(bf16[32,1536]{1,0:T(8,128)(2,1)S(1)} %collective-permute-done.3.refs_0_, bf16[32,1536]{1,0:T(8,128)(2,1)S(1)} %collective-permute-done.6.refs_1_, ...), custom_call_target="tpu_custom_call" | custom-call | tf_op jit(solution)/shard_map/pallas_call | solution.py:109
  27.7 1.4 %shard_map.106 = (bf16[128,3072]{1,0:T(8,128)(2,1)S(1)}, bf16[128,3072]{1,0:T(8,128)(2,1)S(1)}, bf16[128,336]{1,0:T(8,128)(2,1)S(1)}, bf16[128,336]{1,0:T(8,128)...) custom-call(bf16[32,1536]{1,0:T(8,128)(2,1)S(1)} %collective-permute, ...), custom_call_target="tpu_custom_call", output_to_operand_aliasing={{0}: (7, {}), {1}: (8, {})} | custom-call | tf_op jit(solution)/shard_map/pallas_call | solution.py:109
  29.1 0.6 %collective-permute-start.18 = (bf16[128,1536]{1,0:T(8,128)(2,1)S(1)}, bf16[128,1536]{1,0:T(8,128)(2,1)S(1)}, u32[]{:S(2)}, u32[]{:S(2)}) collective-permute-start(bf16[128,1536]{1,0:T(8,128)(2,1)S(1)} %get-tuple-element.72), channel_id=1, source_target_pairs={{0,1},{1,0},{2,3},{3,2},{4,5},{5,4},{6,7},{7,6},{8,9},{9,8},{10,11... | collective-permute-start | bytes 1179656 | tf_op jit(solution)/shard_map/ppermute | solution.py:288
  29.7 0.6 %shard_map.107.own_ref = f32[128,1536]{1,0:T(8,128)S(1)} custom-call(bf16[256,336]{1,0:T(8,128)(2,1)S(1)} %get-tuple-element.71.grads_ref, bf16[336,3072]{1,0:T(8,128)(2,1)S(1)} %get-tuple-element.63.refs_12_.refs_4_.wg_ref, bf16[336,3072]{1,0:T(8,128)(2,1)S(1)} %get-tuple-element.64.refs_13_.refs_5_.wu_ref), custom_call_target="tpu_custom_call" | custom-call | flops 264241152 | bytes 5087232 | tf_op jit(solution)/shard_map/pallas_call | solution.py:109
  30.2 0.8 %collective-permute-done.18.other_ref = bf16[128,1536]{1,0:T(8,128)(2,1)S(1)} collective-permute-done((bf16[128,1536]{1,0:T(8,128)(2,1)S(1)}, bf16[128,1536]{1,0:T(8,128)(2,1)S(1)}, u32[]{:S(2)}, u32[]{:S(2)}) %collective-permute-start.18) | collective-permute-done | bytes 393248 | tf_op jit(solution)/shard_map/ppermute | solution.py:288
  31.0 0.1 shard_map.108
  31.1 1.0 %collective-permute-start.20 = (bf16[32,1536]{1,0:T(8,128)(2,1)S(1)}, bf16[32,1536]{1,0:T(8,128)(2,1)S(1)}, u32[]{:S(2)}, u32[]{:S(2)}) collective-permute-start(bf16[32,1536]{1,0:T(8,128)(2,1)S(1)} %get-tuple-element.81), channel_id=1, source_target_pairs={{0,4},{4,0},{8,12},{12,8},{1,5},{5,1},{9,13},{13,9},{2,6},{6,2},{1... | collective-permute-start | bytes 294920 | tf_op jit(solution)/shard_map/ppermute | solution.py:288
  32.1 1.5 %collective-permute-start.19 = (bf16[32,1664]{1,0:T(8,128)(2,1)S(1)}, bf16[32,1664]{1,0:T(8,128)(2,1)S(1)}, u32[]{:S(2)}, u32[]{:S(2)}) collective-permute-start(bf16[32,1664]{1,0:T(8,128)(2,1)S(1)} %get-tuple-element.74), channel_id=1, source_target_pairs={{0,16},{4,20},{8,24},{12,28},{16,0},{20,4},{24,8},{28,12},{1,17},{... | collective-permute-start | bytes 319496 | tf_op jit(solution)/shard_map/ppermute | solution.py:295
  33.6 1.1 %collective-permute-start.22 = (bf16[32,1664]{1,0:T(8,128)(2,1)S(1)}, bf16[32,1664]{1,0:T(8,128)(2,1)S(1)}, u32[]{:S(2)}, u32[]{:S(2)}) collective-permute-start(bf16[32,1664]{1,0:T(8,128)(2,1)S(1)} %get-tuple-element.89), channel_id=1, source_target_pairs={{0,20},{4,16},{8,28},{12,24},{16,4},{20,0},{24,12},{28,8},{1,21},{... | collective-permute-start | bytes 319496 | tf_op jit(solution)/shard_map/ppermute | solution.py:295
  34.7 1.9 %collective-permute-done.20.right_ref = bf16[32,1536]{1,0:T(8,128)(2,1)S(1)} collective-permute-done((bf16[32,1536]{1,0:T(8,128)(2,1)S(1)}, bf16[32,1536]{1,0:T(8,128)(2,1)S(1)}, u32[]{:S(2)}, u32[]{:S(2)}) %collective-permute-start.20) | collective-permute-done | bytes 98336 | tf_op jit(solution)/shard_map/ppermute | solution.py:288
  36.5 3.6 %collective-permute-start.21 = (bf16[32,1536]{1,0:T(8,128)(2,1)S(1)}, bf16[32,1536]{1,0:T(8,128)(2,1)S(1)}, u32[]{:S(2)}, u32[]{:S(2)}) collective-permute-start(bf16[32,1536]{1,0:T(8,128)(2,1)S(1)} %get-tuple-element.84), channel_id=1, source_target_pairs={{0,24},{4,28},{8,16},{12,20},{16,8},{20,12},{24,0},{28,4},{1,25},{... | collective-permute-start | bytes 294920 | tf_op jit(solution)/shard_map/ppermute | solution.py:295
  40.1 2.0 %convolution_convert_fusion.2 = bf16[336,3072]{1,0:T(8,128)(2,1)} fusion(bf16[128,336]{1,0:T(8,128)(2,1)S(1)} %get-tuple-element.85, bf16[128,3072]{1,0:T(8,128)(2,1)S(1)} %get-tuple-element.86), kind=kOutput, calls=%fused_computation.2 | convolution fusion | flops 265273344 | bytes 2936832 | tf_op jit(solution)/shard_map/dot_general | solution.py:40
  42.1 2.0 %convolution_convert_fusion.1 = bf16[336,3072]{1,0:T(8,128)(2,1)} fusion(bf16[128,336]{1,0:T(8,128)(2,1)S(1)} %get-tuple-element.87, bf16[128,3072]{1,0:T(8,128)(2,1)S(1)} %get-tuple-element.86), kind=kOutput, calls=%fused_computation.1 | convolution fusion | flops 265273344 | bytes 2936832 | tf_op jit(solution)/shard_map/dot_general | solution.py:40
  44.2 0.8 %collective-permute-done.21.refs_0_ = bf16[32,1536]{1,0:T(8,128)(2,1)S(1)} collective-permute-done((bf16[32,1536]{1,0:T(8,128)(2,1)S(1)}, bf16[32,1536]{1,0:T(8,128)(2,1)S(1)}, u32[]{:S(2)}, u32[]{:S(2)}) %collective-permute-start.21) | collective-permute-done | bytes 98336 | tf_op jit(solution)/shard_map/ppermute | solution.py:295
  45.0 0.3 shard_map.110
  45.3 0.1 collective-permute-start.23
  45.4 1.5 %collective-permute-start.24 = (bf16[16,1536]{1,0:T(8,128)(2,1)S(1)}, bf16[16,1536]{1,0:T(8,128)(2,1)S(1)}, u32[]{:S(2)}, u32[]{:S(2)}) collective-permute-start(bf16[16,1536]{1,0:T(8,128)(2,1)S(1)} %get-tuple-element.92), channel_id=1, source_target_pairs={{0,2},{1,3},{2,0},{3,1},{4,6},{5,7},{6,4},{7,5},{8,10},{9,11},{10,... | collective-permute-start | bytes 147464 | tf_op jit(solution)/shard_map/ppermute | solution.py:288
  46.8 0.4 collective-permute-start.25
  47.2 2.0 %fusion = bf16[1,336,3072]{2,1,0:T(8,128)(2,1)} fusion(bf16[128,336]{1,0:T(8,128)(2,1)S(1)} %get-tuple-element.96, bf16[128,3072]{1,0:T(8,128)(2,1)S(1)} %get-tuple-element.97), kind=kOutput, calls=%fused_computation.3 | convolution fusion | flops 265273344 | bytes 2936832 | tf_op jit(solution)/shard_map/dot_general | solution.py:40
  49.3 0.3 collective-permute-done.24.chip_ref
  49.5 1.0 %collective-permute-done.25.both_ref = bf16[16,1536]{1,0:T(8,128)(2,1)S(1)} collective-permute-done((bf16[16,1536]{1,0:T(8,128)(2,1)S(1)}, bf16[16,1536]{1,0:T(8,128)(2,1)S(1)}, u32[]{:S(2)}, u32[]{:S(2)}) %collective-permute-start.25) | collective-permute-done | bytes 49184 | tf_op jit(solution)/shard_map/ppermute | solution.py:288
  50.5 0.7 %shard_map.111 = bf16[16,3072]{1,0:T(8,128)(2,1)} custom-call(bf16[16,1536]{1,0:T(8,128)(2,1)S(1)} %get-tuple-element.90.own_ref, bf16[16,1536]{1,0:T(8,128)(2,1)S(1)} %collective-permute-done.23.core_ref, bf16[16,1536]{1,0:T(8,128)(2,1)S(1)} %collective-permute-done.24.chip_ref, bf16[16,1536]{1,0:T(8,128)(2,1)S(1)} %collective-permute-done.25.both_ref), custom_call_target="tpu_custom_call" | custom-call | tf_op jit(solution)/shard_map/pallas_call | solution.py:109
  (17 shorter events, 0.1 us)
Async XLA Ops:
  1.7 6.1 %collective-permute-start = (bf16[16,1664]{1,0:T(8,128)(2,1)S(1)}, bf16[16,1664]{1,0:T(8,128)(2,1)S(1)}, u32[]{:S(2)}, u32[]{:S(2)}) collective-permute-start(bf16[16,1664]{1,0:T(8,128)(2,1)S(1)} %get-tuple-element.52), channel_id=1, source_target_pairs={{0,2},{1,3},{2,0},{3,1},{4,6},{5,7},{6,4},{7,5},{8,10},{9,11},{10,... | collective-permute-start | bytes 159752 | tf_op jit(solution)/shard_map/ppermute | solution.py:288
  4.7 3.9 %collective-permute-start.1 = (bf16[16,1664]{1,0:T(8,128)(2,1)S(1)}, bf16[16,1664]{1,0:T(8,128)(2,1)S(1)}, u32[]{:S(2)}, u32[]{:S(2)}) collective-permute-start(bf16[16,1664]{1,0:T(8,128)(2,1)S(1)} %get-tuple-element.53), channel_id=1, source_target_pairs={{0,3},{1,2},{2,1},{3,0},{4,7},{5,6},{6,5},{7,4},{8,11},{9,10},{10,... | collective-permute-start | bytes 159752 | tf_op jit(solution)/shard_map/ppermute | solution.py:288
  4.8 3.9 %collective-permute-start.2 = (bf16[16,1664]{1,0:T(8,128)(2,1)S(1)}, bf16[16,1664]{1,0:T(8,128)(2,1)S(1)}, u32[]{:S(2)}, u32[]{:S(2)}) collective-permute-start(bf16[16,1664]{1,0:T(8,128)(2,1)S(1)} %get-tuple-element.54), channel_id=1, source_target_pairs={{0,1},{1,0},{2,3},{3,2},{4,5},{5,4},{6,7},{7,6},{8,9},{9,8},{10,11... | collective-permute-start | bytes 159752 | tf_op jit(solution)/shard_map/ppermute | solution.py:288
  9.0 7.6 %collective-permute-start.9 = (bf16[32,1536]{1,0:T(8,128)(2,1)S(1)}, bf16[32,1536]{1,0:T(8,128)(2,1)S(1)}, u32[]{:S(2)}, u32[]{:S(2)}) collective-permute-start(bf16[32,1536]{1,0:T(8,128)(2,1)S(1)} %get-tuple-element.62.refs_3_), channel_id=1, source_target_pairs={{0,8},{4,12},{8,0},{12,4},{1,9},{5,13},{9,1},{13,5},{2,10},{6,14},... | collective-permute-start | bytes 294920 | tf_op jit(solution)/shard_map/ppermute | solution.py:288
  11.6 4.9 %collective-permute-start.17 = (bf16[32,1536]{1,0:T(8,128)(2,1)S(1)}, bf16[32,1536]{1,0:T(8,128)(2,1)S(1)}, u32[]{:S(2)}, u32[]{:S(2)}) collective-permute-start(bf16[32,1536]{1,0:T(8,128)(2,1)S(1)} %get-tuple-element.62.refs_3_), channel_id=1, source_target_pairs={{0,1},{1,0},{2,3},{3,2},{4,5},{5,4},{6,7},{7,6},{8,9},{9,8},{10,11... | collective-permute-start | bytes 294920 | tf_op jit(solution)/shard_map/ppermute | solution.py:288
  11.6 6.4 %collective-permute-start.6 = (bf16[32,1536]{1,0:T(8,128)(2,1)S(1)}, bf16[32,1536]{1,0:T(8,128)(2,1)S(1)}, u32[]{:S(2)}, u32[]{:S(2)}) collective-permute-start(bf16[32,1536]{1,0:T(8,128)(2,1)S(1)} %get-tuple-element.62.refs_3_), channel_id=1, source_target_pairs={{0,4},{4,0},{8,12},{12,8},{1,5},{5,1},{9,13},{13,9},{2,6},{6,2},{1... | collective-permute-start | bytes 294920 | tf_op jit(solution)/shard_map/ppermute | solution.py:288
  13.2 5.0 %collective-permute-start.12 = (bf16[32,1536]{1,0:T(8,128)(2,1)S(1)}, bf16[32,1536]{1,0:T(8,128)(2,1)S(1)}, u32[]{:S(2)}, u32[]{:S(2)}) collective-permute-start(bf16[32,1536]{1,0:T(8,128)(2,1)S(1)} %get-tuple-element.62.refs_3_), channel_id=1, source_target_pairs={{0,2},{1,3},{2,0},{3,1},{4,6},{5,7},{6,4},{7,5},{8,10},{9,11},{10,... | collective-permute-start | bytes 294920 | tf_op jit(solution)/shard_map/ppermute | solution.py:288
  14.4 6.6 %collective-permute-start.3 = (bf16[32,1536]{1,0:T(8,128)(2,1)S(1)}, bf16[32,1536]{1,0:T(8,128)(2,1)S(1)}, u32[]{:S(2)}, u32[]{:S(2)}) collective-permute-start(bf16[32,1536]{1,0:T(8,128)(2,1)S(1)} %get-tuple-element.62.refs_3_), channel_id=1, source_target_pairs={{0,12},{4,8},{8,4},{12,0},{1,13},{5,9},{9,5},{13,1},{2,14},{6,10},... | collective-permute-start | bytes 294920 | tf_op jit(solution)/shard_map/ppermute | solution.py:288
  16.6 5.2 %collective-permute-start.16 = (bf16[32,1536]{1,0:T(8,128)(2,1)S(1)}, bf16[32,1536]{1,0:T(8,128)(2,1)S(1)}, u32[]{:S(2)}, u32[]{:S(2)}) collective-permute-start(bf16[32,1536]{1,0:T(8,128)(2,1)S(1)} %collective-permute-done.9.refs_2_), channel_id=1, source_target_pairs={{0,1},{1,0},{2,3},{3,2},{4,5},{5,4},{6,7},{7,6},{8,9},{9,8},{10,11... | collective-permute-start | bytes 294920 | tf_op jit(solution)/shard_map/ppermute | solution.py:288
  16.6 5.6 %collective-permute-start.10 = (bf16[32,1536]{1,0:T(8,128)(2,1)S(1)}, bf16[32,1536]{1,0:T(8,128)(2,1)S(1)}, u32[]{:S(2)}, u32[]{:S(2)}) collective-permute-start(bf16[32,1536]{1,0:T(8,128)(2,1)S(1)} %collective-permute-done.9.refs_2_), channel_id=1, source_target_pairs={{0,2},{1,3},{2,0},{3,1},{4,6},{5,7},{6,4},{7,5},{8,10},{9,11},{10,... | collective-permute-start | bytes 294920 | tf_op jit(solution)/shard_map/ppermute | solution.py:288
  18.0 4.3 %collective-permute-start.15 = (bf16[32,1536]{1,0:T(8,128)(2,1)S(1)}, bf16[32,1536]{1,0:T(8,128)(2,1)S(1)}, u32[]{:S(2)}, u32[]{:S(2)}) collective-permute-start(bf16[32,1536]{1,0:T(8,128)(2,1)S(1)} %collective-permute-done.6.refs_1_), channel_id=1, source_target_pairs={{0,1},{1,0},{2,3},{3,2},{4,5},{5,4},{6,7},{7,6},{8,9},{9,8},{10,11... | collective-permute-start | bytes 294920 | tf_op jit(solution)/shard_map/ppermute | solution.py:288
  18.2 6.0 %collective-permute-start.7 = (bf16[32,1536]{1,0:T(8,128)(2,1)S(1)}, bf16[32,1536]{1,0:T(8,128)(2,1)S(1)}, u32[]{:S(2)}, u32[]{:S(2)}) collective-permute-start(bf16[32,1536]{1,0:T(8,128)(2,1)S(1)} %collective-permute-done.6.refs_1_), channel_id=1, source_target_pairs={{0,2},{1,3},{2,0},{3,1},{4,6},{5,7},{6,4},{7,5},{8,10},{9,11},{10,... | collective-permute-start | bytes 294920 | tf_op jit(solution)/shard_map/ppermute | solution.py:288
  20.9 5.1 %collective-permute-start.4 = (bf16[32,1536]{1,0:T(8,128)(2,1)S(1)}, bf16[32,1536]{1,0:T(8,128)(2,1)S(1)}, u32[]{:S(2)}, u32[]{:S(2)}) collective-permute-start(bf16[32,1536]{1,0:T(8,128)(2,1)S(1)} %collective-permute-done.3.refs_0_), channel_id=1, source_target_pairs={{0,2},{1,3},{2,0},{3,1},{4,6},{5,7},{6,4},{7,5},{8,10},{9,11},{10,... | collective-permute-start | bytes 294920 | tf_op jit(solution)/shard_map/ppermute | solution.py:288
  21.8 4.2 %collective-permute-start.14 = (bf16[32,1536]{1,0:T(8,128)(2,1)S(1)}, bf16[32,1536]{1,0:T(8,128)(2,1)S(1)}, u32[]{:S(2)}, u32[]{:S(2)}) collective-permute-start(bf16[32,1536]{1,0:T(8,128)(2,1)S(1)} %collective-permute-done.3.refs_0_), channel_id=1, source_target_pairs={{0,1},{1,0},{2,3},{3,2},{4,5},{5,4},{6,7},{7,6},{8,9},{9,8},{10,11... | collective-permute-start | bytes 294920 | tf_op jit(solution)/shard_map/ppermute | solution.py:288
  22.2 5.5 %collective-permute-start.13 = (bf16[32,1536]{1,0:T(8,128)(2,1)S(1)}, bf16[32,1536]{1,0:T(8,128)(2,1)S(1)}, u32[]{:S(2)}, u32[]{:S(2)}) collective-permute-start(bf16[32,1536]{1,0:T(8,128)(2,1)S(1)} %collective-permute-done.12.refs_11_), channel_id=1, source_target_pairs={{0,1},{1,0},{2,3},{3,2},{4,5},{5,4},{6,7},{7,6},{8,9},{9,8},{10,11... | collective-permute-start | bytes 294920 | tf_op jit(solution)/shard_map/ppermute | solution.py:288
  22.3 5.3 %collective-permute-start.11 = (bf16[32,1536]{1,0:T(8,128)(2,1)S(1)}, bf16[32,1536]{1,0:T(8,128)(2,1)S(1)}, u32[]{:S(2)}, u32[]{:S(2)}) collective-permute-start(bf16[32,1536]{1,0:T(8,128)(2,1)S(1)} %collective-permute-done.10.refs_10_), channel_id=1, source_target_pairs={{0,1},{1,0},{2,3},{3,2},{4,5},{5,4},{6,7},{7,6},{8,9},{9,8},{10,11... | collective-permute-start | bytes 294920 | tf_op jit(solution)/shard_map/ppermute | solution.py:288
  24.3 3.4 %collective-permute-start.8 = (bf16[32,1536]{1,0:T(8,128)(2,1)S(1)}, bf16[32,1536]{1,0:T(8,128)(2,1)S(1)}, u32[]{:S(2)}, u32[]{:S(2)}) collective-permute-start(bf16[32,1536]{1,0:T(8,128)(2,1)S(1)} %collective-permute-done.7.refs_9_), channel_id=1, source_target_pairs={{0,1},{1,0},{2,3},{3,2},{4,5},{5,4},{6,7},{7,6},{8,9},{9,8},{10,11... | collective-permute-start | bytes 294920 | tf_op jit(solution)/shard_map/ppermute | solution.py:288
  26.0 1.7 %collective-permute-start.5 = (bf16[32,1536]{1,0:T(8,128)(2,1)S(1)}, bf16[32,1536]{1,0:T(8,128)(2,1)S(1)}, u32[]{:S(2)}, u32[]{:S(2)}) collective-permute-start(bf16[32,1536]{1,0:T(8,128)(2,1)S(1)} %collective-permute-done.4.refs_8_), channel_id=1, source_target_pairs={{0,1},{1,0},{2,3},{3,2},{4,5},{5,4},{6,7},{7,6},{8,9},{9,8},{10,11... | collective-permute-start | bytes 294920 | tf_op jit(solution)/shard_map/ppermute | solution.py:288
  29.1 1.9 %collective-permute-start.18 = (bf16[128,1536]{1,0:T(8,128)(2,1)S(1)}, bf16[128,1536]{1,0:T(8,128)(2,1)S(1)}, u32[]{:S(2)}, u32[]{:S(2)}) collective-permute-start(bf16[128,1536]{1,0:T(8,128)(2,1)S(1)} %get-tuple-element.72), channel_id=1, source_target_pairs={{0,1},{1,0},{2,3},{3,2},{4,5},{5,4},{6,7},{7,6},{8,9},{9,8},{10,11... | collective-permute-start | bytes 1179656 | tf_op jit(solution)/shard_map/ppermute | solution.py:288
  31.1 5.4 %collective-permute-start.20 = (bf16[32,1536]{1,0:T(8,128)(2,1)S(1)}, bf16[32,1536]{1,0:T(8,128)(2,1)S(1)}, u32[]{:S(2)}, u32[]{:S(2)}) collective-permute-start(bf16[32,1536]{1,0:T(8,128)(2,1)S(1)} %get-tuple-element.81), channel_id=1, source_target_pairs={{0,4},{4,0},{8,12},{12,8},{1,5},{5,1},{9,13},{13,9},{2,6},{6,2},{1... | collective-permute-start | bytes 294920 | tf_op jit(solution)/shard_map/ppermute | solution.py:288
  32.1 12.9 %collective-permute-start.19 = (bf16[32,1664]{1,0:T(8,128)(2,1)S(1)}, bf16[32,1664]{1,0:T(8,128)(2,1)S(1)}, u32[]{:S(2)}, u32[]{:S(2)}) collective-permute-start(bf16[32,1664]{1,0:T(8,128)(2,1)S(1)} %get-tuple-element.74), channel_id=1, source_target_pairs={{0,16},{4,20},{8,24},{12,28},{16,0},{20,4},{24,8},{28,12},{1,17},{... | collective-permute-start | bytes 319496 | tf_op jit(solution)/shard_map/ppermute | solution.py:295
  33.6 11.4 %collective-permute-start.22 = (bf16[32,1664]{1,0:T(8,128)(2,1)S(1)}, bf16[32,1664]{1,0:T(8,128)(2,1)S(1)}, u32[]{:S(2)}, u32[]{:S(2)}) collective-permute-start(bf16[32,1664]{1,0:T(8,128)(2,1)S(1)} %get-tuple-element.89), channel_id=1, source_target_pairs={{0,20},{4,16},{8,28},{12,24},{16,4},{20,0},{24,12},{28,8},{1,21},{... | collective-permute-start | bytes 319496 | tf_op jit(solution)/shard_map/ppermute | solution.py:295
  36.5 8.4 %collective-permute-start.21 = (bf16[32,1536]{1,0:T(8,128)(2,1)S(1)}, bf16[32,1536]{1,0:T(8,128)(2,1)S(1)}, u32[]{:S(2)}, u32[]{:S(2)}) collective-permute-start(bf16[32,1536]{1,0:T(8,128)(2,1)S(1)} %get-tuple-element.84), channel_id=1, source_target_pairs={{0,24},{4,28},{8,16},{12,20},{16,8},{20,12},{24,0},{28,4},{1,25},{... | collective-permute-start | bytes 294920 | tf_op jit(solution)/shard_map/ppermute | solution.py:295
  45.3 4.0 %collective-permute-start.23 = (bf16[16,1536]{1,0:T(8,128)(2,1)S(1)}, bf16[16,1536]{1,0:T(8,128)(2,1)S(1)}, u32[]{:S(2)}, u32[]{:S(2)}) collective-permute-start(bf16[16,1536]{1,0:T(8,128)(2,1)S(1)} %get-tuple-element.91), channel_id=1, source_target_pairs={{0,1},{1,0},{2,3},{3,2},{4,5},{5,4},{6,7},{7,6},{8,9},{9,8},{10,11... | collective-permute-start | bytes 147464 | tf_op jit(solution)/shard_map/ppermute | solution.py:288
  45.4 4.2 %collective-permute-start.24 = (bf16[16,1536]{1,0:T(8,128)(2,1)S(1)}, bf16[16,1536]{1,0:T(8,128)(2,1)S(1)}, u32[]{:S(2)}, u32[]{:S(2)}) collective-permute-start(bf16[16,1536]{1,0:T(8,128)(2,1)S(1)} %get-tuple-element.92), channel_id=1, source_target_pairs={{0,2},{1,3},{2,0},{3,1},{4,6},{5,7},{6,4},{7,5},{8,10},{9,11},{10,... | collective-permute-start | bytes 147464 | tf_op jit(solution)/shard_map/ppermute | solution.py:288
  46.8 3.7 %collective-permute-start.25 = (bf16[16,1536]{1,0:T(8,128)(2,1)S(1)}, bf16[16,1536]{1,0:T(8,128)(2,1)S(1)}, u32[]{:S(2)}, u32[]{:S(2)}) collective-permute-start(bf16[16,1536]{1,0:T(8,128)(2,1)S(1)} %get-tuple-element.93), channel_id=1, source_target_pairs={{0,3},{1,2},{2,1},{3,0},{4,7},{5,6},{6,5},{7,4},{8,11},{9,10},{10,... | collective-permute-start | bytes 147464 | tf_op jit(solution)/shard_map/ppermute | solution.py:288

commit v12 on v8

--- a/solution.py
+++ b/solution.py
@@ -137,15 +137,20 @@
 
 
 def stage_kernel(*refs):
-    weights, outs, sems = refs[:3], refs[3:6], refs[6]
-    third = weights[0].shape[0] // 3
+    weights, (pair_ref, down_ref, sems) = refs[:3], refs[3:]
+    hidden = down_ref.shape[0]
+    padded = pair_ref.shape[0] // 2
+    third = hidden // 3
     sources, targets = [], []
-    for weight, out in zip(weights, outs):
+    for weight, out, start in zip(weights, (pair_ref, pair_ref, down_ref), (0, padded, 0)):
         for part in range(3):
-            rows = pl.ds(part * third, third)
-            sources.append(weight.at[rows, :])
-            targets.append(out.at[rows, :])
-    for copy in bring(sources, targets, sems):
+            sources.append(weight.at[pl.ds(part * third, third), :])
+            targets.append(out.at[pl.ds(start + part * third, third), :])
+    copies = bring(sources, targets, sems)
+    for start in (0, padded):
+        rows = pl.ds(start + hidden, padded - hidden)
+        pair_ref[rows, :] = jnp.zeros((padded - hidden, pair_ref.shape[1]), BF16)
+    for copy in copies:
         copy.wait()
 
 
@@ -192,61 +197,68 @@
     pick_ref[:, :tokens] = pick
 
 
-def add_quarter(steps, blocks, x_ref, dz_ref, weights):
-    piece = blocks[0].shape[1] // 2
+def place_quarter(steps, blocks, x_ref, dz_ref):
+    cap, wide = blocks[0].shape
+    piece = wide // 2
     columns = pl.ds(pl.multiple_of((lax.axis_index("et") ^ steps) * piece, 128), piece)
-    start = 0
-    for block in blocks:
-        rows = pl.ds(start, block.shape[0])
+    for k, block in enumerate(blocks):
+        rows = pl.ds(k * cap, cap)
         x_ref[rows, columns] = block[:, :piece]
         dz_ref[rows, columns] = block[:, piece:]
-        start += block.shape[0]
-    wg_ref, wu_ref, wd_ref = weights
-    x, dz = x_ref[:, columns], dz_ref[:, columns]
+    return columns
+
+
+def products(columns, x_ref, dz_ref, weights):
+    pair_ref, down_ref = weights
     return (
-        contract(x, wg_ref[:, columns], 1, 1),
-        contract(x, wu_ref[:, columns], 1, 1),
-        contract(dz, wd_ref[:, columns], 1, 1),
+        contract(x_ref[:, columns], pair_ref[:, columns], 1, 1),
+        contract(dz_ref[:, columns], down_ref[:, columns], 1, 1),
     )
 
 
 def first_kernel(*refs):
-    weights, (x_ref, dz_ref, *sums) = refs[12:15], refs[15:]
-    for steps in range(3):
-        parts = add_quarter(steps, refs[4 * steps : 4 * steps + 4], x_ref, dz_ref, weights)
-        for out, part in zip(sums, parts):
-            out[...] = out[...] + part if steps else part
-
-
-def half_terms(other, gate_grad, up_grad, weights, half):
+    own, core, chip, weights = refs[:4], refs[4:8], refs[8:12], refs[12:14]
+    x_ref, dz_ref, *sums = refs[14:]
+    place_quarter(0, own, x_ref, dz_ref)
+    place_quarter(1, core, x_ref, dz_ref)
+    quarter = place_quarter(2, chip, x_ref, dz_ref)
+    half = x_ref.shape[1] // 2
+    row = pl.ds(pl.multiple_of(lax.axis_index("et") // 2 * half, 128), half)
+    parts = products(row, x_ref, dz_ref, weights)
+    for out, part, other in zip(sums, parts, products(quarter, x_ref, dz_ref, weights)):
+        out[...] = part + other
+
+
+def half_terms(other, grads, pair_ref, half):
     side = lax.axis_index("et") % 2 ^ other
-    columns = pl.ds(pl.multiple_of(side * half, 128), half)
-    terms = contract(gate_grad, weights[0][:, columns], 1, 0)
-    return terms + contract(up_grad, weights[1][:, columns], 1, 0)
+    return contract(grads, pair_ref[:, pl.ds(pl.multiple_of(side * half, 128), half)], 1, 0)
 
 
 def third_kernel(*refs):
-    both, weights, olds, outs = refs[:4], refs[4:7], refs[9:12], refs[12:]
+    both, weights, olds, outs = refs[:4], refs[4:6], refs[8:10], refs[10:]
     x_ref, dz_ref, act_ref, gg_ref, ug_ref, grads_ref, away_ref = outs
-    slots = x_ref.shape[0]
-    parts = add_quarter(3, both, x_ref, dz_ref, weights)
-    gate, upper, act_grad = (old[...] + part for old, part in zip(olds, parts))
+    hidden = gg_ref.shape[1]
+    padded = grads_ref.shape[1] // 2
+    columns = place_quarter(3, both, x_ref, dz_ref)
+    pair, act_grad = (
+        old[...] + part for old, part in zip(olds, products(columns, x_ref, dz_ref, weights))
+    )
+    gate, upper = pair[:, :hidden], pair[:, padded : padded + hidden]
     sigmoid_gate = jax.nn.sigmoid(gate)
     silu_gate = gate * sigmoid_gate
     gate_grad = (act_grad * upper * sigmoid_gate * (1.0 + gate * (1.0 - sigmoid_gate))).astype(BF16)
     up_grad = (act_grad * silu_gate).astype(BF16)
+    grads_ref[...] = jnp.zeros_like(grads_ref)
+    grads_ref[:, :hidden] = gate_grad
+    grads_ref[:, padded : padded + hidden] = up_grad
+    away_ref[...] = half_terms(1, grads_ref[...], weights[0], away_ref.shape[1]).astype(BF16)
     gg_ref[...] = gate_grad
     ug_ref[...] = up_grad
     act_ref[...] = (silu_gate * upper).astype(BF16)
-    grads_ref[:slots, :] = gate_grad
-    grads_ref[slots:, :] = up_grad
-    away_ref[...] = half_terms(1, gate_grad, up_grad, weights, away_ref.shape[1]).astype(BF16)
-
-
-def own_terms_kernel(grads_ref, wg_ref, wu_ref, out_ref):
-    slots, half = out_ref.shape
-    grads = grads_ref[:slots, :], grads_ref[slots:, :]
-    out_ref[...] = half_terms(0, *grads, (wg_ref, wu_ref), half)
+
+
+def own_terms_kernel(grads_ref, pair_ref, out_ref):
+    out_ref[...] = half_terms(0, grads_ref[...], pair_ref, out_ref.shape[1])
 
 
 def pair_kernel(own_ref, other_ref, pick_ref, *outs):
@@ -302,6 +314,7 @@
     cap = 2 * rows
     slots = 4 * cap
     piece, half = width // 4, width // 2
+    padded = -(-hidden // 128) * 128
 
     packed = call(
         pack_kernel,
@@ -322,7 +335,7 @@
     arrived = [packed[0]] + [swap(packed[s], "et", s) for s in (1, 2, 3)]
     weights = call(
         stage_kernel,
-        [like((hidden, width))] * 3,
+        [like((2 * padded, width)), like((hidden, width))],
         w_gate[0],
         w_up[0],
         w_down[0],
@@ -343,23 +356,24 @@
     chip = [swap(block, "et", 2) for block in own]
     core = [swap(block, "et", 1) for block in own]
     both = [swap(block, "et", 1) for block in chip]
-    wide, sums = [like((slots, width))] * 2, [like((slots, hidden), F32)] * 3
+    wide = [like((slots, width))] * 2
+    sums = [like((slots, 2 * padded), F32), like((slots, hidden), F32)]
     state = call(first_kernel, wide + sums, *own, *core, *chip, *weights, vmem=32)
     x, dz, act, gate_grad, up_grad, grads, away = call(
         third_kernel,
-        wide + [like((slots, hidden))] * 3 + [like((2 * slots, hidden)), like((slots, half))],
+        wide + [like((slots, hidden))] * 3 + [like((slots, 2 * padded)), like((slots, half))],
         *both,
         *weights,
         *state,
         vmem=32,
-        aliases={7: 0, 8: 1},
+        aliases={6: 0, 7: 1},
     )
     theirs = swap(away, "et", 1)
     (own_terms,) = call(
         own_terms_kernel,
         [like((slots, half), F32)],
         grads,
-        *weights[:2],
+        weights[0],
         flops=4 * slots * hidden * half,
         vmem=32,
     )

time: 51.3 us -> 51.1 us (level)
  no operation moved by 1% of the time
where the time goes in v12:
time: 51.1 us; the launch traced here: 50.9 us
  starting transfers between devices  21.8 us (43%)
  waiting for transfers between devices  13.7 us (27%)
  Pallas kernels  8.6 us (17%)
  matrix products  6.08 us (12%)
  between operations  0.77 us (2%)
    ppermute x23, starting transfers between devices, swap(): return lax.ppermute(value, axis, spread(steps))  15.6 us
    ppermute x23, waiting for transfers between devices, swap(): return lax.ppermute(value, axis, spread(steps))  13.2 us
    pallas_call x10, Pallas kernels, call(): pl.pallas_call(kernel, out_shape=outs, in_specs=[space] * len(args), out_...  8.6 us
    ppermute x3, starting transfers between devices, hand(): return lax.ppermute(value, ('pipe', 'dp'), pairs)  6.14 us
    dot_general x3, matrix products, contract(): lax.dot_general(left, right, (((left_dim,), (right_dim,)), ((), ())), pre...  6.08 us
  transfers between devices with their start and end apart: 26, of which 11 were waited for; matrix products, arithmetic and copies ran while one was open for 12% of the time, Pallas kernels for 10%

profile of v12, /device:TPU:0, one launch (start us, length us, event | category | flops | bytes accessed | tf_op | source)
XLA Modules:
  0.0 50.9 jit_solution(14975417510722935195)
XLA Ops:
  0.6 1.1 %shard_map.102 = (bf16[16,1664]{1,0:T(8,128)(2,1)S(1)}, bf16[16,1664]{1,0:T(8,128)(2,1)S(1)}, bf16[16,1664]{1,0:T(8,128)(2,1)S(1)}, bf16[16,1664]{1,0:T(8,128)(2,1)S(1)}) custom-call(bf16[16,3072]{1,0:T(8,128)(2,1)} %bitcast.27, bf16[16,3072]{1,0:T(8,128)(2,1)} %bitcast.28, s32[4,16]{1,0:T(4,128)} %bitcast.30, f32[4,16]{1,0:T(4,128)} %bitcast.31), custom_call_target="tpu_custom_call" | custom-call | bytes 410112 | tf_op jit(solution)/shard_map/pallas_call | solution.py:109
  1.7 0.5 %collective-permute-start = (bf16[16,1664]{1,0:T(8,128)(2,1)S(1)}, bf16[16,1664]{1,0:T(8,128)(2,1)S(1)}, u32[]{:S(2)}, u32[]{:S(2)}) collective-permute-start(bf16[16,1664]{1,0:T(8,128)(2,1)S(1)} %get-tuple-element.49), channel_id=1, source_target_pairs={{0,1},{1,0},{2,3},{3,2},{4,5},{5,4},{6,7},{7,6},{8,9},{9,8},{10,11... | collective-permute-start | bytes 159752 | tf_op jit(solution)/shard_map/ppermute | solution.py:299
  2.2 2.6 %collective-permute-start.1 = (bf16[16,1664]{1,0:T(8,128)(2,1)S(1)}, bf16[16,1664]{1,0:T(8,128)(2,1)S(1)}, u32[]{:S(2)}, u32[]{:S(2)}) collective-permute-start(bf16[16,1664]{1,0:T(8,128)(2,1)S(1)} %get-tuple-element.50), channel_id=1, source_target_pairs={{0,2},{1,3},{2,0},{3,1},{4,6},{5,7},{6,4},{7,5},{8,10},{9,11},{10,... | collective-permute-start | bytes 159752 | tf_op jit(solution)/shard_map/ppermute | solution.py:299
  4.8 0.1 collective-permute-start.2
  4.9 2.8 %shard_map.103 = (bf16[768,3072]{1,0:T(8,128)(2,1)S(1)}, bf16[336,3072]{1,0:T(8,128)(2,1)S(1)}) custom-call(bf16[336,3072]{1,0:T(8,128)(2,1)} %bitcast.22, bf16[336,3072]{1,0:T(8,128)(2,1)} %bitcast.23, bf16[336,3072]{1,0:T(8,128)(2,1)} %bitcast.24), custom_call_target="tpu_custom_call" | custom-call | bytes 12976128 | tf_op jit(solution)/shard_map/pallas_call | solution.py:109
  7.7 0.0 collective-permute-done.refs_1_
  7.8 0.9 %collective-permute-done.2.refs_3_ = bf16[16,1664]{1,0:T(8,128)(2,1)S(1)} collective-permute-done((bf16[16,1664]{1,0:T(8,128)(2,1)S(1)}, bf16[16,1664]{1,0:T(8,128)(2,1)S(1)}, u32[]{:S(2)}, u32[]{:S(2)}) %collective-permute-start.2) | collective-permute-done | bytes 53280 | tf_op jit(solution)/shard_map/ppermute | solution.py:299
  8.6 0.3 shard_map.104
  9.0 2.7 %collective-permute-start.9 = (bf16[32,1536]{1,0:T(8,128)(2,1)S(1)}, bf16[32,1536]{1,0:T(8,128)(2,1)S(1)}, u32[]{:S(2)}, u32[]{:S(2)}) collective-permute-start(bf16[32,1536]{1,0:T(8,128)(2,1)S(1)} %get-tuple-element.58.refs_3_), channel_id=1, source_target_pairs={{0,8},{4,12},{8,0},{12,4},{1,9},{5,13},{9,1},{13,5},{2,10},{6,14},... | collective-permute-start | bytes 294920 | tf_op jit(solution)/shard_map/ppermute | solution.py:299
  11.6 1.6 %collective-permute-start.6 = (bf16[32,1536]{1,0:T(8,128)(2,1)S(1)}, bf16[32,1536]{1,0:T(8,128)(2,1)S(1)}, u32[]{:S(2)}, u32[]{:S(2)}) collective-permute-start(bf16[32,1536]{1,0:T(8,128)(2,1)S(1)} %get-tuple-element.58.refs_3_), channel_id=1, source_target_pairs={{0,4},{4,0},{8,12},{12,8},{1,5},{5,1},{9,13},{13,9},{2,6},{6,2},{1... | collective-permute-start | bytes 294920 | tf_op jit(solution)/shard_map/ppermute | solution.py:299
  13.2 1.1 %collective-permute-start.12 = (bf16[32,1536]{1,0:T(8,128)(2,1)S(1)}, bf16[32,1536]{1,0:T(8,128)(2,1)S(1)}, u32[]{:S(2)}, u32[]{:S(2)}) collective-permute-start(bf16[32,1536]{1,0:T(8,128)(2,1)S(1)} %get-tuple-element.58.refs_3_), channel_id=1, source_target_pairs={{0,2},{1,3},{2,0},{3,1},{4,6},{5,7},{6,4},{7,5},{8,10},{9,11},{10,... | collective-permute-start | bytes 294920 | tf_op jit(solution)/shard_map/ppermute | solution.py:299
  14.3 0.2 collective-permute-start.3
  14.5 2.5 %collective-permute-done.9.refs_2_ = bf16[32,1536]{1,0:T(8,128)(2,1)S(1)} collective-permute-done((bf16[32,1536]{1,0:T(8,128)(2,1)S(1)}, bf16[32,1536]{1,0:T(8,128)(2,1)S(1)}, u32[]{:S(2)}, u32[]{:S(2)}) %collective-permute-start.9) | collective-permute-done | bytes 98336 | tf_op jit(solution)/shard_map/ppermute | solution.py:299
  17.0 0.0 collective-permute-start.16
  17.0 0.0 collective-permute-done.17.refs_7_
  17.0 1.4 %collective-permute-start.10 = (bf16[32,1536]{1,0:T(8,128)(2,1)S(1)}, bf16[32,1536]{1,0:T(8,128)(2,1)S(1)}, u32[]{:S(2)}, u32[]{:S(2)}) collective-permute-start(bf16[32,1536]{1,0:T(8,128)(2,1)S(1)} %collective-permute-done.9.refs_2_), channel_id=1, source_target_pairs={{0,2},{1,3},{2,0},{3,1},{4,6},{5,7},{6,4},{7,5},{8,10},{9,11},{10,... | collective-permute-start | bytes 294920 | tf_op jit(solution)/shard_map/ppermute | solution.py:299
  18.5 0.0 collective-permute-done.6.refs_1_
  18.5 0.2 collective-permute-start.15
  18.7 0.6 %collective-permute-start.7 = (bf16[32,1536]{1,0:T(8,128)(2,1)S(1)}, bf16[32,1536]{1,0:T(8,128)(2,1)S(1)}, u32[]{:S(2)}, u32[]{:S(2)}) collective-permute-start(bf16[32,1536]{1,0:T(8,128)(2,1)S(1)} %collective-permute-done.6.refs_1_), channel_id=1, source_target_pairs={{0,2},{1,3},{2,0},{3,1},{4,6},{5,7},{6,4},{7,5},{8,10},{9,11},{10,... | collective-permute-start | bytes 294920 | tf_op jit(solution)/shard_map/ppermute | solution.py:299
  19.3 1.5 %collective-permute-done.3.refs_0_ = bf16[32,1536]{1,0:T(8,128)(2,1)S(1)} collective-permute-done((bf16[32,1536]{1,0:T(8,128)(2,1)S(1)}, bf16[32,1536]{1,0:T(8,128)(2,1)S(1)}, u32[]{:S(2)}, u32[]{:S(2)}) %collective-permute-start.3) | collective-permute-done | bytes 98336 | tf_op jit(solution)/shard_map/ppermute | solution.py:299
  20.8 0.9 %collective-permute-start.4 = (bf16[32,1536]{1,0:T(8,128)(2,1)S(1)}, bf16[32,1536]{1,0:T(8,128)(2,1)S(1)}, u32[]{:S(2)}, u32[]{:S(2)}) collective-permute-start(bf16[32,1536]{1,0:T(8,128)(2,1)S(1)} %collective-permute-done.3.refs_0_), channel_id=1, source_target_pairs={{0,2},{1,3},{2,0},{3,1},{4,6},{5,7},{6,4},{7,5},{8,10},{9,11},{10,... | collective-permute-start | bytes 294920 | tf_op jit(solution)/shard_map/ppermute | solution.py:299
  21.8 0.8 %collective-permute-done.10.refs_10_ = bf16[32,1536]{1,0:T(8,128)(2,1)S(1)} collective-permute-done((bf16[32,1536]{1,0:T(8,128)(2,1)S(1)}, bf16[32,1536]{1,0:T(8,128)(2,1)S(1)}, u32[]{:S(2)}, u32[]{:S(2)}) %collective-permute-start.10) | collective-permute-done | bytes 98336 | tf_op jit(solution)/shard_map/ppermute | solution.py:299
  22.6 0.5 collective-permute-start.11
  23.2 1.6 %collective-permute-done.7.refs_9_ = bf16[32,1536]{1,0:T(8,128)(2,1)S(1)} collective-permute-done((bf16[32,1536]{1,0:T(8,128)(2,1)S(1)}, bf16[32,1536]{1,0:T(8,128)(2,1)S(1)}, u32[]{:S(2)}, u32[]{:S(2)}) %collective-permute-start.7) | collective-permute-done | bytes 98336 | tf_op jit(solution)/shard_map/ppermute | solution.py:299
  24.7 0.0 collective-permute-start.8
  24.7 1.7 %collective-permute-done.4.refs_8_ = bf16[32,1536]{1,0:T(8,128)(2,1)S(1)} collective-permute-done((bf16[32,1536]{1,0:T(8,128)(2,1)S(1)}, bf16[32,1536]{1,0:T(8,128)(2,1)S(1)}, u32[]{:S(2)}, u32[]{:S(2)}) %collective-permute-start.4) | collective-permute-done | bytes 98336 | tf_op jit(solution)/shard_map/ppermute | solution.py:299
  26.5 1.6 %shard_map.105 = (bf16[128,3072]{1,0:T(8,128)(2,1)S(1)}, bf16[128,3072]{1,0:T(8,128)(2,1)S(1)}, f32[128,768]{1,0:T(8,128)S(1)}, f32[128,336]{1,0:T(8,128)S(1)}) custom-call(bf16[32,1536]{1,0:T(8,128)(2,1)S(1)} %collective-permute-done.3.refs_0_, bf16[32,1536]{1,0:T(8,128)(2,1)S(1)} %collective-permute-done.6.refs_1_, ...), custom_call_target="tpu_custom_call" | custom-call | tf_op jit(solution)/shard_map/pallas_call | solution.py:109
  28.1 1.2 %shard_map.106 = (bf16[128,3072]{1,0:T(8,128)(2,1)S(1)}, bf16[128,3072]{1,0:T(8,128)(2,1)S(1)}, bf16[128,336]{1,0:T(8,128)(2,1)S(1)}, bf16[128,336]{1,0:T(8,128)...) custom-call(bf16[32,1536]{1,0:T(8,128)(2,1)S(1)} %collective-permute, ...), custom_call_target="tpu_custom_call", output_to_operand_aliasing={{0}: (6, {}), {1}: (7, {})} | custom-call | tf_op jit(solution)/shard_map/pallas_call | solution.py:109
  29.3 0.5 %collective-permute-start.18 = (bf16[128,1536]{1,0:T(8,128)(2,1)S(1)}, bf16[128,1536]{1,0:T(8,128)(2,1)S(1)}, u32[]{:S(2)}, u32[]{:S(2)}) collective-permute-start(bf16[128,1536]{1,0:T(8,128)(2,1)S(1)} %get-tuple-element.66), channel_id=1, source_target_pairs={{0,1},{1,0},{2,3},{3,2},{4,5},{5,4},{6,7},{7,6},{8,9},{9,8},{10,11... | collective-permute-start | bytes 1179656 | tf_op jit(solution)/shard_map/ppermute | solution.py:299
  29.9 0.5 shard_map.107.own_ref
  30.4 0.9 %collective-permute-done.18.other_ref = bf16[128,1536]{1,0:T(8,128)(2,1)S(1)} collective-permute-done((bf16[128,1536]{1,0:T(8,128)(2,1)S(1)}, bf16[128,1536]{1,0:T(8,128)(2,1)S(1)}, u32[]{:S(2)}, u32[]{:S(2)}) %collective-permute-start.18) | collective-permute-done | bytes 393248 | tf_op jit(solution)/shard_map/ppermute | solution.py:299
  31.2 0.1 shard_map.108
  31.3 0.7 %collective-permute-start.20 = (bf16[32,1536]{1,0:T(8,128)(2,1)S(1)}, bf16[32,1536]{1,0:T(8,128)(2,1)S(1)}, u32[]{:S(2)}, u32[]{:S(2)}) collective-permute-start(bf16[32,1536]{1,0:T(8,128)(2,1)S(1)} %get-tuple-element.75), channel_id=1, source_target_pairs={{0,4},{4,0},{8,12},{12,8},{1,5},{5,1},{9,13},{13,9},{2,6},{6,2},{1... | collective-permute-start | bytes 294920 | tf_op jit(solution)/shard_map/ppermute | solution.py:299
  32.0 2.3 %collective-permute-start.22 = (bf16[32,1536]{1,0:T(8,128)(2,1)S(1)}, bf16[32,1536]{1,0:T(8,128)(2,1)S(1)}, u32[]{:S(2)}, u32[]{:S(2)}) collective-permute-start(bf16[32,1536]{1,0:T(8,128)(2,1)S(1)} %get-tuple-element.83), channel_id=1, source_target_pairs={{0,20},{4,16},{8,28},{12,24},{16,4},{20,0},{24,12},{28,8},{1,21},{... | collective-permute-start | bytes 294920 | tf_op jit(solution)/shard_map/ppermute | solution.py:306
  34.3 0.5 %collective-permute-start.19 = (bf16[32,1664]{1,0:T(8,128)(2,1)S(1)}, bf16[32,1664]{1,0:T(8,128)(2,1)S(1)}, u32[]{:S(2)}, u32[]{:S(2)}) collective-permute-start(bf16[32,1664]{1,0:T(8,128)(2,1)S(1)} %get-tuple-element.68), channel_id=1, source_target_pairs={{0,16},{4,20},{8,24},{12,28},{16,0},{20,4},{24,8},{28,12},{1,17},{... | collective-permute-start | bytes 319496 | tf_op jit(solution)/shard_map/ppermute | solution.py:306
  34.9 2.1 %collective-permute-done.20.right_ref = bf16[32,1536]{1,0:T(8,128)(2,1)S(1)} collective-permute-done((bf16[32,1536]{1,0:T(8,128)(2,1)S(1)}, bf16[32,1536]{1,0:T(8,128)(2,1)S(1)}, u32[]{:S(2)}, u32[]{:S(2)}) %collective-permute-start.20) | collective-permute-done | bytes 98336 | tf_op jit(solution)/shard_map/ppermute | solution.py:299
  37.0 3.3 %collective-permute-start.21 = (bf16[32,1536]{1,0:T(8,128)(2,1)S(1)}, bf16[32,1536]{1,0:T(8,128)(2,1)S(1)}, u32[]{:S(2)}, u32[]{:S(2)}) collective-permute-start(bf16[32,1536]{1,0:T(8,128)(2,1)S(1)} %get-tuple-element.78), channel_id=1, source_target_pairs={{0,24},{4,28},{8,16},{12,20},{16,8},{20,12},{24,0},{28,4},{1,25},{... | collective-permute-start | bytes 294920 | tf_op jit(solution)/shard_map/ppermute | solution.py:306
  40.3 2.0 %convolution_convert_fusion.2 = bf16[336,3072]{1,0:T(8,128)(2,1)} fusion(bf16[128,336]{1,0:T(8,128)(2,1)S(1)} %get-tuple-element.79, bf16[128,3072]{1,0:T(8,128)(2,1)S(1)} %get-tuple-element.80), kind=kOutput, calls=%fused_computation.2 | convolution fusion | flops 265273344 | bytes 2936832 | tf_op jit(solution)/shard_map/dot_general | solution.py:40
  42.3 2.0 %convolution_convert_fusion.1 = bf16[336,3072]{1,0:T(8,128)(2,1)} fusion(bf16[128,336]{1,0:T(8,128)(2,1)S(1)} %get-tuple-element.81, bf16[128,3072]{1,0:T(8,128)(2,1)S(1)} %get-tuple-element.80), kind=kOutput, calls=%fused_computation.1 | convolution fusion | flops 265273344 | bytes 2936832 | tf_op jit(solution)/shard_map/dot_general | solution.py:40
  44.3 0.5 collective-permute-done.21.refs_0_
  44.8 0.3 shard_map.110
  45.1 0.1 collective-permute-start.23
  45.2 1.3 %collective-permute-start.24 = (bf16[16,1536]{1,0:T(8,128)(2,1)S(1)}, bf16[16,1536]{1,0:T(8,128)(2,1)S(1)}, u32[]{:S(2)}, u32[]{:S(2)}) collective-permute-start(bf16[16,1536]{1,0:T(8,128)(2,1)S(1)} %get-tuple-element.86), channel_id=1, source_target_pairs={{0,2},{1,3},{2,0},{3,1},{4,6},{5,7},{6,4},{7,5},{8,10},{9,11},{10,... | collective-permute-start | bytes 147464 | tf_op jit(solution)/shard_map/ppermute | solution.py:299
  46.6 0.5 %collective-permute-start.25 = (bf16[16,1536]{1,0:T(8,128)(2,1)S(1)}, bf16[16,1536]{1,0:T(8,128)(2,1)S(1)}, u32[]{:S(2)}, u32[]{:S(2)}) collective-permute-start(bf16[16,1536]{1,0:T(8,128)(2,1)S(1)} %get-tuple-element.87), channel_id=1, source_target_pairs={{0,3},{1,2},{2,1},{3,0},{4,7},{5,6},{6,5},{7,4},{8,11},{9,10},{10,... | collective-permute-start | bytes 147464 | tf_op jit(solution)/shard_map/ppermute | solution.py:299
  47.1 2.0 %fusion = bf16[1,336,3072]{2,1,0:T(8,128)(2,1)} fusion(bf16[128,336]{1,0:T(8,128)(2,1)S(1)} %get-tuple-element.90, bf16[128,3072]{1,0:T(8,128)(2,1)S(1)} %get-tuple-element.91), kind=kOutput, calls=%fused_computation.3 | convolution fusion | flops 265273344 | bytes 2936832 | tf_op jit(solution)/shard_map/dot_general | solution.py:40
  49.1 0.3 collective-permute-done.24.chip_ref
  49.4 0.9 %collective-permute-done.25.both_ref = bf16[16,1536]{1,0:T(8,128)(2,1)S(1)} collective-permute-done((bf16[16,1536]{1,0:T(8,128)(2,1)S(1)}, bf16[16,1536]{1,0:T(8,128)(2,1)S(1)}, u32[]{:S(2)}, u32[]{:S(2)}) %collective-permute-start.25) | collective-permute-done | bytes 49184 | tf_op jit(solution)/shard_map/ppermute | solution.py:299
  50.3 0.7 %shard_map.111 = bf16[16,3072]{1,0:T(8,128)(2,1)} custom-call(bf16[16,1536]{1,0:T(8,128)(2,1)S(1)} %get-tuple-element.84.own_ref, bf16[16,1536]{1,0:T(8,128)(2,1)S(1)} %collective-permute-done.23.core_ref, bf16[16,1536]{1,0:T(8,128)(2,1)S(1)} %collective-permute-done.24.chip_ref, bf16[16,1536]{1,0:T(8,128)(2,1)S(1)} %collective-permute-done.25.both_ref), custom_call_target="tpu_custom_call" | custom-call | tf_op jit(solution)/shard_map/pallas_call | solution.py:109
  (17 shorter events, 0.1 us)
Async XLA Ops:
  1.7 6.0 %collective-permute-start = (bf16[16,1664]{1,0:T(8,128)(2,1)S(1)}, bf16[16,1664]{1,0:T(8,128)(2,1)S(1)}, u32[]{:S(2)}, u32[]{:S(2)}) collective-permute-start(bf16[16,1664]{1,0:T(8,128)(2,1)S(1)} %get-tuple-element.49), channel_id=1, source_target_pairs={{0,1},{1,0},{2,3},{3,2},{4,5},{5,4},{6,7},{7,6},{8,9},{9,8},{10,11... | collective-permute-start | bytes 159752 | tf_op jit(solution)/shard_map/ppermute | solution.py:299
  2.2 5.5 %collective-permute-start.1 = (bf16[16,1664]{1,0:T(8,128)(2,1)S(1)}, bf16[16,1664]{1,0:T(8,128)(2,1)S(1)}, u32[]{:S(2)}, u32[]{:S(2)}) collective-permute-start(bf16[16,1664]{1,0:T(8,128)(2,1)S(1)} %get-tuple-element.50), channel_id=1, source_target_pairs={{0,2},{1,3},{2,0},{3,1},{4,6},{5,7},{6,4},{7,5},{8,10},{9,11},{10,... | collective-permute-start | bytes 159752 | tf_op jit(solution)/shard_map/ppermute | solution.py:299
  4.8 3.8 %collective-permute-start.2 = (bf16[16,1664]{1,0:T(8,128)(2,1)S(1)}, bf16[16,1664]{1,0:T(8,128)(2,1)S(1)}, u32[]{:S(2)}, u32[]{:S(2)}) collective-permute-start(bf16[16,1664]{1,0:T(8,128)(2,1)S(1)} %get-tuple-element.51), channel_id=1, source_target_pairs={{0,3},{1,2},{2,1},{3,0},{4,7},{5,6},{6,5},{7,4},{8,11},{9,10},{10,... | collective-permute-start | bytes 159752 | tf_op jit(solution)/shard_map/ppermute | solution.py:299
  9.0 8.1 %collective-permute-start.9 = (bf16[32,1536]{1,0:T(8,128)(2,1)S(1)}, bf16[32,1536]{1,0:T(8,128)(2,1)S(1)}, u32[]{:S(2)}, u32[]{:S(2)}) collective-permute-start(bf16[32,1536]{1,0:T(8,128)(2,1)S(1)} %get-tuple-element.58.refs_3_), channel_id=1, source_target_pairs={{0,8},{4,12},{8,0},{12,4},{1,9},{5,13},{9,1},{13,5},{2,10},{6,14},... | collective-permute-start | bytes 294920 | tf_op jit(solution)/shard_map/ppermute | solution.py:299
  11.6 5.4 %collective-permute-start.17 = (bf16[32,1536]{1,0:T(8,128)(2,1)S(1)}, bf16[32,1536]{1,0:T(8,128)(2,1)S(1)}, u32[]{:S(2)}, u32[]{:S(2)}) collective-permute-start(bf16[32,1536]{1,0:T(8,128)(2,1)S(1)} %get-tuple-element.58.refs_3_), channel_id=1, source_target_pairs={{0,1},{1,0},{2,3},{3,2},{4,5},{5,4},{6,7},{7,6},{8,9},{9,8},{10,11... | collective-permute-start | bytes 294920 | tf_op jit(solution)/shard_map/ppermute | solution.py:299
  11.6 6.8 %collective-permute-start.6 = (bf16[32,1536]{1,0:T(8,128)(2,1)S(1)}, bf16[32,1536]{1,0:T(8,128)(2,1)S(1)}, u32[]{:S(2)}, u32[]{:S(2)}) collective-permute-start(bf16[32,1536]{1,0:T(8,128)(2,1)S(1)} %get-tuple-element.58.refs_3_), channel_id=1, source_target_pairs={{0,4},{4,0},{8,12},{12,8},{1,5},{5,1},{9,13},{13,9},{2,6},{6,2},{1... | collective-permute-start | bytes 294920 | tf_op jit(solution)/shard_map/ppermute | solution.py:299
  13.2 5.5 %collective-permute-start.12 = (bf16[32,1536]{1,0:T(8,128)(2,1)S(1)}, bf16[32,1536]{1,0:T(8,128)(2,1)S(1)}, u32[]{:S(2)}, u32[]{:S(2)}) collective-permute-start(bf16[32,1536]{1,0:T(8,128)(2,1)S(1)} %get-tuple-element.58.refs_3_), channel_id=1, source_target_pairs={{0,2},{1,3},{2,0},{3,1},{4,6},{5,7},{6,4},{7,5},{8,10},{9,11},{10,... | collective-permute-start | bytes 294920 | tf_op jit(solution)/shard_map/ppermute | solution.py:299
  14.3 6.6 %collective-permute-start.3 = (bf16[32,1536]{1,0:T(8,128)(2,1)S(1)}, bf16[32,1536]{1,0:T(8,128)(2,1)S(1)}, u32[]{:S(2)}, u32[]{:S(2)}) collective-permute-start(bf16[32,1536]{1,0:T(8,128)(2,1)S(1)} %get-tuple-element.58.refs_3_), channel_id=1, source_target_pairs={{0,12},{4,8},{8,4},{12,0},{1,13},{5,9},{9,5},{13,1},{2,14},{6,10},... | collective-permute-start | bytes 294920 | tf_op jit(solution)/shard_map/ppermute | solution.py:299
  17.0 4.8 %collective-permute-start.16 = (bf16[32,1536]{1,0:T(8,128)(2,1)S(1)}, bf16[32,1536]{1,0:T(8,128)(2,1)S(1)}, u32[]{:S(2)}, u32[]{:S(2)}) collective-permute-start(bf16[32,1536]{1,0:T(8,128)(2,1)S(1)} %collective-permute-done.9.refs_2_), channel_id=1, source_target_pairs={{0,1},{1,0},{2,3},{3,2},{4,5},{5,4},{6,7},{7,6},{8,9},{9,8},{10,11... | collective-permute-start | bytes 294920 | tf_op jit(solution)/shard_map/ppermute | solution.py:299
  17.0 5.6 %collective-permute-start.10 = (bf16[32,1536]{1,0:T(8,128)(2,1)S(1)}, bf16[32,1536]{1,0:T(8,128)(2,1)S(1)}, u32[]{:S(2)}, u32[]{:S(2)}) collective-permute-start(bf16[32,1536]{1,0:T(8,128)(2,1)S(1)} %collective-permute-done.9.refs_2_), channel_id=1, source_target_pairs={{0,2},{1,3},{2,0},{3,1},{4,6},{5,7},{6,4},{7,5},{8,10},{9,11},{10,... | collective-permute-start | bytes 294920 | tf_op jit(solution)/shard_map/ppermute | solution.py:299
  18.5 4.2 %collective-permute-start.15 = (bf16[32,1536]{1,0:T(8,128)(2,1)S(1)}, bf16[32,1536]{1,0:T(8,128)(2,1)S(1)}, u32[]{:S(2)}, u32[]{:S(2)}) collective-permute-start(bf16[32,1536]{1,0:T(8,128)(2,1)S(1)} %collective-permute-done.6.refs_1_), channel_id=1, source_target_pairs={{0,1},{1,0},{2,3},{3,2},{4,5},{5,4},{6,7},{7,6},{8,9},{9,8},{10,11... | collective-permute-start | bytes 294920 | tf_op jit(solution)/shard_map/ppermute | solution.py:299
  18.7 6.0 %collective-permute-start.7 = (bf16[32,1536]{1,0:T(8,128)(2,1)S(1)}, bf16[32,1536]{1,0:T(8,128)(2,1)S(1)}, u32[]{:S(2)}, u32[]{:S(2)}) collective-permute-start(bf16[32,1536]{1,0:T(8,128)(2,1)S(1)} %collective-permute-done.6.refs_1_), channel_id=1, source_target_pairs={{0,2},{1,3},{2,0},{3,1},{4,6},{5,7},{6,4},{7,5},{8,10},{9,11},{10,... | collective-permute-start | bytes 294920 | tf_op jit(solution)/shard_map/ppermute | solution.py:299
  20.8 5.6 %collective-permute-start.4 = (bf16[32,1536]{1,0:T(8,128)(2,1)S(1)}, bf16[32,1536]{1,0:T(8,128)(2,1)S(1)}, u32[]{:S(2)}, u32[]{:S(2)}) collective-permute-start(bf16[32,1536]{1,0:T(8,128)(2,1)S(1)} %collective-permute-done.3.refs_0_), channel_id=1, source_target_pairs={{0,2},{1,3},{2,0},{3,1},{4,6},{5,7},{6,4},{7,5},{8,10},{9,11},{10,... | collective-permute-start | bytes 294920 | tf_op jit(solution)/shard_map/ppermute | solution.py:299
  21.8 4.7 %collective-permute-start.14 = (bf16[32,1536]{1,0:T(8,128)(2,1)S(1)}, bf16[32,1536]{1,0:T(8,128)(2,1)S(1)}, u32[]{:S(2)}, u32[]{:S(2)}) collective-permute-start(bf16[32,1536]{1,0:T(8,128)(2,1)S(1)} %collective-permute-done.3.refs_0_), channel_id=1, source_target_pairs={{0,1},{1,0},{2,3},{3,2},{4,5},{5,4},{6,7},{7,6},{8,9},{9,8},{10,11... | collective-permute-start | bytes 294920 | tf_op jit(solution)/shard_map/ppermute | solution.py:299
  22.6 5.5 %collective-permute-start.13 = (bf16[32,1536]{1,0:T(8,128)(2,1)S(1)}, bf16[32,1536]{1,0:T(8,128)(2,1)S(1)}, u32[]{:S(2)}, u32[]{:S(2)}) collective-permute-start(bf16[32,1536]{1,0:T(8,128)(2,1)S(1)} %collective-permute-done.12.refs_11_), channel_id=1, source_target_pairs={{0,1},{1,0},{2,3},{3,2},{4,5},{5,4},{6,7},{7,6},{8,9},{9,8},{10,11... | collective-permute-start | bytes 294920 | tf_op jit(solution)/shard_map/ppermute | solution.py:299
  22.6 5.5 %collective-permute-start.11 = (bf16[32,1536]{1,0:T(8,128)(2,1)S(1)}, bf16[32,1536]{1,0:T(8,128)(2,1)S(1)}, u32[]{:S(2)}, u32[]{:S(2)}) collective-permute-start(bf16[32,1536]{1,0:T(8,128)(2,1)S(1)} %collective-permute-done.10.refs_10_), channel_id=1, source_target_pairs={{0,1},{1,0},{2,3},{3,2},{4,5},{5,4},{6,7},{7,6},{8,9},{9,8},{10,11... | collective-permute-start | bytes 294920 | tf_op jit(solution)/shard_map/ppermute | solution.py:299
  24.7 3.4 %collective-permute-start.8 = (bf16[32,1536]{1,0:T(8,128)(2,1)S(1)}, bf16[32,1536]{1,0:T(8,128)(2,1)S(1)}, u32[]{:S(2)}, u32[]{:S(2)}) collective-permute-start(bf16[32,1536]{1,0:T(8,128)(2,1)S(1)} %collective-permute-done.7.refs_9_), channel_id=1, source_target_pairs={{0,1},{1,0},{2,3},{3,2},{4,5},{5,4},{6,7},{7,6},{8,9},{9,8},{10,11... | collective-permute-start | bytes 294920 | tf_op jit(solution)/shard_map/ppermute | solution.py:299
  26.5 1.7 %collective-permute-start.5 = (bf16[32,1536]{1,0:T(8,128)(2,1)S(1)}, bf16[32,1536]{1,0:T(8,128)(2,1)S(1)}, u32[]{:S(2)}, u32[]{:S(2)}) collective-permute-start(bf16[32,1536]{1,0:T(8,128)(2,1)S(1)} %collective-permute-done.4.refs_8_), channel_id=1, source_target_pairs={{0,1},{1,0},{2,3},{3,2},{4,5},{5,4},{6,7},{7,6},{8,9},{9,8},{10,11... | collective-permute-start | bytes 294920 | tf_op jit(solution)/shard_map/ppermute | solution.py:299
  29.3 1.9 %collective-permute-start.18 = (bf16[128,1536]{1,0:T(8,128)(2,1)S(1)}, bf16[128,1536]{1,0:T(8,128)(2,1)S(1)}, u32[]{:S(2)}, u32[]{:S(2)}) collective-permute-start(bf16[128,1536]{1,0:T(8,128)(2,1)S(1)} %get-tuple-element.66), channel_id=1, source_target_pairs={{0,1},{1,0},{2,3},{3,2},{4,5},{5,4},{6,7},{7,6},{8,9},{9,8},{10,11... | collective-permute-start | bytes 1179656 | tf_op jit(solution)/shard_map/ppermute | solution.py:299
  31.3 5.7 %collective-permute-start.20 = (bf16[32,1536]{1,0:T(8,128)(2,1)S(1)}, bf16[32,1536]{1,0:T(8,128)(2,1)S(1)}, u32[]{:S(2)}, u32[]{:S(2)}) collective-permute-start(bf16[32,1536]{1,0:T(8,128)(2,1)S(1)} %get-tuple-element.75), channel_id=1, source_target_pairs={{0,4},{4,0},{8,12},{12,8},{1,5},{5,1},{9,13},{13,9},{2,6},{6,2},{1... | collective-permute-start | bytes 294920 | tf_op jit(solution)/shard_map/ppermute | solution.py:299
  32.0 12.8 %collective-permute-start.22 = (bf16[32,1536]{1,0:T(8,128)(2,1)S(1)}, bf16[32,1536]{1,0:T(8,128)(2,1)S(1)}, u32[]{:S(2)}, u32[]{:S(2)}) collective-permute-start(bf16[32,1536]{1,0:T(8,128)(2,1)S(1)} %get-tuple-element.83), channel_id=1, source_target_pairs={{0,20},{4,16},{8,28},{12,24},{16,4},{20,0},{24,12},{28,8},{1,21},{... | collective-permute-start | bytes 294920 | tf_op jit(solution)/shard_map/ppermute | solution.py:306
  34.3 10.5 %collective-permute-start.19 = (bf16[32,1664]{1,0:T(8,128)(2,1)S(1)}, bf16[32,1664]{1,0:T(8,128)(2,1)S(1)}, u32[]{:S(2)}, u32[]{:S(2)}) collective-permute-start(bf16[32,1664]{1,0:T(8,128)(2,1)S(1)} %get-tuple-element.68), channel_id=1, source_target_pairs={{0,16},{4,20},{8,24},{12,28},{16,0},{20,4},{24,8},{28,12},{1,17},{... | collective-permute-start | bytes 319496 | tf_op jit(solution)/shard_map/ppermute | solution.py:306
  37.0 7.8 %collective-permute-start.21 = (bf16[32,1536]{1,0:T(8,128)(2,1)S(1)}, bf16[32,1536]{1,0:T(8,128)(2,1)S(1)}, u32[]{:S(2)}, u32[]{:S(2)}) collective-permute-start(bf16[32,1536]{1,0:T(8,128)(2,1)S(1)} %get-tuple-element.78), channel_id=1, source_target_pairs={{0,24},{4,28},{8,16},{12,20},{16,8},{20,12},{24,0},{28,4},{1,25},{... | collective-permute-start | bytes 294920 | tf_op jit(solution)/shard_map/ppermute | solution.py:306
  45.1 4.0 %collective-permute-start.23 = (bf16[16,1536]{1,0:T(8,128)(2,1)S(1)}, bf16[16,1536]{1,0:T(8,128)(2,1)S(1)}, u32[]{:S(2)}, u32[]{:S(2)}) collective-permute-start(bf16[16,1536]{1,0:T(8,128)(2,1)S(1)} %get-tuple-element.85), channel_id=1, source_target_pairs={{0,1},{1,0},{2,3},{3,2},{4,5},{5,4},{6,7},{7,6},{8,9},{9,8},{10,11... | collective-permute-start | bytes 147464 | tf_op jit(solution)/shard_map/ppermute | solution.py:299
  45.2 4.2 %collective-permute-start.24 = (bf16[16,1536]{1,0:T(8,128)(2,1)S(1)}, bf16[16,1536]{1,0:T(8,128)(2,1)S(1)}, u32[]{:S(2)}, u32[]{:S(2)}) collective-permute-start(bf16[16,1536]{1,0:T(8,128)(2,1)S(1)} %get-tuple-element.86), channel_id=1, source_target_pairs={{0,2},{1,3},{2,0},{3,1},{4,6},{5,7},{6,4},{7,5},{8,10},{9,11},{10,... | collective-permute-start | bytes 147464 | tf_op jit(solution)/shard_map/ppermute | solution.py:299
  46.6 3.7 %collective-permute-start.25 = (bf16[16,1536]{1,0:T(8,128)(2,1)S(1)}, bf16[16,1536]{1,0:T(8,128)(2,1)S(1)}, u32[]{:S(2)}, u32[]{:S(2)}) collective-permute-start(bf16[16,1536]{1,0:T(8,128)(2,1)S(1)} %get-tuple-element.87), channel_id=1, source_target_pairs={{0,3},{1,2},{2,1},{3,0},{4,7},{5,6},{6,5},{7,4},{8,11},{9,10},{10,... | collective-permute-start | bytes 147464 | tf_op jit(solution)/shard_map/ppermute | solution.py:299

commit v13 on v12

--- a/solution.py
+++ b/solution.py
@@ -236,7 +236,7 @@
 
 def third_kernel(*refs):
     both, weights, olds, outs = refs[:4], refs[4:6], refs[8:10], refs[10:]
-    x_ref, dz_ref, act_ref, gg_ref, ug_ref, grads_ref, away_ref = outs
+    x_ref, dz_ref, act_ref, gg_ref, ug_ref, grads_ref, last_ref, away_ref = outs
     hidden = gg_ref.shape[1]
     padded = grads_ref.shape[1] // 2
     columns = place_quarter(3, both, x_ref, dz_ref)
@@ -251,7 +251,10 @@
     grads_ref[...] = jnp.zeros_like(grads_ref)
     grads_ref[:, :hidden] = gate_grad
     grads_ref[:, padded : padded + hidden] = up_grad
-    away_ref[...] = half_terms(1, grads_ref[...], weights[0], away_ref.shape[1]).astype(BF16)
+    cap = last_ref.shape[0]
+    away = half_terms(1, grads_ref[...], weights[0], away_ref.shape[1]).astype(BF16)
+    last_ref[...] = away[:cap]
+    away_ref[...] = away[cap:]
     gg_ref[...] = gate_grad
     ug_ref[...] = up_grad
     act_ref[...] = (silu_gate * upper).astype(BF16)
@@ -261,17 +264,25 @@
     out_ref[...] = half_terms(0, grads_ref[...], pair_ref, out_ref.shape[1])
 
 
-def pair_kernel(own_ref, other_ref, pick_ref, *outs):
+def last_kernel(own_ref, other_ref, out_ref):
+    own = own_ref[: out_ref.shape[0], :]
+    out_ref[...] = (own + other_ref[...].astype(F32)).astype(BF16)
+
+
+def pair_kernel(own_ref, other_ref, pick_ref, *refs):
+    outs, ready_ref = refs[:3], refs[3]
     cap, half = outs[0].shape
+    ready_ref[...] = jnp.zeros_like(ready_ref)
     for k, out in enumerate(outs):
         rows = pl.ds(k * cap, cap)
-        out[:, :half] = (own_ref[rows, :] + other_ref[rows, :].astype(F32)).astype(BF16)
-    outs[3][:, half:] = pick_ref[...]
-
-
-def add_kernel(left_ref, right_ref, out_ref, ready_ref):
+        own = own_ref[pl.ds((k + 1) * cap, cap), :]
+        out[:, :half] = (own + other_ref[rows, :].astype(F32)).astype(BF16)
+    outs[2][:, half:] = pick_ref[...]
+
+
+def add_kernel(left_ref, right_ref, first_ref, out_ref, ready_ref):
     out_ref[...] = (left_ref[...].astype(F32) + right_ref[...].astype(F32)).astype(BF16)
-    ready_ref[...] = jnp.zeros_like(ready_ref)
+    ready_ref[...] = first_ref[...]
 
 
 def expand_kernel(own_ref, ready_ref, *refs):
@@ -359,15 +370,18 @@
     wide = [like((slots, width))] * 2
     sums = [like((slots, 2 * padded), F32), like((slots, hidden), F32)]
     state = call(first_kernel, wide + sums, *own, *core, *chip, *weights, vmem=32)
-    x, dz, act, gate_grad, up_grad, grads, away = call(
+    x, dz, act, gate_grad, up_grad, grads, away_last, away = call(
         third_kernel,
-        wide + [like((slots, hidden))] * 3 + [like((slots, 2 * padded)), like((slots, half))],
+        wide
+        + [like((slots, hidden))] * 3
+        + [like((slots, 2 * padded)), like((cap, half)), like((3 * cap, half))],
         *both,
         *weights,
         *state,
         vmem=32,
         aliases={6: 0, 7: 1},
     )
+    their_last = swap(away_last, "et", 1)
     theirs = swap(away, "et", 1)
     (own_terms,) = call(
         own_terms_kernel,
@@ -377,9 +391,10 @@
         flops=4 * slots * hidden * half,
         vmem=32,
     )
-    to_last, to_near, to_far, home = call(
+    (to_last,) = call(last_kernel, [like((cap, half))], own_terms, their_last)
+    to_near, to_far, home, first = call(
         pair_kernel,
-        [like((cap, half))] * 3 + [like((cap, half + FLAG))],
+        [like((cap, half))] * 2 + [like((cap, half + FLAG)), like((8, 128), F32)],
         own_terms,
         theirs,
         pick,
@@ -387,16 +402,16 @@
     from_last = swap(to_last, "dp", 1)
     home = hand(home, pipe_size, 0)
     from_near = hand(to_near, pipe_size, 1)
+    x, gate_grad, first = lax.optimization_barrier((x, gate_grad, first))
+    grad_gate = contract(gate_grad, x, 0, 0).astype(BF16)
+    from_last, grad_gate = lax.optimization_barrier((from_last, grad_gate))
     to_far, ready = call(
-        add_kernel, [like((cap, half)), like((8, 128), F32)], to_far, from_last
-    )
-    x, dz, act, gate_grad, up_grad, ready = lax.optimization_barrier(
-        (x, dz, act, gate_grad, up_grad, ready)
-    )
-    grad_gate = contract(gate_grad, x, 0, 0).astype(BF16)
+        add_kernel, [like((cap, half)), like((8, 128), F32)], to_far, from_last, first
+    )
+    x, dz, act, up_grad, ready = lax.optimization_barrier((x, dz, act, up_grad, ready))
     grad_up = contract(up_grad, x, 0, 0).astype(BF16)
     from_far = hand(to_far, pipe_size, 2)
-    from_far, grad_gate, grad_up = lax.optimization_barrier((from_far, grad_gate, grad_up))
+    from_far, grad_up = lax.optimization_barrier((from_far, grad_up))
     by_token = call(
         expand_kernel,
         [like((rows, half))] * 4,

time: 51.1 us -> 51.6 us (level)
    ppermute x3, waiting for transfers between devices: 0.5 us -> 2.94 us  [hand(): return lax.ppermute(value, ('pipe', 'dp'), pairs)]
    ppermute x23 -> x24, waiting for transfers between devices: 13.2 us -> 11.2 us  [swap(): return lax.ppermute(value, axis, spread(steps))]
    ppermute x23 -> x24, starting transfers between devices: 15.6 us -> 15.7 us  [swap(): return lax.ppermute(value, axis, spread(steps))]
    pallas_call x10 -> x11, Pallas kernels: 8.6 us -> 8.61 us  [call(): pl.pallas_call(kernel, out_shape=outs, in_specs=[space] * len(args), out_...]
  transfers between devices with their start and end apart: 26 -> 27, of which waited for: 11 -> 10; matrix products, arithmetic and copies ran while one was open for 12% -> 12% of each run, Pallas kernels for 10% -> 10%
where the time goes in v13:
time: 51.6 us; the launch traced here: 51.4 us
  starting transfers between devices  21.9 us (42%)
  waiting for transfers between devices  14.1 us (27%)
  Pallas kernels  8.61 us (17%)
  matrix products  6.07 us (12%)
  between operations  0.77 us (1%)
    ppermute x24, starting transfers between devices, swap(): return lax.ppermute(value, axis, spread(steps))  15.7 us
    ppermute x24, waiting for transfers between devices, swap(): return lax.ppermute(value, axis, spread(steps))  11.2 us
    pallas_call x11, Pallas kernels, call(): pl.pallas_call(kernel, out_shape=outs, in_specs=[space] * len(args), out_...  8.61 us
    ppermute x3, starting transfers between devices, hand(): return lax.ppermute(value, ('pipe', 'dp'), pairs)  6.19 us
    dot_general x3, matrix products, contract(): lax.dot_general(left, right, (((left_dim,), (right_dim,)), ((), ())), pre...  6.07 us
    ppermute x3, waiting for transfers between devices, hand(): return lax.ppermute(value, ('pipe', 'dp'), pairs)  2.94 us
  transfers between devices with their start and end apart: 27, of which 10 were waited for; matrix products, arithmetic and copies ran while one was open for 12% of the time, Pallas kernels for 10%

profile of v13, /device:TPU:0, one launch (start us, length us, event | category | flops | bytes accessed | tf_op | source)
XLA Modules:
  0.0 51.4 jit_solution(9333301989978170489)
XLA Ops:
  0.6 1.1 %shard_map.102 = (bf16[16,1664]{1,0:T(8,128)(2,1)S(1)}, bf16[16,1664]{1,0:T(8,128)(2,1)S(1)}, bf16[16,1664]{1,0:T(8,128)(2,1)S(1)}, bf16[16,1664]{1,0:T(8,128)(2,1)S(1)}) custom-call(bf16[16,3072]{1,0:T(8,128)(2,1)} %bitcast.27, bf16[16,3072]{1,0:T(8,128)(2,1)} %bitcast.28, s32[4,16]{1,0:T(4,128)} %bitcast.30, f32[4,16]{1,0:T(4,128)} %bitcast.31), custom_call_target="tpu_custom_call" | custom-call | bytes 410112 | tf_op jit(solution)/shard_map/pallas_call | solution.py:109
  1.7 0.5 %collective-permute-start = (bf16[16,1664]{1,0:T(8,128)(2,1)S(1)}, bf16[16,1664]{1,0:T(8,128)(2,1)S(1)}, u32[]{:S(2)}, u32[]{:S(2)}) collective-permute-start(bf16[16,1664]{1,0:T(8,128)(2,1)S(1)} %get-tuple-element.53), channel_id=1, source_target_pairs={{0,1},{1,0},{2,3},{3,2},{4,5},{5,4},{6,7},{7,6},{8,9},{9,8},{10,11... | collective-permute-start | bytes 159752 | tf_op jit(solution)/shard_map/ppermute | solution.py:310
  2.2 2.6 %collective-permute-start.1 = (bf16[16,1664]{1,0:T(8,128)(2,1)S(1)}, bf16[16,1664]{1,0:T(8,128)(2,1)S(1)}, u32[]{:S(2)}, u32[]{:S(2)}) collective-permute-start(bf16[16,1664]{1,0:T(8,128)(2,1)S(1)} %get-tuple-element.54), channel_id=1, source_target_pairs={{0,2},{1,3},{2,0},{3,1},{4,6},{5,7},{6,4},{7,5},{8,10},{9,11},{10,... | collective-permute-start | bytes 159752 | tf_op jit(solution)/shard_map/ppermute | solution.py:310
  4.8 0.1 collective-permute-start.2
  4.9 2.8 %shard_map.103 = (bf16[768,3072]{1,0:T(8,128)(2,1)S(1)}, bf16[336,3072]{1,0:T(8,128)(2,1)S(1)}) custom-call(bf16[336,3072]{1,0:T(8,128)(2,1)} %bitcast.22, bf16[336,3072]{1,0:T(8,128)(2,1)} %bitcast.23, bf16[336,3072]{1,0:T(8,128)(2,1)} %bitcast.24), custom_call_target="tpu_custom_call" | custom-call | bytes 12976128 | tf_op jit(solution)/shard_map/pallas_call | solution.py:109
  7.7 0.0 collective-permute-done.1.refs_2_
  7.8 0.9 %collective-permute-done.2.refs_3_ = bf16[16,1664]{1,0:T(8,128)(2,1)S(1)} collective-permute-done((bf16[16,1664]{1,0:T(8,128)(2,1)S(1)}, bf16[16,1664]{1,0:T(8,128)(2,1)S(1)}, u32[]{:S(2)}, u32[]{:S(2)}) %collective-permute-start.2) | collective-permute-done | bytes 53280 | tf_op jit(solution)/shard_map/ppermute | solution.py:310
  8.6 0.3 shard_map.104
  9.0 2.7 %collective-permute-start.9 = (bf16[32,1536]{1,0:T(8,128)(2,1)S(1)}, bf16[32,1536]{1,0:T(8,128)(2,1)S(1)}, u32[]{:S(2)}, u32[]{:S(2)}) collective-permute-start(bf16[32,1536]{1,0:T(8,128)(2,1)S(1)} %get-tuple-element.62.refs_3_), channel_id=1, source_target_pairs={{0,8},{4,12},{8,0},{12,4},{1,9},{5,13},{9,1},{13,5},{2,10},{6,14},... | collective-permute-start | bytes 294920 | tf_op jit(solution)/shard_map/ppermute | solution.py:310
  11.6 0.0 collective-permute-start.17
  11.6 1.6 %collective-permute-start.6 = (bf16[32,1536]{1,0:T(8,128)(2,1)S(1)}, bf16[32,1536]{1,0:T(8,128)(2,1)S(1)}, u32[]{:S(2)}, u32[]{:S(2)}) collective-permute-start(bf16[32,1536]{1,0:T(8,128)(2,1)S(1)} %get-tuple-element.62.refs_3_), channel_id=1, source_target_pairs={{0,4},{4,0},{8,12},{12,8},{1,5},{5,1},{9,13},{13,9},{2,6},{6,2},{1... | collective-permute-start | bytes 294920 | tf_op jit(solution)/shard_map/ppermute | solution.py:310
  13.2 1.1 %collective-permute-start.12 = (bf16[32,1536]{1,0:T(8,128)(2,1)S(1)}, bf16[32,1536]{1,0:T(8,128)(2,1)S(1)}, u32[]{:S(2)}, u32[]{:S(2)}) collective-permute-start(bf16[32,1536]{1,0:T(8,128)(2,1)S(1)} %get-tuple-element.62.refs_3_), channel_id=1, source_target_pairs={{0,2},{1,3},{2,0},{3,1},{4,6},{5,7},{6,4},{7,5},{8,10},{9,11},{10,... | collective-permute-start | bytes 294920 | tf_op jit(solution)/shard_map/ppermute | solution.py:310
  14.3 0.2 collective-permute-start.3
  14.5 2.5 %collective-permute-done.9.refs_2_ = bf16[32,1536]{1,0:T(8,128)(2,1)S(1)} collective-permute-done((bf16[32,1536]{1,0:T(8,128)(2,1)S(1)}, bf16[32,1536]{1,0:T(8,128)(2,1)S(1)}, u32[]{:S(2)}, u32[]{:S(2)}) %collective-permute-start.9) | collective-permute-done | bytes 98336 | tf_op jit(solution)/shard_map/ppermute | solution.py:310
  17.0 1.4 %collective-permute-start.10 = (bf16[32,1536]{1,0:T(8,128)(2,1)S(1)}, bf16[32,1536]{1,0:T(8,128)(2,1)S(1)}, u32[]{:S(2)}, u32[]{:S(2)}) collective-permute-start(bf16[32,1536]{1,0:T(8,128)(2,1)S(1)} %collective-permute-done.9.refs_2_), channel_id=1, source_target_pairs={{0,2},{1,3},{2,0},{3,1},{4,6},{5,7},{6,4},{7,5},{8,10},{9,11},{10,... | collective-permute-start | bytes 294920 | tf_op jit(solution)/shard_map/ppermute | solution.py:310
  18.5 0.0 collective-permute-done.6.refs_1_
  18.5 0.2 collective-permute-start.15
  18.7 0.0 collective-permute-done.12.refs_11_
  18.7 0.6 %collective-permute-start.7 = (bf16[32,1536]{1,0:T(8,128)(2,1)S(1)}, bf16[32,1536]{1,0:T(8,128)(2,1)S(1)}, u32[]{:S(2)}, u32[]{:S(2)}) collective-permute-start(bf16[32,1536]{1,0:T(8,128)(2,1)S(1)} %collective-permute-done.6.refs_1_), channel_id=1, source_target_pairs={{0,2},{1,3},{2,0},{3,1},{4,6},{5,7},{6,4},{7,5},{8,10},{9,11},{10,... | collective-permute-start | bytes 294920 | tf_op jit(solution)/shard_map/ppermute | solution.py:310
  19.3 1.5 %collective-permute-done.3.refs_0_ = bf16[32,1536]{1,0:T(8,128)(2,1)S(1)} collective-permute-done((bf16[32,1536]{1,0:T(8,128)(2,1)S(1)}, bf16[32,1536]{1,0:T(8,128)(2,1)S(1)}, u32[]{:S(2)}, u32[]{:S(2)}) %collective-permute-start.3) | collective-permute-done | bytes 98336 | tf_op jit(solution)/shard_map/ppermute | solution.py:310
  20.8 0.9 %collective-permute-start.4 = (bf16[32,1536]{1,0:T(8,128)(2,1)S(1)}, bf16[32,1536]{1,0:T(8,128)(2,1)S(1)}, u32[]{:S(2)}, u32[]{:S(2)}) collective-permute-start(bf16[32,1536]{1,0:T(8,128)(2,1)S(1)} %collective-permute-done.3.refs_0_), channel_id=1, source_target_pairs={{0,2},{1,3},{2,0},{3,1},{4,6},{5,7},{6,4},{7,5},{8,10},{9,11},{10,... | collective-permute-start | bytes 294920 | tf_op jit(solution)/shard_map/ppermute | solution.py:310
  21.8 0.0 collective-permute-done.16.refs_6_
  21.8 0.8 %collective-permute-done.10.refs_10_ = bf16[32,1536]{1,0:T(8,128)(2,1)S(1)} collective-permute-done((bf16[32,1536]{1,0:T(8,128)(2,1)S(1)}, bf16[32,1536]{1,0:T(8,128)(2,1)S(1)}, u32[]{:S(2)}, u32[]{:S(2)}) %collective-permute-start.10) | collective-permute-done | bytes 98336 | tf_op jit(solution)/shard_map/ppermute | solution.py:310
  22.6 0.5 collective-permute-start.11
  23.2 1.6 %collective-permute-done.7.refs_9_ = bf16[32,1536]{1,0:T(8,128)(2,1)S(1)} collective-permute-done((bf16[32,1536]{1,0:T(8,128)(2,1)S(1)}, bf16[32,1536]{1,0:T(8,128)(2,1)S(1)}, u32[]{:S(2)}, u32[]{:S(2)}) %collective-permute-start.7) | collective-permute-done | bytes 98336 | tf_op jit(solution)/shard_map/ppermute | solution.py:310
  24.7 1.7 %collective-permute-done.4.refs_8_ = bf16[32,1536]{1,0:T(8,128)(2,1)S(1)} collective-permute-done((bf16[32,1536]{1,0:T(8,128)(2,1)S(1)}, bf16[32,1536]{1,0:T(8,128)(2,1)S(1)}, u32[]{:S(2)}, u32[]{:S(2)}) %collective-permute-start.4) | collective-permute-done | bytes 98336 | tf_op jit(solution)/shard_map/ppermute | solution.py:310
  26.5 1.6 %shard_map.105 = (bf16[128,3072]{1,0:T(8,128)(2,1)S(1)}, bf16[128,3072]{1,0:T(8,128)(2,1)S(1)}, f32[128,768]{1,0:T(8,128)S(1)}, f32[128,336]{1,0:T(8,128)S(1)}) custom-call(bf16[32,1536]{1,0:T(8,128)(2,1)S(1)} %collective-permute-done.3.refs_0_, bf16[32,1536]{1,0:T(8,128)(2,1)S(1)} %collective-permute-done.6.refs_1_, ...), custom_call_target="tpu_custom_call" | custom-call | tf_op jit(solution)/shard_map/pallas_call | solution.py:109
  28.1 1.2 %shard_map.106 = (bf16[128,3072]{1,0:T(8,128)(2,1)S(1)}, bf16[128,3072]{1,0:T(8,128)(2,1)S(1)}, bf16[128,336]{1,0:T(8,128)(2,1)S(1)}, bf16[128,336]{1,0:T(8,128)...) custom-call(bf16[32,1536]{1,0:T(8,128)(2,1)S(1)} %collective-permute, ...), custom_call_target="tpu_custom_call", output_to_operand_aliasing={{0}: (6, {}), {1}: (7, {})} | custom-call | tf_op jit(solution)/shard_map/pallas_call | solution.py:109
  29.3 0.5 %collective-permute-start.18 = (bf16[96,1536]{1,0:T(8,128)(2,1)S(1)}, bf16[96,1536]{1,0:T(8,128)(2,1)S(1)}, u32[]{:S(2)}, u32[]{:S(2)}) collective-permute-start(bf16[96,1536]{1,0:T(8,128)(2,1)S(1)} %get-tuple-element.70), channel_id=1, source_target_pairs={{0,1},{1,0},{2,3},{3,2},{4,5},{5,4},{6,7},{7,6},{8,9},{9,8},{10,11... | collective-permute-start | bytes 884744 | tf_op jit(solution)/shard_map/ppermute | solution.py:310
  29.9 0.1 collective-permute-start.20
  30.0 0.5 shard_map.107.own_ref
  30.5 0.8 %collective-permute-done.20.other_ref = bf16[32,1536]{1,0:T(8,128)(2,1)S(1)} collective-permute-done((bf16[32,1536]{1,0:T(8,128)(2,1)S(1)}, bf16[32,1536]{1,0:T(8,128)(2,1)S(1)}, u32[]{:S(2)}, u32[]{:S(2)}) %collective-permute-start.20) | collective-permute-done | bytes 98336 | tf_op jit(solution)/shard_map/ppermute | solution.py:310
  31.3 0.7 %collective-permute-start.21 = (bf16[32,1536]{1,0:T(8,128)(2,1)S(1)}, bf16[32,1536]{1,0:T(8,128)(2,1)S(1)}, u32[]{:S(2)}, u32[]{:S(2)}) collective-permute-start(bf16[32,1536]{1,0:T(8,128)(2,1)S(1)} %shard_map.109), channel_id=1, source_target_pairs={{0,4},{4,0},{8,12},{12,8},{1,5},{5,1},{9,13},{13,9},{2,6},{6,2},{1... | collective-permute-start | bytes 294920 | tf_op jit(solution)/shard_map/ppermute | solution.py:310
  32.0 0.1 shard_map.108
  32.0 2.4 %collective-permute-start.23 = (bf16[32,1536]{1,0:T(8,128)(2,1)S(1)}, bf16[32,1536]{1,0:T(8,128)(2,1)S(1)}, u32[]{:S(2)}, u32[]{:S(2)}) collective-permute-start(bf16[32,1536]{1,0:T(8,128)(2,1)S(1)} %get-tuple-element.91), channel_id=1, source_target_pairs={{0,20},{4,16},{8,28},{12,24},{16,4},{20,0},{24,12},{28,8},{1,21},{... | collective-permute-start | bytes 294920 | tf_op jit(solution)/shard_map/ppermute | solution.py:317
  34.4 0.5 %collective-permute-start.19 = (bf16[32,1664]{1,0:T(8,128)(2,1)S(1)}, bf16[32,1664]{1,0:T(8,128)(2,1)S(1)}, u32[]{:S(2)}, u32[]{:S(2)}) collective-permute-start(bf16[32,1664]{1,0:T(8,128)(2,1)S(1)} %get-tuple-element.72), channel_id=1, source_target_pairs={{0,16},{4,20},{8,24},{12,28},{16,0},{20,4},{24,8},{28,12},{1,17},{... | collective-permute-start | bytes 319496 | tf_op jit(solution)/shard_map/ppermute | solution.py:317
  35.0 2.0 %convolution_convert_fusion.2 = bf16[336,3072]{1,0:T(8,128)(2,1)} fusion(bf16[128,336]{1,0:T(8,128)(2,1)S(1)} %get-tuple-element.82, bf16[128,3072]{1,0:T(8,128)(2,1)S(1)} %get-tuple-element.89), kind=kOutput, calls=%fused_computation.2 | convolution fusion | flops 265273344 | bytes 2936832 | tf_op jit(solution)/shard_map/dot_general | solution.py:40
  37.0 3.2 %collective-permute-start.22 = (bf16[32,1536]{1,0:T(8,128)(2,1)S(1)}, bf16[32,1536]{1,0:T(8,128)(2,1)S(1)}, u32[]{:S(2)}, u32[]{:S(2)}) collective-permute-start(bf16[32,1536]{1,0:T(8,128)(2,1)S(1)} %get-tuple-element.87), channel_id=1, source_target_pairs={{0,24},{4,28},{8,16},{12,20},{16,8},{20,12},{24,0},{28,4},{1,25},{... | collective-permute-start | bytes 294920 | tf_op jit(solution)/shard_map/ppermute | solution.py:317
  40.3 2.0 %convolution_convert_fusion.1 = bf16[336,3072]{1,0:T(8,128)(2,1)} fusion(bf16[128,336]{1,0:T(8,128)(2,1)S(1)} %get-tuple-element.88, bf16[128,3072]{1,0:T(8,128)(2,1)S(1)} %get-tuple-element.89), kind=kOutput, calls=%fused_computation.1 | convolution fusion | flops 265273344 | bytes 2936832 | tf_op jit(solution)/shard_map/dot_general | solution.py:40
  42.3 2.9 %collective-permute-done.22.refs_0_ = bf16[32,1536]{1,0:T(8,128)(2,1)S(1)} collective-permute-done((bf16[32,1536]{1,0:T(8,128)(2,1)S(1)}, bf16[32,1536]{1,0:T(8,128)(2,1)S(1)}, u32[]{:S(2)}, u32[]{:S(2)}) %collective-permute-start.22) | collective-permute-done | bytes 98336 | tf_op jit(solution)/shard_map/ppermute | solution.py:317
  45.2 0.3 shard_map.111
  45.5 0.1 collective-permute-start.24
  45.6 1.5 %collective-permute-start.25 = (bf16[16,1536]{1,0:T(8,128)(2,1)S(1)}, bf16[16,1536]{1,0:T(8,128)(2,1)S(1)}, u32[]{:S(2)}, u32[]{:S(2)}) collective-permute-start(bf16[16,1536]{1,0:T(8,128)(2,1)S(1)} %get-tuple-element.94), channel_id=1, source_target_pairs={{0,2},{1,3},{2,0},{3,1},{4,6},{5,7},{6,4},{7,5},{8,10},{9,11},{10,... | collective-permute-start | bytes 147464 | tf_op jit(solution)/shard_map/ppermute | solution.py:310
  47.1 0.4 collective-permute-start.26
  47.5 2.0 %fusion = bf16[1,336,3072]{2,1,0:T(8,128)(2,1)} fusion(bf16[128,336]{1,0:T(8,128)(2,1)S(1)} %get-tuple-element.98, bf16[128,3072]{1,0:T(8,128)(2,1)S(1)} %get-tuple-element.99), kind=kOutput, calls=%fused_computation.3 | convolution fusion | flops 265273344 | bytes 2936832 | tf_op jit(solution)/shard_map/dot_general | solution.py:40
  49.5 0.3 collective-permute-done.25.chip_ref
  49.8 1.0 %collective-permute-done.26.both_ref = bf16[16,1536]{1,0:T(8,128)(2,1)S(1)} collective-permute-done((bf16[16,1536]{1,0:T(8,128)(2,1)S(1)}, bf16[16,1536]{1,0:T(8,128)(2,1)S(1)}, u32[]{:S(2)}, u32[]{:S(2)}) %collective-permute-start.26) | collective-permute-done | bytes 49184 | tf_op jit(solution)/shard_map/ppermute | solution.py:310
  50.8 0.7 %shard_map.112 = bf16[16,3072]{1,0:T(8,128)(2,1)} custom-call(bf16[16,1536]{1,0:T(8,128)(2,1)S(1)} %get-tuple-element.92.own_ref, bf16[16,1536]{1,0:T(8,128)(2,1)S(1)} %collective-permute-done.24.core_ref, bf16[16,1536]{1,0:T(8,128)(2,1)S(1)} %collective-permute-done.25.chip_ref, bf16[16,1536]{1,0:T(8,128)(2,1)S(1)} %collective-permute-done.26.both_ref), custom_call_target="tpu_custom_call" | custom-call | tf_op jit(solution)/shard_map/pallas_call | solution.py:109
  (20 shorter events, 0.1 us)
Async XLA Ops:
  1.7 6.0 %collective-permute-start = (bf16[16,1664]{1,0:T(8,128)(2,1)S(1)}, bf16[16,1664]{1,0:T(8,128)(2,1)S(1)}, u32[]{:S(2)}, u32[]{:S(2)}) collective-permute-start(bf16[16,1664]{1,0:T(8,128)(2,1)S(1)} %get-tuple-element.53), channel_id=1, source_target_pairs={{0,1},{1,0},{2,3},{3,2},{4,5},{5,4},{6,7},{7,6},{8,9},{9,8},{10,11... | collective-permute-start | bytes 159752 | tf_op jit(solution)/shard_map/ppermute | solution.py:310
  2.2 5.5 %collective-permute-start.1 = (bf16[16,1664]{1,0:T(8,128)(2,1)S(1)}, bf16[16,1664]{1,0:T(8,128)(2,1)S(1)}, u32[]{:S(2)}, u32[]{:S(2)}) collective-permute-start(bf16[16,1664]{1,0:T(8,128)(2,1)S(1)} %get-tuple-element.54), channel_id=1, source_target_pairs={{0,2},{1,3},{2,0},{3,1},{4,6},{5,7},{6,4},{7,5},{8,10},{9,11},{10,... | collective-permute-start | bytes 159752 | tf_op jit(solution)/shard_map/ppermute | solution.py:310
  4.8 3.8 %collective-permute-start.2 = (bf16[16,1664]{1,0:T(8,128)(2,1)S(1)}, bf16[16,1664]{1,0:T(8,128)(2,1)S(1)}, u32[]{:S(2)}, u32[]{:S(2)}) collective-permute-start(bf16[16,1664]{1,0:T(8,128)(2,1)S(1)} %get-tuple-element.55), channel_id=1, source_target_pairs={{0,3},{1,2},{2,1},{3,0},{4,7},{5,6},{6,5},{7,4},{8,11},{9,10},{10,... | collective-permute-start | bytes 159752 | tf_op jit(solution)/shard_map/ppermute | solution.py:310
  9.0 8.1 %collective-permute-start.9 = (bf16[32,1536]{1,0:T(8,128)(2,1)S(1)}, bf16[32,1536]{1,0:T(8,128)(2,1)S(1)}, u32[]{:S(2)}, u32[]{:S(2)}) collective-permute-start(bf16[32,1536]{1,0:T(8,128)(2,1)S(1)} %get-tuple-element.62.refs_3_), channel_id=1, source_target_pairs={{0,8},{4,12},{8,0},{12,4},{1,9},{5,13},{9,1},{13,5},{2,10},{6,14},... | collective-permute-start | bytes 294920 | tf_op jit(solution)/shard_map/ppermute | solution.py:310
  11.6 5.4 %collective-permute-start.17 = (bf16[32,1536]{1,0:T(8,128)(2,1)S(1)}, bf16[32,1536]{1,0:T(8,128)(2,1)S(1)}, u32[]{:S(2)}, u32[]{:S(2)}) collective-permute-start(bf16[32,1536]{1,0:T(8,128)(2,1)S(1)} %get-tuple-element.62.refs_3_), channel_id=1, source_target_pairs={{0,1},{1,0},{2,3},{3,2},{4,5},{5,4},{6,7},{7,6},{8,9},{9,8},{10,11... | collective-permute-start | bytes 294920 | tf_op jit(solution)/shard_map/ppermute | solution.py:310
  11.6 6.8 %collective-permute-start.6 = (bf16[32,1536]{1,0:T(8,128)(2,1)S(1)}, bf16[32,1536]{1,0:T(8,128)(2,1)S(1)}, u32[]{:S(2)}, u32[]{:S(2)}) collective-permute-start(bf16[32,1536]{1,0:T(8,128)(2,1)S(1)} %get-tuple-element.62.refs_3_), channel_id=1, source_target_pairs={{0,4},{4,0},{8,12},{12,8},{1,5},{5,1},{9,13},{13,9},{2,6},{6,2},{1... | collective-permute-start | bytes 294920 | tf_op jit(solution)/shard_map/ppermute | solution.py:310
  13.2 5.5 %collective-permute-start.12 = (bf16[32,1536]{1,0:T(8,128)(2,1)S(1)}, bf16[32,1536]{1,0:T(8,128)(2,1)S(1)}, u32[]{:S(2)}, u32[]{:S(2)}) collective-permute-start(bf16[32,1536]{1,0:T(8,128)(2,1)S(1)} %get-tuple-element.62.refs_3_), channel_id=1, source_target_pairs={{0,2},{1,3},{2,0},{3,1},{4,6},{5,7},{6,4},{7,5},{8,10},{9,11},{10,... | collective-permute-start | bytes 294920 | tf_op jit(solution)/shard_map/ppermute | solution.py:310
  14.3 6.6 %collective-permute-start.3 = (bf16[32,1536]{1,0:T(8,128)(2,1)S(1)}, bf16[32,1536]{1,0:T(8,128)(2,1)S(1)}, u32[]{:S(2)}, u32[]{:S(2)}) collective-permute-start(bf16[32,1536]{1,0:T(8,128)(2,1)S(1)} %get-tuple-element.62.refs_3_), channel_id=1, source_target_pairs={{0,12},{4,8},{8,4},{12,0},{1,13},{5,9},{9,5},{13,1},{2,14},{6,10},... | collective-permute-start | bytes 294920 | tf_op jit(solution)/shard_map/ppermute | solution.py:310
  17.0 4.8 %collective-permute-start.16 = (bf16[32,1536]{1,0:T(8,128)(2,1)S(1)}, bf16[32,1536]{1,0:T(8,128)(2,1)S(1)}, u32[]{:S(2)}, u32[]{:S(2)}) collective-permute-start(bf16[32,1536]{1,0:T(8,128)(2,1)S(1)} %collective-permute-done.9.refs_2_), channel_id=1, source_target_pairs={{0,1},{1,0},{2,3},{3,2},{4,5},{5,4},{6,7},{7,6},{8,9},{9,8},{10,11... | collective-permute-start | bytes 294920 | tf_op jit(solution)/shard_map/ppermute | solution.py:310
  17.0 5.6 %collective-permute-start.10 = (bf16[32,1536]{1,0:T(8,128)(2,1)S(1)}, bf16[32,1536]{1,0:T(8,128)(2,1)S(1)}, u32[]{:S(2)}, u32[]{:S(2)}) collective-permute-start(bf16[32,1536]{1,0:T(8,128)(2,1)S(1)} %collective-permute-done.9.refs_2_), channel_id=1, source_target_pairs={{0,2},{1,3},{2,0},{3,1},{4,6},{5,7},{6,4},{7,5},{8,10},{9,11},{10,... | collective-permute-start | bytes 294920 | tf_op jit(solution)/shard_map/ppermute | solution.py:310
  18.5 4.2 %collective-permute-start.15 = (bf16[32,1536]{1,0:T(8,128)(2,1)S(1)}, bf16[32,1536]{1,0:T(8,128)(2,1)S(1)}, u32[]{:S(2)}, u32[]{:S(2)}) collective-permute-start(bf16[32,1536]{1,0:T(8,128)(2,1)S(1)} %collective-permute-done.6.refs_1_), channel_id=1, source_target_pairs={{0,1},{1,0},{2,3},{3,2},{4,5},{5,4},{6,7},{7,6},{8,9},{9,8},{10,11... | collective-permute-start | bytes 294920 | tf_op jit(solution)/shard_map/ppermute | solution.py:310
  18.7 6.0 %collective-permute-start.7 = (bf16[32,1536]{1,0:T(8,128)(2,1)S(1)}, bf16[32,1536]{1,0:T(8,128)(2,1)S(1)}, u32[]{:S(2)}, u32[]{:S(2)}) collective-permute-start(bf16[32,1536]{1,0:T(8,128)(2,1)S(1)} %collective-permute-done.6.refs_1_), channel_id=1, source_target_pairs={{0,2},{1,3},{2,0},{3,1},{4,6},{5,7},{6,4},{7,5},{8,10},{9,11},{10,... | collective-permute-start | bytes 294920 | tf_op jit(solution)/shard_map/ppermute | solution.py:310
  20.8 5.6 %collective-permute-start.4 = (bf16[32,1536]{1,0:T(8,128)(2,1)S(1)}, bf16[32,1536]{1,0:T(8,128)(2,1)S(1)}, u32[]{:S(2)}, u32[]{:S(2)}) collective-permute-start(bf16[32,1536]{1,0:T(8,128)(2,1)S(1)} %collective-permute-done.3.refs_0_), channel_id=1, source_target_pairs={{0,2},{1,3},{2,0},{3,1},{4,6},{5,7},{6,4},{7,5},{8,10},{9,11},{10,... | collective-permute-start | bytes 294920 | tf_op jit(solution)/shard_map/ppermute | solution.py:310
  21.8 4.7 %collective-permute-start.14 = (bf16[32,1536]{1,0:T(8,128)(2,1)S(1)}, bf16[32,1536]{1,0:T(8,128)(2,1)S(1)}, u32[]{:S(2)}, u32[]{:S(2)}) collective-permute-start(bf16[32,1536]{1,0:T(8,128)(2,1)S(1)} %collective-permute-done.3.refs_0_), channel_id=1, source_target_pairs={{0,1},{1,0},{2,3},{3,2},{4,5},{5,4},{6,7},{7,6},{8,9},{9,8},{10,11... | collective-permute-start | bytes 294920 | tf_op jit(solution)/shard_map/ppermute | solution.py:310
  22.6 5.5 %collective-permute-start.13 = (bf16[32,1536]{1,0:T(8,128)(2,1)S(1)}, bf16[32,1536]{1,0:T(8,128)(2,1)S(1)}, u32[]{:S(2)}, u32[]{:S(2)}) collective-permute-start(bf16[32,1536]{1,0:T(8,128)(2,1)S(1)} %collective-permute-done.12.refs_11_), channel_id=1, source_target_pairs={{0,1},{1,0},{2,3},{3,2},{4,5},{5,4},{6,7},{7,6},{8,9},{9,8},{10,11... | collective-permute-start | bytes 294920 | tf_op jit(solution)/shard_map/ppermute | solution.py:310
  22.6 5.5 %collective-permute-start.11 = (bf16[32,1536]{1,0:T(8,128)(2,1)S(1)}, bf16[32,1536]{1,0:T(8,128)(2,1)S(1)}, u32[]{:S(2)}, u32[]{:S(2)}) collective-permute-start(bf16[32,1536]{1,0:T(8,128)(2,1)S(1)} %collective-permute-done.10.refs_10_), channel_id=1, source_target_pairs={{0,1},{1,0},{2,3},{3,2},{4,5},{5,4},{6,7},{7,6},{8,9},{9,8},{10,11... | collective-permute-start | bytes 294920 | tf_op jit(solution)/shard_map/ppermute | solution.py:310
  24.7 3.4 %collective-permute-start.8 = (bf16[32,1536]{1,0:T(8,128)(2,1)S(1)}, bf16[32,1536]{1,0:T(8,128)(2,1)S(1)}, u32[]{:S(2)}, u32[]{:S(2)}) collective-permute-start(bf16[32,1536]{1,0:T(8,128)(2,1)S(1)} %collective-permute-done.7.refs_9_), channel_id=1, source_target_pairs={{0,1},{1,0},{2,3},{3,2},{4,5},{5,4},{6,7},{7,6},{8,9},{9,8},{10,11... | collective-permute-start | bytes 294920 | tf_op jit(solution)/shard_map/ppermute | solution.py:310
  26.5 1.7 %collective-permute-start.5 = (bf16[32,1536]{1,0:T(8,128)(2,1)S(1)}, bf16[32,1536]{1,0:T(8,128)(2,1)S(1)}, u32[]{:S(2)}, u32[]{:S(2)}) collective-permute-start(bf16[32,1536]{1,0:T(8,128)(2,1)S(1)} %collective-permute-done.4.refs_8_), channel_id=1, source_target_pairs={{0,1},{1,0},{2,3},{3,2},{4,5},{5,4},{6,7},{7,6},{8,9},{9,8},{10,11... | collective-permute-start | bytes 294920 | tf_op jit(solution)/shard_map/ppermute | solution.py:310
  29.3 2.6 %collective-permute-start.18 = (bf16[96,1536]{1,0:T(8,128)(2,1)S(1)}, bf16[96,1536]{1,0:T(8,128)(2,1)S(1)}, u32[]{:S(2)}, u32[]{:S(2)}) collective-permute-start(bf16[96,1536]{1,0:T(8,128)(2,1)S(1)} %get-tuple-element.70), channel_id=1, source_target_pairs={{0,1},{1,0},{2,3},{3,2},{4,5},{5,4},{6,7},{7,6},{8,9},{9,8},{10,11... | collective-permute-start | bytes 884744 | tf_op jit(solution)/shard_map/ppermute | solution.py:310
  29.9 1.3 %collective-permute-start.20 = (bf16[32,1536]{1,0:T(8,128)(2,1)S(1)}, bf16[32,1536]{1,0:T(8,128)(2,1)S(1)}, u32[]{:S(2)}, u32[]{:S(2)}) collective-permute-start(bf16[32,1536]{1,0:T(8,128)(2,1)S(1)} %get-tuple-element.81), channel_id=1, source_target_pairs={{0,1},{1,0},{2,3},{3,2},{4,5},{5,4},{6,7},{7,6},{8,9},{9,8},{10,11... | collective-permute-start | bytes 294920 | tf_op jit(solution)/shard_map/ppermute | solution.py:310
  31.3 5.7 %collective-permute-start.21 = (bf16[32,1536]{1,0:T(8,128)(2,1)S(1)}, bf16[32,1536]{1,0:T(8,128)(2,1)S(1)}, u32[]{:S(2)}, u32[]{:S(2)}) collective-permute-start(bf16[32,1536]{1,0:T(8,128)(2,1)S(1)} %shard_map.109), channel_id=1, source_target_pairs={{0,4},{4,0},{8,12},{12,8},{1,5},{5,1},{9,13},{13,9},{2,6},{6,2},{1... | collective-permute-start | bytes 294920 | tf_op jit(solution)/shard_map/ppermute | solution.py:310
  32.0 13.2 %collective-permute-start.23 = (bf16[32,1536]{1,0:T(8,128)(2,1)S(1)}, bf16[32,1536]{1,0:T(8,128)(2,1)S(1)}, u32[]{:S(2)}, u32[]{:S(2)}) collective-permute-start(bf16[32,1536]{1,0:T(8,128)(2,1)S(1)} %get-tuple-element.91), channel_id=1, source_target_pairs={{0,20},{4,16},{8,28},{12,24},{16,4},{20,0},{24,12},{28,8},{1,21},{... | collective-permute-start | bytes 294920 | tf_op jit(solution)/shard_map/ppermute | solution.py:317
  34.4 10.8 %collective-permute-start.19 = (bf16[32,1664]{1,0:T(8,128)(2,1)S(1)}, bf16[32,1664]{1,0:T(8,128)(2,1)S(1)}, u32[]{:S(2)}, u32[]{:S(2)}) collective-permute-start(bf16[32,1664]{1,0:T(8,128)(2,1)S(1)} %get-tuple-element.72), channel_id=1, source_target_pairs={{0,16},{4,20},{8,24},{12,28},{16,0},{20,4},{24,8},{28,12},{1,17},{... | collective-permute-start | bytes 319496 | tf_op jit(solution)/shard_map/ppermute | solution.py:317
  37.0 8.2 %collective-permute-start.22 = (bf16[32,1536]{1,0:T(8,128)(2,1)S(1)}, bf16[32,1536]{1,0:T(8,128)(2,1)S(1)}, u32[]{:S(2)}, u32[]{:S(2)}) collective-permute-start(bf16[32,1536]{1,0:T(8,128)(2,1)S(1)} %get-tuple-element.87), channel_id=1, source_target_pairs={{0,24},{4,28},{8,16},{12,20},{16,8},{20,12},{24,0},{28,4},{1,25},{... | collective-permute-start | bytes 294920 | tf_op jit(solution)/shard_map/ppermute | solution.py:317
  45.5 4.0 %collective-permute-start.24 = (bf16[16,1536]{1,0:T(8,128)(2,1)S(1)}, bf16[16,1536]{1,0:T(8,128)(2,1)S(1)}, u32[]{:S(2)}, u32[]{:S(2)}) collective-permute-start(bf16[16,1536]{1,0:T(8,128)(2,1)S(1)} %get-tuple-element.93), channel_id=1, source_target_pairs={{0,1},{1,0},{2,3},{3,2},{4,5},{5,4},{6,7},{7,6},{8,9},{9,8},{10,11... | collective-permute-start | bytes 147464 | tf_op jit(solution)/shard_map/ppermute | solution.py:310
  45.6 4.2 %collective-permute-start.25 = (bf16[16,1536]{1,0:T(8,128)(2,1)S(1)}, bf16[16,1536]{1,0:T(8,128)(2,1)S(1)}, u32[]{:S(2)}, u32[]{:S(2)}) collective-permute-start(bf16[16,1536]{1,0:T(8,128)(2,1)S(1)} %get-tuple-element.94), channel_id=1, source_target_pairs={{0,2},{1,3},{2,0},{3,1},{4,6},{5,7},{6,4},{7,5},{8,10},{9,11},{10,... | collective-permute-start | bytes 147464 | tf_op jit(solution)/shard_map/ppermute | solution.py:310
  47.1 3.7 %collective-permute-start.26 = (bf16[16,1536]{1,0:T(8,128)(2,1)S(1)}, bf16[16,1536]{1,0:T(8,128)(2,1)S(1)}, u32[]{:S(2)}, u32[]{:S(2)}) collective-permute-start(bf16[16,1536]{1,0:T(8,128)(2,1)S(1)} %get-tuple-element.95), channel_id=1, source_target_pairs={{0,3},{1,2},{2,1},{3,0},{4,7},{5,6},{6,5},{7,4},{8,11},{9,10},{10,... | collective-permute-start | bytes 147464 | tf_op jit(solution)/shard_map/ppermute | solution.py:310

commit v14 on v12

--- a/solution.py
+++ b/solution.py
@@ -286,7 +286,7 @@
         out[...] = tokens_ref[pl.ds(pl.multiple_of((e ^ steps) * rows, 16), rows), :]
 
 
-def finish_kernel(own_ref, core_ref, chip_ref, both_ref, out_ref):
+def finish_kernel(own_ref, chip_ref, both_ref, core_ref, out_ref):
     half = own_ref.shape[1]
     core = lax.axis_index("et") % 2
     mine = own_ref[...].astype(F32) + chip_ref[...].astype(F32)
@@ -406,7 +406,7 @@
         from_near,
         scratch=[pltpu.VMEM((FLAG, half), BF16)],
     )
-    back = [by_token[0]] + [swap(by_token[s], "et", s) for s in (1, 2, 3)]
+    back = [by_token[0]] + [swap(by_token[s], "et", s) for s in (2, 3, 1)]
     (handed,) = call(finish_kernel, [like((rows, width))], *back)
     grad_down = contract(act, dz, 0, 0).astype(BF16)
     return (handed[None, None], grad_gate[None], grad_up[None], grad_down[None])

time: 51.1 us -> 51.2 us (level)
  transfers between devices with their start and end apart: 26 -> 26, of which waited for: 11 -> 10; matrix products, arithmetic and copies ran while one was open for 12% -> 12% of each run, Pallas kernels for 10% -> 10%
where the time goes in v14:
time: 51.2 us; the launch traced here: 51 us
  starting transfers between devices  22 us (43%)
  waiting for transfers between devices  13.5 us (26%)
  Pallas kernels  8.6 us (17%)
  matrix products  6.08 us (12%)
  between operations  0.76 us (1%)
    ppermute x23, starting transfers between devices, swap(): return lax.ppermute(value, axis, spread(steps))  15.9 us
    ppermute x23, waiting for transfers between devices, swap(): return lax.ppermute(value, axis, spread(steps))  13 us
    pallas_call x10, Pallas kernels, call(): pl.pallas_call(kernel, out_shape=outs, in_specs=[space] * len(args), out_...  8.6 us
    ppermute x3, starting transfers between devices, hand(): return lax.ppermute(value, ('pipe', 'dp'), pairs)  6.14 us
    dot_general x3, matrix products, contract(): lax.dot_general(left, right, (((left_dim,), (right_dim,)), ((), ())), pre...  6.08 us
  transfers between devices with their start and end apart: 26, of which 10 were waited for; matrix products, arithmetic and copies ran while one was open for 12% of the time, Pallas kernels for 10%

profile of v14, /device:TPU:0, one launch (start us, length us, event | category | flops | bytes accessed | tf_op | source)
XLA Modules:
  0.0 51.0 jit_solution(206646729003330824)
XLA Ops:
  0.6 1.1 %shard_map.102 = (bf16[16,1664]{1,0:T(8,128)(2,1)S(1)}, bf16[16,1664]{1,0:T(8,128)(2,1)S(1)}, bf16[16,1664]{1,0:T(8,128)(2,1)S(1)}, bf16[16,1664]{1,0:T(8,128)(2,1)S(1)}) custom-call(bf16[16,3072]{1,0:T(8,128)(2,1)} %bitcast.27, bf16[16,3072]{1,0:T(8,128)(2,1)} %bitcast.28, s32[4,16]{1,0:T(4,128)} %bitcast.30, f32[4,16]{1,0:T(4,128)} %bitcast.31), custom_call_target="tpu_custom_call" | custom-call | bytes 410112 | tf_op jit(solution)/shard_map/pallas_call | solution.py:109
  1.7 0.5 %collective-permute-start = (bf16[16,1664]{1,0:T(8,128)(2,1)S(1)}, bf16[16,1664]{1,0:T(8,128)(2,1)S(1)}, u32[]{:S(2)}, u32[]{:S(2)}) collective-permute-start(bf16[16,1664]{1,0:T(8,128)(2,1)S(1)} %get-tuple-element.49), channel_id=1, source_target_pairs={{0,1},{1,0},{2,3},{3,2},{4,5},{5,4},{6,7},{7,6},{8,9},{9,8},{10,11... | collective-permute-start | bytes 159752 | tf_op jit(solution)/shard_map/ppermute | solution.py:299
  2.2 2.6 %collective-permute-start.1 = (bf16[16,1664]{1,0:T(8,128)(2,1)S(1)}, bf16[16,1664]{1,0:T(8,128)(2,1)S(1)}, u32[]{:S(2)}, u32[]{:S(2)}) collective-permute-start(bf16[16,1664]{1,0:T(8,128)(2,1)S(1)} %get-tuple-element.50), channel_id=1, source_target_pairs={{0,2},{1,3},{2,0},{3,1},{4,6},{5,7},{6,4},{7,5},{8,10},{9,11},{10,... | collective-permute-start | bytes 159752 | tf_op jit(solution)/shard_map/ppermute | solution.py:299
  4.8 0.1 collective-permute-start.2
  4.9 2.8 %shard_map.103 = (bf16[768,3072]{1,0:T(8,128)(2,1)S(1)}, bf16[336,3072]{1,0:T(8,128)(2,1)S(1)}) custom-call(bf16[336,3072]{1,0:T(8,128)(2,1)} %bitcast.22, bf16[336,3072]{1,0:T(8,128)(2,1)} %bitcast.23, bf16[336,3072]{1,0:T(8,128)(2,1)} %bitcast.24), custom_call_target="tpu_custom_call" | custom-call | bytes 12976128 | tf_op jit(solution)/shard_map/pallas_call | solution.py:109
  7.7 0.0 collective-permute-done.refs_1_
  7.8 0.9 %collective-permute-done.2.refs_3_ = bf16[16,1664]{1,0:T(8,128)(2,1)S(1)} collective-permute-done((bf16[16,1664]{1,0:T(8,128)(2,1)S(1)}, bf16[16,1664]{1,0:T(8,128)(2,1)S(1)}, u32[]{:S(2)}, u32[]{:S(2)}) %collective-permute-start.2) | collective-permute-done | bytes 53280 | tf_op jit(solution)/shard_map/ppermute | solution.py:299
  8.6 0.3 shard_map.104
  9.0 2.7 %collective-permute-start.9 = (bf16[32,1536]{1,0:T(8,128)(2,1)S(1)}, bf16[32,1536]{1,0:T(8,128)(2,1)S(1)}, u32[]{:S(2)}, u32[]{:S(2)}) collective-permute-start(bf16[32,1536]{1,0:T(8,128)(2,1)S(1)} %get-tuple-element.58.refs_3_), channel_id=1, source_target_pairs={{0,8},{4,12},{8,0},{12,4},{1,9},{5,13},{9,1},{13,5},{2,10},{6,14},... | collective-permute-start | bytes 294920 | tf_op jit(solution)/shard_map/ppermute | solution.py:299
  11.6 1.6 %collective-permute-start.6 = (bf16[32,1536]{1,0:T(8,128)(2,1)S(1)}, bf16[32,1536]{1,0:T(8,128)(2,1)S(1)}, u32[]{:S(2)}, u32[]{:S(2)}) collective-permute-start(bf16[32,1536]{1,0:T(8,128)(2,1)S(1)} %get-tuple-element.58.refs_3_), channel_id=1, source_target_pairs={{0,4},{4,0},{8,12},{12,8},{1,5},{5,1},{9,13},{13,9},{2,6},{6,2},{1... | collective-permute-start | bytes 294920 | tf_op jit(solution)/shard_map/ppermute | solution.py:299
  13.2 1.1 %collective-permute-start.12 = (bf16[32,1536]{1,0:T(8,128)(2,1)S(1)}, bf16[32,1536]{1,0:T(8,128)(2,1)S(1)}, u32[]{:S(2)}, u32[]{:S(2)}) collective-permute-start(bf16[32,1536]{1,0:T(8,128)(2,1)S(1)} %get-tuple-element.58.refs_3_), channel_id=1, source_target_pairs={{0,2},{1,3},{2,0},{3,1},{4,6},{5,7},{6,4},{7,5},{8,10},{9,11},{10,... | collective-permute-start | bytes 294920 | tf_op jit(solution)/shard_map/ppermute | solution.py:299
  14.3 0.2 collective-permute-start.3
  14.5 2.5 %collective-permute-done.9.refs_2_ = bf16[32,1536]{1,0:T(8,128)(2,1)S(1)} collective-permute-done((bf16[32,1536]{1,0:T(8,128)(2,1)S(1)}, bf16[32,1536]{1,0:T(8,128)(2,1)S(1)}, u32[]{:S(2)}, u32[]{:S(2)}) %collective-permute-start.9) | collective-permute-done | bytes 98336 | tf_op jit(solution)/shard_map/ppermute | solution.py:299
  17.0 0.0 collective-permute-start.16
  17.0 0.0 collective-permute-done.17.refs_7_
  17.0 1.4 %collective-permute-start.10 = (bf16[32,1536]{1,0:T(8,128)(2,1)S(1)}, bf16[32,1536]{1,0:T(8,128)(2,1)S(1)}, u32[]{:S(2)}, u32[]{:S(2)}) collective-permute-start(bf16[32,1536]{1,0:T(8,128)(2,1)S(1)} %collective-permute-done.9.refs_2_), channel_id=1, source_target_pairs={{0,2},{1,3},{2,0},{3,1},{4,6},{5,7},{6,4},{7,5},{8,10},{9,11},{10,... | collective-permute-start | bytes 294920 | tf_op jit(solution)/shard_map/ppermute | solution.py:299
  18.5 0.2 collective-permute-start.15
  18.7 0.6 %collective-permute-start.7 = (bf16[32,1536]{1,0:T(8,128)(2,1)S(1)}, bf16[32,1536]{1,0:T(8,128)(2,1)S(1)}, u32[]{:S(2)}, u32[]{:S(2)}) collective-permute-start(bf16[32,1536]{1,0:T(8,128)(2,1)S(1)} %collective-permute-done.6.refs_1_), channel_id=1, source_target_pairs={{0,2},{1,3},{2,0},{3,1},{4,6},{5,7},{6,4},{7,5},{8,10},{9,11},{10,... | collective-permute-start | bytes 294920 | tf_op jit(solution)/shard_map/ppermute | solution.py:299
  19.3 1.5 %collective-permute-done.3.refs_0_ = bf16[32,1536]{1,0:T(8,128)(2,1)S(1)} collective-permute-done((bf16[32,1536]{1,0:T(8,128)(2,1)S(1)}, bf16[32,1536]{1,0:T(8,128)(2,1)S(1)}, u32[]{:S(2)}, u32[]{:S(2)}) %collective-permute-start.3) | collective-permute-done | bytes 98336 | tf_op jit(solution)/shard_map/ppermute | solution.py:299
  20.8 0.9 %collective-permute-start.4 = (bf16[32,1536]{1,0:T(8,128)(2,1)S(1)}, bf16[32,1536]{1,0:T(8,128)(2,1)S(1)}, u32[]{:S(2)}, u32[]{:S(2)}) collective-permute-start(bf16[32,1536]{1,0:T(8,128)(2,1)S(1)} %collective-permute-done.3.refs_0_), channel_id=1, source_target_pairs={{0,2},{1,3},{2,0},{3,1},{4,6},{5,7},{6,4},{7,5},{8,10},{9,11},{10,... | collective-permute-start | bytes 294920 | tf_op jit(solution)/shard_map/ppermute | solution.py:299
  21.8 0.8 %collective-permute-done.10.refs_10_ = bf16[32,1536]{1,0:T(8,128)(2,1)S(1)} collective-permute-done((bf16[32,1536]{1,0:T(8,128)(2,1)S(1)}, bf16[32,1536]{1,0:T(8,128)(2,1)S(1)}, u32[]{:S(2)}, u32[]{:S(2)}) %collective-permute-start.10) | collective-permute-done | bytes 98336 | tf_op jit(solution)/shard_map/ppermute | solution.py:299
  22.6 0.5 collective-permute-start.11
  23.2 1.6 %collective-permute-done.7.refs_9_ = bf16[32,1536]{1,0:T(8,128)(2,1)S(1)} collective-permute-done((bf16[32,1536]{1,0:T(8,128)(2,1)S(1)}, bf16[32,1536]{1,0:T(8,128)(2,1)S(1)}, u32[]{:S(2)}, u32[]{:S(2)}) %collective-permute-start.7) | collective-permute-done | bytes 98336 | tf_op jit(solution)/shard_map/ppermute | solution.py:299
  24.7 1.7 %collective-permute-done.4.refs_8_ = bf16[32,1536]{1,0:T(8,128)(2,1)S(1)} collective-permute-done((bf16[32,1536]{1,0:T(8,128)(2,1)S(1)}, bf16[32,1536]{1,0:T(8,128)(2,1)S(1)}, u32[]{:S(2)}, u32[]{:S(2)}) %collective-permute-start.4) | collective-permute-done | bytes 98336 | tf_op jit(solution)/shard_map/ppermute | solution.py:299
  26.5 0.0 collective-permute-start.5
  26.5 0.0 collective-permute-done.14.refs_4_
  26.5 1.6 %shard_map.105 = (bf16[128,3072]{1,0:T(8,128)(2,1)S(1)}, bf16[128,3072]{1,0:T(8,128)(2,1)S(1)}, f32[128,768]{1,0:T(8,128)S(1)}, f32[128,336]{1,0:T(8,128)S(1)}) custom-call(bf16[32,1536]{1,0:T(8,128)(2,1)S(1)} %collective-permute-done.3.refs_0_, bf16[32,1536]{1,0:T(8,128)(2,1)S(1)} %collective-permute-done.6.refs_1_, ...), custom_call_target="tpu_custom_call" | custom-call | tf_op jit(solution)/shard_map/pallas_call | solution.py:109
  28.1 0.0 collective-permute-done.13.refs_3_
  28.1 0.0 collective-permute-done.11.refs_2_
  28.1 1.2 %shard_map.106 = (bf16[128,3072]{1,0:T(8,128)(2,1)S(1)}, bf16[128,3072]{1,0:T(8,128)(2,1)S(1)}, bf16[128,336]{1,0:T(8,128)(2,1)S(1)}, bf16[128,336]{1,0:T(8,128)...) custom-call(bf16[32,1536]{1,0:T(8,128)(2,1)S(1)} %collective-permute, ...), custom_call_target="tpu_custom_call", output_to_operand_aliasing={{0}: (6, {}), {1}: (7, {})} | custom-call | tf_op jit(solution)/shard_map/pallas_call | solution.py:109
  29.3 0.5 %collective-permute-start.18 = (bf16[128,1536]{1,0:T(8,128)(2,1)S(1)}, bf16[128,1536]{1,0:T(8,128)(2,1)S(1)}, u32[]{:S(2)}, u32[]{:S(2)}) collective-permute-start(bf16[128,1536]{1,0:T(8,128)(2,1)S(1)} %get-tuple-element.66), channel_id=1, source_target_pairs={{0,1},{1,0},{2,3},{3,2},{4,5},{5,4},{6,7},{7,6},{8,9},{9,8},{10,11... | collective-permute-start | bytes 1179656 | tf_op jit(solution)/shard_map/ppermute | solution.py:299
  29.9 0.5 shard_map.107.own_ref
  30.4 0.9 %collective-permute-done.18.other_ref = bf16[128,1536]{1,0:T(8,128)(2,1)S(1)} collective-permute-done((bf16[128,1536]{1,0:T(8,128)(2,1)S(1)}, bf16[128,1536]{1,0:T(8,128)(2,1)S(1)}, u32[]{:S(2)}, u32[]{:S(2)}) %collective-permute-start.18) | collective-permute-done | bytes 393248 | tf_op jit(solution)/shard_map/ppermute | solution.py:299
  31.2 0.1 shard_map.108
  31.3 0.7 %collective-permute-start.20 = (bf16[32,1536]{1,0:T(8,128)(2,1)S(1)}, bf16[32,1536]{1,0:T(8,128)(2,1)S(1)}, u32[]{:S(2)}, u32[]{:S(2)}) collective-permute-start(bf16[32,1536]{1,0:T(8,128)(2,1)S(1)} %get-tuple-element.75), channel_id=1, source_target_pairs={{0,4},{4,0},{8,12},{12,8},{1,5},{5,1},{9,13},{13,9},{2,6},{6,2},{1... | collective-permute-start | bytes 294920 | tf_op jit(solution)/shard_map/ppermute | solution.py:299
  32.0 2.3 %collective-permute-start.22 = (bf16[32,1536]{1,0:T(8,128)(2,1)S(1)}, bf16[32,1536]{1,0:T(8,128)(2,1)S(1)}, u32[]{:S(2)}, u32[]{:S(2)}) collective-permute-start(bf16[32,1536]{1,0:T(8,128)(2,1)S(1)} %get-tuple-element.83), channel_id=1, source_target_pairs={{0,20},{4,16},{8,28},{12,24},{16,4},{20,0},{24,12},{28,8},{1,21},{... | collective-permute-start | bytes 294920 | tf_op jit(solution)/shard_map/ppermute | solution.py:306
  34.3 0.5 %collective-permute-start.19 = (bf16[32,1664]{1,0:T(8,128)(2,1)S(1)}, bf16[32,1664]{1,0:T(8,128)(2,1)S(1)}, u32[]{:S(2)}, u32[]{:S(2)}) collective-permute-start(bf16[32,1664]{1,0:T(8,128)(2,1)S(1)} %get-tuple-element.68), channel_id=1, source_target_pairs={{0,16},{4,20},{8,24},{12,28},{16,0},{20,4},{24,8},{28,12},{1,17},{... | collective-permute-start | bytes 319496 | tf_op jit(solution)/shard_map/ppermute | solution.py:306
  34.9 2.1 %collective-permute-done.20.right_ref = bf16[32,1536]{1,0:T(8,128)(2,1)S(1)} collective-permute-done((bf16[32,1536]{1,0:T(8,128)(2,1)S(1)}, bf16[32,1536]{1,0:T(8,128)(2,1)S(1)}, u32[]{:S(2)}, u32[]{:S(2)}) %collective-permute-start.20) | collective-permute-done | bytes 98336 | tf_op jit(solution)/shard_map/ppermute | solution.py:299
  37.0 3.3 %collective-permute-start.21 = (bf16[32,1536]{1,0:T(8,128)(2,1)S(1)}, bf16[32,1536]{1,0:T(8,128)(2,1)S(1)}, u32[]{:S(2)}, u32[]{:S(2)}) collective-permute-start(bf16[32,1536]{1,0:T(8,128)(2,1)S(1)} %get-tuple-element.78), channel_id=1, source_target_pairs={{0,24},{4,28},{8,16},{12,20},{16,8},{20,12},{24,0},{28,4},{1,25},{... | collective-permute-start | bytes 294920 | tf_op jit(solution)/shard_map/ppermute | solution.py:306
  40.3 2.0 %convolution_convert_fusion.2 = bf16[336,3072]{1,0:T(8,128)(2,1)} fusion(bf16[128,336]{1,0:T(8,128)(2,1)S(1)} %get-tuple-element.79, bf16[128,3072]{1,0:T(8,128)(2,1)S(1)} %get-tuple-element.80), kind=kOutput, calls=%fused_computation.2 | convolution fusion | flops 265273344 | bytes 2936832 | tf_op jit(solution)/shard_map/dot_general | solution.py:40
  42.3 2.0 %convolution_convert_fusion.1 = bf16[336,3072]{1,0:T(8,128)(2,1)} fusion(bf16[128,336]{1,0:T(8,128)(2,1)S(1)} %get-tuple-element.81, bf16[128,3072]{1,0:T(8,128)(2,1)S(1)} %get-tuple-element.80), kind=kOutput, calls=%fused_computation.1 | convolution fusion | flops 265273344 | bytes 2936832 | tf_op jit(solution)/shard_map/dot_general | solution.py:40
  44.3 0.5 collective-permute-done.21.refs_0_
  44.8 0.3 shard_map.110
  45.1 1.3 %collective-permute-start.23 = (bf16[16,1536]{1,0:T(8,128)(2,1)S(1)}, bf16[16,1536]{1,0:T(8,128)(2,1)S(1)}, u32[]{:S(2)}, u32[]{:S(2)}) collective-permute-start(bf16[16,1536]{1,0:T(8,128)(2,1)S(1)} %get-tuple-element.85), channel_id=1, source_target_pairs={{0,2},{1,3},{2,0},{3,1},{4,6},{5,7},{6,4},{7,5},{8,10},{9,11},{10,... | collective-permute-start | bytes 147464 | tf_op jit(solution)/shard_map/ppermute | solution.py:299
  46.5 0.9 %collective-permute-start.25 = (bf16[16,1536]{1,0:T(8,128)(2,1)S(1)}, bf16[16,1536]{1,0:T(8,128)(2,1)S(1)}, u32[]{:S(2)}, u32[]{:S(2)}) collective-permute-start(bf16[16,1536]{1,0:T(8,128)(2,1)S(1)} %get-tuple-element.87), channel_id=1, source_target_pairs={{0,1},{1,0},{2,3},{3,2},{4,5},{5,4},{6,7},{7,6},{8,9},{9,8},{10,11... | collective-permute-start | bytes 147464 | tf_op jit(solution)/shard_map/ppermute | solution.py:299
  47.4 2.0 %fusion = bf16[1,336,3072]{2,1,0:T(8,128)(2,1)} fusion(bf16[128,336]{1,0:T(8,128)(2,1)S(1)} %get-tuple-element.90, bf16[128,3072]{1,0:T(8,128)(2,1)S(1)} %get-tuple-element.91), kind=kOutput, calls=%fused_computation.3 | convolution fusion | flops 265273344 | bytes 2936832 | tf_op jit(solution)/shard_map/dot_general | solution.py:40
  49.4 1.0 %collective-permute-done.24.both_ref = bf16[16,1536]{1,0:T(8,128)(2,1)S(1)} collective-permute-done((bf16[16,1536]{1,0:T(8,128)(2,1)S(1)}, bf16[16,1536]{1,0:T(8,128)(2,1)S(1)}, u32[]{:S(2)}, u32[]{:S(2)}) %collective-permute-start.24) | collective-permute-done | bytes 49184 | tf_op jit(solution)/shard_map/ppermute | solution.py:299
  50.4 0.7 %shard_map.111 = bf16[16,3072]{1,0:T(8,128)(2,1)} custom-call(bf16[16,1536]{1,0:T(8,128)(2,1)S(1)} %get-tuple-element.84.own_ref, bf16[16,1536]{1,0:T(8,128)(2,1)S(1)} %collective-permute-done.23.chip_ref, bf16[16,1536]{1,0:T(8,128)(2,1)S(1)} %collective-permute-done.24.both_ref, bf16[16,1536]{1,0:T(8,128)(2,1)S(1)} %collective-permute-done.25.core_ref), custom_call_target="tpu_custom_call" | custom-call | tf_op jit(solution)/shard_map/pallas_call | solution.py:109
  (17 shorter events, 0.1 us)
Async XLA Ops:
  1.7 6.0 %collective-permute-start = (bf16[16,1664]{1,0:T(8,128)(2,1)S(1)}, bf16[16,1664]{1,0:T(8,128)(2,1)S(1)}, u32[]{:S(2)}, u32[]{:S(2)}) collective-permute-start(bf16[16,1664]{1,0:T(8,128)(2,1)S(1)} %get-tuple-element.49), channel_id=1, source_target_pairs={{0,1},{1,0},{2,3},{3,2},{4,5},{5,4},{6,7},{7,6},{8,9},{9,8},{10,11... | collective-permute-start | bytes 159752 | tf_op jit(solution)/shard_map/ppermute | solution.py:299
  2.2 5.5 %collective-permute-start.1 = (bf16[16,1664]{1,0:T(8,128)(2,1)S(1)}, bf16[16,1664]{1,0:T(8,128)(2,1)S(1)}, u32[]{:S(2)}, u32[]{:S(2)}) collective-permute-start(bf16[16,1664]{1,0:T(8,128)(2,1)S(1)} %get-tuple-element.50), channel_id=1, source_target_pairs={{0,2},{1,3},{2,0},{3,1},{4,6},{5,7},{6,4},{7,5},{8,10},{9,11},{10,... | collective-permute-start | bytes 159752 | tf_op jit(solution)/shard_map/ppermute | solution.py:299
  4.8 3.8 %collective-permute-start.2 = (bf16[16,1664]{1,0:T(8,128)(2,1)S(1)}, bf16[16,1664]{1,0:T(8,128)(2,1)S(1)}, u32[]{:S(2)}, u32[]{:S(2)}) collective-permute-start(bf16[16,1664]{1,0:T(8,128)(2,1)S(1)} %get-tuple-element.51), channel_id=1, source_target_pairs={{0,3},{1,2},{2,1},{3,0},{4,7},{5,6},{6,5},{7,4},{8,11},{9,10},{10,... | collective-permute-start | bytes 159752 | tf_op jit(solution)/shard_map/ppermute | solution.py:299
  9.0 8.1 %collective-permute-start.9 = (bf16[32,1536]{1,0:T(8,128)(2,1)S(1)}, bf16[32,1536]{1,0:T(8,128)(2,1)S(1)}, u32[]{:S(2)}, u32[]{:S(2)}) collective-permute-start(bf16[32,1536]{1,0:T(8,128)(2,1)S(1)} %get-tuple-element.58.refs_3_), channel_id=1, source_target_pairs={{0,8},{4,12},{8,0},{12,4},{1,9},{5,13},{9,1},{13,5},{2,10},{6,14},... | collective-permute-start | bytes 294920 | tf_op jit(solution)/shard_map/ppermute | solution.py:299
  11.6 5.4 %collective-permute-start.17 = (bf16[32,1536]{1,0:T(8,128)(2,1)S(1)}, bf16[32,1536]{1,0:T(8,128)(2,1)S(1)}, u32[]{:S(2)}, u32[]{:S(2)}) collective-permute-start(bf16[32,1536]{1,0:T(8,128)(2,1)S(1)} %get-tuple-element.58.refs_3_), channel_id=1, source_target_pairs={{0,1},{1,0},{2,3},{3,2},{4,5},{5,4},{6,7},{7,6},{8,9},{9,8},{10,11... | collective-permute-start | bytes 294920 | tf_op jit(solution)/shard_map/ppermute | solution.py:299
  11.6 6.8 %collective-permute-start.6 = (bf16[32,1536]{1,0:T(8,128)(2,1)S(1)}, bf16[32,1536]{1,0:T(8,128)(2,1)S(1)}, u32[]{:S(2)}, u32[]{:S(2)}) collective-permute-start(bf16[32,1536]{1,0:T(8,128)(2,1)S(1)} %get-tuple-element.58.refs_3_), channel_id=1, source_target_pairs={{0,4},{4,0},{8,12},{12,8},{1,5},{5,1},{9,13},{13,9},{2,6},{6,2},{1... | collective-permute-start | bytes 294920 | tf_op jit(solution)/shard_map/ppermute | solution.py:299
  13.2 5.5 %collective-permute-start.12 = (bf16[32,1536]{1,0:T(8,128)(2,1)S(1)}, bf16[32,1536]{1,0:T(8,128)(2,1)S(1)}, u32[]{:S(2)}, u32[]{:S(2)}) collective-permute-start(bf16[32,1536]{1,0:T(8,128)(2,1)S(1)} %get-tuple-element.58.refs_3_), channel_id=1, source_target_pairs={{0,2},{1,3},{2,0},{3,1},{4,6},{5,7},{6,4},{7,5},{8,10},{9,11},{10,... | collective-permute-start | bytes 294920 | tf_op jit(solution)/shard_map/ppermute | solution.py:299
  14.3 6.6 %collective-permute-start.3 = (bf16[32,1536]{1,0:T(8,128)(2,1)S(1)}, bf16[32,1536]{1,0:T(8,128)(2,1)S(1)}, u32[]{:S(2)}, u32[]{:S(2)}) collective-permute-start(bf16[32,1536]{1,0:T(8,128)(2,1)S(1)} %get-tuple-element.58.refs_3_), channel_id=1, source_target_pairs={{0,12},{4,8},{8,4},{12,0},{1,13},{5,9},{9,5},{13,1},{2,14},{6,10},... | collective-permute-start | bytes 294920 | tf_op jit(solution)/shard_map/ppermute | solution.py:299
  17.0 4.8 %collective-permute-start.16 = (bf16[32,1536]{1,0:T(8,128)(2,1)S(1)}, bf16[32,1536]{1,0:T(8,128)(2,1)S(1)}, u32[]{:S(2)}, u32[]{:S(2)}) collective-permute-start(bf16[32,1536]{1,0:T(8,128)(2,1)S(1)} %collective-permute-done.9.refs_2_), channel_id=1, source_target_pairs={{0,1},{1,0},{2,3},{3,2},{4,5},{5,4},{6,7},{7,6},{8,9},{9,8},{10,11... | collective-permute-start | bytes 294920 | tf_op jit(solution)/shard_map/ppermute | solution.py:299
  17.0 5.6 %collective-permute-start.10 = (bf16[32,1536]{1,0:T(8,128)(2,1)S(1)}, bf16[32,1536]{1,0:T(8,128)(2,1)S(1)}, u32[]{:S(2)}, u32[]{:S(2)}) collective-permute-start(bf16[32,1536]{1,0:T(8,128)(2,1)S(1)} %collective-permute-done.9.refs_2_), channel_id=1, source_target_pairs={{0,2},{1,3},{2,0},{3,1},{4,6},{5,7},{6,4},{7,5},{8,10},{9,11},{10,... | collective-permute-start | bytes 294920 | tf_op jit(solution)/shard_map/ppermute | solution.py:299
  18.5 4.2 %collective-permute-start.15 = (bf16[32,1536]{1,0:T(8,128)(2,1)S(1)}, bf16[32,1536]{1,0:T(8,128)(2,1)S(1)}, u32[]{:S(2)}, u32[]{:S(2)}) collective-permute-start(bf16[32,1536]{1,0:T(8,128)(2,1)S(1)} %collective-permute-done.6.refs_1_), channel_id=1, source_target_pairs={{0,1},{1,0},{2,3},{3,2},{4,5},{5,4},{6,7},{7,6},{8,9},{9,8},{10,11... | collective-permute-start | bytes 294920 | tf_op jit(solution)/shard_map/ppermute | solution.py:299
  18.7 6.0 %collective-permute-start.7 = (bf16[32,1536]{1,0:T(8,128)(2,1)S(1)}, bf16[32,1536]{1,0:T(8,128)(2,1)S(1)}, u32[]{:S(2)}, u32[]{:S(2)}) collective-permute-start(bf16[32,1536]{1,0:T(8,128)(2,1)S(1)} %collective-permute-done.6.refs_1_), channel_id=1, source_target_pairs={{0,2},{1,3},{2,0},{3,1},{4,6},{5,7},{6,4},{7,5},{8,10},{9,11},{10,... | collective-permute-start | bytes 294920 | tf_op jit(solution)/shard_map/ppermute | solution.py:299
  20.8 5.6 %collective-permute-start.4 = (bf16[32,1536]{1,0:T(8,128)(2,1)S(1)}, bf16[32,1536]{1,0:T(8,128)(2,1)S(1)}, u32[]{:S(2)}, u32[]{:S(2)}) collective-permute-start(bf16[32,1536]{1,0:T(8,128)(2,1)S(1)} %collective-permute-done.3.refs_0_), channel_id=1, source_target_pairs={{0,2},{1,3},{2,0},{3,1},{4,6},{5,7},{6,4},{7,5},{8,10},{9,11},{10,... | collective-permute-start | bytes 294920 | tf_op jit(solution)/shard_map/ppermute | solution.py:299
  21.8 4.7 %collective-permute-start.14 = (bf16[32,1536]{1,0:T(8,128)(2,1)S(1)}, bf16[32,1536]{1,0:T(8,128)(2,1)S(1)}, u32[]{:S(2)}, u32[]{:S(2)}) collective-permute-start(bf16[32,1536]{1,0:T(8,128)(2,1)S(1)} %collective-permute-done.3.refs_0_), channel_id=1, source_target_pairs={{0,1},{1,0},{2,3},{3,2},{4,5},{5,4},{6,7},{7,6},{8,9},{9,8},{10,11... | collective-permute-start | bytes 294920 | tf_op jit(solution)/shard_map/ppermute | solution.py:299
  22.6 5.5 %collective-permute-start.13 = (bf16[32,1536]{1,0:T(8,128)(2,1)S(1)}, bf16[32,1536]{1,0:T(8,128)(2,1)S(1)}, u32[]{:S(2)}, u32[]{:S(2)}) collective-permute-start(bf16[32,1536]{1,0:T(8,128)(2,1)S(1)} %collective-permute-done.12.refs_11_), channel_id=1, source_target_pairs={{0,1},{1,0},{2,3},{3,2},{4,5},{5,4},{6,7},{7,6},{8,9},{9,8},{10,11... | collective-permute-start | bytes 294920 | tf_op jit(solution)/shard_map/ppermute | solution.py:299
  22.6 5.5 %collective-permute-start.11 = (bf16[32,1536]{1,0:T(8,128)(2,1)S(1)}, bf16[32,1536]{1,0:T(8,128)(2,1)S(1)}, u32[]{:S(2)}, u32[]{:S(2)}) collective-permute-start(bf16[32,1536]{1,0:T(8,128)(2,1)S(1)} %collective-permute-done.10.refs_10_), channel_id=1, source_target_pairs={{0,1},{1,0},{2,3},{3,2},{4,5},{5,4},{6,7},{7,6},{8,9},{9,8},{10,11... | collective-permute-start | bytes 294920 | tf_op jit(solution)/shard_map/ppermute | solution.py:299
  24.7 3.4 %collective-permute-start.8 = (bf16[32,1536]{1,0:T(8,128)(2,1)S(1)}, bf16[32,1536]{1,0:T(8,128)(2,1)S(1)}, u32[]{:S(2)}, u32[]{:S(2)}) collective-permute-start(bf16[32,1536]{1,0:T(8,128)(2,1)S(1)} %collective-permute-done.7.refs_9_), channel_id=1, source_target_pairs={{0,1},{1,0},{2,3},{3,2},{4,5},{5,4},{6,7},{7,6},{8,9},{9,8},{10,11... | collective-permute-start | bytes 294920 | tf_op jit(solution)/shard_map/ppermute | solution.py:299
  26.5 1.7 %collective-permute-start.5 = (bf16[32,1536]{1,0:T(8,128)(2,1)S(1)}, bf16[32,1536]{1,0:T(8,128)(2,1)S(1)}, u32[]{:S(2)}, u32[]{:S(2)}) collective-permute-start(bf16[32,1536]{1,0:T(8,128)(2,1)S(1)} %collective-permute-done.4.refs_8_), channel_id=1, source_target_pairs={{0,1},{1,0},{2,3},{3,2},{4,5},{5,4},{6,7},{7,6},{8,9},{9,8},{10,11... | collective-permute-start | bytes 294920 | tf_op jit(solution)/shard_map/ppermute | solution.py:299
  29.3 1.9 %collective-permute-start.18 = (bf16[128,1536]{1,0:T(8,128)(2,1)S(1)}, bf16[128,1536]{1,0:T(8,128)(2,1)S(1)}, u32[]{:S(2)}, u32[]{:S(2)}) collective-permute-start(bf16[128,1536]{1,0:T(8,128)(2,1)S(1)} %get-tuple-element.66), channel_id=1, source_target_pairs={{0,1},{1,0},{2,3},{3,2},{4,5},{5,4},{6,7},{7,6},{8,9},{9,8},{10,11... | collective-permute-start | bytes 1179656 | tf_op jit(solution)/shard_map/ppermute | solution.py:299
  31.3 5.7 %collective-permute-start.20 = (bf16[32,1536]{1,0:T(8,128)(2,1)S(1)}, bf16[32,1536]{1,0:T(8,128)(2,1)S(1)}, u32[]{:S(2)}, u32[]{:S(2)}) collective-permute-start(bf16[32,1536]{1,0:T(8,128)(2,1)S(1)} %get-tuple-element.75), channel_id=1, source_target_pairs={{0,4},{4,0},{8,12},{12,8},{1,5},{5,1},{9,13},{13,9},{2,6},{6,2},{1... | collective-permute-start | bytes 294920 | tf_op jit(solution)/shard_map/ppermute | solution.py:299
  32.0 12.8 %collective-permute-start.22 = (bf16[32,1536]{1,0:T(8,128)(2,1)S(1)}, bf16[32,1536]{1,0:T(8,128)(2,1)S(1)}, u32[]{:S(2)}, u32[]{:S(2)}) collective-permute-start(bf16[32,1536]{1,0:T(8,128)(2,1)S(1)} %get-tuple-element.83), channel_id=1, source_target_pairs={{0,20},{4,16},{8,28},{12,24},{16,4},{20,0},{24,12},{28,8},{1,21},{... | collective-permute-start | bytes 294920 | tf_op jit(solution)/shard_map/ppermute | solution.py:306
  34.3 10.5 %collective-permute-start.19 = (bf16[32,1664]{1,0:T(8,128)(2,1)S(1)}, bf16[32,1664]{1,0:T(8,128)(2,1)S(1)}, u32[]{:S(2)}, u32[]{:S(2)}) collective-permute-start(bf16[32,1664]{1,0:T(8,128)(2,1)S(1)} %get-tuple-element.68), channel_id=1, source_target_pairs={{0,16},{4,20},{8,24},{12,28},{16,0},{20,4},{24,8},{28,12},{1,17},{... | collective-permute-start | bytes 319496 | tf_op jit(solution)/shard_map/ppermute | solution.py:306
  37.0 7.8 %collective-permute-start.21 = (bf16[32,1536]{1,0:T(8,128)(2,1)S(1)}, bf16[32,1536]{1,0:T(8,128)(2,1)S(1)}, u32[]{:S(2)}, u32[]{:S(2)}) collective-permute-start(bf16[32,1536]{1,0:T(8,128)(2,1)S(1)} %get-tuple-element.78), channel_id=1, source_target_pairs={{0,24},{4,28},{8,16},{12,20},{16,8},{20,12},{24,0},{28,4},{1,25},{... | collective-permute-start | bytes 294920 | tf_op jit(solution)/shard_map/ppermute | solution.py:306
  45.1 4.2 %collective-permute-start.23 = (bf16[16,1536]{1,0:T(8,128)(2,1)S(1)}, bf16[16,1536]{1,0:T(8,128)(2,1)S(1)}, u32[]{:S(2)}, u32[]{:S(2)}) collective-permute-start(bf16[16,1536]{1,0:T(8,128)(2,1)S(1)} %get-tuple-element.85), channel_id=1, source_target_pairs={{0,2},{1,3},{2,0},{3,1},{4,6},{5,7},{6,4},{7,5},{8,10},{9,11},{10,... | collective-permute-start | bytes 147464 | tf_op jit(solution)/shard_map/ppermute | solution.py:299
  46.5 3.9 %collective-permute-start.24 = (bf16[16,1536]{1,0:T(8,128)(2,1)S(1)}, bf16[16,1536]{1,0:T(8,128)(2,1)S(1)}, u32[]{:S(2)}, u32[]{:S(2)}) collective-permute-start(bf16[16,1536]{1,0:T(8,128)(2,1)S(1)} %get-tuple-element.86), channel_id=1, source_target_pairs={{0,3},{1,2},{2,1},{3,0},{4,7},{5,6},{6,5},{7,4},{8,11},{9,10},{10,... | collective-permute-start | bytes 147464 | tf_op jit(solution)/shard_map/ppermute | solution.py:299
  46.5 3.9 %collective-permute-start.25 = (bf16[16,1536]{1,0:T(8,128)(2,1)S(1)}, bf16[16,1536]{1,0:T(8,128)(2,1)S(1)}, u32[]{:S(2)}, u32[]{:S(2)}) collective-permute-start(bf16[16,1536]{1,0:T(8,128)(2,1)S(1)} %get-tuple-element.87), channel_id=1, source_target_pairs={{0,1},{1,0},{2,3},{3,2},{4,5},{5,4},{6,7},{7,6},{8,9},{9,8},{10,11... | collective-permute-start | bytes 147464 | tf_op jit(solution)/shard_map/ppermute | solution.py:299
